TPU v7x, 32 devices: a whole 2x2x4 slice. The times are simulated.
32 devices in a mesh: gx: 8 (over y, x, core), gy: 4 (over z).
Axes of the slice: x: 2, y: 2, z: 4, core: 2. Of those that a mesh axis runs over, the one named last changes fastest.
Arguments:
- particles: bfloat16 [4096, 128], P(('gx', 'gy')), may hold values from -6 to 6
- send_counts: int32 [32, 32], P(('gx', 'gy')), may hold values from 0 to 8, as said below
- cell_lists: int32 [32, 256], P(('gx', 'gy')), may hold values from 0 to 4095
- base_field: bfloat16 [64, 8, 64, 256], P(None, 'gx', 'gy'), may hold values from -6 to 6
- proj_weight: bfloat16 [128, 64], replicated, may hold values from -0.5 to 0.5
- conv_weight: bfloat16 [27, 64, 64], replicated, may hold values from -0.15625 to 0.15625
- cotangent: bfloat16 [64, 8, 64, 256], P(None, 'gx', 'gy'), may hold values from -6 to 6
Outputs:
- out_field: bfloat16 [64, 8, 64, 256], P(None, 'gx', 'gy')
- row_grads: float32 [4096, 128], P(('gx', 'gy'))
- conv_grad: float32 [27, 64, 64], replicated
- proj_grad: float32 [128, 64], replicated
Inputs may be any that keep to these rules, and one draw needn't show every extreme that they name: `send_counts`: row s holds how many of source s's 128 rows go to each owner; each row sums to 128; source s's particle rows are listed grouped by owner in increasing order; at most 8 from one source to one owner, and some owner receives 8 from every source. `cell_lists`: entry s * 8 + r of owner d's row is the local cell of the r-th row that source s sends to d; entries of unused slots are ignored.
All inputs are finite; a program needn't handle non-finite values.
Results may differ from a plain program's by a relative error of at most 0.0041.
Values may be sent and summed in bfloat16 or wider, within the bound.
No kernel may reach another device: no remote copies, remote signals or barrier semaphores. Data moves between devices by JAX's collectives and lax.ppermute only.
A program may use at most 64 MiB of HBM per device.

v0:
```python
import math

import jax
import jax.numpy as jnp
from jax import lax
from jax.sharding import PartitionSpec as P


def padded_2(block, sides, width):
    for axis, dim in sides:
        count = lax.axis_size(axis)
        forward = [(i, i + 1) for i in range(count - 1)]
        forward.append((count - 1, 0))
        backward = [(target, source) for source, target in forward]
        low = lax.ppermute(
            lax.slice_in_dim(block, block.shape[dim] - width, None, axis=dim), axis, forward
        )
        high = lax.ppermute(lax.slice_in_dim(block, 0, width, axis=dim), axis, backward)
        block = jnp.concatenate([low, block, high], axis=dim)
    return block


def taps():
    return [(dx, dy, dz) for dx in (-1, 0, 1) for dy in (-1, 0, 1) for dz in (-1, 0, 1)]


def wrap_depth(padded):
    return jnp.concatenate([padded[..., -1:], padded, padded[..., :1]], axis=3)


def route_out(payload, ndev, slots):
    width = payload.shape[1]
    moved = lax.all_to_all(
        payload.reshape(ndev, slots, width), ("gx", "gy"), split_axis=0, concat_axis=0, tiled=True
    )
    return moved.reshape(ndev * slots, width)


def route_back(payload, ndev, slots):
    width = payload.shape[1]
    moved = lax.all_to_all(
        payload.reshape(ndev, slots, width), ("gx", "gy"), split_axis=0, concat_axis=0, tiled=True
    )
    return moved.reshape(ndev * slots, width)


def paint(projected, cells, count):
    block = math.gcd(count, 2048)

    def one_block(start):
        ids = start + jnp.arange(block, dtype=jnp.int32)
        onehot = (cells[:, None] == ids[None, :]).astype(jnp.bfloat16)
        return lax.dot_general(
            projected, onehot, (((0,), (0,)), ((), ())), preferred_element_type=jnp.float32
        )

    starts = jnp.arange(count // block, dtype=jnp.int32) * block
    blocks = lax.map(one_block, starts)
    return blocks.transpose(1, 0, 2).reshape(projected.shape[1], count)


def cut_window(full_pad, offs, sizes):
    dx, dy, dz = offs
    cx, cy, nz = sizes
    return full_pad[:, 1 + dx : 1 + dx + cx, 1 + dy : 1 + dy + cy, 1 + dz : 1 + dz + nz]


def local(particles, send_counts, cell_lists, base_field, proj_weight, conv_weight, cotangent):
    ndev = send_counts.shape[1]
    nrows, feats = particles.shape
    chans, cx, cy, nz = base_field.shape
    sizes = (cx, cy, nz)
    slots = cell_lists.shape[1] // ndev
    count = cx * cy * nz
    counts = send_counts[0]
    offsets = jnp.cumsum(counts) - counts
    lanes = jnp.arange(slots, dtype=jnp.int32)
    index = offsets[:, None] + lanes[None, :]
    valid = lanes[None, :] < counts[:, None]
    picked = jnp.take(particles, jnp.clip(index, 0, nrows - 1).reshape(-1), axis=0)
    outgoing = jnp.where(valid.reshape(-1, 1), picked, jnp.zeros_like(picked))
    arrived = route_out(
        jnp.dot(outgoing, proj_weight, preferred_element_type=jnp.float32).astype(jnp.bfloat16),
        ndev,
        slots,
    )
    cells = cell_lists[0]
    painted = paint(arrived, cells, count).reshape(chans, cx, cy, nz)
    field = (base_field.astype(jnp.float32) + painted).astype(jnp.bfloat16)
    all_taps = list(enumerate(taps()))
    pre = jnp.zeros((chans, cx, cy, nz), jnp.float32)
    padded = wrap_depth(padded_2(field, (("gx", 1), ("gy", 2)), 1))
    for k, offs in all_taps:
        window = cut_window(padded, offs, sizes)
        pre = pre + jnp.einsum(
            "oi,ixyz->oxyz", conv_weight[k], window, preferred_element_type=jnp.float32
        )
    sig = jax.nn.sigmoid(pre)
    out_field = (field.astype(jnp.float32) + pre * sig).astype(jnp.bfloat16)
    pre_grad = (cotangent.astype(jnp.float32) * sig * (1.0 + pre * (1.0 - sig))).astype(
        jnp.bfloat16
    )
    field_grad = cotangent.astype(jnp.float32)
    tap_grads = [None] * 27

    def back_terms(field_grad, group, full_grad):
        for k, (dx, dy, dz) in group:
            back = cut_window(full_grad, (-dx, -dy, -dz), sizes)
            field_grad = field_grad + jnp.einsum(
                "oi,oxyz->ixyz", conv_weight[k], back, preferred_element_type=jnp.float32
            )
            window = cut_window(padded, (dx, dy, dz), sizes)
            tap_grads[k] = jnp.einsum(
                "oxyz,ixyz->oi", pre_grad, window, preferred_element_type=jnp.float32
            )
        return field_grad

    full_grad = wrap_depth(padded_2(pre_grad, (("gx", 1), ("gy", 2)), 1))
    field_grad = back_terms(field_grad, all_taps, full_grad)
    slot_grad = jnp.take(field_grad.reshape(chans, count), cells, axis=1).T.astype(jnp.bfloat16)
    weight_t = proj_weight.T
    returned = route_back(slot_grad.astype(jnp.float32), ndev, slots).astype(jnp.bfloat16)
    grad_slots = jnp.dot(returned, weight_t, preferred_element_type=jnp.float32)
    local_proj = jnp.dot(outgoing.T, returned, preferred_element_type=jnp.float32)
    conv_sum, proj_sum = lax.psum((jnp.stack(tap_grads), local_proj), ("gx", "gy"))
    conv_grad = conv_sum / jnp.sqrt(jnp.float32(count * ndev))
    proj_grad = proj_sum / jnp.sqrt(jnp.float32(nrows * ndev))
    places = jnp.arange(nrows, dtype=jnp.int32)
    ends = offsets + counts
    owner = jnp.sum((ends[None, :] <= places[:, None]).astype(jnp.int32), axis=1)
    slot_of = owner * slots + places - jnp.take(offsets, owner)
    row_grads = jnp.take(grad_slots, slot_of, axis=0)
    return (out_field, row_grads, conv_grad, proj_grad)


def solution(mesh):
    in_specs = (
        P(("gx", "gy"), None),
        P(("gx", "gy"), None),
        P(("gx", "gy"), None),
        P(None, "gx", "gy", None),
        P(),
        P(),
        P(None, "gx", "gy", None),
    )
    out_specs = (P(None, "gx", "gy", None), P(("gx", "gy"), None), P(), P())
    return jax.shard_map(local, mesh=mesh, in_specs=in_specs, out_specs=out_specs, check_vma=False)
```

profile of v0, /device:TPU:0, one launch (start us, length us, event | category | flops | bytes accessed | tf_op | source)
XLA Modules:
  0.0 281.4 jit_solution(913975737827912976)
XLA Ops:
  7.2 0.7 copy.80
  9.1 0.7 iota_compare_fusion.1
  9.9 0.9 gather_fusion
  10.7 1.0 convolution_convert_fusion
  11.8 0.7 reshape.704
  12.6 7.3 %all-to-all-start = ((bf16[32,2,256]{2,1,0:T(2,128)(2,1)}), bf16[32,2,256]{2,1,0:T(2,128)(2,1)S(1)}, u32[]{:S(2)}, u32[]{:S(2)}) async-start(bf16[32,2,256]{2,1,0:T(2,128)(2,1)} %reshape.704), calls=%async_computation | async-start | bytes 65536 | tf_op jit(solution)/shard_map/all_to_all | solution.py:33
  20.7 1.2 gather_fusion.1
  22.0 5.2 %all-to-all-done = bf16[32,2,256]{2,1,0:T(2,128)(2,1)S(1)} async-done(((bf16[32,2,256]{2,1,0:T(2,128)(2,1)}), bf16[32,2,256]{2,1,0:T(2,128)(2,1)S(1)}, u32[]{:S(2)}, u32[]{:S(2)}) %all-to-all-start) | async-done | bytes 32800 | tf_op jit(solution)/shard_map/all_to_all | solution.py:33
  27.3 5.0 %while.10 = (s32[]{:T(128)}, f32[2,64,2048]{2,1,0:T(8,128)S(1)}, s32[1,256]{1,0:T(1,128)}, s32[2]{0:T(128)S(1)}, bf16[256,64]{1,0:T(8,128)(2,1)S(1)}, /*index=5*/s32[]{:T(128)}) while((s32[]{:T(128)}, f32[2,64,2048]{2,1,0:T(8,128)S(1)}, s32[1,256]{1,0:T(1,128)}, s32[2]{0:T(128)S(1)}, bf16[256,64]{1,0:T(8,128)(2,1)S(1)}, ...), condition=%wide.region_2.3_spmd, body=%wide.region_1.2_spmd.sunk | while | flops 67635200 | bytes 607321 | solution.py:58
  28.6 1.2 fusion.308
  31.0 1.2 fusion.308
  32.3 0.8 copy.82
  33.1 0.8 reshape_reshape.3
  34.0 0.7 fusion.74
  34.8 2.6 collective-permute-start.1
  37.7 12.1 %collective-permute-done = bf16[64,1,16,256]{3,0,2,1:T(8,128)(2,1)S(1)} collective-permute-done((bf16[64,1,16,256]{3,0,2,1:T(8,128)(2,1)S(1)}, bf16[64,1,16,256]{3,0,2,1:T(8,128)(2,1)S(1)}, u32[]{:S(2)}, u32[]{:S(2)}) %collective-permute-start) | collective-permute-done | bytes 524320 | tf_op jit(solution)/shard_map/ppermute | solution.py:15
  50.3 3.4 %collective-permute-start.3 = (bf16[64,3,1,256]{3,0,2,1:T(8,128)(2,1)S(1)}, bf16[64,3,1,256]{3,0,2,1:T(8,128)(2,1)S(1)}, u32[]{:S(2)}, u32[]{:S(2)}) collective-permute-start(bf16[64,3,1,256]{3,0,2,1:T(8,128)(2,1)S(1)} %get-tuple-element.71), channel_id=1, source_target_pairs={{1,0},{2,1},{3,2},{0,3},{5,4},{6,5},{7,6},{4,7},{9,8},{10,9},{11,1... | collective-permute-start | bytes 294920 | tf_op jit(solution)/shard_map/ppermute | solution.py:18
  54.3 2.5 collective-permute-done.2
  57.6 2.9 %maximum_maximum_fusion = (bf16[64,3,18,257]{3,0,2,1:T(8,128)(2,1)S(1)}, bf16[64,3,18,257]{3,0,2,1:T(8,128)(2,1)S(1)}) fusion(bf16[64,3,1,256]{3,0,2,1:T(8,128)(2,1)S(1)} %collective-permute-done.3, bf16[64,1,16,256]{3,0,2,1:T(8,128)(2,1)S(1)} %collective-permute-done.1, bf16[64,1,16,256]{3,0,2,1:T(8,128)(2,1)S(1)} %fusion.74, ...), kind=kLoop, calls=%fused_computation.10 | loop fusion | flops 21316608 | bytes 5336064 | tf_op jit(solution)/shard_map/concatenate | solution.py:28
  66.9 1.3 fusion.204
  68.8 2.3 fusion.16
  71.1 1.9 fusion.72
  73.0 0.9 fusion.70
  73.9 2.6 collective-permute-start.5
  76.5 0.9 fusion.69
  77.4 1.0 fusion.68
  78.4 0.9 fusion.67
  79.3 0.9 fusion.66
  80.2 1.0 fusion.65
  81.2 0.9 fusion.64
  82.1 0.9 fusion.63
  83.0 1.0 fusion.62
  84.0 0.9 fusion.61
  84.9 0.9 fusion.60
  85.8 1.0 fusion.59
  86.8 0.9 fusion.58
  87.7 0.9 fusion.57
  88.6 1.0 fusion.56
  89.6 0.9 fusion.55
  90.5 0.9 fusion.54
  91.4 1.0 fusion.53
  92.4 0.9 fusion.52
  93.3 0.9 fusion.51
  94.2 1.0 fusion.50
  95.2 0.9 fusion.49
  96.1 0.9 fusion.48
  97.0 1.0 fusion.47
  98.0 0.9 fusion.46
  98.9 0.9 fusion.45
  99.8 1.0 fusion.44
  100.8 1.1 copy.114
  102.3 3.5 %collective-permute-start.7 = (bf16[64,3,1,256]{3,0,2,1:T(8,128)(2,1)S(1)}, bf16[64,3,1,256]{3,0,2,1:T(8,128)(2,1)S(1)}, u32[]{:S(2)}, u32[]{:S(2)}) collective-permute-start(bf16[64,3,1,256]{3,0,2,1:T(8,128)(2,1)S(1)} %get-tuple-element.69), channel_id=1, source_target_pairs={{1,0},{2,1},{3,2},{0,3},{5,4},{6,5},{7,6},{4,7},{9,8},{10,9},{11,1... | collective-permute-start | bytes 294920 | tf_op jit(solution)/shard_map/ppermute | solution.py:18
  106.4 1.5 collective-permute-done.7
  108.0 4.4 %collective-permute-done.6 = bf16[64,3,1,256]{3,0,2,1:T(8,128)(2,1)S(1)} collective-permute-done((bf16[64,3,1,256]{3,0,2,1:T(8,128)(2,1)S(1)}, bf16[64,3,1,256]{3,0,2,1:T(8,128)(2,1)S(1)}, u32[]{:S(2)}, u32[]{:S(2)}) %collective-permute-start.6) | collective-permute-done | bytes 98336 | tf_op jit(solution)/shard_map/ppermute | solution.py:15
  113.1 2.9 %pad_maximum_fusion.1 = (bf16[64,3,18,257]{3,0,2,1:T(8,128)(2,1)S(1)}, bf16[64,3,18,257]{3,0,2,1:T(8,128)(2,1)S(1)}) fusion(bf16[64,3,18,1]{3,0,2,1:T(8,128)(2,1)S(1)} %get-tuple-element.56, bf16[64,3,1,256]{3,0,2,1:T(8,128)(2,1)S(1)} %collective-permute-done.7, bf16[64,1,16,256]{3,0,2,1:T(8,128)(2,1)S(1)} %collective-permute-done.5, ...), kind=kLoop, calls=%fused_computation.12 | loop fusion | flops 21316608 | bytes 5336064 | tf_op jit(solution)/shard_map/concatenate | solution.py:28
  123.1 1.4 fusion.43
  125.5 1.1 fusion.41
  127.1 0.9 gather_fusion.2
  128.0 0.7 reshape.706
  128.8 2.6 all-to-all-start.1
  131.3 98.5 %all-reduce.2.cloned.1.call-done = f32[27,64,64]{2,1,0:T(8,128)} async-done(((f32[27,64,64]{2,1,0:T(8,128)}), f32[27,64,64]{2,1,0:T(8,128)}) %all-reduce.2.cloned.1.call-update) | async-done | bytes 442384 | tf_op jit(solution)/shard_map/psum | solution.py:125
  229.8 2.2 broadcast_multiply_fusion
  232.6 40.0 %psum.15 = f32[128,64]{0,1:T(8,128)S(1)} all-reduce(f32[128,64]{0,1:T(8,128)S(1)} %fusion.157), channel_id=1, replica_groups=mesh['gx'=8,'gy'=4] {'gx','gy'}, use_global_device_ids=true, to_apply=%region_5.6 | all-reduce | flops 8192 | bytes 65536 | tf_op jit(solution)/shard_map/psum | solution.py:125
  273.9 0.7 broadcast_select_fusion
  (117 shorter events, 26.0 us)
Async XLA Ops:
  7.2 2.7 copy-start
  12.6 14.6 %all-to-all-start = ((bf16[32,2,256]{2,1,0:T(2,128)(2,1)}), bf16[32,2,256]{2,1,0:T(2,128)(2,1)S(1)}, u32[]{:S(2)}, u32[]{:S(2)}) async-start(bf16[32,2,256]{2,1,0:T(2,128)(2,1)} %reshape.704), calls=%async_computation | async-start | bytes 65536 | tf_op jit(solution)/shard_map/all_to_all | solution.py:33
  19.9 209.9 %all-reduce.2.cloned.1.call-start = ((), (), s32[]{:S(2)}) async-start(), calls=%async_computation.2 | async-start | bytes 1769472 | tf_op jit(solution)/shard_map/psum | solution.py:125
  32.3 1.7 copy-start.5
  32.3 5.2 %copy-start.7 = (s32[1,256]{1,0:T(1,128)S(1)}, s32[1,256]{1,0:T(1,128)}, u32[]{:S(2)}) copy-start(s32[1,256]{1,0:T(1,128)} %get-tuple-element.145) | copy-start | bytes 3076
  32.3 5.2 %copy-start.3 = (bf16[27,64,64]{2,1,0:T(8,128)(2,1)S(1)}, bf16[27,64,64]{2,1,0:T(8,128)(2,1)}, u32[]{:S(2)}) copy-start(bf16[27,64,64]{2,1,0:T(8,128)(2,1)} %param.14) | copy-start | bytes 663556
  34.7 15.1 %collective-permute-start = (bf16[64,1,16,256]{3,0,2,1:T(8,128)(2,1)S(1)}, bf16[64,1,16,256]{3,0,2,1:T(8,128)(2,1)S(1)}, u32[]{:S(2)}, u32[]{:S(2)}) collective-permute-start(bf16[64,1,16,256]{3,0,2,1:T(8,128)(2,1)S(1)} %fusion.74), channel_id=1, source_target_pairs={{0,4},{4,8},{8,12},{12,16},{16,20},{20,24},{24,28},{28,0},{1,5},{5... | collective-permute-start | bytes 1572872 | tf_op jit(solution)/shard_map/ppermute | solution.py:15
  34.8 15.1 %collective-permute-start.1 = (bf16[64,1,16,256]{3,0,2,1:T(8,128)(2,1)S(1)}, bf16[64,1,16,256]{3,0,2,1:T(8,128)(2,1)S(1)}, u32[]{:S(2)}, u32[]{:S(2)}) collective-permute-start(bf16[64,1,16,256]{3,0,2,1:T(8,128)(2,1)S(1)} %fusion.74), channel_id=1, source_target_pairs={{4,0},{8,4},{12,8},{16,12},{20,16},{24,20},{28,24},{0,28},{5,1},{9... | collective-permute-start | bytes 1572872 | tf_op jit(solution)/shard_map/ppermute | solution.py:18
  49.9 6.9 %collective-permute-start.2 = (bf16[64,3,1,256]{3,0,2,1:T(8,128)(2,1)S(1)}, bf16[64,3,1,256]{3,0,2,1:T(8,128)(2,1)S(1)}, u32[]{:S(2)}, u32[]{:S(2)}) collective-permute-start(bf16[64,3,1,256]{3,0,2,1:T(8,128)(2,1)S(1)} %get-tuple-element.70), channel_id=1, source_target_pairs={{0,1},{1,2},{2,3},{3,0},{4,5},{5,6},{6,7},{7,4},{8,9},{9,10},{10,1... | collective-permute-start | bytes 294920 | tf_op jit(solution)/shard_map/ppermute | solution.py:15
  50.3 6.5 %collective-permute-start.3 = (bf16[64,3,1,256]{3,0,2,1:T(8,128)(2,1)S(1)}, bf16[64,3,1,256]{3,0,2,1:T(8,128)(2,1)S(1)}, u32[]{:S(2)}, u32[]{:S(2)}) collective-permute-start(bf16[64,3,1,256]{3,0,2,1:T(8,128)(2,1)S(1)} %get-tuple-element.71), channel_id=1, source_target_pairs={{1,0},{2,1},{3,2},{0,3},{5,4},{6,5},{7,6},{4,7},{9,8},{10,9},{11,1... | collective-permute-start | bytes 294920 | tf_op jit(solution)/shard_map/ppermute | solution.py:18
  68.7 2.3 copy-start.2
  73.9 28.4 %collective-permute-start.4 = (bf16[64,1,16,256]{3,0,2,1:T(8,128)(2,1)S(1)}, bf16[64,1,16,256]{3,0,2,1:T(8,128)(2,1)S(1)}, u32[]{:S(2)}, u32[]{:S(2)}) collective-permute-start(bf16[64,1,16,256]{3,0,2,1:T(8,128)(2,1)S(1)} %get-tuple-element.72), channel_id=1, source_target_pairs={{0,4},{4,8},{8,12},{12,16},{16,20},{20,24},{24,28},{28,0},{1,5},{5... | collective-permute-start | bytes 1572872 | tf_op jit(solution)/shard_map/ppermute | solution.py:15
  73.9 28.4 %collective-permute-start.5 = (bf16[64,1,16,256]{3,0,2,1:T(8,128)(2,1)S(1)}, bf16[64,1,16,256]{3,0,2,1:T(8,128)(2,1)S(1)}, u32[]{:S(2)}, u32[]{:S(2)}) collective-permute-start(bf16[64,1,16,256]{3,0,2,1:T(8,128)(2,1)S(1)} %get-tuple-element.72), channel_id=1, source_target_pairs={{4,0},{8,4},{12,8},{16,12},{20,16},{24,20},{28,24},{0,28},{5,1},{9... | collective-permute-start | bytes 1572872 | tf_op jit(solution)/shard_map/ppermute | solution.py:18
  98.0 3.9 %copy-start.4 = (bf16[27,64,64]{2,1,0:T(8,128)(2,1)S(1)}, bf16[27,64,64]{2,1,0:T(8,128)(2,1)}, u32[]{:S(2)}) copy-start(bf16[27,64,64]{2,1,0:T(8,128)(2,1)} %param.14) | copy-start | bytes 663556
  102.3 5.7 %collective-permute-start.7 = (bf16[64,3,1,256]{3,0,2,1:T(8,128)(2,1)S(1)}, bf16[64,3,1,256]{3,0,2,1:T(8,128)(2,1)S(1)}, u32[]{:S(2)}, u32[]{:S(2)}) collective-permute-start(bf16[64,3,1,256]{3,0,2,1:T(8,128)(2,1)S(1)} %get-tuple-element.69), channel_id=1, source_target_pairs={{1,0},{2,1},{3,2},{0,3},{5,4},{6,5},{7,6},{4,7},{9,8},{10,9},{11,1... | collective-permute-start | bytes 294920 | tf_op jit(solution)/shard_map/ppermute | solution.py:18
  105.7 6.6 %collective-permute-start.6 = (bf16[64,3,1,256]{3,0,2,1:T(8,128)(2,1)S(1)}, bf16[64,3,1,256]{3,0,2,1:T(8,128)(2,1)S(1)}, u32[]{:S(2)}, u32[]{:S(2)}) collective-permute-start(bf16[64,3,1,256]{3,0,2,1:T(8,128)(2,1)S(1)} %get-tuple-element.68), channel_id=1, source_target_pairs={{0,1},{1,2},{2,3},{3,0},{4,5},{5,6},{6,7},{7,4},{8,9},{9,10},{10,1... | collective-permute-start | bytes 294920 | tf_op jit(solution)/shard_map/ppermute | solution.py:15
  125.5 149.1 %copy-start.1 = (bf16[128,128]{1,0:T(8,128)(2,1)S(1)}, bf16[128,128]{1,0:T(8,128)(2,1)}, u32[]{:S(2)}) copy-start(bf16[128,128]{1,0:T(8,128)(2,1)} %param.9) | copy-start | bytes 98308
  126.6 105.8 %copy-start.6 = (bf16[128,64]{0,1:T(8,128)(2,1)S(1)}, bf16[128,64]{0,1:T(8,128)(2,1)}, u32[]{:S(2)}) copy-start(bf16[128,64]{0,1:T(8,128)(2,1)} %param.13) | copy-start | bytes 49156
  128.8 103.3 %all-to-all-start.1 = ((bf16[32,2,256]{2,1,0:T(2,128)(2,1)}), bf16[32,2,256]{2,1,0:T(2,128)(2,1)S(1)}, u32[]{:S(2)}, u32[]{:S(2)}) async-start(bf16[32,2,256]{2,1,0:T(2,128)(2,1)} %reshape.706), calls=%async_computation.1 | async-start | bytes 65536 | tf_op jit(solution)/shard_map/all_to_all | solution.py:41
Sparse Core Ops, SparseCore 0:
  100.9 128.8 all-reduce.1
where the time goes:
time: 282 us; the launch traced here: 281 us
  waiting for transfers between devices  124 us (44%)
  matrix products  53.1 us (19%)
  blocking collectives  40 us (14%)
  starting transfers between devices  22.6 us (8%)
  other arithmetic  15.1 us (5%)
  between operations  14.7 us (5%)
  local copies, waits for them, and re-layouts  11.8 us (4%)
    psum x1, waiting for transfers between devices, local(): lax.psum((jnp.stack(tap_grads), local_proj), ('gx', 'gy'))  98.5 us
    psum x1, blocking collectives, local(): lax.psum((jnp.stack(tap_grads), local_proj), ('gx', 'gy'))  40 us
    dot_general x27, matrix products, back_terms(): jnp.einsum('oxyz,ixyz->oi', pre_grad, window, preferred_element_type=jnp....  25.1 us
    ppermute x4, waiting for transfers between devices, padded_2(): lax.ppermute(lax.slice_in_dim(block, block.shape[dim] - width, None, axis...  18.9 us
    dot_general x27, matrix products, local(): jnp.einsum('oi,ixyz->oxyz', conv_weight[k], window, preferred_element_typ...  12.7 us
    ppermute x4, starting transfers between devices, padded_2(): lax.ppermute(lax.slice_in_dim(block, 0, width, axis=dim), axis, backward)  12.2 us
    dot_general x27, matrix products, back_terms(): jnp.einsum('oi,oxyz->ixyz', conv_weight[k], back, preferred_element_type=...  11.4 us
    all_to_all x1, starting transfers between devices, route_out(): lax.all_to_all(payload.reshape(ndev, slots, width), ('gx', 'gy'), split_a...  7.3 us
  transfers between devices with their start and end apart: 11, of which 6 were waited for; matrix products, arithmetic and copies ran while one was open for 17% of the time, Pallas kernels for 0%

commit v1 on v0

v1 whole, which is shorter than its diff:
```python
import functools
import math

import jax
import jax.numpy as jnp
from jax import lax
from jax.experimental import pallas as pl
from jax.experimental.pallas import tpu as pltpu
from jax.sharding import PartitionSpec as P

AXES = ("gx", "gy")
F32, BF16, I32 = jnp.float32, jnp.bfloat16, jnp.int32
LIMIT = 40 * 1024 * 1024
PAIRS = (((-1, 0), (1, 0)), ((0, -1), (0, 1)), ((-1, -1), (-1, 1)), ((1, -1), (1, 1)))
NT = (((1,), (1,)), ((), ()))
NN = (((1,), (0,)), ((), ()))


def mm(a, b, dims=NN):
    return lax.dot_general(a, b, dims, preferred_element_type=F32)


def call(kernel, outs, args, flops, scratch=()):
    traffic = sum(math.prod(a.shape) * a.dtype.itemsize for a in (*args, *outs))
    return pl.pallas_call(
        kernel,
        out_shape=[jax.ShapeDtypeStruct(o.shape, o.dtype) for o in outs],
        in_specs=[pl.BlockSpec(memory_space=pltpu.VMEM)] * len(args),
        out_specs=[pl.BlockSpec(memory_space=pltpu.VMEM)] * len(outs),
        scratch_shapes=list(scratch),
        compiler_params=pltpu.CompilerParams(vmem_limit_bytes=LIMIT),
        cost_estimate=pl.CostEstimate(flops=flops, bytes_accessed=traffic, transcendentals=0),
    )(*args)


def shape(dims, dtype):
    return jax.ShapeDtypeStruct(dims, dtype)


def send(block, di, dj, ngx, ngy):
    pairs = []
    for i in range(ngx):
        for j in range(ngy):
            pairs.append((i * ngy + j, ((i + di) % ngx) * ngy + (j + dj) % ngy))
    return lax.ppermute(block, AXES, pairs)


def exchange(payload, ndev):
    rows, width = payload.shape
    moved = lax.all_to_all(
        payload.reshape(ndev, rows // ndev, width), AXES, split_axis=0, concat_axis=0, tiled=True
    )
    return moved.reshape(rows, width)


def rolled(x, di, dj):
    for axis, shift in ((0, di), (1, dj)):
        if shift == 1:
            head, tail = lax.slice_in_dim(x, 1, None, axis=axis), lax.slice_in_dim(x, 0, 1, axis=axis)
            x = jnp.concatenate([head, tail], axis=axis)
        elif shift == -1:
            count = x.shape[axis]
            head = lax.slice_in_dim(x, count - 1, count, axis=axis)
            x = jnp.concatenate([head, lax.slice_in_dim(x, 0, count - 1, axis=axis)], axis=axis)
    return x


def pick_kernel(ngx, ngy, cap, counts_ref, rows_ref, proj_t_ref, out_ref):
    ndev = ngx * ngy
    nrows, feats = rows_ref.shape
    slots = ndev * cap
    counts = counts_ref[...].astype(F32)
    rows = rows_ref[...]
    proj_t = proj_t_ref[...]
    both = mm(rows, jnp.concatenate([proj_t, proj_t], axis=0), NT).astype(BF16)
    slot = lax.broadcasted_iota(I32, (slots, ndev), 0)
    lane = lax.broadcasted_iota(I32, (slots, ndev), 1)
    owner = slot // cap
    start = jnp.sum(jnp.where(lane < owner, counts, 0.0), axis=1, keepdims=True)
    held = jnp.sum(jnp.where(lane == owner, counts, 0.0), axis=1, keepdims=True)
    place = (lax.broadcasted_iota(I32, (slots, nrows), 0) % cap).astype(F32)
    row = lax.broadcasted_iota(I32, (slots, nrows), 1).astype(F32)
    onehot = jnp.where((row == place + start) & (place < held), 1.0, 0.0).astype(BF16)
    raw = mm(onehot, rows).reshape(ndev, cap, feats)
    projected = mm(onehot, both).reshape(ngx, ngy, cap, feats)
    left = lax.broadcasted_iota(I32, projected.shape, 3) < feats // 2
    parts = [raw]
    for first, second in PAIRS:
        pair = jnp.where(left, rolled(projected, *first), rolled(projected, *second))
        parts.append(pair.reshape(ndev, cap, feats))
    out = jnp.stack(parts, axis=1)
    out_ref[...] = out.reshape(out_ref.shape).astype(BF16)


def lists_of(block, nl, slots):
    block = block.astype(F32)
    y = jnp.concatenate([block[n : n + 1] for n in range(nl)], axis=1)[:, :slots]
    z = jnp.concatenate([block[nl + n : nl + n + 1] for n in range(nl)], axis=1)[:, :slots]
    return y.astype(I32), z.astype(I32)


def field_kernel(
    ndev, cap, chans, cy, nz,
    recv_ref, cells_ref, base_ref, cot_ref, west_ref, east_ref, north_ref, south_ref,
    nw_ref, sw_ref, ne_ref, se_ref, proj_t_ref, wf_ref, wb_ref,
    out_ref, x_ref, s_ref, raw_ref, to_west_ref, to_east_ref, own_ref,
    masked, hot, ylist, cot_all,
):
    slots = ndev * cap
    nl = -(-slots // nz)
    width = recv_ref.shape[1]
    arrived = recv_ref[...].astype(F32).reshape(ndev, 1 + len(PAIRS), cap, width)
    raw = arrived[:, 0].reshape(slots, width).astype(BF16)
    raw_ref[...] = raw
    rows_of = {(0, 0): mm(proj_t_ref[...], raw, NT).astype(BF16)}
    for q, (first, second) in enumerate(PAIRS):
        flipped = arrived[:, q + 1].reshape(slots, width).T.astype(BF16)
        rows_of[first], rows_of[second] = flipped[:chans], flipped[chans:]
    cells = cells_ref[...]
    where = {
        (0, 0): (cells // nz, cells % nz),
        (-1, 0): lists_of(west_ref[cy], nl, slots),
        (1, 0): lists_of(east_ref[cy], nl, slots),
    }
    for key, ref in (
        ((0, -1), north_ref), ((0, 1), south_ref), ((-1, -1), nw_ref),
        ((-1, 1), sw_ref), ((1, -1), ne_ref), ((1, 1), se_ref),
    ):
        where[key] = lists_of(ref[2], nl, slots)
    depth = lax.broadcasted_iota(I32, (nz, slots), 0)
    mains = {-1: west_ref, 0: base_ref, 1: east_ref}
    edges = {
        (-1, -1): nw_ref, (-1, 1): sw_ref, (0, -1): north_ref,
        (0, 1): south_ref, (1, -1): ne_ref, (1, 1): se_ref,
    }
    for dx in (-1, 0, 1):
        lanes = pl.ds((dx + 1) * chans, chans)
        y, z = where[dx, 0]
        onehot = jnp.where(depth == z, 1.0, 0.0).astype(BF16)
        hot[dx + 1] = onehot
        ylist[dx + 1] = jnp.broadcast_to(y, ylist.shape[1:])
        values = rows_of[dx, 0]
        for n in range(cy):
            masked[pl.ds(n * chans, chans)] = values * jnp.where(y == n, 1.0, 0.0).astype(BF16)
        painted = mm(masked[...], onehot, NT)
        for n in range(cy):
            part = painted[n * chans : (n + 1) * chans]
            x_ref[n + 2, lanes] = (mains[dx][n].astype(F32) + part).astype(BF16)
        for dj in (-1, 1):
            y, z = where[dx, dj]
            onehot = jnp.where(depth == z, 1.0, 0.0).astype(BF16)
            values = rows_of[dx, dj]
            first = cy - 2 if dj < 0 else 0
            lhs = jnp.concatenate(
                [values * jnp.where(y == first + n, 1.0, 0.0).astype(BF16) for n in range(2)], axis=0
            )
            painted = mm(lhs, onehot, NT)
            for n in range(2):
                part = painted[n * chans : (n + 1) * chans]
                target = n if dj < 0 else cy + 2 + n
                x_ref[target, lanes] = (edges[dx, dj][n].astype(F32) + part).astype(BF16)
    cot_all[0] = north_ref[3]
    cot_all[1 : cy + 1] = cot_ref[...]
    cot_all[cy + 1] = south_ref[3]
    own = pl.ds(chans, chans)

    def forward(t, carry):
        taps = x_ref[pl.ds(t, 3)].reshape(9 * chans, nz)
        acc = mm(wf_ref[...], taps)
        pre = acc[chans : 2 * chans]
        pre = pre + pltpu.roll(acc[:chans], 1, 1) + pltpu.roll(acc[2 * chans :], nz - 1, 1)
        sig = jax.nn.sigmoid(pre)
        out_ref[t] = (x_ref[t + 1, own].astype(F32) + pre * sig).astype(BF16)
        grad = cot_all[t].astype(F32) * sig * (1.0 + pre * (1.0 - sig))
        grad = grad.astype(BF16)
        wide = grad.astype(F32)
        s_ref[t, pl.ds(0, chans)] = pltpu.roll(wide, nz - 1, 1).astype(BF16)
        s_ref[t, own] = grad
        s_ref[t, pl.ds(2 * chans, chans)] = pltpu.roll(wide, 1, 1).astype(BF16)
        return carry

    lax.fori_loop(0, cy + 2, forward, 0)

    def slot_terms(n, sums):
        taps = s_ref[pl.ds(n, 3)].reshape(9 * chans, nz)
        plane = mm(wb_ref[...], taps)
        new = []
        for dx in range(3):
            part = plane[dx * chans : (dx + 1) * chans]
            if dx == 1:
                part = part + cot_all[n + 1].astype(F32)
            at_slots = mm(part.astype(BF16), hot[dx])
            here = ylist[dx][:1] == n
            new.append(sums[dx] + jnp.where(here, at_slots, 0.0))
        return tuple(new)

    zero = jnp.zeros((chans, slots), F32)
    west, mine, east = lax.fori_loop(0, cy, slot_terms, (zero, zero, zero))
    to_west_ref[...] = west.astype(BF16)
    to_east_ref[...] = east.astype(BF16)
    own_ref[...] = mine


def taps_kernel(chans, cy, x_ref, s_ref, out_ref, total):
    nz = x_ref.shape[2]
    total[...] = jnp.zeros_like(total)

    def step(n, carry):
        taps = x_ref[pl.ds(n + 1, 3)].reshape(9 * chans, nz)
        total[...] += mm(s_ref[n + 1], taps, NT)
        return carry

    lax.fori_loop(0, cy, step, 0)
    rows = 3 * chans
    width = 2 * chans
    for n in range(4):
        out_ref[pl.ds(n * rows, rows)] = total[:, n * width : (n + 1) * width].astype(BF16)
    last = total[:, 4 * width :]
    last = jnp.concatenate([last[: rows // 2], last[rows // 2 :]], axis=1)
    out_ref[pl.ds(4 * rows, rows // 2)] = last.astype(BF16)


def slots_kernel(ndev, cap, own_ref, a_ref, b_ref, raw_ref, grads_ref, out_ref):
    chans, slots = own_ref.shape
    width = raw_ref.shape[1]
    total = own_ref[...] + a_ref[...].astype(F32) + b_ref[...].astype(F32)
    grad = total.astype(BF16)
    proj = mm(grad, raw_ref[...])
    back = grad.astype(F32).T
    back = jnp.concatenate([back, jnp.zeros((slots, width - chans), F32)], axis=1)
    share = out_ref.shape[0] // ndev - cap
    rows = grads_ref.shape[0] + chans
    pad = jnp.zeros((share * ndev - rows, width), F32)
    sums = jnp.concatenate([grads_ref[...].astype(F32), proj, pad], axis=0)
    out = jnp.concatenate(
        [sums.reshape(ndev, share, width), back.reshape(ndev, cap, width)], axis=1
    )
    out_ref[...] = out.reshape(out_ref.shape).astype(BF16)


def rows_kernel(ndev, cap, recv_ref, counts_ref, proj_t_ref, rows_ref, sums_ref):
    nrows = rows_ref.shape[0]
    chans = proj_t_ref.shape[0]
    width = recv_ref.shape[1]
    slots = ndev * cap
    share = recv_ref.shape[0] // ndev - cap
    arrived = recv_ref[...].astype(F32).reshape(ndev, share + cap, width)
    sums = jnp.sum(arrived[:, :share], axis=0)
    sums_ref[...] = jnp.broadcast_to(sums[None], (ndev, share, width)).reshape(
        sums_ref.shape
    ).astype(BF16)
    back = arrived[:, share:].reshape(slots, width)[:, :chans].astype(BF16)
    counts = counts_ref[...].astype(F32)
    place = lax.broadcasted_iota(I32, (nrows, ndev), 0).astype(F32)
    lane = lax.broadcasted_iota(I32, (ndev, ndev), 1)
    upto = lax.broadcasted_iota(I32, (ndev, ndev), 0) <= lane
    ends = mm(counts.astype(BF16), jnp.where(upto, 1.0, 0.0).astype(BF16))
    before = ends <= place
    owner = jnp.sum(jnp.where(before, 1.0, 0.0), axis=1, keepdims=True)
    start = jnp.sum(jnp.where(before, counts, 0.0), axis=1, keepdims=True)
    slot = owner * cap + place[:, :1] - start
    onehot = jnp.where(
        lax.broadcasted_iota(I32, (nrows, slots), 1).astype(F32) == slot, 1.0, 0.0
    ).astype(BF16)
    picked = mm(onehot, back).astype(BF16)
    rows_ref[...] = mm(picked, proj_t_ref[...])


def finish_kernel(conv_scale, proj_scale, recv_ref, conv_ref, proj_ref):
    taps, chans, _ = conv_ref.shape
    rows, width = 3 * chans, 2 * chans
    half = rows // 2
    for t in range(9):
        dy, dx = t // 3, t % 3
        for dz in range(3):
            if t < 8:
                block = recv_ref[pl.ds((t // 2) * rows + dz * chans, chans)].astype(F32)
                part = block[:, :chans] if t % 2 == 0 else block[:, chans:]
                conv_ref[dx * 9 + dy * 3 + dz] = part * conv_scale
        if t == 8:
            block = recv_ref[pl.ds(4 * rows, half)].astype(F32)
            column = jnp.concatenate([block[:, :chans], block[:, chans:]], axis=0)
            for dz in range(3):
                conv_ref[dx * 9 + dy * 3 + dz] = column[dz * chans : (dz + 1) * chans] * conv_scale
    proj_ref[...] = recv_ref[pl.ds(4 * rows + half, chans)].astype(F32) * proj_scale


def local(particles, send_counts, cell_lists, base_field, proj_weight, conv_weight, cotangent):
    ngx, ngy = lax.axis_size("gx"), lax.axis_size("gy")
    ndev = ngx * ngy
    nrows, feats = particles.shape
    chans, cx, cy, nz = base_field.shape
    slots = cell_lists.shape[1]
    cap = slots // ndev
    count = cx * cy * nz
    assert cx == 1 and feats == 2 * chans
    proj_t = proj_weight.T

    base = base_field[:, 0].transpose(1, 0, 2)
    cot = cotangent[:, 0].transpose(1, 0, 2)
    nl = -(-slots // nz)
    lists = jnp.stack([cell_lists[0] // nz, cell_lists[0] % nz]).astype(BF16)
    lists = jnp.pad(lists, ((0, 0), (0, nl * nz - slots))).reshape(2 * nl, nz)
    lists = jnp.pad(lists, ((0, chans - 2 * nl), (0, 0)))[None]
    whole = jnp.concatenate([base, lists], axis=0)
    low = jnp.concatenate([base[:2], lists], axis=0)
    high = jnp.concatenate([base[cy - 2 :], lists], axis=0)
    move = functools.partial(send, ngx=ngx, ngy=ngy)
    west, east = move(whole, 1, 0), move(whole, -1, 0)
    north = move(jnp.concatenate([high, cot[cy - 1 :]], axis=0), 0, 1)
    south = move(jnp.concatenate([low, cot[:1]], axis=0), 0, -1)
    nw, sw = move(high, 1, 1), move(low, 1, -1)
    ne, se = move(high, -1, 1), move(low, -1, -1)

    (payload,) = call(
        functools.partial(pick_kernel, ngx, ngy, cap),
        [shape((ndev * (1 + len(PAIRS)) * cap, feats), BF16)],
        (send_counts, particles, proj_t),
        4 * slots * nrows * feats,
    )
    recv = exchange(payload, ndev)

    taps = conv_weight.reshape(3, 3, 3, chans, chans)
    wf = taps.transpose(2, 3, 1, 0, 4).reshape(3 * chans, 9 * chans)
    wb = taps[:, ::-1].transpose(0, 4, 1, 2, 3).reshape(3 * chans, 9 * chans)

    rows = 3 * chans
    out_rows, x_all, s_all, raw, to_west, to_east, own = call(
        functools.partial(field_kernel, ndev, cap, chans, cy, nz),
        [
            shape((cy + 2, chans, nz), BF16),
            shape((cy + 4, rows, nz), BF16),
            shape((cy + 2, rows, nz), BF16),
            shape((slots, feats), BF16),
            shape((chans, slots), BF16),
            shape((chans, slots), BF16),
            shape((chans, slots), F32),
        ],
        (recv, cell_lists, base, cot, west, east, north, south, nw, sw, ne, se, proj_t, wf, wb),
        4 * rows * rows * 3 * count,
        (
            pltpu.VMEM((cy * chans, slots), BF16),
            pltpu.VMEM((3, nz, slots), BF16),
            pltpu.VMEM((3, 8, slots), I32),
            pltpu.VMEM((cy + 2, chans, nz), BF16),
        ),
    )
    from_east = move(to_west, -1, 0)
    from_west = move(to_east, 1, 0)
    grad_rows = 27 * chans * chans // feats
    (tap_grads,) = call(
        functools.partial(taps_kernel, chans, cy),
        [shape((grad_rows, feats), BF16)],
        (x_all, s_all),
        2 * rows * rows * 3 * count,
        (pltpu.VMEM((rows, 9 * chans), F32),),
    )
    share = -(-(grad_rows + chans) // (8 * ndev)) * 8
    (payload,) = call(
        functools.partial(slots_kernel, ndev, cap),
        [shape((ndev * (share + cap), feats), BF16)],
        (own, from_east, from_west, raw, tap_grads),
        2 * chans * slots * feats,
    )
    recv = exchange(payload, ndev)
    row_grads, sums = call(
        functools.partial(rows_kernel, ndev, cap),
        [shape((nrows, feats), F32), shape((ndev * share, feats), BF16)],
        (recv, send_counts, proj_t),
        2 * nrows * slots * chans,
    )
    recv = exchange(sums, ndev)
    conv_grad, proj_grad = call(
        functools.partial(
            finish_kernel, 1.0 / math.sqrt(count * ndev), 1.0 / math.sqrt(nrows * ndev)
        ),
        [shape((27, chans, chans), F32), shape((chans, feats), F32)],
        (recv,),
        1000,
    )
    out_field = out_rows[1 : cy + 1].transpose(1, 0, 2)[:, None]
    return (out_field, row_grads, conv_grad, proj_grad.T)


def solution(mesh):
    in_specs = (
        P(("gx", "gy"), None),
        P(("gx", "gy"), None),
        P(("gx", "gy"), None),
        P(None, "gx", "gy", None),
        P(),
        P(),
        P(None, "gx", "gy", None),
    )
    out_specs = (P(None, "gx", "gy", None), P(("gx", "gy"), None), P(), P())
    return jax.shard_map(local, mesh=mesh, in_specs=in_specs, out_specs=out_specs, check_vma=False)
```

time: 282 us -> 103 us (0.37)
  waiting for transfers between devices: 124 us -> 12.2 us
  matrix products: 53.1 us -> 0 us
  Pallas kernels: 0 us -> 24.9 us
  blocking collectives: 40 us -> 15.6 us
  between operations: 14.7 us -> 0.8 us
  other arithmetic: 15.1 us -> 2.96 us
  starting transfers between devices: 22.6 us -> 29.3 us
  local copies, waits for them, and re-layouts: 11.8 us -> 16.2 us
    psum x1 -> x0, waiting for transfers between devices: 98.5 us -> none  [local(): lax.psum((jnp.stack(tap_grads), local_proj), ('gx', 'gy'))]
    dot_general x86 -> x0, matrix products: 53.1 us -> none  [the longest x27 25.1 us: back_terms(): jnp.einsum('oxyz,ixyz->oi', pre_grad, window, preferred_element_type=jnp....]
    psum x1 -> x0, blocking collectives: 40 us -> none  [local(): lax.psum((jnp.stack(tap_grads), local_proj), ('gx', 'gy'))]
    pallas_call x0 -> x6, Pallas kernels: none -> 24.9 us  [call(): pl.pallas_call(kernel, out_shape=[jax.ShapeDtypeStruct(o.shape, o.dtype)...]
    ppermute x8 -> x10, waiting for transfers between devices: 20.5 us -> 3.16 us  [send(): return lax.ppermute(block, AXES, pairs)]
    all_to_all x0 -> x1, blocking collectives: none -> 15.6 us  [exchange(): lax.all_to_all(payload.reshape(ndev, rows // ndev, width), AXES, split_ax...]
    ppermute x8 -> x10, starting transfers between devices: 12.7 us -> 20 us  [send(): return lax.ppermute(block, AXES, pairs)]
    reshape x1 -> x4, local copies, waits for them, and re-layouts: 0.48 us -> 7.21 us  [the longest x2 4.26 us: local(): taps = conv_weight.reshape(3, 3, 3, chans, chans)]
  transfers between devices with their start and end apart: 11 -> 12, of which waited for: 6 -> 3; matrix products, arithmetic and copies ran while one was open for 17% -> 13% of each run, Pallas kernels for 0% -> 5%
where the time goes in v1:
time: 103 us; the launch traced here: 102 us
  starting transfers between devices  29.3 us (28%)
  Pallas kernels  24.9 us (24%)
  local copies, waits for them, and re-layouts  16.2 us (16%)
  blocking collectives  15.6 us (15%)
  waiting for transfers between devices  12.2 us (12%)
  other arithmetic  2.96 us (3%)
    pallas_call x6, Pallas kernels, call(): pl.pallas_call(kernel, out_shape=[jax.ShapeDtypeStruct(o.shape, o.dtype)...  24.9 us
    ppermute x10, starting transfers between devices, send(): return lax.ppermute(block, AXES, pairs)  20 us
    all_to_all x1, blocking collectives, exchange(): lax.all_to_all(payload.reshape(ndev, rows // ndev, width), AXES, split_ax...  15.6 us
    all_to_all x2, starting transfers between devices, exchange(): lax.all_to_all(payload.reshape(ndev, rows // ndev, width), AXES, split_ax...  9.35 us
    all_to_all x2, waiting for transfers between devices, exchange(): lax.all_to_all(payload.reshape(ndev, rows // ndev, width), AXES, split_ax...  9.06 us
    unnamed x19, local copies, waits for them, and re-layouts  6.88 us
    reshape x2, local copies, waits for them, and re-layouts, local(): taps = conv_weight.reshape(3, 3, 3, chans, chans)  4.26 us
    ppermute x10, waiting for transfers between devices, send(): return lax.ppermute(block, AXES, pairs)  3.16 us
  transfers between devices with their start and end apart: 12, of which 3 were waited for; matrix products, arithmetic and copies ran while one was open for 13% of the time, Pallas kernels for 5%

profile of v1, /device:TPU:0, one launch (start us, length us, event | category | flops | bytes accessed | tf_op | source)
XLA Modules:
  0.0 102.0 jit_solution(3877889879584406120)
XLA Ops:
  0.6 0.0 copy-start.2
  0.6 0.0 copy-start
  0.7 0.0 copy-start.1
  0.7 0.7 fusion.7
  1.4 1.2 %copy.26 = bf16[64,1,16,256]{3,0,2,1:T(8,128)(2,1)S(1)} copy(bf16[64,1,16,256]{3,2,1,0:T(8,128)(2,1)} %param.10) | data formatting | bytes 1048576 | tf_op args[3]
  2.6 0.9 pad_maximum_fusion
  3.5 3.3 %collective-permute-start.1 = (bf16[17,64,256]{2,1,0:T(8,128)(2,1)}, bf16[17,64,256]{2,1,0:T(8,128)(2,1)S(1)}, u32[]{:S(2)}, u32[]{:S(2)}) collective-permute-start(bf16[17,64,256]{2,1,0:T(8,128)(2,1)} %pad_maximum_fusion), channel_id=1, source_target_pairs={{0,28},{1,29},{2,30},{3,31},{4,0},{5,1},{6,2},{7,3},{8,4},{9,5},{1... | collective-permute-start | bytes 1671176 | tf_op jit(solution)/shard_map/ppermute | solution.py:45
  6.8 0.0 collective-permute-start
  6.8 0.0 copy-done.2
  6.8 0.0 copy-done
  6.8 0.0 copy-done.1
  6.8 1.0 %shard_map.102 = bf16[1280,128]{1,0:T(8,128)(2,1)} custom-call(s32[1,32]{1,0:T(1,128)S(1)} %copy-done.2, bf16[128,128]{1,0:T(8,128)(2,1)S(1)} %copy-done.1, bf16[64,128]{1,0:T(8,128)(2,1)S(1)} %bitcast.39), custom_call_target="tpu_custom_call" | custom-call | flops 16777216 | bytes 376960 | tf_op jit(solution)/shard_map/pallas_call | solution.py:25
  7.9 6.0 %all-to-all-start = ((bf16[32,40,128]{2,1,0:T(8,128)(2,1)}), bf16[32,40,128]{2,1,0:T(8,128)(2,1)S(1)}, u32[]{:S(2)}, u32[]{:S(2)}) async-start(bf16[32,40,128]{2,1,0:T(8,128)(2,1)} %bitcast.1), calls=%async_computation | async-start | bytes 655360 | tf_op jit(solution)/shard_map/all_to_all | solution.py:50
  13.9 0.7 pad_maximum_fusion.3
  14.6 5.2 %collective-permute-start.7 = (bf16[3,64,256]{2,1,0:T(8,128)(2,1)S(1)}, bf16[3,64,256]{2,1,0:T(8,128)(2,1)S(1)}, u32[]{:S(2)}, u32[]{:S(2)}) collective-permute-start(bf16[3,64,256]{2,1,0:T(8,128)(2,1)S(1)} %get-tuple-element.40), channel_id=1, source_target_pairs={{0,31},{1,28},{2,29},{3,30},{4,3},{5,0},{6,1},{7,2},{8,7},{9,4},{1... | collective-permute-start | bytes 294920 | tf_op jit(solution)/shard_map/ppermute | solution.py:45
  19.8 0.0 collective-permute-start.5
  19.8 3.5 %collective-permute-start.6 = (bf16[3,64,256]{2,1,0:T(8,128)(2,1)}, bf16[3,64,256]{2,1,0:T(8,128)(2,1)S(1)}, u32[]{:S(2)}, u32[]{:S(2)}) collective-permute-start(bf16[3,64,256]{2,1,0:T(8,128)(2,1)} %get-tuple-element.41), channel_id=1, source_target_pairs={{0,29},{1,30},{2,31},{3,28},{4,1},{5,2},{6,3},{7,0},{8,5},{9,6},{1... | collective-permute-start | bytes 294920 | tf_op jit(solution)/shard_map/ppermute | solution.py:45
  23.3 1.2 %copy.25 = bf16[64,1,16,256]{3,0,2,1:T(8,128)(2,1)S(1)} copy(bf16[64,1,16,256]{3,2,1,0:T(8,128)(2,1)} %param.13) | data formatting | bytes 1048576 | tf_op args[6]
  24.6 0.7 fusion.1
  25.3 0.0 collective-permute-done.7.se_ref
  25.3 2.3 %collective-permute-start.3 = (bf16[4,64,256]{2,1,0:T(8,128)(2,1)}, bf16[4,64,256]{2,1,0:T(8,128)(2,1)S(1)}, u32[]{:S(2)}, u32[]{:S(2)}) collective-permute-start(bf16[4,64,256]{2,1,0:T(8,128)(2,1)} %get-tuple-element.42), channel_id=1, source_target_pairs={{0,3},{1,0},{2,1},{3,2},{4,7},{5,4},{6,5},{7,6},{8,11},{9,8},{10,9... | collective-permute-start | bytes 393224 | tf_op jit(solution)/shard_map/ppermute | solution.py:45
  27.6 0.1 collective-permute-done.5.sw_ref
  27.7 5.0 %collective-permute-start.2 = (bf16[4,64,256]{2,1,0:T(8,128)(2,1)}, bf16[4,64,256]{2,1,0:T(8,128)(2,1)S(1)}, u32[]{:S(2)}, u32[]{:S(2)}) collective-permute-start(bf16[4,64,256]{2,1,0:T(8,128)(2,1)} %get-tuple-element.43), channel_id=1, source_target_pairs={{0,1},{1,2},{2,3},{3,0},{4,5},{5,6},{6,7},{7,4},{8,9},{9,10},{10,1... | collective-permute-start | bytes 393224 | tf_op jit(solution)/shard_map/ppermute | solution.py:45
  32.7 2.0 %copy.19 = bf16[3,3,3,64,64]{3,2,1,4,0:T(4,128)(2,1)} copy(bf16[3,3,3,64,64]{4,3,2,1,0:T(8,128)(2,1)} %bitcast.43) | data formatting | bytes 442368 | tf_op jit(solution)/shard_map/reshape | solution.py:323
  34.7 0.0 copy-start.3
  34.7 2.2 %copy.24 = bf16[3,3,3,64,64]{4,0,1,3,2:T(4,128)(2,1)} copy(bf16[3,3,3,64,64]{4,3,2,1,0:T(8,128)(2,1)} %bitcast.44) | data formatting | bytes 442368 | tf_op jit(solution)/shard_map/reshape | solution.py:323
  37.0 0.0 collective-permute-done.6.ne_ref
  37.0 0.0 copy-start.6
  37.0 0.6 copy-done.6
  37.6 0.0 collective-permute-start.4
  37.6 2.1 %reverse_bitcast_fusion = bf16[3,64,3,3,64]{4,3,2,1,0:T(4,128)(2,1)} fusion(bf16[3,3,3,64,64]{3,2,1,4,0:T(4,128)(2,1)} %copy.19), kind=kLoop, calls=%fused_computation.1 | loop fusion | bytes 442368 | tf_op jit(solution)/shard_map/transpose | solution.py:325
  39.7 1.5 %reshape.39.wb_ref = bf16[192,576]{1,0:T(8,128)(2,1)S(1)} reshape(bf16[3,64,3,3,64]{4,3,2,1,0:T(4,128)(2,1)} %reverse_bitcast_fusion) | data formatting | bytes 442368 | tf_op jit(solution)/shard_map/reshape | solution.py:325
  41.2 1.5 %reshape.38.wf_ref = bf16[192,576]{1,0:T(8,128)(2,1)S(1)} reshape(bf16[3,64,3,3,64]{4,3,2,1,0:T(4,128)(2,1)} %bitcast.42) | data formatting | bytes 442368 | tf_op jit(solution)/shard_map/reshape | solution.py:324
  42.7 3.0 %collective-permute-done.4.nw_ref = bf16[3,64,256]{2,1,0:T(8,128)(2,1)} collective-permute-done((bf16[3,64,256]{2,1,0:T(8,128)(2,1)}, bf16[3,64,256]{2,1,0:T(8,128)(2,1)}, u32[]{:S(2)}, u32[]{:S(2)}) %collective-permute-start.4) | collective-permute-done | bytes 98336 | tf_op jit(solution)/shard_map/ppermute | solution.py:45
  45.7 0.0 collective-permute-done.3.south_ref
  45.7 0.0 collective-permute-done.2.north_ref
  45.7 0.0 collective-permute-done.1.east_ref
  45.7 0.0 collective-permute-done.west_ref
  45.7 0.0 copy-start.4
  45.7 0.8 copy-done.4
  46.5 0.0 all-to-all-done
  46.5 0.0 copy-done.3
  46.5 0.0 copy-start.5
  46.5 1.1 %copy-done.5 = bf16[17,64,256]{2,1,0:T(8,128)(2,1)S(1)} copy-done((bf16[17,64,256]{2,1,0:T(8,128)(2,1)S(1)}, bf16[17,64,256]{2,1,0:T(8,128)(2,1)}, u32[]{:S(2)}) %copy-start.5) | copy-done | bytes 557080
  47.6 0.0 copy-start.7
  47.6 0.9 copy-done.7
  48.5 17.0 %shard_map.103 = (bf16[18,64,256]{2,1,0:T(8,128)(2,1)S(1)}, bf16[20,192,256]{2,1,0:T(8,128)(2,1)S(1)}, bf16[18,192,256]{2,1,0:T(8,128)(2,1)S(1)}, bf16[256,128]{...) custom-call(bf16[1280,128]{1,0:T(8,128)(2,1)S(1)} %bitcast.38, ...), custom_call_target="tpu_custom_call" | custom-call | flops 1811939328 | bytes 8127488 | tf_op jit(solution)/shard_map/pallas_call | solution.py:25
  65.5 0.1 collective-permute-start.8
  65.6 0.5 collective-permute-start.9
  66.1 4.5 %shard_map.104.grads_ref = bf16[864,128]{1,0:T(8,128)(2,1)S(1)} custom-call(bf16[20,192,256]{2,1,0:T(8,128)(2,1)S(1)} %get-tuple-element.20.x_ref, bf16[18,192,256]{2,1,0:T(8,128)(2,1)S(1)} %get-tuple-element.21.s_ref), custom_call_target="tpu_custom_call" | custom-call | flops 905969664 | bytes 3956736 | tf_op jit(solution)/shard_map/pallas_call | solution.py:25
  70.5 0.0 collective-permute-done.8.a_ref
  70.5 0.0 collective-permute-done.9.b_ref
  70.5 0.1 shard_map.105
  70.7 15.6 %all_to_all.15 = bf16[32,40,128]{2,1,0:T(8,128)(2,1)S(1)} all-to-all(bf16[32,40,128]{2,1,0:T(8,128)(2,1)S(1)} %bitcast.33), channel_id=1, replica_groups=mesh['gx'=8,'gy'=4] {'gx','gy'}, dimensions={0} | all-to-all | bytes 655360 | tf_op jit(solution)/shard_map/all_to_all | solution.py:50
  86.3 1.1 %shard_map.106 = (f32[128,128]{1,0:T(8,128)}, bf16[1024,128]{1,0:T(8,128)(2,1)}) custom-call(bf16[1280,128]{1,0:T(8,128)(2,1)S(1)} %bitcast.34, s32[1,32]{1,0:T(1,128)S(1)} %copy-done.2, bf16[64,128]{1,0:T(8,128)(2,1)S(1)} %bitcast.41), custom_call_target="tpu_custom_call" | custom-call | flops 4194304 | bytes 671872 | tf_op jit(solution)/shard_map/pallas_call | solution.py:25
  87.4 3.3 %all-to-all-start.2 = ((bf16[32,32,128]{2,1,0:T(8,128)(2,1)}), bf16[32,32,128]{2,1,0:T(8,128)(2,1)S(1)}, u32[]{:S(2)}, u32[]{:S(2)}) async-start(bf16[32,32,128]{2,1,0:T(8,128)(2,1)} %bitcast.17), calls=%async_computation.2 | async-start | bytes 524288 | tf_op jit(solution)/shard_map/all_to_all | solution.py:50
  90.8 1.1 %copy.20 = bf16[64,1,16,256]{3,2,1,0:T(8,128)(2,1)} copy(bf16[64,1,16,256]{3,0,2,1:T(8,128)(2,1)S(1)} %slice_bitcast_fusion) | data formatting | bytes 1048576
  91.9 9.1 %all-to-all-done.2 = bf16[32,32,128]{2,1,0:T(8,128)(2,1)S(1)} async-done(((bf16[32,32,128]{2,1,0:T(8,128)(2,1)}), bf16[32,32,128]{2,1,0:T(8,128)(2,1)S(1)}, u32[]{:S(2)}, u32[]{:S(2)}) %all-to-all-start.2) | async-done | bytes 262176 | tf_op jit(solution)/shard_map/all_to_all | solution.py:50
  101.0 1.1 %shard_map.107 = (f32[27,64,64]{2,1,0:T(8,128)}, f32[64,128]{1,0:T(8,128)}) custom-call(bf16[1024,128]{1,0:T(8,128)(2,1)S(1)} %bitcast.35), custom_call_target="tpu_custom_call" | custom-call | flops 1000 | bytes 737280 | tf_op jit(solution)/shard_map/pallas_call | solution.py:25
  (5 shorter events, 0.1 us)
Async XLA Ops:
  0.6 6.2 %copy-start.2 = (s32[1,32]{1,0:T(1,128)S(1)}, s32[1,32]{1,0:T(1,128)}, u32[]{:S(2)}) copy-start(s32[1,32]{1,0:T(1,128)} %counts_ref.3) | copy-start | bytes 388
  0.6 6.2 %copy-start = (bf16[128,64]{0,1:T(8,128)(2,1)S(1)}, bf16[128,64]{0,1:T(8,128)(2,1)}, u32[]{:S(2)}) copy-start(bf16[128,64]{0,1:T(8,128)(2,1)} %param.11) | copy-start | bytes 49156
  0.7 6.2 %copy-start.1 = (bf16[128,128]{1,0:T(8,128)(2,1)S(1)}, bf16[128,128]{1,0:T(8,128)(2,1)}, u32[]{:S(2)}) copy-start(bf16[128,128]{1,0:T(8,128)(2,1)} %rows_ref.1) | copy-start | bytes 98308
  3.5 42.2 %collective-permute-start.1 = (bf16[17,64,256]{2,1,0:T(8,128)(2,1)}, bf16[17,64,256]{2,1,0:T(8,128)(2,1)S(1)}, u32[]{:S(2)}, u32[]{:S(2)}) collective-permute-start(bf16[17,64,256]{2,1,0:T(8,128)(2,1)} %pad_maximum_fusion), channel_id=1, source_target_pairs={{0,28},{1,29},{2,30},{3,31},{4,0},{5,1},{6,2},{7,3},{8,4},{9,5},{1... | collective-permute-start | bytes 1671176 | tf_op jit(solution)/shard_map/ppermute | solution.py:45
  6.8 38.9 %collective-permute-start = (bf16[17,64,256]{2,1,0:T(8,128)(2,1)}, bf16[17,64,256]{2,1,0:T(8,128)(2,1)S(1)}, u32[]{:S(2)}, u32[]{:S(2)}) collective-permute-start(bf16[17,64,256]{2,1,0:T(8,128)(2,1)} %pad_maximum_fusion), channel_id=1, source_target_pairs={{0,4},{1,5},{2,6},{3,7},{4,8},{5,9},{6,10},{7,11},{8,12},{9,13},{1... | collective-permute-start | bytes 1671176 | tf_op jit(solution)/shard_map/ppermute | solution.py:45
  7.9 38.7 %all-to-all-start = ((bf16[32,40,128]{2,1,0:T(8,128)(2,1)}), bf16[32,40,128]{2,1,0:T(8,128)(2,1)S(1)}, u32[]{:S(2)}, u32[]{:S(2)}) async-start(bf16[32,40,128]{2,1,0:T(8,128)(2,1)} %bitcast.1), calls=%async_computation | async-start | bytes 655360 | tf_op jit(solution)/shard_map/all_to_all | solution.py:50
  14.6 10.7 %collective-permute-start.7 = (bf16[3,64,256]{2,1,0:T(8,128)(2,1)S(1)}, bf16[3,64,256]{2,1,0:T(8,128)(2,1)S(1)}, u32[]{:S(2)}, u32[]{:S(2)}) collective-permute-start(bf16[3,64,256]{2,1,0:T(8,128)(2,1)S(1)} %get-tuple-element.40), channel_id=1, source_target_pairs={{0,31},{1,28},{2,29},{3,30},{4,3},{5,0},{6,1},{7,2},{8,7},{9,4},{1... | collective-permute-start | bytes 294920 | tf_op jit(solution)/shard_map/ppermute | solution.py:45
  19.8 7.9 %collective-permute-start.5 = (bf16[3,64,256]{2,1,0:T(8,128)(2,1)S(1)}, bf16[3,64,256]{2,1,0:T(8,128)(2,1)S(1)}, u32[]{:S(2)}, u32[]{:S(2)}) collective-permute-start(bf16[3,64,256]{2,1,0:T(8,128)(2,1)S(1)} %get-tuple-element.40), channel_id=1, source_target_pairs={{0,7},{1,4},{2,5},{3,6},{4,11},{5,8},{6,9},{7,10},{8,15},{9,12},{1... | collective-permute-start | bytes 294920 | tf_op jit(solution)/shard_map/ppermute | solution.py:45
  19.8 17.2 %collective-permute-start.6 = (bf16[3,64,256]{2,1,0:T(8,128)(2,1)}, bf16[3,64,256]{2,1,0:T(8,128)(2,1)S(1)}, u32[]{:S(2)}, u32[]{:S(2)}) collective-permute-start(bf16[3,64,256]{2,1,0:T(8,128)(2,1)} %get-tuple-element.41), channel_id=1, source_target_pairs={{0,29},{1,30},{2,31},{3,28},{4,1},{5,2},{6,3},{7,0},{8,5},{9,6},{1... | collective-permute-start | bytes 294920 | tf_op jit(solution)/shard_map/ppermute | solution.py:45
  25.3 20.4 %collective-permute-start.3 = (bf16[4,64,256]{2,1,0:T(8,128)(2,1)}, bf16[4,64,256]{2,1,0:T(8,128)(2,1)S(1)}, u32[]{:S(2)}, u32[]{:S(2)}) collective-permute-start(bf16[4,64,256]{2,1,0:T(8,128)(2,1)} %get-tuple-element.42), channel_id=1, source_target_pairs={{0,3},{1,0},{2,1},{3,2},{4,7},{5,4},{6,5},{7,6},{8,11},{9,8},{10,9... | collective-permute-start | bytes 393224 | tf_op jit(solution)/shard_map/ppermute | solution.py:45
  27.7 18.0 %collective-permute-start.2 = (bf16[4,64,256]{2,1,0:T(8,128)(2,1)}, bf16[4,64,256]{2,1,0:T(8,128)(2,1)S(1)}, u32[]{:S(2)}, u32[]{:S(2)}) collective-permute-start(bf16[4,64,256]{2,1,0:T(8,128)(2,1)} %get-tuple-element.43), channel_id=1, source_target_pairs={{0,1},{1,2},{2,3},{3,0},{4,5},{5,6},{6,7},{7,4},{8,9},{9,10},{10,1... | collective-permute-start | bytes 393224 | tf_op jit(solution)/shard_map/ppermute | solution.py:45
  34.7 11.8 %copy-start.3 = (s32[1,256]{1,0:T(1,128)S(1)}, s32[1,256]{1,0:T(1,128)}, u32[]{:S(2)}) copy-start(s32[1,256]{1,0:T(1,128)} %cells_ref.1) | copy-start | bytes 3076
  37.0 0.6 copy-start.6
  37.6 8.1 %collective-permute-start.4 = (bf16[3,64,256]{2,1,0:T(8,128)(2,1)}, bf16[3,64,256]{2,1,0:T(8,128)(2,1)}, u32[]{:S(2)}, u32[]{:S(2)}) collective-permute-start(bf16[3,64,256]{2,1,0:T(8,128)(2,1)} %get-tuple-element.41), channel_id=1, source_target_pairs={{0,5},{1,6},{2,7},{3,4},{4,9},{5,10},{6,11},{7,8},{8,13},{9,14},{1... | collective-permute-start | bytes 294920 | tf_op jit(solution)/shard_map/ppermute | solution.py:45
  45.7 0.8 copy-start.4
  46.5 1.1 %copy-start.5 = (bf16[17,64,256]{2,1,0:T(8,128)(2,1)S(1)}, bf16[17,64,256]{2,1,0:T(8,128)(2,1)}, u32[]{:S(2)}) copy-start(bf16[17,64,256]{2,1,0:T(8,128)(2,1)} %copy-done.4) | copy-start | bytes 1671172
  47.6 0.9 copy-start.7
  65.5 5.0 %collective-permute-start.8 = (bf16[64,256]{1,0:T(8,128)(2,1)S(1)}, bf16[64,256]{1,0:T(8,128)(2,1)S(1)}, u32[]{:S(2)}, u32[]{:S(2)}) collective-permute-start(bf16[64,256]{1,0:T(8,128)(2,1)S(1)} %get-tuple-element.17), channel_id=1, source_target_pairs={{0,28},{1,29},{2,30},{3,31},{4,0},{5,1},{6,2},{7,3},{8,4},{9,5},{1... | collective-permute-start | bytes 98312 | tf_op jit(solution)/shard_map/ppermute | solution.py:45
  65.6 5.0 %collective-permute-start.9 = (bf16[64,256]{1,0:T(8,128)(2,1)S(1)}, bf16[64,256]{1,0:T(8,128)(2,1)S(1)}, u32[]{:S(2)}, u32[]{:S(2)}) collective-permute-start(bf16[64,256]{1,0:T(8,128)(2,1)S(1)} %get-tuple-element.18), channel_id=1, source_target_pairs={{0,4},{1,5},{2,6},{3,7},{4,8},{5,9},{6,10},{7,11},{8,12},{9,13},{1... | collective-permute-start | bytes 98312 | tf_op jit(solution)/shard_map/ppermute | solution.py:45
  87.4 13.5 %all-to-all-start.2 = ((bf16[32,32,128]{2,1,0:T(8,128)(2,1)}), bf16[32,32,128]{2,1,0:T(8,128)(2,1)S(1)}, u32[]{:S(2)}, u32[]{:S(2)}) async-start(bf16[32,32,128]{2,1,0:T(8,128)(2,1)} %bitcast.17), calls=%async_computation.2 | async-start | bytes 524288 | tf_op jit(solution)/shard_map/all_to_all | solution.py:50

commit v2 on v1

v2 whole, which is shorter than its diff:
```python
import functools
import math

import jax
import jax.numpy as jnp
from jax import lax
from jax.experimental import pallas as pl
from jax.experimental.pallas import tpu as pltpu
from jax.sharding import PartitionSpec as P

AXES = ("gx", "gy")
F32, BF16, I32 = jnp.float32, jnp.bfloat16, jnp.int32
LIMIT = 40 * 1024 * 1024
NT = (((1,), (1,)), ((), ()))
NN = (((1,), (0,)), ((), ()))


def mm(a, b, dims=NN):
    return lax.dot_general(a, b, dims, preferred_element_type=F32)


def call(kernel, outs, args, flops, scratch=()):
    traffic = sum(math.prod(a.shape) * a.dtype.itemsize for a in (*args, *outs))
    return pl.pallas_call(
        kernel,
        out_shape=[jax.ShapeDtypeStruct(o.shape, o.dtype) for o in outs],
        in_specs=[pl.BlockSpec(memory_space=pltpu.VMEM)] * len(args),
        out_specs=[pl.BlockSpec(memory_space=pltpu.VMEM)] * len(outs),
        scratch_shapes=list(scratch),
        compiler_params=pltpu.CompilerParams(vmem_limit_bytes=LIMIT),
        cost_estimate=pl.CostEstimate(flops=flops, bytes_accessed=traffic, transcendentals=0),
    )(*args)


def shape(dims, dtype):
    return jax.ShapeDtypeStruct(dims, dtype)


def send(block, di, dj, ngx, ngy):
    pairs = []
    for i in range(ngx):
        for j in range(ngy):
            pairs.append((i * ngy + j, ((i + di) % ngx) * ngy + (j + dj) % ngy))
    return lax.ppermute(block, AXES, pairs)


def exchange(payload, ndev):
    rows, width = payload.shape
    moved = lax.all_to_all(
        payload.reshape(ndev, rows // ndev, width), AXES, split_axis=0, concat_axis=0, tiled=True
    )
    return moved.reshape(rows, width)


def rolled(x, di, dj):
    for axis, shift in ((0, di), (1, dj)):
        if shift == 1:
            head, tail = lax.slice_in_dim(x, 1, None, axis=axis), lax.slice_in_dim(x, 0, 1, axis=axis)
            x = jnp.concatenate([head, tail], axis=axis)
        elif shift == -1:
            count = x.shape[axis]
            head = lax.slice_in_dim(x, count - 1, count, axis=axis)
            x = jnp.concatenate([head, lax.slice_in_dim(x, 0, count - 1, axis=axis)], axis=axis)
    return x


def widths(nl, slots, block):
    block = block.astype(F32)
    y = jnp.concatenate([block[n : n + 1] for n in range(nl)], axis=1)[:, :slots]
    z = jnp.concatenate([block[nl + n : nl + n + 1] for n in range(nl)], axis=1)[:, :slots]
    return y.astype(I32), z.astype(I32)


def picked_depth(z, nz):
    depth = lax.broadcasted_iota(I32, (nz, z.shape[1]), 0)
    return jnp.where(depth == z, 1.0, 0.0).astype(BF16)


def rows_in(recv_ref, ndev, cap):
    width = recv_ref.shape[1]
    arrived = recv_ref[...].astype(F32).reshape(ndev, 3, cap, width)
    return [arrived[:, n].reshape(ndev * cap, width).astype(BF16) for n in range(3)]


def stacked(grad):
    nz = grad.shape[1]
    wide = grad.astype(F32)
    return jnp.concatenate(
        [pltpu.roll(wide, nz - 1, 1), wide, pltpu.roll(wide, 1, 1)], axis=0
    ).astype(BF16)


def finish_row(acc, field, cot):
    chans, nz = field.shape
    pre = acc[chans : 2 * chans]
    pre = pre + pltpu.roll(acc[:chans], 1, 1) + pltpu.roll(acc[2 * chans :], nz - 1, 1)
    sig = jax.nn.sigmoid(pre)
    out = field.astype(F32) + pre * sig
    grad = cot.astype(F32) * sig * (1.0 + pre * (1.0 - sig))
    return out.astype(BF16), grad.astype(BF16)


def plane_kernel(base_ref, lists_ref, out_ref):
    chans, cy, nz = base_ref.shape
    turned = jnp.swapaxes(base_ref[...].astype(F32), 0, 1)
    out_ref[pl.ds(0, cy * chans)] = turned.reshape(cy * chans, nz).astype(BF16)
    out_ref[pl.ds(cy * chans, lists_ref.shape[0])] = lists_ref[...]


def pick_kernel(ngx, ngy, cap, counts_ref, rows_ref, plane_ref, out_ref):
    ndev = ngx * ngy
    nrows, feats = rows_ref.shape
    slots = ndev * cap
    counts = counts_ref[...].astype(F32)
    slot = lax.broadcasted_iota(I32, (slots, ndev), 0)
    lane = lax.broadcasted_iota(I32, (slots, ndev), 1)
    owner = slot // cap
    start = jnp.sum(jnp.where(lane < owner, counts, 0.0), axis=1, keepdims=True)
    held = jnp.sum(jnp.where(lane == owner, counts, 0.0), axis=1, keepdims=True)
    place = (lax.broadcasted_iota(I32, (slots, nrows), 0) % cap).astype(F32)
    row = lax.broadcasted_iota(I32, (slots, nrows), 1).astype(F32)
    onehot = jnp.where((row == place + start) & (place < held), 1.0, 0.0).astype(BF16)
    raw = mm(onehot, rows_ref[...]).reshape(ngx, ngy, cap, feats)
    parts = [rolled(raw, dx, 0).reshape(ndev, cap, feats) for dx in (-1, 0, 1)]
    out_ref[...] = jnp.stack(parts, axis=1).reshape(out_ref.shape).astype(BF16)


def paint_kernel(
    ndev, cap, chans, cy, nz,
    recv_ref, own_ref, west_ref, east_ref, proj_t_ref,
    x_ref, first_ref, last_ref, masked,
):
    slots = ndev * cap
    nl = -(-slots // nz)
    raws = rows_in(recv_ref, ndev, cap)
    for dx, ref in enumerate((west_ref, own_ref, east_ref)):
        lanes = pl.ds(dx * chans, chans)
        y, z = widths(nl, slots, ref[pl.ds(cy * chans, ref.shape[0] - cy * chans)])
        values = mm(proj_t_ref[...], raws[dx], NT).astype(BF16)
        for n in range(cy):
            masked[pl.ds(n * chans, chans)] = values * jnp.where(y == n, 1.0, 0.0).astype(BF16)
        painted = mm(masked[...], picked_depth(z, nz), NT)
        for n in range(cy):
            rows = pl.ds(n * chans, chans)
            part = painted[n * chans : (n + 1) * chans]
            field = (ref[rows].astype(F32) + part).astype(BF16)
            x_ref[n, lanes] = field
            if n == 0:
                first_ref[lanes] = field
            if n == cy - 1:
                last_ref[lanes] = field


def conv_kernel(
    chans, cy, x_ref, cot_ref, wf_ref,
    out_ref, s_ref, top_ref, bottom_ref, total_ref, acc,
):
    rows = 3 * chans
    own = pl.ds(chans, chans)
    zeros = jnp.zeros(s_ref.shape[1:], BF16)
    for t in (0, 1, cy, cy + 1):
        s_ref[t] = zeros
    out_ref[0] = zeros[:chans]
    out_ref[cy - 1] = zeros[:chans]
    acc[0] = jnp.zeros(acc.shape[1:], F32)

    def spread(n):
        terms = mm(wf_ref[...], x_ref[n])
        acc[n + 1] = terms[:rows]
        acc[n] += terms[rows : 2 * rows]
        return terms[2 * rows :]

    spread(0)
    top_ref[...] = acc[0] + spread(1)

    def forward(n, carry):
        done = spread(n) + acc[n - 1]
        y = n - 1
        out, grad = finish_row(done, x_ref[y, own], cot_ref[y])
        out_ref[y] = out
        s_ref[y + 1] = stacked(grad)
        return carry

    lax.fori_loop(2, cy, forward, 0, unroll=2)
    bottom_ref[...] = acc[cy - 1]
    total_ref[...] = jnp.zeros_like(total_ref)

    def taps(n, carry):
        grads = s_ref[pl.ds(n, 3)].reshape(3 * rows, s_ref.shape[2])
        total_ref[...] += mm(grads, x_ref[n], NT)
        return carry

    lax.fori_loop(0, cy, taps, 0, unroll=2)


def edge_kernel(
    chans, cy, top_ref, bottom_ref, north_ref, south_ref, first_ref, last_ref, cot_ref, wf_ref,
    out_ref, up_ref, down_ref,
):
    rows = 3 * chans
    own = pl.ds(chans, chans)
    top = top_ref[...] + mm(wf_ref[pl.ds(0, rows)], north_ref[...])
    out_ref[0], up_ref[...] = finish_row(top, first_ref[own], cot_ref[0])
    bottom = bottom_ref[...] + mm(wf_ref[pl.ds(2 * rows, rows)], south_ref[...])
    out_ref[1], down_ref[...] = finish_row(bottom, last_ref[own], cot_ref[cy - 1])


def at_slots(parts, ylists, hots, first, total):
    chans = total[0].shape[0]
    new = []
    for dx in range(3):
        found = mm(parts[dx], hots[dx])
        value = total[dx]
        for n in range(len(first)):
            here = ylists[dx] == first[n]
            value = value + jnp.where(here, found[n * chans : (n + 1) * chans], 0.0)
        new.append(value)
    return new


def slot_kernel(
    ndev, cap, chans, cy, nz,
    x_ref, s_ref, north_ref, south_ref, up_ref, down_ref, cot_ref, total_ref, wb_ref,
    own_ref, west_ref, east_ref,
    grads_ref, sums_ref, edge_ref, acc, plane, total,
):
    rows = 3 * chans
    slots = ndev * cap
    nl = -(-slots // nz)
    up, down = stacked(up_ref[...]), stacked(down_ref[...])
    for block, high, middle, low in (
        (0, x_ref[1], x_ref[0], north_ref[...]),
        (cy - 1, south_ref[...], x_ref[cy - 1], x_ref[cy - 2]),
    ):
        grads = up if block == 0 else down
        for n, field in enumerate((high, middle, low)):
            at = pl.ds(n * rows, rows)
            base = total_ref[at] if block == 0 else total[at]
            total[at] = base + mm(grads, field, NT)
    grads_ref[pl.ds(0, 3 * rows)] = total[:, : 2 * chans].astype(BF16)
    last = total[:, 2 * chans :]
    half = 3 * rows // 2
    last = jnp.concatenate([last[:half], last[half:]], axis=1)
    grads_ref[pl.ds(3 * rows, half)] = last.astype(BF16)

    def keep(n, value):
        for dx in range(3):
            part = value[dx * chans : (dx + 1) * chans]
            if dx == 1:
                part = part + cot_ref[n].astype(F32)
            plane[dx, pl.ds((n - 1) * chans, chans)] = part.astype(BF16)

    def spread(n, grads):
        terms = mm(wb_ref[...], grads)
        acc[n + 1] = terms[2 * rows :]
        acc[n] += terms[rows : 2 * rows]
        return terms[:rows]

    acc[0] = jnp.zeros(acc.shape[1:], F32)
    spread(0, up)
    edge_ref[0] = acc[0] + spread(1, s_ref[2])

    def backward(n, carry):
        keep(n - 1, spread(n, s_ref[n + 1]) + acc[n - 1])
        return carry

    lax.fori_loop(2, cy - 1, backward, 0, unroll=2)
    keep(cy - 2, spread(cy - 1, down) + acc[cy - 2])
    edge_ref[1] = acc[cy - 1]
    ylists, hots = [], []
    for ref in (west_ref, own_ref, east_ref):
        y, z = widths(nl, slots, ref[pl.ds(cy * chans, ref.shape[0] - cy * chans)])
        ylists.append(y)
        hots.append(picked_depth(z, nz))
    zero = jnp.zeros((chans, slots), F32)
    found = at_slots([plane[dx] for dx in range(3)], ylists, hots, range(1, cy - 1), [zero] * 3)
    for dx in range(3):
        sums_ref[dx] = found[dx]


def return_kernel(
    ndev, cap, chans, cy, nz,
    sums_ref, edge_ref, before_ref, after_ref, cot_ref, wb_ref,
    own_ref, west_ref, east_ref, recv_ref, grads_ref, out_ref,
):
    rows = 3 * chans
    slots = ndev * cap
    nl = -(-slots // nz)
    top = edge_ref[0] + mm(wb_ref[pl.ds(2 * rows, rows)], stacked(before_ref[...]))
    bottom = edge_ref[1] + mm(wb_ref[pl.ds(0, rows)], stacked(after_ref[...]))
    ylists, hots, parts = [], [], []
    for dx, ref in enumerate((west_ref, own_ref, east_ref)):
        y, z = widths(nl, slots, ref[pl.ds(cy * chans, ref.shape[0] - cy * chans)])
        ylists.append(y)
        hots.append(picked_depth(z, nz))
        at = slice(dx * chans, (dx + 1) * chans)
        pair = [top[at], bottom[at]]
        if dx == 1:
            pair = [pair[0] + cot_ref[0].astype(F32), pair[1] + cot_ref[cy - 1].astype(F32)]
        parts.append(jnp.concatenate(pair, axis=0).astype(BF16))
    found = at_slots(parts, ylists, hots, (0, cy - 1), [sums_ref[dx] for dx in range(3)])
    raws = rows_in(recv_ref, ndev, cap)
    proj = sum(mm(found[dx].astype(BF16), raws[dx]) for dx in range(3))
    proj_high = proj.astype(BF16).astype(F32)
    sides = jnp.concatenate([found[0], found[2]], axis=0).T
    middle = jnp.concatenate([found[1], jnp.zeros_like(found[1])], axis=0).T
    width = out_ref.shape[1]
    share = out_ref.shape[0] // ndev - 2 * cap
    used = grads_ref.shape[0] + 2 * chans
    pad = jnp.zeros((share * ndev - used, width), F32)
    halves = [v.reshape(2 * chans // share, share // 2, width) for v in (proj_high, proj - proj_high)]
    proj = jnp.stack(halves, axis=1).reshape(2 * chans, width)
    sums = jnp.concatenate([grads_ref[...].astype(F32), proj, pad], axis=0)
    out = jnp.concatenate(
        [
            sums.reshape(ndev, share, width),
            sides.reshape(ndev, cap, width),
            middle.reshape(ndev, cap, width),
        ],
        axis=1,
    )
    out_ref[...] = out.reshape(out_ref.shape).astype(BF16)


def rows_kernel(
    ngx, ngy, cap, chans, recv_ref, index_ref, counts_ref, proj_t_ref, rows_ref, sums_ref
):
    ndev = ngx * ngy
    nrows = rows_ref.shape[0]
    width = recv_ref.shape[1]
    slots = ndev * cap
    share = recv_ref.shape[0] // ndev - 2 * cap
    arrived = recv_ref[...].astype(F32).reshape(ndev, share + 2 * cap, width)
    sums = jnp.sum(arrived[:, :share], axis=0)
    half = share // 2
    whole = sums[:half] + sums[half:]
    high = whole.astype(BF16).astype(F32)
    split = jnp.concatenate([high, whole - high], axis=0)
    device = jnp.broadcast_to(index_ref[...], sums.shape)
    sums = jnp.where(device * share >= 27 * chans * chans // width, split, sums)
    sums_ref[...] = jnp.broadcast_to(sums[None], (ndev, share, width)).reshape(
        sums_ref.shape
    ).astype(BF16)
    sides = arrived[:, share : share + cap].reshape(ngx, ngy, cap, width)
    left = lax.broadcasted_iota(I32, sides.shape, 3) < chans
    sides = jnp.where(left, rolled(sides, 1, 0), rolled(sides, -1, 0)).reshape(slots, width)
    middle = arrived[:, share + cap :].reshape(slots, width)
    counts = counts_ref[...].astype(F32)
    place = lax.broadcasted_iota(I32, (nrows, ndev), 0).astype(F32)
    lane = lax.broadcasted_iota(I32, (ndev, ndev), 1)
    upto = lax.broadcasted_iota(I32, (ndev, ndev), 0) <= lane
    ends = mm(counts.astype(BF16), jnp.where(upto, 1.0, 0.0).astype(BF16))
    before = ends <= place
    owner = jnp.sum(jnp.where(before, 1.0, 0.0), axis=1, keepdims=True)
    start = jnp.sum(jnp.where(before, counts, 0.0), axis=1, keepdims=True)
    slot = owner * cap + place[:, :1] - start
    onehot = jnp.where(
        lax.broadcasted_iota(I32, (nrows, slots), 1).astype(F32) == slot, 1.0, 0.0
    ).astype(BF16)
    proj_t = proj_t_ref[...]
    both = jnp.concatenate([proj_t, proj_t], axis=0)
    sides = mm(onehot, sides.astype(BF16)).astype(BF16)
    middle = mm(onehot, middle.astype(BF16)).astype(BF16)
    rows_ref[...] = mm(sides, both) + mm(middle, both)


def finish_kernel(conv_scale, proj_scale, share, recv_ref, conv_ref, proj_ref):
    taps, chans, _ = conv_ref.shape
    rows = 9 * chans
    half = rows // 2
    packed = recv_ref[pl.ds(rows, half)].astype(F32)
    column = jnp.concatenate([packed[:, :chans], packed[:, chans:]], axis=0)
    for b in range(3):
        for dz in range(3):
            first = (b * 3 + dz) * chans
            block = recv_ref[pl.ds(first, chans)].astype(F32)
            k = (2 - b) * 3 + dz
            conv_ref[k] = block[:, :chans] * conv_scale
            conv_ref[9 + k] = block[:, chans:] * conv_scale
            conv_ref[18 + k] = column[first : first + chans] * conv_scale
    width = recv_ref.shape[1]
    terms = recv_ref[pl.ds(rows + half, 2 * chans)].astype(F32)
    terms = terms.reshape(2 * chans // share, 2, share // 2, width)
    proj_ref[...] = jnp.sum(terms, axis=1).reshape(chans, width) * proj_scale


def local(particles, send_counts, cell_lists, base_field, proj_weight, conv_weight, cotangent):
    ngx, ngy = lax.axis_size("gx"), lax.axis_size("gy")
    ndev = ngx * ngy
    nrows, feats = particles.shape
    chans, cx, cy, nz = base_field.shape
    slots = cell_lists.shape[1]
    cap = slots // ndev
    count = cx * cy * nz
    assert cx == 1 and feats == 2 * chans
    proj_t = proj_weight.T
    move = functools.partial(send, ngx=ngx, ngy=ngy)
    rows = 3 * chans
    one = 2 * rows * rows * nz

    nl = -(-slots // nz)
    tail = -(-2 * nl // 16) * 16
    lists = jnp.stack([cell_lists[0] // nz, cell_lists[0] % nz]).astype(BF16)
    lists = jnp.pad(lists, ((0, 0), (0, nl * nz - slots))).reshape(2 * nl, nz)
    lists = jnp.pad(lists, ((0, tail - 2 * nl), (0, 0)))
    (plane,) = call(
        plane_kernel,
        [shape((cy * chans + tail, nz), BF16)],
        (base_field.reshape(chans, cy, nz), lists),
        1000,
    )
    west, east = move(plane, 1, 0), move(plane, -1, 0)
    (payload,) = call(
        functools.partial(pick_kernel, ngx, ngy, cap),
        [shape((ndev * 3 * cap, feats), BF16)],
        (send_counts, particles, plane),
        2 * slots * nrows * feats,
    )
    recv = exchange(payload, ndev)

    cot = cotangent[:, 0].transpose(1, 0, 2)
    taps = conv_weight.reshape(3, 3, 3, chans, chans)
    wf = taps.transpose(1, 2, 3, 0, 4).reshape(9 * chans, rows)
    wb = taps.transpose(1, 0, 4, 2, 3).reshape(9 * chans, rows)

    x_all, first, last = call(
        functools.partial(paint_kernel, ndev, cap, chans, cy, nz),
        [shape((cy, rows, nz), BF16), shape((rows, nz), BF16), shape((rows, nz), BF16)],
        (recv, plane, west, east, proj_t),
        6 * slots * count * chans // nz * nz // 16,
        (pltpu.VMEM((cy * chans, slots), BF16),),
    )
    north, south = move(last, 0, 1), move(first, 0, -1)
    out_rows, s_all, top, bottom, total = call(
        functools.partial(conv_kernel, chans, cy),
        [
            shape((cy, chans, nz), BF16),
            shape((cy + 2, rows, nz), BF16),
            shape((rows, nz), F32),
            shape((rows, nz), F32),
            shape((9 * chans, rows), F32),
        ],
        (x_all, cot, wf),
        2 * cy * 3 * one,
        (pltpu.VMEM((cy + 1, rows, nz), F32),),
    )
    out_edge, up, down = call(
        functools.partial(edge_kernel, chans, cy),
        [shape((2, chans, nz), BF16), shape((chans, nz), BF16), shape((chans, nz), BF16)],
        (top, bottom, north, south, first, last, cot, wf),
        2 * one,
    )
    before, after = move(down, 0, 1), move(up, 0, -1)
    grad_rows = 27 * chans * chans // feats
    tap_grads, sums, edge = call(
        functools.partial(slot_kernel, ndev, cap, chans, cy, nz),
        [
            shape((grad_rows, feats), BF16),
            shape((3, chans, slots), F32),
            shape((2, rows, nz), F32),
        ],
        (x_all, s_all, north, south, up, down, cot, total, wb, plane, west, east),
        cy * 3 * one,
        (
            pltpu.VMEM((cy + 1, rows, nz), F32),
            pltpu.VMEM((3, (cy - 2) * chans, nz), BF16),
            pltpu.VMEM((9 * chans, rows), F32),
        ),
    )
    share = -(-(grad_rows + 2 * chans) // (16 * ndev)) * 16
    (payload,) = call(
        functools.partial(return_kernel, ndev, cap, chans, cy, nz),
        [shape((ndev * (share + 2 * cap), feats), BF16)],
        (sums, edge, before, after, cot, wb, plane, west, east, recv, tap_grads),
        2 * one,
    )
    recv = exchange(payload, ndev)
    index = (lax.axis_index("gx") * ngy + lax.axis_index("gy")).astype(I32).reshape(1, 1)
    row_grads, sums = call(
        functools.partial(rows_kernel, ngx, ngy, cap, chans),
        [shape((nrows, feats), F32), shape((ndev * share, feats), BF16)],
        (recv, index, send_counts, proj_t),
        2 * nrows * slots * chans,
    )
    recv = exchange(sums, ndev)
    conv_grad, proj_grad = call(
        functools.partial(
            finish_kernel, 1.0 / math.sqrt(count * ndev), 1.0 / math.sqrt(nrows * ndev), share
        ),
        [shape((27, chans, chans), F32), shape((chans, feats), F32)],
        (recv,),
        1000,
    )
    out_field = jnp.concatenate([out_edge[:1], out_rows[1 : cy - 1], out_edge[1:]], axis=0)
    return (out_field.transpose(1, 0, 2)[:, None], row_grads, conv_grad, proj_grad.T)


def solution(mesh):
    in_specs = (
        P(("gx", "gy"), None),
        P(("gx", "gy"), None),
        P(("gx", "gy"), None),
        P(None, "gx", "gy", None),
        P(),
        P(),
        P(None, "gx", "gy", None),
    )
    out_specs = (P(None, "gx", "gy", None), P(("gx", "gy"), None), P(), P())
    return jax.shard_map(local, mesh=mesh, in_specs=in_specs, out_specs=out_specs, check_vma=False)
```

time: 103 us -> 76.4 us (0.74)
  blocking collectives: 15.6 us -> 0 us
  waiting for transfers between devices: 12.2 us -> 24.5 us
  Pallas kernels: 24.9 us -> 17.1 us
  local copies, waits for them, and re-layouts: 16.2 us -> 9.14 us
  starting transfers between devices: 29.3 us -> 23.5 us
  other arithmetic: 2.96 us -> 0.78 us
    all_to_all x1 -> x0, blocking collectives: 15.6 us -> none  [exchange(): lax.all_to_all(payload.reshape(ndev, rows // ndev, width), AXES, split_ax...]
    all_to_all x2 -> x3, waiting for transfers between devices: 9.06 us -> 24.5 us  [exchange(): lax.all_to_all(payload.reshape(ndev, rows // ndev, width), AXES, split_ax...]
    ppermute x10 -> x6, starting transfers between devices: 20 us -> 11.2 us  [send(): return lax.ppermute(block, AXES, pairs)]
    pallas_call x6 -> x9, Pallas kernels: 24.9 us -> 17.1 us  [call(): pl.pallas_call(kernel, out_shape=[jax.ShapeDtypeStruct(o.shape, o.dtype)...]
    ppermute x10 -> x6, waiting for transfers between devices: 3.16 us -> 0.02 us  [send(): return lax.ppermute(block, AXES, pairs)]
    all_to_all x2 -> x3, starting transfers between devices: 9.35 us -> 12.3 us  [exchange(): lax.all_to_all(payload.reshape(ndev, rows // ndev, width), AXES, split_ax...]
    concatenate x3 -> x0, other arithmetic: 2.24 us -> none  [the longest x1 0.86 us: local(): whole = jnp.concatenate([base, lists], axis=0)]
    reshape x2, local copies, waits for them, and re-layouts: 4.26 us -> 2.13 us  [local(): taps = conv_weight.reshape(3, 3, 3, chans, chans)]
  transfers between devices with their start and end apart: 12 -> 9, of which waited for: 3 -> 3; matrix products, arithmetic and copies ran while one was open for 13% -> 9% of each run, Pallas kernels for 5% -> 16%
where the time goes in v2:
time: 76.4 us; the launch traced here: 75.9 us
  waiting for transfers between devices  24.5 us (32%)
  starting transfers between devices  23.5 us (31%)
  Pallas kernels  17.1 us (22%)
  local copies, waits for them, and re-layouts  9.14 us (12%)
  between operations  0.84 us (1%)
  other arithmetic  0.78 us (1%)
    all_to_all x3, waiting for transfers between devices, exchange(): lax.all_to_all(payload.reshape(ndev, rows // ndev, width), AXES, split_ax...  24.5 us
    pallas_call x9, Pallas kernels, call(): pl.pallas_call(kernel, out_shape=[jax.ShapeDtypeStruct(o.shape, o.dtype)...  17.1 us
    all_to_all x3, starting transfers between devices, exchange(): lax.all_to_all(payload.reshape(ndev, rows // ndev, width), AXES, split_ax...  12.3 us
    ppermute x6, starting transfers between devices, send(): return lax.ppermute(block, AXES, pairs)  11.2 us
    unnamed x14, local copies, waits for them, and re-layouts  4.76 us
    reshape x2, local copies, waits for them, and re-layouts, local(): taps = conv_weight.reshape(3, 3, 3, chans, chans)  2.13 us
    reshape x2, local copies, waits for them, and re-layouts, local(): wb = taps.transpose(1, 0, 4, 2, 3).reshape(9 * chans, rows)  1.64 us
  transfers between devices with their start and end apart: 9, of which 3 were waited for; matrix products, arithmetic and copies ran while one was open for 9% of the time, Pallas kernels for 16%

profile of v2, /device:TPU:0, one launch (start us, length us, event | category | flops | bytes accessed | tf_op | source)
XLA Modules:
  0.0 75.9 jit_solution(18436260349091595934)
XLA Ops:
  0.6 0.7 fusion.4
  1.3 0.0 copy-start
  1.4 1.0 %copy-done = bf16[64,1,16,256]{3,2,1,0:T(8,128)(2,1)S(1)} copy-done((bf16[64,1,16,256]{3,2,1,0:T(8,128)(2,1)S(1)}, bf16[64,1,16,256]{3,2,1,0:T(8,128)(2,1)}, u32[]{:S(2)}) %copy-start) | copy-done | bytes 524312
  2.4 0.0 copy-start.5
  2.4 0.3 shard_map.102.plane_ref.own_ref
  2.7 0.5 collective-permute-start
  3.2 2.9 %collective-permute-start.1 = (bf16[1040,256]{1,0:T(8,128)(2,1)S(1)}, bf16[1040,256]{1,0:T(8,128)(2,1)S(1)}, u32[]{:S(2)}, u32[]{:S(2)}) collective-permute-start(bf16[1040,256]{1,0:T(8,128)(2,1)S(1)} %shard_map.102.plane_ref.own_ref), channel_id=1, source_target_pairs={{0,28},{1,29},{2,30},{3,31},{4,0},{5,1},{6,2},{7,3},{8,4},{9,5},{1... | collective-permute-start | bytes 1597448 | tf_op jit(solution)/shard_map/ppermute | solution.py:44
  6.1 0.0 copy-start.2
  6.1 0.8 copy-done.2
  6.9 0.0 copy-start.3
  6.9 0.7 copy-done.3
  7.5 0.9 %shard_map.103 = bf16[768,128]{1,0:T(8,128)(2,1)} custom-call(s32[1,32]{1,0:T(1,128)S(1)} %copy-done.3, bf16[128,128]{1,0:T(8,128)(2,1)S(1)} %copy-done.2, bf16[1040,256]{1,0:T(8,128)(2,1)S(1)} %shard_map.102.plane_ref.own_ref), custom_call_target="tpu_custom_call" | custom-call | flops 8388608 | bytes 761984 | tf_op jit(solution)/shard_map/pallas_call | solution.py:24
  8.5 5.6 %all-to-all-start = ((bf16[32,24,128]{2,1,0:T(8,128)(2,1)}), bf16[32,24,128]{2,1,0:T(8,128)(2,1)S(1)}, u32[]{:S(2)}, u32[]{:S(2)}) async-start(bf16[32,24,128]{2,1,0:T(8,128)(2,1)} %bitcast.1), calls=%async_computation | async-start | bytes 393216 | tf_op jit(solution)/shard_map/all_to_all | solution.py:49
  14.1 0.0 copy-done.5
  14.1 0.9 %copy.16 = bf16[3,3,3,64,64]{3,2,1,4,0:T(4,128)(2,1)S(1)} copy(bf16[3,3,3,64,64]{4,3,2,1,0:T(8,128)(2,1)S(1)} %bitcast.41) | data formatting | bytes 442368 | tf_op jit(solution)/shard_map/reshape | solution.py:422
  15.1 1.2 %copy.25 = bf16[3,3,3,64,64]{4,0,1,3,2:T(4,128)(2,1)} copy(bf16[3,3,3,64,64]{4,3,2,1,0:T(8,128)(2,1)S(1)} %bitcast.42) | data formatting | bytes 442368 | tf_op jit(solution)/shard_map/reshape | solution.py:422
  16.3 0.0 copy-start.1
  16.3 1.2 %copy.26 = bf16[64,1,16,256]{3,0,2,1:T(8,128)(2,1)S(1)} copy(bf16[64,1,16,256]{3,2,1,0:T(8,128)(2,1)} %param.13) | data formatting | bytes 1048576 | tf_op args[6]
  17.5 0.4 reshape.45
  17.9 0.2 copy.17.wf_ref
  18.1 1.5 %reshape.46 = bf16[576,192]{0,1:T(8,128)(2,1)S(1)} reshape(bf16[3,3,64,3,64]{2,1,0,4,3:T(4,128)(2,1)} %bitcast.39) | data formatting | bytes 442368 | tf_op jit(solution)/shard_map/reshape | solution.py:424
  19.6 0.2 copy.20.wb_ref
  19.7 3.7 %all-to-all-done = bf16[32,24,128]{2,1,0:T(8,128)(2,1)S(1)} async-done(((bf16[32,24,128]{2,1,0:T(8,128)(2,1)}), bf16[32,24,128]{2,1,0:T(8,128)(2,1)S(1)}, u32[]{:S(2)}, u32[]{:S(2)}) %all-to-all-start) | async-done | bytes 196640 | tf_op jit(solution)/shard_map/all_to_all | solution.py:49
  23.5 0.0 collective-permute-done.west_ref
  23.5 0.0 collective-permute-done.1.east_ref
  23.5 0.0 copy-done.1
  23.5 1.1 %shard_map.104 = (bf16[16,192,256]{2,1,0:T(8,128)(2,1)S(1)}, bf16[192,256]{1,0:T(8,128)(2,1)S(1)}, bf16[192,256]{1,0:T(8,128)(2,1)S(1)}) custom-call(bf16[768,128]{1,0:T(8,128)(2,1)S(1)} %bitcast.32, bf16[1040,256]{1,0:T(8,128)(2,1)S(1)} %shard_map.102.plane_ref.own_ref, bf16[1040,256]{1,0:T(8,128)(2,1)S(1)} %collective-permute-done.west_ref, ...), custom_call_target="tpu_custom_call" | custom-call | flops 25165824 | bytes 3579904 | tf_op jit(solution)/shard_map/pallas_call | solution.py:24
  24.6 0.1 collective-permute-start.2
  24.6 3.8 %collective-permute-start.3 = (bf16[192,256]{1,0:T(8,128)(2,1)S(1)}, bf16[192,256]{1,0:T(8,128)(2,1)S(1)}, u32[]{:S(2)}, u32[]{:S(2)}) collective-permute-start(bf16[192,256]{1,0:T(8,128)(2,1)S(1)} %get-tuple-element.26.first_ref), channel_id=1, source_target_pairs={{0,3},{1,0},{2,1},{3,2},{4,7},{5,4},{6,5},{7,6},{8,11},{9,8},{10,9... | collective-permute-start | bytes 294920 | tf_op jit(solution)/shard_map/ppermute | solution.py:44
  28.4 7.3 %shard_map.105 = (bf16[16,64,256]{2,1,0:T(8,128)(2,1)S(1)}, bf16[18,192,256]{2,1,0:T(8,128)(2,1)S(1)}, f32[192,256]{1,0:T(8,128)S(1)}, f32[192,256]{1,0:T(8,128)S(1)}, f32[576,192]{1,0:T(8,128)S(1)}) custom-call(bf16[16,192,256]{2,1,0:T(8,128)(2,1)S(1)} %get-tuple-element.22.x_ref, bf16[16,64,256]{2,1,0:T(8,128)(2,1)S(1)} %bitcast.28, ...), custom_call_target="tpu_custom_call" | custom-call | flops 1811939328 | bytes 5447680 | tf_op jit(solution)/shard_map/pallas_call | solution.py:24
  35.8 0.0 collective-permute-done.2.north_ref
  35.8 0.0 collective-permute-done.3.south_ref
  35.8 0.3 shard_map.106
  36.2 0.1 collective-permute-start.4
  36.2 3.8 %collective-permute-start.5 = (bf16[64,256]{1,0:T(8,128)(2,1)S(1)}, bf16[64,256]{1,0:T(8,128)(2,1)S(1)}, u32[]{:S(2)}, u32[]{:S(2)}) collective-permute-start(bf16[64,256]{1,0:T(8,128)(2,1)S(1)} %get-tuple-element.30.up_ref), channel_id=1, source_target_pairs={{0,3},{1,0},{2,1},{3,2},{4,7},{5,4},{6,5},{7,6},{8,11},{9,8},{10,9... | collective-permute-start | bytes 98312 | tf_op jit(solution)/shard_map/ppermute | solution.py:44
  40.0 3.5 %shard_map.107 = (bf16[864,128]{1,0:T(8,128)(2,1)S(1)}, f32[3,64,256]{2,1,0:T(8,128)S(1)}, f32[2,192,256]{2,1,0:T(8,128)S(1)}) custom-call(bf16[16,192,256]{2,1,0:T(8,128)(2,1)S(1)} %get-tuple-element.22.x_ref, bf16[18,192,256]{2,1,0:T(8,128)(2,1)S(1)} %get-tuple-element.29.s_ref, bf16[192,256]{1,0:T(8,128)(2,1)S(1)} %collective-permute-done.2.north_ref, ...), custom_call_target="tpu_custom_call" | custom-call | flops 905969664 | bytes 7200768 | tf_op jit(solution)/shard_map/pallas_call | solution.py:24
  43.6 0.0 collective-permute-done.4.before_ref
  43.6 0.0 collective-permute-done.5.after_ref
  43.6 0.0 copy-start.4
  43.6 1.3 %shard_map.108 = bf16[1536,128]{1,0:T(8,128)(2,1)} custom-call(f32[3,64,256]{2,1,0:T(8,128)S(1)} %get-tuple-element.33.sums_ref, f32[2,192,256]{2,1,0:T(8,128)S(1)} %get-tuple-element.34.edge_ref, bf16[64,256]{1,0:T(8,128)(2,1)S(1)} %collective-permute-done.4.before_ref, bf16[64,256]{1,0:T(8,128)(2,1)S(1)} %collective-permute-done.5.after_ref, ...), custom_call_target="tpu_custom_call" | custom-call | flops 37748736 | bytes 3809280 | tf_op jit(solution)/shard_map/pallas_call | solution.py:24
  44.9 2.8 %all-to-all-start.1 = ((bf16[32,48,128]{2,1,0:T(8,128)(2,1)}), bf16[32,48,128]{2,1,0:T(8,128)(2,1)S(1)}, u32[]{:S(2)}, u32[]{:S(2)}) async-start(bf16[32,48,128]{2,1,0:T(8,128)(2,1)} %bitcast.12), calls=%async_computation.1 | async-start | bytes 786432 | tf_op jit(solution)/shard_map/all_to_all | solution.py:49
  47.8 11.8 %all-to-all-done.1 = bf16[32,48,128]{2,1,0:T(8,128)(2,1)S(1)} async-done(((bf16[32,48,128]{2,1,0:T(8,128)(2,1)}), bf16[32,48,128]{2,1,0:T(8,128)(2,1)S(1)}, u32[]{:S(2)}, u32[]{:S(2)}) %all-to-all-start.1) | async-done | bytes 393248 | tf_op jit(solution)/shard_map/all_to_all | solution.py:49
  59.6 0.0 copy-done.4
  59.6 1.2 %shard_map.109 = (f32[128,128]{1,0:T(8,128)}, bf16[1024,128]{1,0:T(8,128)(2,1)}) custom-call(bf16[1536,128]{1,0:T(8,128)(2,1)S(1)} %bitcast.34, s32[1,1]{1,0:T(1,128)} %bitcast.14.index_ref, s32[1,32]{1,0:T(1,128)S(1)} %copy-done.4, bf16[64,128]{1,0:T(8,128)(2,1)S(1)} %bitcast.38), custom_call_target="tpu_custom_call" | custom-call | flops 4194304 | bytes 737412 | tf_op jit(solution)/shard_map/pallas_call | solution.py:24
  60.7 3.9 %all-to-all-start.2 = ((bf16[32,32,128]{2,1,0:T(8,128)(2,1)}), bf16[32,32,128]{2,1,0:T(8,128)(2,1)S(1)}, u32[]{:S(2)}, u32[]{:S(2)}) async-start(bf16[32,32,128]{2,1,0:T(8,128)(2,1)} %bitcast.15), calls=%async_computation.2 | async-start | bytes 524288 | tf_op jit(solution)/shard_map/all_to_all | solution.py:49
  64.7 0.1 maximum_bitcast_fusion
  64.7 1.1 %copy.22 = bf16[64,1,16,256]{3,2,1,0:T(8,128)(2,1)} copy(bf16[64,1,16,256]{3,0,2,1:T(8,128)(2,1)S(1)} %maximum_bitcast_fusion) | data formatting | bytes 1048576
  65.8 9.0 %all-to-all-done.2 = bf16[32,32,128]{2,1,0:T(8,128)(2,1)S(1)} async-done(((bf16[32,32,128]{2,1,0:T(8,128)(2,1)}), bf16[32,32,128]{2,1,0:T(8,128)(2,1)S(1)}, u32[]{:S(2)}, u32[]{:S(2)}) %all-to-all-start.2) | async-done | bytes 262176 | tf_op jit(solution)/shard_map/all_to_all | solution.py:49
  74.8 1.1 %shard_map.110 = (f32[27,64,64]{2,1,0:T(8,128)}, f32[64,128]{1,0:T(8,128)}) custom-call(bf16[1024,128]{1,0:T(8,128)(2,1)S(1)} %bitcast.35), custom_call_target="tpu_custom_call" | custom-call | flops 1000 | bytes 737280 | tf_op jit(solution)/shard_map/pallas_call | solution.py:24
  (4 shorter events, 0.1 us)
Async XLA Ops:
  1.3 1.0 %copy-start = (bf16[64,1,16,256]{3,2,1,0:T(8,128)(2,1)S(1)}, bf16[64,1,16,256]{3,2,1,0:T(8,128)(2,1)}, u32[]{:S(2)}) copy-start(bf16[64,1,16,256]{3,2,1,0:T(8,128)(2,1)} %param.10) | copy-start | bytes 1572868
  2.4 11.7 %copy-start.5 = (bf16[27,64,64]{2,1,0:T(8,128)(2,1)S(1)}, bf16[27,64,64]{2,1,0:T(8,128)(2,1)}, u32[]{:S(2)}) copy-start(bf16[27,64,64]{2,1,0:T(8,128)(2,1)} %param.12) | copy-start | bytes 663556
  2.7 20.8 %collective-permute-start = (bf16[1040,256]{1,0:T(8,128)(2,1)S(1)}, bf16[1040,256]{1,0:T(8,128)(2,1)S(1)}, u32[]{:S(2)}, u32[]{:S(2)}) collective-permute-start(bf16[1040,256]{1,0:T(8,128)(2,1)S(1)} %shard_map.102.plane_ref.own_ref), channel_id=1, source_target_pairs={{0,4},{1,5},{2,6},{3,7},{4,8},{5,9},{6,10},{7,11},{8,12},{9,13},{1... | collective-permute-start | bytes 1597448 | tf_op jit(solution)/shard_map/ppermute | solution.py:44
  3.2 20.3 %collective-permute-start.1 = (bf16[1040,256]{1,0:T(8,128)(2,1)S(1)}, bf16[1040,256]{1,0:T(8,128)(2,1)S(1)}, u32[]{:S(2)}, u32[]{:S(2)}) collective-permute-start(bf16[1040,256]{1,0:T(8,128)(2,1)S(1)} %shard_map.102.plane_ref.own_ref), channel_id=1, source_target_pairs={{0,28},{1,29},{2,30},{3,31},{4,0},{5,1},{6,2},{7,3},{8,4},{9,5},{1... | collective-permute-start | bytes 1597448 | tf_op jit(solution)/shard_map/ppermute | solution.py:44
  6.1 0.8 copy-start.2
  6.9 0.7 copy-start.3
  8.5 15.0 %all-to-all-start = ((bf16[32,24,128]{2,1,0:T(8,128)(2,1)}), bf16[32,24,128]{2,1,0:T(8,128)(2,1)S(1)}, u32[]{:S(2)}, u32[]{:S(2)}) async-start(bf16[32,24,128]{2,1,0:T(8,128)(2,1)} %bitcast.1), calls=%async_computation | async-start | bytes 393216 | tf_op jit(solution)/shard_map/all_to_all | solution.py:49
  16.3 7.2 %copy-start.1 = (bf16[128,64]{0,1:T(8,128)(2,1)S(1)}, bf16[128,64]{0,1:T(8,128)(2,1)}, u32[]{:S(2)}) copy-start(bf16[128,64]{0,1:T(8,128)(2,1)} %param.11) | copy-start | bytes 49156
  24.6 11.2 %collective-permute-start.2 = (bf16[192,256]{1,0:T(8,128)(2,1)S(1)}, bf16[192,256]{1,0:T(8,128)(2,1)S(1)}, u32[]{:S(2)}, u32[]{:S(2)}) collective-permute-start(bf16[192,256]{1,0:T(8,128)(2,1)S(1)} %get-tuple-element.25.last_ref), channel_id=1, source_target_pairs={{0,1},{1,2},{2,3},{3,0},{4,5},{5,6},{6,7},{7,4},{8,9},{9,10},{10,1... | collective-permute-start | bytes 294920 | tf_op jit(solution)/shard_map/ppermute | solution.py:44
  24.6 11.2 %collective-permute-start.3 = (bf16[192,256]{1,0:T(8,128)(2,1)S(1)}, bf16[192,256]{1,0:T(8,128)(2,1)S(1)}, u32[]{:S(2)}, u32[]{:S(2)}) collective-permute-start(bf16[192,256]{1,0:T(8,128)(2,1)S(1)} %get-tuple-element.26.first_ref), channel_id=1, source_target_pairs={{0,3},{1,0},{2,1},{3,2},{4,7},{5,4},{6,5},{7,6},{8,11},{9,8},{10,9... | collective-permute-start | bytes 294920 | tf_op jit(solution)/shard_map/ppermute | solution.py:44
  36.2 7.4 %collective-permute-start.4 = (bf16[64,256]{1,0:T(8,128)(2,1)S(1)}, bf16[64,256]{1,0:T(8,128)(2,1)S(1)}, u32[]{:S(2)}, u32[]{:S(2)}) collective-permute-start(bf16[64,256]{1,0:T(8,128)(2,1)S(1)} %get-tuple-element.31.down_ref), channel_id=1, source_target_pairs={{0,1},{1,2},{2,3},{3,0},{4,5},{5,6},{6,7},{7,4},{8,9},{9,10},{10,1... | collective-permute-start | bytes 98312 | tf_op jit(solution)/shard_map/ppermute | solution.py:44
  36.2 7.4 %collective-permute-start.5 = (bf16[64,256]{1,0:T(8,128)(2,1)S(1)}, bf16[64,256]{1,0:T(8,128)(2,1)S(1)}, u32[]{:S(2)}, u32[]{:S(2)}) collective-permute-start(bf16[64,256]{1,0:T(8,128)(2,1)S(1)} %get-tuple-element.30.up_ref), channel_id=1, source_target_pairs={{0,3},{1,0},{2,1},{3,2},{4,7},{5,4},{6,5},{7,6},{8,11},{9,8},{10,9... | collective-permute-start | bytes 98312 | tf_op jit(solution)/shard_map/ppermute | solution.py:44
  43.6 16.0 %copy-start.4 = (s32[1,32]{1,0:T(1,128)S(1)}, s32[1,32]{1,0:T(1,128)}, u32[]{:S(2)}) copy-start(s32[1,32]{1,0:T(1,128)} %counts_ref.3) | copy-start | bytes 388
  44.9 14.7 %all-to-all-start.1 = ((bf16[32,48,128]{2,1,0:T(8,128)(2,1)}), bf16[32,48,128]{2,1,0:T(8,128)(2,1)S(1)}, u32[]{:S(2)}, u32[]{:S(2)}) async-start(bf16[32,48,128]{2,1,0:T(8,128)(2,1)} %bitcast.12), calls=%async_computation.1 | async-start | bytes 786432 | tf_op jit(solution)/shard_map/all_to_all | solution.py:49
  60.7 14.1 %all-to-all-start.2 = ((bf16[32,32,128]{2,1,0:T(8,128)(2,1)}), bf16[32,32,128]{2,1,0:T(8,128)(2,1)S(1)}, u32[]{:S(2)}, u32[]{:S(2)}) async-start(bf16[32,32,128]{2,1,0:T(8,128)(2,1)} %bitcast.15), calls=%async_computation.2 | async-start | bytes 524288 | tf_op jit(solution)/shard_map/all_to_all | solution.py:49

commit v3 on v2

--- a/solution.py
+++ b/solution.py
@@ -100,11 +100,25 @@
     return out.astype(BF16), grad.astype(BF16)
 
 
-def plane_kernel(base_ref, lists_ref, out_ref):
+def plane_kernel(base_ref, cells_ref, rows_ref, counts_ref, out_ref, rows_out_ref, counts_out_ref):
     chans, cy, nz = base_ref.shape
+    rows_out_ref[...] = rows_ref[...]
+    counts_out_ref[...] = counts_ref[...]
     turned = jnp.swapaxes(base_ref[...].astype(F32), 0, 1)
     out_ref[pl.ds(0, cy * chans)] = turned.reshape(cy * chans, nz).astype(BF16)
-    out_ref[pl.ds(cy * chans, lists_ref.shape[0])] = lists_ref[...]
+    cells = cells_ref[...]
+    slots = cells.shape[1]
+    nl = -(-slots // nz)
+    tail = out_ref.shape[0] - cy * chans
+    lines = []
+    for values in (cells // nz, cells % nz):
+        values = values.astype(F32)
+        if nl * nz > slots:
+            values = jnp.concatenate([values, jnp.zeros((1, nl * nz - slots), F32)], axis=1)
+        lines += [values[:, n * nz : (n + 1) * nz] for n in range(nl)]
+    if tail > 2 * nl:
+        lines.append(jnp.zeros((tail - 2 * nl, nz), F32))
+    out_ref[pl.ds(cy * chans, tail)] = jnp.concatenate(lines, axis=0).astype(BF16)
 
 
 def pick_kernel(ngx, ngy, cap, counts_ref, rows_ref, plane_ref, out_ref):
@@ -127,7 +141,7 @@
 
 def paint_kernel(
     ndev, cap, chans, cy, nz,
-    recv_ref, own_ref, west_ref, east_ref, proj_t_ref,
+    recv_ref, own_ref, west_ref, east_ref, proj_t_ref, cot_ref,
     x_ref, first_ref, last_ref, masked,
 ):
     slots = ndev * cap
@@ -145,24 +159,33 @@
             part = painted[n * chans : (n + 1) * chans]
             field = (ref[rows].astype(F32) + part).astype(BF16)
             x_ref[n, lanes] = field
-            if n == 0:
-                first_ref[lanes] = field
-            if n == cy - 1:
-                last_ref[lanes] = field
+            if n < 2:
+                first_ref[pl.ds((3 * n + dx) * chans, chans)] = field
+            if n >= cy - 2:
+                last_ref[pl.ds((3 * (n - cy + 2) + dx) * chans, chans)] = field
+    first_ref[pl.ds(6 * chans, chans)] = cot_ref[0]
+    last_ref[pl.ds(6 * chans, chans)] = cot_ref[cy - 1]
+
+
+def list_of(ref, cy, chans, slots):
+    tail = ref.shape[0] - cy * chans
+    return widths(-(-slots // ref.shape[1]), slots, ref[pl.ds(cy * chans, tail)])
 
 
 def conv_kernel(
-    chans, cy, x_ref, cot_ref, wf_ref,
-    out_ref, s_ref, top_ref, bottom_ref, total_ref, acc,
+    ndev, cap, chans, cy, x_ref, cot_ref, wf_ref, wb_ref, own_ref, west_ref, east_ref,
+    out_ref, total_ref, pre_ref, slot_ref, sums_ref, acc, grads, back, plane,
 ):
     rows = 3 * chans
+    nz = x_ref.shape[2]
+    slots = ndev * cap
     own = pl.ds(chans, chans)
-    zeros = jnp.zeros(s_ref.shape[1:], BF16)
+    zeros = jnp.zeros((rows, nz), BF16)
     for t in (0, 1, cy, cy + 1):
-        s_ref[t] = zeros
+        grads[t] = zeros
     out_ref[0] = zeros[:chans]
     out_ref[cy - 1] = zeros[:chans]
-    acc[0] = jnp.zeros(acc.shape[1:], F32)
+    acc[0] = jnp.zeros((rows, nz), F32)
 
     def spread(n):
         terms = mm(wf_ref[...], x_ref[n])
@@ -170,147 +193,118 @@
         acc[n] += terms[rows : 2 * rows]
         return terms[2 * rows :]
 
-    spread(0)
-    top_ref[...] = acc[0] + spread(1)
+    pre_ref[0] = spread(0)
+    pre_ref[1] = acc[0] + spread(1)
 
     def forward(n, carry):
         done = spread(n) + acc[n - 1]
         y = n - 1
         out, grad = finish_row(done, x_ref[y, own], cot_ref[y])
         out_ref[y] = out
-        s_ref[y + 1] = stacked(grad)
+        grads[y + 1] = stacked(grad)
         return carry
 
     lax.fori_loop(2, cy, forward, 0, unroll=2)
-    bottom_ref[...] = acc[cy - 1]
+    pre_ref[2] = acc[cy - 1]
+    pre_ref[3] = acc[cy]
     total_ref[...] = jnp.zeros_like(total_ref)
-
-    def taps(n, carry):
-        grads = s_ref[pl.ds(n, 3)].reshape(3 * rows, s_ref.shape[2])
-        total_ref[...] += mm(grads, x_ref[n], NT)
+    back[0] = jnp.zeros((rows, nz), F32)
+    back[1] = jnp.zeros((rows, nz), F32)
+
+    def taps(n):
+        window = grads[pl.ds(n, 3)].reshape(3 * rows, nz)
+        total_ref[...] += mm(window, x_ref[n], NT)
+
+    def spread_back(n):
+        terms = mm(wb_ref[...], grads[n + 1])
+        back[n + 1] = terms[2 * rows :]
+        back[n] += terms[rows : 2 * rows]
+        return terms[:rows]
+
+    def backward(n, carry):
+        taps(n)
+        value = spread_back(n) + back[n - 1]
+        for dx in range(3):
+            part = value[dx * chans : (dx + 1) * chans]
+            if dx == 1:
+                part = part + cot_ref[n - 1].astype(F32)
+            plane[dx, pl.ds((n - 3) * chans, chans)] = part.astype(BF16)
         return carry
 
-    lax.fori_loop(0, cy, taps, 0, unroll=2)
+    taps(0)
+    taps(1)
+    slot_ref[0] = spread_back(1)
+    taps(2)
+    slot_ref[1] = spread_back(2) + back[1]
+    lax.fori_loop(3, cy - 1, backward, 0, unroll=2)
+    taps(cy - 1)
+    slot_ref[2] = back[cy - 2]
+    slot_ref[3] = back[cy - 1]
+    zero = jnp.zeros((chans, slots), F32)
+    for dx, ref in enumerate((west_ref, own_ref, east_ref)):
+        sums_ref[dx] = at_slots(plane[dx], list_of(ref, cy, chans, slots), range(2, cy - 2), zero)
+
+
+def at_slots(part, cells, first, total):
+    chans = total.shape[0]
+    y, z = cells
+    found = mm(part, picked_depth(z, part.shape[1]))
+    for n, row in enumerate(first):
+        total = total + jnp.where(y == row, found[n * chans : (n + 1) * chans], 0.0)
+    return total
 
 
 def edge_kernel(
-    chans, cy, top_ref, bottom_ref, north_ref, south_ref, first_ref, last_ref, cot_ref, wf_ref,
-    out_ref, up_ref, down_ref,
-):
-    rows = 3 * chans
-    own = pl.ds(chans, chans)
-    top = top_ref[...] + mm(wf_ref[pl.ds(0, rows)], north_ref[...])
-    out_ref[0], up_ref[...] = finish_row(top, first_ref[own], cot_ref[0])
-    bottom = bottom_ref[...] + mm(wf_ref[pl.ds(2 * rows, rows)], south_ref[...])
-    out_ref[1], down_ref[...] = finish_row(bottom, last_ref[own], cot_ref[cy - 1])
-
-
-def at_slots(parts, ylists, hots, first, total):
-    chans = total[0].shape[0]
-    new = []
-    for dx in range(3):
-        found = mm(parts[dx], hots[dx])
-        value = total[dx]
-        for n in range(len(first)):
-            here = ylists[dx] == first[n]
-            value = value + jnp.where(here, found[n * chans : (n + 1) * chans], 0.0)
-        new.append(value)
-    return new
-
-
-def slot_kernel(
-    ndev, cap, chans, cy, nz,
-    x_ref, s_ref, north_ref, south_ref, up_ref, down_ref, cot_ref, total_ref, wb_ref,
-    own_ref, west_ref, east_ref,
-    grads_ref, sums_ref, edge_ref, acc, plane, total,
+    ndev, cap, chans, cy,
+    pre_ref, slot_ref, sums_ref, total_ref, north_ref, south_ref, first_ref, last_ref,
+    wf_ref, wb_ref, cot_ref, own_ref, west_ref, east_ref, recv_ref,
+    out_ref, send_ref, total,
 ):
     rows = 3 * chans
     slots = ndev * cap
-    nl = -(-slots // nz)
-    up, down = stacked(up_ref[...]), stacked(down_ref[...])
-    for block, high, middle, low in (
-        (0, x_ref[1], x_ref[0], north_ref[...]),
-        (cy - 1, south_ref[...], x_ref[cy - 1], x_ref[cy - 2]),
-    ):
-        grads = up if block == 0 else down
-        for n, field in enumerate((high, middle, low)):
-            at = pl.ds(n * rows, rows)
-            base = total_ref[at] if block == 0 else total[at]
-            total[at] = base + mm(grads, field, NT)
-    grads_ref[pl.ds(0, 3 * rows)] = total[:, : 2 * chans].astype(BF16)
-    last = total[:, 2 * chans :]
-    half = 3 * rows // 2
-    last = jnp.concatenate([last[:half], last[half:]], axis=1)
-    grads_ref[pl.ds(3 * rows, half)] = last.astype(BF16)
-
-    def keep(n, value):
-        for dx in range(3):
-            part = value[dx * chans : (dx + 1) * chans]
-            if dx == 1:
-                part = part + cot_ref[n].astype(F32)
-            plane[dx, pl.ds((n - 1) * chans, chans)] = part.astype(BF16)
-
-    def spread(n, grads):
-        terms = mm(wb_ref[...], grads)
-        acc[n + 1] = terms[2 * rows :]
-        acc[n] += terms[rows : 2 * rows]
-        return terms[:rows]
-
-    acc[0] = jnp.zeros(acc.shape[1:], F32)
-    spread(0, up)
-    edge_ref[0] = acc[0] + spread(1, s_ref[2])
-
-    def backward(n, carry):
-        keep(n - 1, spread(n, s_ref[n + 1]) + acc[n - 1])
-        return carry
-
-    lax.fori_loop(2, cy - 1, backward, 0, unroll=2)
-    keep(cy - 2, spread(cy - 1, down) + acc[cy - 2])
-    edge_ref[1] = acc[cy - 1]
-    ylists, hots = [], []
-    for ref in (west_ref, own_ref, east_ref):
-        y, z = widths(nl, slots, ref[pl.ds(cy * chans, ref.shape[0] - cy * chans)])
-        ylists.append(y)
-        hots.append(picked_depth(z, nz))
-    zero = jnp.zeros((chans, slots), F32)
-    found = at_slots([plane[dx] for dx in range(3)], ylists, hots, range(1, cy - 1), [zero] * 3)
-    for dx in range(3):
-        sums_ref[dx] = found[dx]
-
-
-def return_kernel(
-    ndev, cap, chans, cy, nz,
-    sums_ref, edge_ref, before_ref, after_ref, cot_ref, wb_ref,
-    own_ref, west_ref, east_ref, recv_ref, grads_ref, out_ref,
-):
-    rows = 3 * chans
-    slots = ndev * cap
-    nl = -(-slots // nz)
-    top = edge_ref[0] + mm(wb_ref[pl.ds(2 * rows, rows)], stacked(before_ref[...]))
-    bottom = edge_ref[1] + mm(wb_ref[pl.ds(0, rows)], stacked(after_ref[...]))
-    ylists, hots, parts = [], [], []
+    own = slice(chans, 2 * chans)
+    fields = [ref[pl.ds(n * rows, rows)] for ref in (north_ref, first_ref, last_ref, south_ref) for n in (0, 1)]
+    cots = [ref[pl.ds(2 * rows, chans)] for ref in (north_ref, first_ref, last_ref, south_ref)]
+    near = mm(wf_ref[pl.ds(0, 2 * rows)], fields[1])
+    pre = [pre_ref[0] + near[rows:] + mm(wf_ref[pl.ds(0, rows)], fields[0]), pre_ref[1] + near[:rows]]
+    near = mm(wf_ref[pl.ds(rows, 2 * rows)], fields[6])
+    pre += [pre_ref[2] + near[rows:], pre_ref[3] + near[:rows] + mm(wf_ref[pl.ds(2 * rows, rows)], fields[7])]
+    at = (1, 2, 5, 6)
+    ends = [finish_row(pre[n], fields[at[n]][own], cots[n]) for n in range(4)]
+    out_ref[0], out_ref[1] = ends[1][0], ends[2][0]
+    grads = [stacked(grad) for _, grad in ends]
+    for n in range(3):
+        here = pl.ds(n * rows, rows)
+        total[here] = total_ref[here] + (mm(grads[1], fields[3 - n], NT) + mm(grads[2], fields[6 - n], NT))
+    inner = mm(wb_ref[pl.ds(rows, 2 * rows)], grads[1])
+    top = slot_ref[0] + inner[:rows] + mm(wb_ref[pl.ds(2 * rows, rows)], grads[0])
+    second = slot_ref[1] + inner[rows:]
+    inner = mm(wb_ref[pl.ds(0, 2 * rows)], grads[2])
+    third = slot_ref[2] + inner[:rows]
+    bottom = slot_ref[3] + inner[rows:] + mm(wb_ref[pl.ds(0, rows)], grads[3])
+    found = []
     for dx, ref in enumerate((west_ref, own_ref, east_ref)):
-        y, z = widths(nl, slots, ref[pl.ds(cy * chans, ref.shape[0] - cy * chans)])
-        ylists.append(y)
-        hots.append(picked_depth(z, nz))
-        at = slice(dx * chans, (dx + 1) * chans)
-        pair = [top[at], bottom[at]]
+        parts = [value[dx * chans : (dx + 1) * chans] for value in (top, second, third, bottom)]
         if dx == 1:
-            pair = [pair[0] + cot_ref[0].astype(F32), pair[1] + cot_ref[cy - 1].astype(F32)]
-        parts.append(jnp.concatenate(pair, axis=0).astype(BF16))
-    found = at_slots(parts, ylists, hots, (0, cy - 1), [sums_ref[dx] for dx in range(3)])
+            inner = (cots[1], cot_ref[1], cot_ref[cy - 2], cots[2])
+            parts = [part + cot.astype(F32) for part, cot in zip(parts, inner)]
+        part = jnp.concatenate(parts, axis=0).astype(BF16)
+        cells = list_of(ref, cy, chans, slots)
+        found.append(at_slots(part, cells, (0, 1, cy - 2, cy - 1), sums_ref[dx]))
     raws = rows_in(recv_ref, ndev, cap)
     proj = sum(mm(found[dx].astype(BF16), raws[dx]) for dx in range(3))
     proj_high = proj.astype(BF16).astype(F32)
     sides = jnp.concatenate([found[0], found[2]], axis=0).T
     middle = jnp.concatenate([found[1], jnp.zeros_like(found[1])], axis=0).T
-    width = out_ref.shape[1]
-    share = out_ref.shape[0] // ndev - 2 * cap
-    used = grads_ref.shape[0] + 2 * chans
-    pad = jnp.zeros((share * ndev - used, width), F32)
+    width = send_ref.shape[1]
+    share = send_ref.shape[0] // ndev - 2 * cap
+    taps = total[:, 2 * chans :]
+    half = 3 * rows // 2
+    taps = jnp.concatenate([taps[:half], taps[half:]], axis=1)
     halves = [v.reshape(2 * chans // share, share // 2, width) for v in (proj_high, proj - proj_high)]
     proj = jnp.stack(halves, axis=1).reshape(2 * chans, width)
-    sums = jnp.concatenate([grads_ref[...].astype(F32), proj, pad], axis=0)
+    pad = jnp.zeros((share * ndev - 3 * rows - half - 2 * chans, width), F32)
+    sums = jnp.concatenate([total[:, : 2 * chans], taps, proj, pad], axis=0)
     out = jnp.concatenate(
         [
             sums.reshape(ndev, share, width),
@@ -319,7 +313,7 @@
         ],
         axis=1,
     )
-    out_ref[...] = out.reshape(out_ref.shape).astype(BF16)
+    send_ref[...] = out.reshape(send_ref.shape).astype(BF16)
 
 
 def rows_kernel(
@@ -398,22 +392,18 @@
     rows = 3 * chans
     one = 2 * rows * rows * nz
 
-    nl = -(-slots // nz)
-    tail = -(-2 * nl // 16) * 16
-    lists = jnp.stack([cell_lists[0] // nz, cell_lists[0] % nz]).astype(BF16)
-    lists = jnp.pad(lists, ((0, 0), (0, nl * nz - slots))).reshape(2 * nl, nz)
-    lists = jnp.pad(lists, ((0, tail - 2 * nl), (0, 0)))
-    (plane,) = call(
+    tail = -(-2 * -(-slots // nz) // 16) * 16
+    plane, particles, counts = call(
         plane_kernel,
-        [shape((cy * chans + tail, nz), BF16)],
-        (base_field.reshape(chans, cy, nz), lists),
+        [shape((cy * chans + tail, nz), BF16), particles, send_counts],
+        (base_field.reshape(chans, cy, nz), cell_lists, particles, send_counts),
         1000,
     )
     west, east = move(plane, 1, 0), move(plane, -1, 0)
     (payload,) = call(
         functools.partial(pick_kernel, ngx, ngy, cap),
         [shape((ndev * 3 * cap, feats), BF16)],
-        (send_counts, particles, plane),
+        (counts, particles, plane),
         2 * slots * nrows * feats,
     )
     recv = exchange(payload, ndev)
@@ -425,61 +415,48 @@
 
     x_all, first, last = call(
         functools.partial(paint_kernel, ndev, cap, chans, cy, nz),
-        [shape((cy, rows, nz), BF16), shape((rows, nz), BF16), shape((rows, nz), BF16)],
-        (recv, plane, west, east, proj_t),
-        6 * slots * count * chans // nz * nz // 16,
+        [shape((cy, rows, nz), BF16)] + [shape((2 * rows + chans, nz), BF16)] * 2,
+        (recv, plane, west, east, proj_t, cot),
+        6 * slots * count * chans,
         (pltpu.VMEM((cy * chans, slots), BF16),),
     )
     north, south = move(last, 0, 1), move(first, 0, -1)
-    out_rows, s_all, top, bottom, total = call(
-        functools.partial(conv_kernel, chans, cy),
+    out_rows, total, pre_edge, slot_edge, sums = call(
+        functools.partial(conv_kernel, ndev, cap, chans, cy),
         [
             shape((cy, chans, nz), BF16),
-            shape((cy + 2, rows, nz), BF16),
-            shape((rows, nz), F32),
-            shape((rows, nz), F32),
             shape((9 * chans, rows), F32),
+            shape((4, rows, nz), F32),
+            shape((4, rows, nz), F32),
+            shape((3, chans, slots), F32),
         ],
-        (x_all, cot, wf),
-        2 * cy * 3 * one,
-        (pltpu.VMEM((cy + 1, rows, nz), F32),),
-    )
-    out_edge, up, down = call(
-        functools.partial(edge_kernel, chans, cy),
-        [shape((2, chans, nz), BF16), shape((chans, nz), BF16), shape((chans, nz), BF16)],
-        (top, bottom, north, south, first, last, cot, wf),
-        2 * one,
-    )
-    before, after = move(down, 0, 1), move(up, 0, -1)
-    grad_rows = 27 * chans * chans // feats
-    tap_grads, sums, edge = call(
-        functools.partial(slot_kernel, ndev, cap, chans, cy, nz),
-        [
-            shape((grad_rows, feats), BF16),
-            shape((3, chans, slots), F32),
-            shape((2, rows, nz), F32),
-        ],
-        (x_all, s_all, north, south, up, down, cot, total, wb, plane, west, east),
-        cy * 3 * one,
+        (x_all, cot, wf, wb, plane, west, east),
+        3 * cy * 3 * one,
         (
             pltpu.VMEM((cy + 1, rows, nz), F32),
-            pltpu.VMEM((3, (cy - 2) * chans, nz), BF16),
-            pltpu.VMEM((9 * chans, rows), F32),
+            pltpu.VMEM((cy + 2, rows, nz), BF16),
+            pltpu.VMEM((cy, rows, nz), F32),
+            pltpu.VMEM((3, (cy - 4) * chans, nz), BF16),
         ),
     )
+    grad_rows = 27 * chans * chans // feats
     share = -(-(grad_rows + 2 * chans) // (16 * ndev)) * 16
-    (payload,) = call(
-        functools.partial(return_kernel, ndev, cap, chans, cy, nz),
-        [shape((ndev * (share + 2 * cap), feats), BF16)],
-        (sums, edge, before, after, cot, wb, plane, west, east, recv, tap_grads),
-        2 * one,
+    out_edge, payload = call(
+        functools.partial(edge_kernel, ndev, cap, chans, cy),
+        [shape((2, chans, nz), BF16), shape((ndev * (share + 2 * cap), feats), BF16)],
+        (
+            pre_edge, slot_edge, sums, total, north, south, first, last,
+            wf, wb, cot, plane, west, east, recv,
+        ),
+        12 * one,
+        (pltpu.VMEM((9 * chans, rows), F32),),
     )
     recv = exchange(payload, ndev)
     index = (lax.axis_index("gx") * ngy + lax.axis_index("gy")).astype(I32).reshape(1, 1)
     row_grads, sums = call(
         functools.partial(rows_kernel, ngx, ngy, cap, chans),
         [shape((nrows, feats), F32), shape((ndev * share, feats), BF16)],
-        (recv, index, send_counts, proj_t),
+        (recv, index, counts, proj_t),
         2 * nrows * slots * chans,
     )
     recv = exchange(sums, ndev)

time: 76.4 us -> 72.2 us (0.945)
  starting transfers between devices: 23.5 us -> 20.3 us
  Pallas kernels: 17.1 us -> 14.4 us
  local copies, waits for them, and re-layouts: 9.14 us -> 10.5 us
  waiting for transfers between devices: 24.5 us -> 25.5 us
    ppermute x6 -> x4, starting transfers between devices: 11.2 us -> 7.33 us  [send(): return lax.ppermute(block, AXES, pairs)]
    pallas_call x9 -> x7, Pallas kernels: 17.1 us -> 14.4 us  [call(): pl.pallas_call(kernel, out_shape=[jax.ShapeDtypeStruct(o.shape, o.dtype)...]
    unnamed x14 -> x16, local copies, waits for them, and re-layouts: 4.76 us -> 6.16 us
    ppermute x6 -> x4, waiting for transfers between devices: 0.02 us -> 1 us  [send(): return lax.ppermute(block, AXES, pairs)]
  transfers between devices with their start and end apart: 9 -> 7, of which waited for: 3 -> 4; matrix products, arithmetic and copies ran while one was open for 9% -> 9% of each run, Pallas kernels for 16% -> 13%
where the time goes in v3:
time: 72.2 us; the launch traced here: 71.7 us
  waiting for transfers between devices  25.5 us (35%)
  starting transfers between devices  20.3 us (28%)
  Pallas kernels  14.4 us (20%)
  local copies, waits for them, and re-layouts  10.5 us (15%)
  between operations  0.79 us (1%)
    all_to_all x3, waiting for transfers between devices, exchange(): lax.all_to_all(payload.reshape(ndev, rows // ndev, width), AXES, split_ax...  24.5 us
    pallas_call x7, Pallas kernels, call(): pl.pallas_call(kernel, out_shape=[jax.ShapeDtypeStruct(o.shape, o.dtype)...  14.4 us
    all_to_all x3, starting transfers between devices, exchange(): lax.all_to_all(payload.reshape(ndev, rows // ndev, width), AXES, split_ax...  13 us
    ppermute x4, starting transfers between devices, send(): return lax.ppermute(block, AXES, pairs)  7.33 us
    unnamed x16, local copies, waits for them, and re-layouts  6.16 us
    reshape x2, local copies, waits for them, and re-layouts, local(): taps = conv_weight.reshape(3, 3, 3, chans, chans)  2.13 us
    reshape x2, local copies, waits for them, and re-layouts, local(): wb = taps.transpose(1, 0, 4, 2, 3).reshape(9 * chans, rows)  1.65 us
  transfers between devices with their start and end apart: 7, of which 4 were waited for; matrix products, arithmetic and copies ran while one was open for 9% of the time, Pallas kernels for 13%

profile of v3, /device:TPU:0, one launch (start us, length us, event | category | flops | bytes accessed | tf_op | source)
XLA Modules:
  0.0 71.7 jit_solution(17184030626967754236)
XLA Ops:
  0.6 0.0 copy-start
  0.6 1.0 %copy-done = bf16[64,1,16,256]{3,2,1,0:T(8,128)(2,1)S(1)} copy-done((bf16[64,1,16,256]{3,2,1,0:T(8,128)(2,1)S(1)}, bf16[64,1,16,256]{3,2,1,0:T(8,128)(2,1)}, u32[]{:S(2)}) %copy-start) | copy-done | bytes 524312
  1.7 0.0 copy-start.3
  1.7 0.8 %copy-done.3 = bf16[128,128]{1,0:T(8,128)(2,1)S(1)} copy-done((bf16[128,128]{1,0:T(8,128)(2,1)S(1)}, bf16[128,128]{1,0:T(8,128)(2,1)}, u32[]{:S(2)}) %copy-start.3) | copy-done | bytes 32792
  2.4 0.0 copy-start.4
  2.4 0.7 copy-done.4
  3.1 0.0 copy-start.5
  3.1 0.7 copy-done.5
  3.8 0.0 copy-start.6
  3.8 0.3 shard_map.102
  4.0 0.5 collective-permute-start
  4.6 2.9 %collective-permute-start.1 = (bf16[1040,256]{1,0:T(8,128)(2,1)S(1)}, bf16[1040,256]{1,0:T(8,128)(2,1)S(1)}, u32[]{:S(2)}, u32[]{:S(2)}) collective-permute-start(bf16[1040,256]{1,0:T(8,128)(2,1)S(1)} %get-tuple-element.23.plane_ref.own_ref), channel_id=1, source_target_pairs={{0,28},{1,29},{2,30},{3,31},{4,0},{5,1},{6,2},{7,3},{8,4},{9,5},{1... | collective-permute-start | bytes 1597448 | tf_op jit(solution)/shard_map/ppermute | solution.py:44
  7.5 0.9 %shard_map.103 = bf16[768,128]{1,0:T(8,128)(2,1)} custom-call(s32[1,32]{1,0:T(1,128)S(1)} %get-tuple-element.21.counts_ref, bf16[128,128]{1,0:T(8,128)(2,1)S(1)} %get-tuple-element.22.rows_ref, bf16[1040,256]{1,0:T(8,128)(2,1)S(1)} %get-tuple-element.23.plane_ref.own_ref), custom_call_target="tpu_custom_call" | custom-call | flops 8388608 | bytes 761984 | tf_op jit(solution)/shard_map/pallas_call | solution.py:24
  8.4 5.6 %all-to-all-start = ((bf16[32,24,128]{2,1,0:T(8,128)(2,1)}), bf16[32,24,128]{2,1,0:T(8,128)(2,1)S(1)}, u32[]{:S(2)}, u32[]{:S(2)}) async-start(bf16[32,24,128]{2,1,0:T(8,128)(2,1)} %bitcast.1), calls=%async_computation | async-start | bytes 393216 | tf_op jit(solution)/shard_map/all_to_all | solution.py:49
  14.1 0.0 copy-done.6
  14.1 0.9 %copy.16 = bf16[3,3,3,64,64]{3,2,1,4,0:T(4,128)(2,1)S(1)} copy(bf16[3,3,3,64,64]{4,3,2,1,0:T(8,128)(2,1)S(1)} %bitcast.41) | data formatting | bytes 442368 | tf_op jit(solution)/shard_map/reshape | solution.py:412
  15.0 1.2 %copy.25 = bf16[3,3,3,64,64]{4,0,1,3,2:T(4,128)(2,1)} copy(bf16[3,3,3,64,64]{4,3,2,1,0:T(8,128)(2,1)S(1)} %bitcast.42) | data formatting | bytes 442368 | tf_op jit(solution)/shard_map/reshape | solution.py:412
  16.2 1.2 %copy.26 = bf16[64,1,16,256]{3,0,2,1:T(8,128)(2,1)S(1)} copy(bf16[64,1,16,256]{3,2,1,0:T(8,128)(2,1)} %param.13) | data formatting | bytes 1048576 | tf_op args[6]
  17.4 0.0 copy-start.2
  17.5 0.4 reshape.45
  17.9 0.2 copy.18.wf_ref
  18.0 1.5 %reshape.46 = bf16[576,192]{0,1:T(8,128)(2,1)S(1)} reshape(bf16[3,3,64,3,64]{2,1,0,4,3:T(4,128)(2,1)} %bitcast.39) | data formatting | bytes 442368 | tf_op jit(solution)/shard_map/reshape | solution.py:414
  19.5 0.2 copy.19.wb_ref
  19.7 3.7 %all-to-all-done = bf16[32,24,128]{2,1,0:T(8,128)(2,1)S(1)} async-done(((bf16[32,24,128]{2,1,0:T(8,128)(2,1)}), bf16[32,24,128]{2,1,0:T(8,128)(2,1)S(1)}, u32[]{:S(2)}, u32[]{:S(2)}) %all-to-all-start) | async-done | bytes 196640 | tf_op jit(solution)/shard_map/all_to_all | solution.py:49
  23.4 0.0 collective-permute-done.west_ref
  23.4 0.0 collective-permute-done.1.east_ref
  23.4 0.0 copy-done.2
  23.4 1.1 %shard_map.104 = (bf16[16,192,256]{2,1,0:T(8,128)(2,1)S(1)}, bf16[448,256]{1,0:T(8,128)(2,1)S(1)}, bf16[448,256]{1,0:T(8,128)(2,1)S(1)}) custom-call(bf16[768,128]{1,0:T(8,128)(2,1)S(1)} %bitcast.31, bf16[1040,256]{1,0:T(8,128)(2,1)S(1)} %get-tuple-element.23.plane_ref.own_ref, bf16[1040,256]{1,0:T(8,128)(2,1)S(1)} %collective-permute-done.west_ref, ...), custom_call_target="tpu_custom_call" | custom-call | flops 402653184 | bytes 4366336 | tf_op jit(solution)/shard_map/pallas_call | solution.py:24
  24.5 1.2 %collective-permute-start.2 = (bf16[448,256]{1,0:T(8,128)(2,1)S(1)}, bf16[448,256]{1,0:T(8,128)(2,1)S(1)}, u32[]{:S(2)}, u32[]{:S(2)}) collective-permute-start(bf16[448,256]{1,0:T(8,128)(2,1)S(1)} %get-tuple-element.29.last_ref), channel_id=1, source_target_pairs={{0,1},{1,2},{2,3},{3,0},{4,5},{5,6},{6,7},{7,4},{8,9},{9,10},{10,1... | collective-permute-start | bytes 688136 | tf_op jit(solution)/shard_map/ppermute | solution.py:44
  25.7 2.7 %collective-permute-start.3 = (bf16[448,256]{1,0:T(8,128)(2,1)S(1)}, bf16[448,256]{1,0:T(8,128)(2,1)S(1)}, u32[]{:S(2)}, u32[]{:S(2)}) collective-permute-start(bf16[448,256]{1,0:T(8,128)(2,1)S(1)} %get-tuple-element.30.first_ref), channel_id=1, source_target_pairs={{0,3},{1,0},{2,1},{3,2},{4,7},{5,4},{6,5},{7,6},{8,11},{9,8},{10,9... | collective-permute-start | bytes 688136 | tf_op jit(solution)/shard_map/ppermute | solution.py:44
  28.4 8.5 %shard_map.105 = (bf16[16,64,256]{2,1,0:T(8,128)(2,1)S(1)}, f32[576,192]{1,0:T(8,128)S(1)}, f32[4,192,256]{2,1,0:T(8,128)S(1)}, f32[4,192,256]{2,1,0:T(8,128)S(1)}, f32[3,64,256]{2,1,0:T(8,128)S(1)}) custom-call(bf16[16,192,256]{2,1,0:T(8,128)(2,1)S(1)} %get-tuple-element.24.x_ref, bf16[16,64,256]{2,1,0:T(8,128)(2,1)S(1)} %bitcast.29, ...), custom_call_target="tpu_custom_call" | custom-call | flops 2717908992 | bytes 6873088 | tf_op jit(solution)/shard_map/pallas_call | solution.py:24
  36.9 0.0 collective-permute-done.2.north_ref
  37.0 1.0 %collective-permute-done.3.south_ref = bf16[448,256]{1,0:T(8,128)(2,1)S(1)} collective-permute-done((bf16[448,256]{1,0:T(8,128)(2,1)S(1)}, bf16[448,256]{1,0:T(8,128)(2,1)S(1)}, u32[]{:S(2)}, u32[]{:S(2)}) %collective-permute-start.3) | collective-permute-done | bytes 229408 | tf_op jit(solution)/shard_map/ppermute | solution.py:44
  37.9 1.3 %shard_map.106 = (bf16[2,64,256]{2,1,0:T(8,128)(2,1)S(1)}, bf16[1536,128]{1,0:T(8,128)(2,1)S(1)}) custom-call(f32[4,192,256]{2,1,0:T(8,128)S(1)} %get-tuple-element.25.pre_ref, f32[4,192,256]{2,1,0:T(8,128)S(1)} %get-tuple-element.26.slot_ref, f32[3,64,256]{2,1,0:T(8,128)S(1)} %get-tuple-element.27.sums_ref, f32[576,192]{1,0:T(8,128)S(1)} %get-tuple-element.28.total_ref, ...), custom_call_target="tpu_custom_call" | custom-call | flops 226492416 | bytes 6348800 | tf_op jit(solution)/shard_map/pallas_call | solution.py:24
  39.3 0.0 copy-start.1
  39.3 0.7 %copy-done.1 = bf16[1536,128]{1,0:T(8,128)(2,1)} copy-done((bf16[1536,128]{1,0:T(8,128)(2,1)}, bf16[1536,128]{1,0:T(8,128)(2,1)S(1)}, u32[]{:S(2)}) %copy-start.1) | copy-done | bytes 393240
  40.0 3.5 %all-to-all-start.1 = ((bf16[32,48,128]{2,1,0:T(8,128)(2,1)}), bf16[32,48,128]{2,1,0:T(8,128)(2,1)S(1)}, u32[]{:S(2)}, u32[]{:S(2)}) async-start(bf16[32,48,128]{2,1,0:T(8,128)(2,1)} %bitcast.36), calls=%async_computation.1 | async-start | bytes 786432 | tf_op jit(solution)/shard_map/all_to_all | solution.py:49
  43.5 11.8 %all-to-all-done.1 = bf16[32,48,128]{2,1,0:T(8,128)(2,1)S(1)} async-done(((bf16[32,48,128]{2,1,0:T(8,128)(2,1)}), bf16[32,48,128]{2,1,0:T(8,128)(2,1)S(1)}, u32[]{:S(2)}, u32[]{:S(2)}) %all-to-all-start.1) | async-done | bytes 393248 | tf_op jit(solution)/shard_map/all_to_all | solution.py:49
  55.3 1.2 %shard_map.107 = (f32[128,128]{1,0:T(8,128)}, bf16[1024,128]{1,0:T(8,128)(2,1)}) custom-call(bf16[1536,128]{1,0:T(8,128)(2,1)S(1)} %bitcast.33, s32[1,1]{1,0:T(1,128)} %bitcast.13.index_ref, s32[1,32]{1,0:T(1,128)S(1)} %get-tuple-element.21.counts_ref, bf16[64,128]{1,0:T(8,128)(2,1)S(1)} %bitcast.38), custom_call_target="tpu_custom_call" | custom-call | flops 4194304 | bytes 737412 | tf_op jit(solution)/shard_map/pallas_call | solution.py:24
  56.5 3.9 %all-to-all-start.2 = ((bf16[32,32,128]{2,1,0:T(8,128)(2,1)}), bf16[32,32,128]{2,1,0:T(8,128)(2,1)S(1)}, u32[]{:S(2)}, u32[]{:S(2)}) async-start(bf16[32,32,128]{2,1,0:T(8,128)(2,1)} %bitcast.14), calls=%async_computation.2 | async-start | bytes 524288 | tf_op jit(solution)/shard_map/all_to_all | solution.py:49
  60.4 0.1 maximum_bitcast_fusion
  60.5 1.1 %copy.22 = bf16[64,1,16,256]{3,2,1,0:T(8,128)(2,1)} copy(bf16[64,1,16,256]{3,0,2,1:T(8,128)(2,1)S(1)} %maximum_bitcast_fusion) | data formatting | bytes 1048576
  61.6 9.0 %all-to-all-done.2 = bf16[32,32,128]{2,1,0:T(8,128)(2,1)S(1)} async-done(((bf16[32,32,128]{2,1,0:T(8,128)(2,1)}), bf16[32,32,128]{2,1,0:T(8,128)(2,1)S(1)}, u32[]{:S(2)}, u32[]{:S(2)}) %all-to-all-start.2) | async-done | bytes 262176 | tf_op jit(solution)/shard_map/all_to_all | solution.py:49
  70.6 1.1 %shard_map.108 = (f32[27,64,64]{2,1,0:T(8,128)}, f32[64,128]{1,0:T(8,128)}) custom-call(bf16[1024,128]{1,0:T(8,128)(2,1)S(1)} %bitcast.34), custom_call_target="tpu_custom_call" | custom-call | flops 1000 | bytes 737280 | tf_op jit(solution)/shard_map/pallas_call | solution.py:24
  (2 shorter events, 0.0 us)
Async XLA Ops:
  0.6 1.0 %copy-start = (bf16[64,1,16,256]{3,2,1,0:T(8,128)(2,1)S(1)}, bf16[64,1,16,256]{3,2,1,0:T(8,128)(2,1)}, u32[]{:S(2)}) copy-start(bf16[64,1,16,256]{3,2,1,0:T(8,128)(2,1)} %param.10) | copy-start | bytes 1572868
  1.7 0.8 %copy-start.3 = (bf16[128,128]{1,0:T(8,128)(2,1)S(1)}, bf16[128,128]{1,0:T(8,128)(2,1)}, u32[]{:S(2)}) copy-start(bf16[128,128]{1,0:T(8,128)(2,1)} %rows_ref.1) | copy-start | bytes 98308
  2.4 0.7 copy-start.4
  3.1 0.7 copy-start.5
  3.8 10.3 %copy-start.6 = (bf16[27,64,64]{2,1,0:T(8,128)(2,1)S(1)}, bf16[27,64,64]{2,1,0:T(8,128)(2,1)}, u32[]{:S(2)}) copy-start(bf16[27,64,64]{2,1,0:T(8,128)(2,1)} %param.12) | copy-start | bytes 663556
  4.0 19.4 %collective-permute-start = (bf16[1040,256]{1,0:T(8,128)(2,1)S(1)}, bf16[1040,256]{1,0:T(8,128)(2,1)S(1)}, u32[]{:S(2)}, u32[]{:S(2)}) collective-permute-start(bf16[1040,256]{1,0:T(8,128)(2,1)S(1)} %get-tuple-element.23.plane_ref.own_ref), channel_id=1, source_target_pairs={{0,4},{1,5},{2,6},{3,7},{4,8},{5,9},{6,10},{7,11},{8,12},{9,13},{1... | collective-permute-start | bytes 1597448 | tf_op jit(solution)/shard_map/ppermute | solution.py:44
  4.6 18.9 %collective-permute-start.1 = (bf16[1040,256]{1,0:T(8,128)(2,1)S(1)}, bf16[1040,256]{1,0:T(8,128)(2,1)S(1)}, u32[]{:S(2)}, u32[]{:S(2)}) collective-permute-start(bf16[1040,256]{1,0:T(8,128)(2,1)S(1)} %get-tuple-element.23.plane_ref.own_ref), channel_id=1, source_target_pairs={{0,28},{1,29},{2,30},{3,31},{4,0},{5,1},{6,2},{7,3},{8,4},{9,5},{1... | collective-permute-start | bytes 1597448 | tf_op jit(solution)/shard_map/ppermute | solution.py:44
  8.4 15.0 %all-to-all-start = ((bf16[32,24,128]{2,1,0:T(8,128)(2,1)}), bf16[32,24,128]{2,1,0:T(8,128)(2,1)S(1)}, u32[]{:S(2)}, u32[]{:S(2)}) async-start(bf16[32,24,128]{2,1,0:T(8,128)(2,1)} %bitcast.1), calls=%async_computation | async-start | bytes 393216 | tf_op jit(solution)/shard_map/all_to_all | solution.py:49
  17.4 6.0 %copy-start.2 = (bf16[128,64]{0,1:T(8,128)(2,1)S(1)}, bf16[128,64]{0,1:T(8,128)(2,1)}, u32[]{:S(2)}) copy-start(bf16[128,64]{0,1:T(8,128)(2,1)} %param.11) | copy-start | bytes 49156
  24.5 12.4 %collective-permute-start.2 = (bf16[448,256]{1,0:T(8,128)(2,1)S(1)}, bf16[448,256]{1,0:T(8,128)(2,1)S(1)}, u32[]{:S(2)}, u32[]{:S(2)}) collective-permute-start(bf16[448,256]{1,0:T(8,128)(2,1)S(1)} %get-tuple-element.29.last_ref), channel_id=1, source_target_pairs={{0,1},{1,2},{2,3},{3,0},{4,5},{5,6},{6,7},{7,4},{8,9},{9,10},{10,1... | collective-permute-start | bytes 688136 | tf_op jit(solution)/shard_map/ppermute | solution.py:44
  25.7 12.2 %collective-permute-start.3 = (bf16[448,256]{1,0:T(8,128)(2,1)S(1)}, bf16[448,256]{1,0:T(8,128)(2,1)S(1)}, u32[]{:S(2)}, u32[]{:S(2)}) collective-permute-start(bf16[448,256]{1,0:T(8,128)(2,1)S(1)} %get-tuple-element.30.first_ref), channel_id=1, source_target_pairs={{0,3},{1,0},{2,1},{3,2},{4,7},{5,4},{6,5},{7,6},{8,11},{9,8},{10,9... | collective-permute-start | bytes 688136 | tf_op jit(solution)/shard_map/ppermute | solution.py:44
  39.3 0.7 %copy-start.1 = (bf16[1536,128]{1,0:T(8,128)(2,1)}, bf16[1536,128]{1,0:T(8,128)(2,1)S(1)}, u32[]{:S(2)}) copy-start(bf16[1536,128]{1,0:T(8,128)(2,1)S(1)} %get-tuple-element.33) | copy-start | bytes 1179652
  40.0 15.3 %all-to-all-start.1 = ((bf16[32,48,128]{2,1,0:T(8,128)(2,1)}), bf16[32,48,128]{2,1,0:T(8,128)(2,1)S(1)}, u32[]{:S(2)}, u32[]{:S(2)}) async-start(bf16[32,48,128]{2,1,0:T(8,128)(2,1)} %bitcast.36), calls=%async_computation.1 | async-start | bytes 786432 | tf_op jit(solution)/shard_map/all_to_all | solution.py:49
  56.5 14.1 %all-to-all-start.2 = ((bf16[32,32,128]{2,1,0:T(8,128)(2,1)}), bf16[32,32,128]{2,1,0:T(8,128)(2,1)S(1)}, u32[]{:S(2)}, u32[]{:S(2)}) async-start(bf16[32,32,128]{2,1,0:T(8,128)(2,1)} %bitcast.14), calls=%async_computation.2 | async-start | bytes 524288 | tf_op jit(solution)/shard_map/all_to_all | solution.py:49

commit v4 on v3

--- a/solution.py
+++ b/solution.py
@@ -19,14 +19,17 @@
     return lax.dot_general(a, b, dims, preferred_element_type=F32)
 
 
-def call(kernel, outs, args, flops, scratch=()):
+def call(kernel, outs, args, flops, scratch=(), far=(), far_out=(), aliases=None):
     traffic = sum(math.prod(a.shape) * a.dtype.itemsize for a in (*args, *outs))
+    near = pl.BlockSpec(memory_space=pltpu.VMEM)
+    there = pl.BlockSpec(memory_space=pltpu.HBM)
     return pl.pallas_call(
         kernel,
         out_shape=[jax.ShapeDtypeStruct(o.shape, o.dtype) for o in outs],
-        in_specs=[pl.BlockSpec(memory_space=pltpu.VMEM)] * len(args),
-        out_specs=[pl.BlockSpec(memory_space=pltpu.VMEM)] * len(outs),
+        in_specs=[there if n in far else near for n in range(len(args))],
+        out_specs=[there if n in far_out else near for n in range(len(outs))],
         scratch_shapes=list(scratch),
+        input_output_aliases=aliases or {},
         compiler_params=pltpu.CompilerParams(vmem_limit_bytes=LIMIT),
         cost_estimate=pl.CostEstimate(flops=flops, bytes_accessed=traffic, transcendentals=0),
     )(*args)
@@ -100,12 +103,20 @@
     return out.astype(BF16), grad.astype(BF16)
 
 
-def plane_kernel(base_ref, cells_ref, rows_ref, counts_ref, out_ref, rows_out_ref, counts_out_ref):
+def first_kernel(
+    ngx, ngy, cap, base_far, cells_far, rows_far, counts_far,
+    out_ref, send_ref, base_ref, cells_ref, rows_ref, counts_ref, sems,
+):
+    pairs = (
+        (rows_far, rows_ref), (counts_far, counts_ref), (cells_far, cells_ref), (base_far, base_ref)
+    )
+    copies = [pltpu.make_async_copy(src, dst, sems.at[n]) for n, (src, dst) in enumerate(pairs)]
+    for copy in copies:
+        copy.start()
     chans, cy, nz = base_ref.shape
-    rows_out_ref[...] = rows_ref[...]
-    counts_out_ref[...] = counts_ref[...]
-    turned = jnp.swapaxes(base_ref[...].astype(F32), 0, 1)
-    out_ref[pl.ds(0, cy * chans)] = turned.reshape(cy * chans, nz).astype(BF16)
+    for copy in copies[:3]:
+        copy.wait()
+    pick(ngx, ngy, cap, counts_ref, rows_ref, send_ref)
     cells = cells_ref[...]
     slots = cells.shape[1]
     nl = -(-slots // nz)
@@ -119,9 +130,16 @@
     if tail > 2 * nl:
         lines.append(jnp.zeros((tail - 2 * nl, nz), F32))
     out_ref[pl.ds(cy * chans, tail)] = jnp.concatenate(lines, axis=0).astype(BF16)
-
-
-def pick_kernel(ngx, ngy, cap, counts_ref, rows_ref, plane_ref, out_ref):
+    copies[3].wait()
+    turned = jnp.swapaxes(base_ref[...].astype(F32), 0, 1)
+    out_ref[pl.ds(0, cy * chans)] = turned.reshape(cy * chans, nz).astype(BF16)
+
+
+def same_kernel(in_ref, out_ref):
+    pass
+
+
+def pick(ngx, ngy, cap, counts_ref, rows_ref, out_ref):
     ndev = ngx * ngy
     nrows, feats = rows_ref.shape
     slots = ndev * cap
@@ -139,30 +157,30 @@
     out_ref[...] = jnp.stack(parts, axis=1).reshape(out_ref.shape).astype(BF16)
 
 
-def paint_kernel(
-    ndev, cap, chans, cy, nz,
-    recv_ref, own_ref, west_ref, east_ref, proj_t_ref, cot_ref,
-    x_ref, first_ref, last_ref, masked,
+def painted_rows(values, cells, nz, ns, masked):
+    chans = values.shape[0]
+    y, z = cells
+    for n, row in enumerate(ns):
+        masked[pl.ds(n * chans, chans)] = values * jnp.where(y == row, 1.0, 0.0).astype(BF16)
+    return mm(masked[pl.ds(0, len(ns) * chans)], picked_depth(z, nz), NT)
+
+
+def outer_kernel(
+    ndev, cap, chans, cy, recv_ref, own_ref, west_ref, east_ref, proj_t_ref, cot_ref,
+    first_ref, last_ref, masked,
 ):
     slots = ndev * cap
-    nl = -(-slots // nz)
+    nz = own_ref.shape[1]
     raws = rows_in(recv_ref, ndev, cap)
+    ns = (0, 1, cy - 2, cy - 1)
     for dx, ref in enumerate((west_ref, own_ref, east_ref)):
-        lanes = pl.ds(dx * chans, chans)
-        y, z = widths(nl, slots, ref[pl.ds(cy * chans, ref.shape[0] - cy * chans)])
         values = mm(proj_t_ref[...], raws[dx], NT).astype(BF16)
-        for n in range(cy):
-            masked[pl.ds(n * chans, chans)] = values * jnp.where(y == n, 1.0, 0.0).astype(BF16)
-        painted = mm(masked[...], picked_depth(z, nz), NT)
-        for n in range(cy):
-            rows = pl.ds(n * chans, chans)
+        painted = painted_rows(values, list_of(ref, cy, chans, slots), nz, ns, masked)
+        for n, row in enumerate(ns):
             part = painted[n * chans : (n + 1) * chans]
-            field = (ref[rows].astype(F32) + part).astype(BF16)
-            x_ref[n, lanes] = field
-            if n < 2:
-                first_ref[pl.ds((3 * n + dx) * chans, chans)] = field
-            if n >= cy - 2:
-                last_ref[pl.ds((3 * (n - cy + 2) + dx) * chans, chans)] = field
+            field = (ref[pl.ds(row * chans, chans)].astype(F32) + part).astype(BF16)
+            target = first_ref if n < 2 else last_ref
+            target[pl.ds((3 * (n % 2) + dx) * chans, chans)] = field
     first_ref[pl.ds(6 * chans, chans)] = cot_ref[0]
     last_ref[pl.ds(6 * chans, chans)] = cot_ref[cy - 1]
 
@@ -173,12 +191,20 @@
 
 
 def conv_kernel(
-    ndev, cap, chans, cy, x_ref, cot_ref, wf_ref, wb_ref, own_ref, west_ref, east_ref,
-    out_ref, total_ref, pre_ref, slot_ref, sums_ref, acc, grads, back, plane,
+    ndev, cap, chans, cy, recv_ref, proj_t_ref, cot_ref, wf_ref, wb_ref, own_ref, west_ref, east_ref,
+    out_ref, total_ref, pre_ref, slot_ref, sums_ref, x_ref, acc, grads, back, plane, masked,
 ):
     rows = 3 * chans
     nz = x_ref.shape[2]
     slots = ndev * cap
+    raws = rows_in(recv_ref, ndev, cap)
+    for dx, ref in enumerate((west_ref, own_ref, east_ref)):
+        values = mm(proj_t_ref[...], raws[dx], NT).astype(BF16)
+        painted = painted_rows(values, list_of(ref, cy, chans, slots), nz, range(cy), masked)
+        for n in range(cy):
+            part = painted[n * chans : (n + 1) * chans]
+            field = ref[pl.ds(n * chans, chans)].astype(F32) + part
+            x_ref[n, pl.ds(dx * chans, chans)] = field.astype(BF16)
     own = pl.ds(chans, chans)
     zeros = jnp.zeros((rows, nz), BF16)
     for t in (0, 1, cy, cy + 1):
@@ -258,7 +284,7 @@
     ndev, cap, chans, cy,
     pre_ref, slot_ref, sums_ref, total_ref, north_ref, south_ref, first_ref, last_ref,
     wf_ref, wb_ref, cot_ref, own_ref, west_ref, east_ref, recv_ref,
-    out_ref, send_ref, total,
+    out_ref, send_far, total, sums_send, slots_send, sems,
 ):
     rows = 3 * chans
     slots = ndev * cap
@@ -296,8 +322,8 @@
     proj_high = proj.astype(BF16).astype(F32)
     sides = jnp.concatenate([found[0], found[2]], axis=0).T
     middle = jnp.concatenate([found[1], jnp.zeros_like(found[1])], axis=0).T
-    width = send_ref.shape[1]
-    share = send_ref.shape[0] // ndev - 2 * cap
+    width = send_far.shape[2]
+    share = send_far.shape[1] - 2 * cap
     taps = total[:, 2 * chans :]
     half = 3 * rows // 2
     taps = jnp.concatenate([taps[:half], taps[half:]], axis=1)
@@ -305,15 +331,17 @@
     proj = jnp.stack(halves, axis=1).reshape(2 * chans, width)
     pad = jnp.zeros((share * ndev - 3 * rows - half - 2 * chans, width), F32)
     sums = jnp.concatenate([total[:, : 2 * chans], taps, proj, pad], axis=0)
-    out = jnp.concatenate(
-        [
-            sums.reshape(ndev, share, width),
-            sides.reshape(ndev, cap, width),
-            middle.reshape(ndev, cap, width),
-        ],
-        axis=1,
-    )
-    send_ref[...] = out.reshape(send_ref.shape).astype(BF16)
+    sums_send[...] = sums.reshape(sums_send.shape).astype(BF16)
+    back = [sides.reshape(ndev, cap, width), middle.reshape(ndev, cap, width)]
+    slots_send[...] = jnp.concatenate(back, axis=1).astype(BF16)
+    copies = [
+        pltpu.make_async_copy(sums_send, send_far.at[:, pl.ds(0, share)], sems.at[0]),
+        pltpu.make_async_copy(slots_send, send_far.at[:, pl.ds(share, 2 * cap)], sems.at[1]),
+    ]
+    for copy in copies:
+        copy.start()
+    for copy in copies:
+        copy.wait()
 
 
 def rows_kernel(
@@ -393,19 +421,23 @@
     one = 2 * rows * rows * nz
 
     tail = -(-2 * -(-slots // nz) // 16) * 16
-    plane, particles, counts = call(
-        plane_kernel,
-        [shape((cy * chans + tail, nz), BF16), particles, send_counts],
-        (base_field.reshape(chans, cy, nz), cell_lists, particles, send_counts),
-        1000,
+    base = base_field.reshape(chans, cy, nz)
+    plane, payload = call(
+        functools.partial(first_kernel, ngx, ngy, cap),
+        [shape((cy * chans + tail, nz), BF16), shape((ndev * 3 * cap, feats), BF16)],
+        (base, cell_lists, particles, send_counts),
+        2 * slots * nrows * feats,
+        (
+            pltpu.VMEM(base.shape, BF16),
+            pltpu.VMEM(cell_lists.shape, I32),
+            pltpu.VMEM(particles.shape, BF16),
+            pltpu.VMEM(send_counts.shape, I32),
+            pltpu.SemaphoreType.DMA((4,)),
+        ),
+        far=range(4),
     )
     west, east = move(plane, 1, 0), move(plane, -1, 0)
-    (payload,) = call(
-        functools.partial(pick_kernel, ngx, ngy, cap),
-        [shape((ndev * 3 * cap, feats), BF16)],
-        (counts, particles, plane),
-        2 * slots * nrows * feats,
-    )
+    (payload,) = call(same_kernel, [payload], (payload,), 0, far=(0,), far_out=(0,), aliases={0: 0})
     recv = exchange(payload, ndev)
 
     cot = cotangent[:, 0].transpose(1, 0, 2)
@@ -413,12 +445,12 @@
     wf = taps.transpose(1, 2, 3, 0, 4).reshape(9 * chans, rows)
     wb = taps.transpose(1, 0, 4, 2, 3).reshape(9 * chans, rows)
 
-    x_all, first, last = call(
-        functools.partial(paint_kernel, ndev, cap, chans, cy, nz),
-        [shape((cy, rows, nz), BF16)] + [shape((2 * rows + chans, nz), BF16)] * 2,
+    first, last = call(
+        functools.partial(outer_kernel, ndev, cap, chans, cy),
+        [shape((2 * rows + chans, nz), BF16)] * 2,
         (recv, plane, west, east, proj_t, cot),
-        6 * slots * count * chans,
-        (pltpu.VMEM((cy * chans, slots), BF16),),
+        2 * slots * count * chans,
+        (pltpu.VMEM((4 * chans, slots), BF16),),
     )
     north, south = move(last, 0, 1), move(first, 0, -1)
     out_rows, total, pre_edge, slot_edge, sums = call(
@@ -430,33 +462,42 @@
             shape((4, rows, nz), F32),
             shape((3, chans, slots), F32),
         ],
-        (x_all, cot, wf, wb, plane, west, east),
+        (recv, proj_t, cot, wf, wb, plane, west, east),
         3 * cy * 3 * one,
         (
+            pltpu.VMEM((cy, rows, nz), BF16),
             pltpu.VMEM((cy + 1, rows, nz), F32),
             pltpu.VMEM((cy + 2, rows, nz), BF16),
             pltpu.VMEM((cy, rows, nz), F32),
             pltpu.VMEM((3, (cy - 4) * chans, nz), BF16),
+            pltpu.VMEM((cy * chans, slots), BF16),
         ),
     )
     grad_rows = 27 * chans * chans // feats
     share = -(-(grad_rows + 2 * chans) // (16 * ndev)) * 16
     out_edge, payload = call(
         functools.partial(edge_kernel, ndev, cap, chans, cy),
-        [shape((2, chans, nz), BF16), shape((ndev * (share + 2 * cap), feats), BF16)],
+        [shape((2, chans, nz), BF16), shape((ndev, share + 2 * cap, feats), BF16)],
         (
             pre_edge, slot_edge, sums, total, north, south, first, last,
             wf, wb, cot, plane, west, east, recv,
         ),
         12 * one,
-        (pltpu.VMEM((9 * chans, rows), F32),),
-    )
+        (
+            pltpu.VMEM((9 * chans, rows), F32),
+            pltpu.VMEM((ndev, share, feats), BF16),
+            pltpu.VMEM((ndev, 2 * cap, feats), BF16),
+            pltpu.SemaphoreType.DMA((2,)),
+        ),
+        far_out=(1,),
+    )
+    payload = payload.reshape(-1, feats)
     recv = exchange(payload, ndev)
     index = (lax.axis_index("gx") * ngy + lax.axis_index("gy")).astype(I32).reshape(1, 1)
     row_grads, sums = call(
         functools.partial(rows_kernel, ngx, ngy, cap, chans),
         [shape((nrows, feats), F32), shape((ndev * share, feats), BF16)],
-        (recv, index, counts, proj_t),
+        (recv, index, send_counts, proj_t),
         2 * nrows * slots * chans,
     )
     recv = exchange(sums, ndev)

time: 72.2 us -> 71.8 us (level)
  local copies, waits for them, and re-layouts: 10.5 us -> 9.49 us
    reshape x2, local copies, waits for them, and re-layouts: 1.65 us -> 0.56 us  [local(): wb = taps.transpose(1, 0, 4, 2, 3).reshape(9 * chans, rows)]
    reshape x2, local copies, waits for them, and re-layouts: 0.56 us -> 1.65 us  [local(): wf = taps.transpose(1, 2, 3, 0, 4).reshape(9 * chans, rows)]
    all_to_all x3, waiting for transfers between devices: 24.5 us -> 25.3 us  [exchange(): lax.all_to_all(payload.reshape(ndev, rows // ndev, width), AXES, split_ax...]
where the time goes in v4:
time: 71.8 us; the launch traced here: 71.3 us
  waiting for transfers between devices  26.1 us (36%)
  starting transfers between devices  20.3 us (28%)
  Pallas kernels  14.6 us (20%)
  local copies, waits for them, and re-layouts  9.49 us (13%)
  between operations  0.82 us (1%)
    all_to_all x3, waiting for transfers between devices, exchange(): lax.all_to_all(payload.reshape(ndev, rows // ndev, width), AXES, split_ax...  25.3 us
    pallas_call x7, Pallas kernels, call(): pl.pallas_call(kernel, out_shape=[jax.ShapeDtypeStruct(o.shape, o.dtype)...  14.6 us
    all_to_all x3, starting transfers between devices, exchange(): lax.all_to_all(payload.reshape(ndev, rows // ndev, width), AXES, split_ax...  13 us
    ppermute x4, starting transfers between devices, send(): return lax.ppermute(block, AXES, pairs)  7.33 us
    unnamed x16, local copies, waits for them, and re-layouts  5.52 us
    reshape x2, local copies, waits for them, and re-layouts, local(): taps = conv_weight.reshape(3, 3, 3, chans, chans)  1.72 us
    reshape x2, local copies, waits for them, and re-layouts, local(): wf = taps.transpose(1, 2, 3, 0, 4).reshape(9 * chans, rows)  1.65 us
  transfers between devices with their start and end apart: 7, of which 4 were waited for; matrix products, arithmetic and copies ran while one was open for 9% of the time, Pallas kernels for 13%

profile of v4, /device:TPU:0, one launch (start us, length us, event | category | flops | bytes accessed | tf_op | source)
XLA Modules:
  0.0 71.3 jit_solution(14026959557443882291)
XLA Ops:
  0.6 0.0 copy-start.4
  0.6 0.0 copy-start.5
  0.7 0.6 copy-done.4
  1.3 0.0 copy-done.5
  1.3 0.0 copy-start
  1.3 1.0 %copy-done = bf16[64,1,16,256]{3,2,1,0:T(8,128)(2,1)S(1)} copy-done((bf16[64,1,16,256]{3,2,1,0:T(8,128)(2,1)S(1)}, bf16[64,1,16,256]{3,2,1,0:T(8,128)(2,1)}, u32[]{:S(2)}) %copy-start) | copy-done | bytes 524312
  2.4 0.0 copy-start.3
  2.4 0.8 %copy-done.3 = bf16[128,128]{1,0:T(8,128)(2,1)S(1)} copy-done((bf16[128,128]{1,0:T(8,128)(2,1)S(1)}, bf16[128,128]{1,0:T(8,128)(2,1)}, u32[]{:S(2)}) %copy-start.3) | copy-done | bytes 32792
  3.1 1.0 %shard_map.102 = (bf16[1040,256]{1,0:T(8,128)(2,1)S(1)}, bf16[768,128]{1,0:T(8,128)(2,1)}) custom-call(bf16[64,16,256]{2,1,0:T(8,128)(2,1)S(1)} %bitcast.35, s32[1,256]{1,0:T(1,128)S(1)} %copy-done.5, bf16[128,128]{1,0:T(8,128)(2,1)S(1)} %copy-done.3, s32[1,32]{1,0:T(1,128)S(1)} %copy-done.4), custom_call_target="tpu_custom_call" | custom-call | flops 8388608 | bytes 1287296 | tf_op jit(solution)/shard_map/pallas_call | solution.py:26
  4.2 0.0 copy-start.6
  4.2 0.5 collective-permute-start
  4.7 2.9 %collective-permute-start.1 = (bf16[1040,256]{1,0:T(8,128)(2,1)S(1)}, bf16[1040,256]{1,0:T(8,128)(2,1)S(1)}, u32[]{:S(2)}, u32[]{:S(2)}) collective-permute-start(bf16[1040,256]{1,0:T(8,128)(2,1)S(1)} %get-tuple-element.20.own_ref), channel_id=1, source_target_pairs={{0,28},{1,29},{2,30},{3,31},{4,0},{5,1},{6,2},{7,3},{8,4},{9,5},{1... | collective-permute-start | bytes 1597448 | tf_op jit(solution)/shard_map/ppermute | solution.py:47
  7.6 5.6 %all-to-all-start = ((bf16[32,24,128]{2,1,0:T(8,128)(2,1)}), bf16[32,24,128]{2,1,0:T(8,128)(2,1)S(1)}, u32[]{:S(2)}, u32[]{:S(2)}) async-start(bf16[32,24,128]{2,1,0:T(8,128)(2,1)} %bitcast.1), calls=%async_computation | async-start | bytes 393216 | tf_op jit(solution)/shard_map/all_to_all | solution.py:52
  13.3 0.0 copy-done.6
  13.3 1.3 %copy.17 = bf16[3,3,3,64,64]{3,2,1,4,0:T(4,128)(2,1)} copy(bf16[3,3,3,64,64]{4,3,2,1,0:T(8,128)(2,1)S(1)} %bitcast.41) | data formatting | bytes 442368 | tf_op jit(solution)/shard_map/reshape | solution.py:444
  14.6 0.4 copy.26
  15.0 1.5 %reshape.42 = bf16[576,192]{0,1:T(8,128)(2,1)S(1)} reshape(bf16[3,3,64,3,64]{2,1,0,4,3:T(4,128)(2,1)} %bitcast.40) | data formatting | bytes 442368 | tf_op jit(solution)/shard_map/reshape | solution.py:445
  16.5 0.2 copy.19.wf_ref
  16.7 0.4 reshape.43
  17.1 0.2 copy.20.wb_ref
  17.3 0.0 copy-start.2
  17.3 1.2 %copy.27 = bf16[64,1,16,256]{3,0,2,1:T(8,128)(2,1)S(1)} copy(bf16[64,1,16,256]{3,2,1,0:T(8,128)(2,1)} %param.13) | data formatting | bytes 1048576 | tf_op args[6]
  18.5 4.5 %all-to-all-done = bf16[32,24,128]{2,1,0:T(8,128)(2,1)S(1)} async-done(((bf16[32,24,128]{2,1,0:T(8,128)(2,1)}), bf16[32,24,128]{2,1,0:T(8,128)(2,1)S(1)}, u32[]{:S(2)}, u32[]{:S(2)}) %all-to-all-start) | async-done | bytes 196640 | tf_op jit(solution)/shard_map/all_to_all | solution.py:52
  22.9 0.0 collective-permute-done.west_ref
  23.0 0.0 collective-permute-done.1.east_ref
  23.0 0.0 copy-done.2
  23.0 0.6 shard_map.105
  23.6 1.8 %collective-permute-start.2 = (bf16[448,256]{1,0:T(8,128)(2,1)S(1)}, bf16[448,256]{1,0:T(8,128)(2,1)S(1)}, u32[]{:S(2)}, u32[]{:S(2)}) collective-permute-start(bf16[448,256]{1,0:T(8,128)(2,1)S(1)} %get-tuple-element.25.last_ref), channel_id=1, source_target_pairs={{0,1},{1,2},{2,3},{3,0},{4,5},{5,6},{6,7},{7,4},{8,9},{9,10},{10,1... | collective-permute-start | bytes 688136 | tf_op jit(solution)/shard_map/ppermute | solution.py:47
  25.3 2.1 %collective-permute-start.3 = (bf16[448,256]{1,0:T(8,128)(2,1)S(1)}, bf16[448,256]{1,0:T(8,128)(2,1)S(1)}, u32[]{:S(2)}, u32[]{:S(2)}) collective-permute-start(bf16[448,256]{1,0:T(8,128)(2,1)S(1)} %get-tuple-element.26.first_ref), channel_id=1, source_target_pairs={{0,3},{1,0},{2,1},{3,2},{4,7},{5,4},{6,5},{7,6},{8,11},{9,8},{10,9... | collective-permute-start | bytes 688136 | tf_op jit(solution)/shard_map/ppermute | solution.py:47
  27.4 9.3 %shard_map.104 = (bf16[16,64,256]{2,1,0:T(8,128)(2,1)S(1)}, f32[576,192]{1,0:T(8,128)S(1)}, f32[4,192,256]{2,1,0:T(8,128)S(1)}, f32[4,192,256]{2,1,0:T(8,128)S(1)}, f32[3,64,256]{2,1,0:T(8,128)S(1)}) custom-call(bf16[768,128]{1,0:T(8,128)(2,1)S(1)} %bitcast.31, bf16[64,128]{1,0:T(8,128)(2,1)S(1)} %bitcast.37, bf16[16,64,256]{2,1,0:T(8,128)(2,1)S(1)} %bitcast.28, ...), custom_call_target="tpu_custom_call" | custom-call | flops 2717908992 | bytes 5513216 | tf_op jit(solution)/shard_map/pallas_call | solution.py:26
  36.8 0.0 collective-permute-done.2.north_ref
  36.8 0.8 %collective-permute-done.3.south_ref = bf16[448,256]{1,0:T(8,128)(2,1)S(1)} collective-permute-done((bf16[448,256]{1,0:T(8,128)(2,1)S(1)}, bf16[448,256]{1,0:T(8,128)(2,1)S(1)}, u32[]{:S(2)}, u32[]{:S(2)}) %collective-permute-start.3) | collective-permute-done | bytes 229408 | tf_op jit(solution)/shard_map/ppermute | solution.py:47
  37.6 1.4 %shard_map.106 = (bf16[2,64,256]{2,1,0:T(8,128)(2,1)S(1)}, bf16[32,48,128]{2,1,0:T(8,128)(2,1)S(1)}) custom-call(f32[4,192,256]{2,1,0:T(8,128)S(1)} %get-tuple-element.21.pre_ref, f32[4,192,256]{2,1,0:T(8,128)S(1)} %get-tuple-element.22.slot_ref, f32[3,64,256]{2,1,0:T(8,128)S(1)} %get-tuple-element.23.sums_ref, f32[576,192]{1,0:T(8,128)S(1)} %get-tuple-element.24.total_ref, ...), custom_call_target="tpu_custom_call" | custom-call | flops 226492416 | bytes 6348800 | tf_op jit(solution)/shard_map/pallas_call | solution.py:26
  39.0 0.0 copy-start.1
  39.0 0.7 %copy-done.1 = bf16[32,48,128]{2,1,0:T(8,128)(2,1)} copy-done((bf16[32,48,128]{2,1,0:T(8,128)(2,1)}, bf16[32,48,128]{2,1,0:T(8,128)(2,1)S(1)}, u32[]{:S(2)}) %copy-start.1) | copy-done | bytes 393240
  39.7 3.5 %all-to-all-start.1 = ((bf16[32,48,128]{2,1,0:T(8,128)(2,1)}), bf16[32,48,128]{2,1,0:T(8,128)(2,1)S(1)}, u32[]{:S(2)}, u32[]{:S(2)}) async-start(bf16[32,48,128]{2,1,0:T(8,128)(2,1)} %copy-done.1), calls=%async_computation.1 | async-start | bytes 786432 | tf_op jit(solution)/shard_map/all_to_all | solution.py:52
  43.2 11.8 %all-to-all-done.1 = bf16[32,48,128]{2,1,0:T(8,128)(2,1)S(1)} async-done(((bf16[32,48,128]{2,1,0:T(8,128)(2,1)}), bf16[32,48,128]{2,1,0:T(8,128)(2,1)S(1)}, u32[]{:S(2)}, u32[]{:S(2)}) %all-to-all-start.1) | async-done | bytes 393248 | tf_op jit(solution)/shard_map/all_to_all | solution.py:52
  55.0 1.2 %shard_map.107 = (f32[128,128]{1,0:T(8,128)}, bf16[1024,128]{1,0:T(8,128)(2,1)}) custom-call(bf16[1536,128]{1,0:T(8,128)(2,1)S(1)} %bitcast.33, s32[1,1]{1,0:T(1,128)} %bitcast.13.index_ref, s32[1,32]{1,0:T(1,128)S(1)} %copy-done.4, bf16[64,128]{1,0:T(8,128)(2,1)S(1)} %bitcast.38), custom_call_target="tpu_custom_call" | custom-call | flops 4194304 | bytes 737412 | tf_op jit(solution)/shard_map/pallas_call | solution.py:26
  56.2 3.9 %all-to-all-start.2 = ((bf16[32,32,128]{2,1,0:T(8,128)(2,1)}), bf16[32,32,128]{2,1,0:T(8,128)(2,1)S(1)}, u32[]{:S(2)}, u32[]{:S(2)}) async-start(bf16[32,32,128]{2,1,0:T(8,128)(2,1)} %bitcast.14), calls=%async_computation.2 | async-start | bytes 524288 | tf_op jit(solution)/shard_map/all_to_all | solution.py:52
  60.1 0.1 maximum_bitcast_fusion
  60.2 1.1 %copy.23 = bf16[64,1,16,256]{3,2,1,0:T(8,128)(2,1)} copy(bf16[64,1,16,256]{3,0,2,1:T(8,128)(2,1)S(1)} %maximum_bitcast_fusion) | data formatting | bytes 1048576
  61.3 9.0 %all-to-all-done.2 = bf16[32,32,128]{2,1,0:T(8,128)(2,1)S(1)} async-done(((bf16[32,32,128]{2,1,0:T(8,128)(2,1)}), bf16[32,32,128]{2,1,0:T(8,128)(2,1)S(1)}, u32[]{:S(2)}, u32[]{:S(2)}) %all-to-all-start.2) | async-done | bytes 262176 | tf_op jit(solution)/shard_map/all_to_all | solution.py:52
  70.3 1.1 %shard_map.108 = (f32[27,64,64]{2,1,0:T(8,128)}, f32[64,128]{1,0:T(8,128)}) custom-call(bf16[1024,128]{1,0:T(8,128)(2,1)S(1)} %bitcast.34), custom_call_target="tpu_custom_call" | custom-call | flops 1000 | bytes 737280 | tf_op jit(solution)/shard_map/pallas_call | solution.py:26
  (3 shorter events, 0.0 us)
Async XLA Ops:
  0.6 0.7 copy-start.4
  0.6 0.7 copy-start.5
  1.3 1.0 %copy-start = (bf16[64,1,16,256]{3,2,1,0:T(8,128)(2,1)S(1)}, bf16[64,1,16,256]{3,2,1,0:T(8,128)(2,1)}, u32[]{:S(2)}) copy-start(bf16[64,1,16,256]{3,2,1,0:T(8,128)(2,1)} %param.10) | copy-start | bytes 1572868
  2.4 0.8 %copy-start.3 = (bf16[128,128]{1,0:T(8,128)(2,1)S(1)}, bf16[128,128]{1,0:T(8,128)(2,1)}, u32[]{:S(2)}) copy-start(bf16[128,128]{1,0:T(8,128)(2,1)} %rows_far.1) | copy-start | bytes 98308
  4.2 9.1 %copy-start.6 = (bf16[27,64,64]{2,1,0:T(8,128)(2,1)S(1)}, bf16[27,64,64]{2,1,0:T(8,128)(2,1)}, u32[]{:S(2)}) copy-start(bf16[27,64,64]{2,1,0:T(8,128)(2,1)} %param.12) | copy-start | bytes 663556
  4.2 18.8 %collective-permute-start = (bf16[1040,256]{1,0:T(8,128)(2,1)S(1)}, bf16[1040,256]{1,0:T(8,128)(2,1)S(1)}, u32[]{:S(2)}, u32[]{:S(2)}) collective-permute-start(bf16[1040,256]{1,0:T(8,128)(2,1)S(1)} %get-tuple-element.20.own_ref), channel_id=1, source_target_pairs={{0,4},{1,5},{2,6},{3,7},{4,8},{5,9},{6,10},{7,11},{8,12},{9,13},{1... | collective-permute-start | bytes 1597448 | tf_op jit(solution)/shard_map/ppermute | solution.py:47
  4.7 18.3 %collective-permute-start.1 = (bf16[1040,256]{1,0:T(8,128)(2,1)S(1)}, bf16[1040,256]{1,0:T(8,128)(2,1)S(1)}, u32[]{:S(2)}, u32[]{:S(2)}) collective-permute-start(bf16[1040,256]{1,0:T(8,128)(2,1)S(1)} %get-tuple-element.20.own_ref), channel_id=1, source_target_pairs={{0,28},{1,29},{2,30},{3,31},{4,0},{5,1},{6,2},{7,3},{8,4},{9,5},{1... | collective-permute-start | bytes 1597448 | tf_op jit(solution)/shard_map/ppermute | solution.py:47
  7.6 15.3 %all-to-all-start = ((bf16[32,24,128]{2,1,0:T(8,128)(2,1)}), bf16[32,24,128]{2,1,0:T(8,128)(2,1)S(1)}, u32[]{:S(2)}, u32[]{:S(2)}) async-start(bf16[32,24,128]{2,1,0:T(8,128)(2,1)} %bitcast.1), calls=%async_computation | async-start | bytes 393216 | tf_op jit(solution)/shard_map/all_to_all | solution.py:52
  17.3 5.7 %copy-start.2 = (bf16[128,64]{0,1:T(8,128)(2,1)S(1)}, bf16[128,64]{0,1:T(8,128)(2,1)}, u32[]{:S(2)}) copy-start(bf16[128,64]{0,1:T(8,128)(2,1)} %param.11) | copy-start | bytes 49156
  23.6 13.2 %collective-permute-start.2 = (bf16[448,256]{1,0:T(8,128)(2,1)S(1)}, bf16[448,256]{1,0:T(8,128)(2,1)S(1)}, u32[]{:S(2)}, u32[]{:S(2)}) collective-permute-start(bf16[448,256]{1,0:T(8,128)(2,1)S(1)} %get-tuple-element.25.last_ref), channel_id=1, source_target_pairs={{0,1},{1,2},{2,3},{3,0},{4,5},{5,6},{6,7},{7,4},{8,9},{9,10},{10,1... | collective-permute-start | bytes 688136 | tf_op jit(solution)/shard_map/ppermute | solution.py:47
  25.3 12.3 %collective-permute-start.3 = (bf16[448,256]{1,0:T(8,128)(2,1)S(1)}, bf16[448,256]{1,0:T(8,128)(2,1)S(1)}, u32[]{:S(2)}, u32[]{:S(2)}) collective-permute-start(bf16[448,256]{1,0:T(8,128)(2,1)S(1)} %get-tuple-element.26.first_ref), channel_id=1, source_target_pairs={{0,3},{1,0},{2,1},{3,2},{4,7},{5,4},{6,5},{7,6},{8,11},{9,8},{10,9... | collective-permute-start | bytes 688136 | tf_op jit(solution)/shard_map/ppermute | solution.py:47
  39.0 0.7 %copy-start.1 = (bf16[32,48,128]{2,1,0:T(8,128)(2,1)}, bf16[32,48,128]{2,1,0:T(8,128)(2,1)S(1)}, u32[]{:S(2)}) copy-start(bf16[32,48,128]{2,1,0:T(8,128)(2,1)S(1)} %get-tuple-element.29) | copy-start | bytes 1179652
  39.7 15.3 %all-to-all-start.1 = ((bf16[32,48,128]{2,1,0:T(8,128)(2,1)}), bf16[32,48,128]{2,1,0:T(8,128)(2,1)S(1)}, u32[]{:S(2)}, u32[]{:S(2)}) async-start(bf16[32,48,128]{2,1,0:T(8,128)(2,1)} %copy-done.1), calls=%async_computation.1 | async-start | bytes 786432 | tf_op jit(solution)/shard_map/all_to_all | solution.py:52
  56.2 14.1 %all-to-all-start.2 = ((bf16[32,32,128]{2,1,0:T(8,128)(2,1)}), bf16[32,32,128]{2,1,0:T(8,128)(2,1)S(1)}, u32[]{:S(2)}, u32[]{:S(2)}) async-start(bf16[32,32,128]{2,1,0:T(8,128)(2,1)} %bitcast.14), calls=%async_computation.2 | async-start | bytes 524288 | tf_op jit(solution)/shard_map/all_to_all | solution.py:52

commit v5 on v4

--- a/solution.py
+++ b/solution.py
@@ -11,6 +11,7 @@
 AXES = ("gx", "gy")
 F32, BF16, I32 = jnp.float32, jnp.bfloat16, jnp.int32
 LIMIT = 40 * 1024 * 1024
+ALL = 60 * 1024 * 1024
 NT = (((1,), (1,)), ((), ()))
 NN = (((1,), (0,)), ((), ()))
 
@@ -19,7 +20,7 @@
     return lax.dot_general(a, b, dims, preferred_element_type=F32)
 
 
-def call(kernel, outs, args, flops, scratch=(), far=(), far_out=(), aliases=None):
+def call(kernel, outs, args, flops, scratch=(), far=(), far_out=(), aliases=None, limit=LIMIT):
     traffic = sum(math.prod(a.shape) * a.dtype.itemsize for a in (*args, *outs))
     near = pl.BlockSpec(memory_space=pltpu.VMEM)
     there = pl.BlockSpec(memory_space=pltpu.HBM)
@@ -30,7 +31,7 @@
         out_specs=[there if n in far_out else near for n in range(len(outs))],
         scratch_shapes=list(scratch),
         input_output_aliases=aliases or {},
-        compiler_params=pltpu.CompilerParams(vmem_limit_bytes=LIMIT),
+        compiler_params=pltpu.CompilerParams(vmem_limit_bytes=limit),
         cost_estimate=pl.CostEstimate(flops=flops, bytes_accessed=traffic, transcendentals=0),
     )(*args)
 
@@ -302,6 +303,18 @@
     for n in range(3):
         here = pl.ds(n * rows, rows)
         total[here] = total_ref[here] + (mm(grads[1], fields[3 - n], NT) + mm(grads[2], fields[6 - n], NT))
+    width = send_far.shape[2]
+    share = send_far.shape[1] - 2 * cap
+    half = 3 * rows // 2
+    taps = total[:, 2 * chans :]
+    taps = jnp.concatenate([taps[:half], taps[half:]], axis=1)
+    taps = jnp.concatenate([total[:, : 2 * chans], taps], axis=0)
+    full = taps.shape[0] // share
+    sums_send[pl.ds(0, full)] = taps.reshape(full, share, width).astype(BF16)
+    early = pltpu.make_async_copy(
+        sums_send.at[pl.ds(0, full)], send_far.at[pl.ds(0, full), pl.ds(0, share)], sems.at[0]
+    )
+    early.start()
     inner = mm(wb_ref[pl.ds(rows, 2 * rows)], grads[1])
     top = slot_ref[0] + inner[:rows] + mm(wb_ref[pl.ds(2 * rows, rows)], grads[0])
     second = slot_ref[1] + inner[rows:]
@@ -322,51 +335,52 @@
     proj_high = proj.astype(BF16).astype(F32)
     sides = jnp.concatenate([found[0], found[2]], axis=0).T
     middle = jnp.concatenate([found[1], jnp.zeros_like(found[1])], axis=0).T
-    width = send_far.shape[2]
-    share = send_far.shape[1] - 2 * cap
-    taps = total[:, 2 * chans :]
-    half = 3 * rows // 2
-    taps = jnp.concatenate([taps[:half], taps[half:]], axis=1)
     halves = [v.reshape(2 * chans // share, share // 2, width) for v in (proj_high, proj - proj_high)]
-    proj = jnp.stack(halves, axis=1).reshape(2 * chans, width)
-    pad = jnp.zeros((share * ndev - 3 * rows - half - 2 * chans, width), F32)
-    sums = jnp.concatenate([total[:, : 2 * chans], taps, proj, pad], axis=0)
-    sums_send[...] = sums.reshape(sums_send.shape).astype(BF16)
+    proj = jnp.stack(halves, axis=1).reshape(2 * chans // share * 2, share // 2, width)
+    rest = ndev - full
+    pad = jnp.zeros(((rest * 2 - proj.shape[0]), share // 2, width), F32)
+    proj = jnp.concatenate([proj, pad], axis=0).reshape(rest, share, width)
+    sums_send[pl.ds(full, rest)] = proj.astype(BF16)
     back = [sides.reshape(ndev, cap, width), middle.reshape(ndev, cap, width)]
     slots_send[...] = jnp.concatenate(back, axis=1).astype(BF16)
     copies = [
-        pltpu.make_async_copy(sums_send, send_far.at[:, pl.ds(0, share)], sems.at[0]),
-        pltpu.make_async_copy(slots_send, send_far.at[:, pl.ds(share, 2 * cap)], sems.at[1]),
+        pltpu.make_async_copy(
+            sums_send.at[pl.ds(full, rest)], send_far.at[pl.ds(full, rest), pl.ds(0, share)], sems.at[1]
+        ),
+        pltpu.make_async_copy(slots_send, send_far.at[:, pl.ds(share, 2 * cap)], sems.at[2]),
     ]
     for copy in copies:
         copy.start()
+    early.wait()
     for copy in copies:
         copy.wait()
 
 
-def rows_kernel(
-    ngx, ngy, cap, chans, recv_ref, index_ref, counts_ref, proj_t_ref, rows_ref, sums_ref
-):
-    ndev = ngx * ngy
-    nrows = rows_ref.shape[0]
-    width = recv_ref.shape[1]
-    slots = ndev * cap
-    share = recv_ref.shape[0] // ndev - 2 * cap
-    arrived = recv_ref[...].astype(F32).reshape(ndev, share + 2 * cap, width)
-    sums = jnp.sum(arrived[:, :share], axis=0)
+def sums_kernel(chans, cap, recv_ref, index_ref, sums_ref):
+    ndev, each, width = recv_ref.shape
+    share = each - 2 * cap
+    sums = jnp.sum(recv_ref[:, pl.ds(0, share)].astype(F32), axis=0)
     half = share // 2
     whole = sums[:half] + sums[half:]
     high = whole.astype(BF16).astype(F32)
     split = jnp.concatenate([high, whole - high], axis=0)
     device = jnp.broadcast_to(index_ref[...], sums.shape)
-    sums = jnp.where(device * share >= 27 * chans * chans // width, split, sums)
-    sums_ref[...] = jnp.broadcast_to(sums[None], (ndev, share, width)).reshape(
-        sums_ref.shape
-    ).astype(BF16)
-    sides = arrived[:, share : share + cap].reshape(ngx, ngy, cap, width)
+    sums = jnp.where(device * share >= 27 * chans * chans // width, split, sums).astype(BF16)
+    for n in range(ndev):
+        sums_ref[n] = sums
+
+
+def rows_kernel(ngx, ngy, cap, chans, recv_ref, counts_ref, proj_t_ref, rows_ref):
+    ndev = ngx * ngy
+    nrows = rows_ref.shape[0]
+    width = recv_ref.shape[2]
+    slots = ndev * cap
+    share = recv_ref.shape[1] - 2 * cap
+    arrived = recv_ref[:, pl.ds(share, 2 * cap)].astype(F32)
+    sides = arrived[:, :cap].reshape(ngx, ngy, cap, width)
     left = lax.broadcasted_iota(I32, sides.shape, 3) < chans
     sides = jnp.where(left, rolled(sides, 1, 0), rolled(sides, -1, 0)).reshape(slots, width)
-    middle = arrived[:, share + cap :].reshape(slots, width)
+    middle = arrived[:, cap:].reshape(slots, width)
     counts = counts_ref[...].astype(F32)
     place = lax.broadcasted_iota(I32, (nrows, ndev), 0).astype(F32)
     lane = lax.broadcasted_iota(I32, (ndev, ndev), 1)
@@ -386,24 +400,32 @@
     rows_ref[...] = mm(sides, both) + mm(middle, both)
 
 
-def finish_kernel(conv_scale, proj_scale, share, recv_ref, conv_ref, proj_ref):
+def finish_kernel(conv_scale, proj_scale, share, recv_ref, conv_far, proj_ref, conv_ref, sems):
     taps, chans, _ = conv_ref.shape
     rows = 9 * chans
     half = rows // 2
+    third = taps // 3
     packed = recv_ref[pl.ds(rows, half)].astype(F32)
     column = jnp.concatenate([packed[:, :chans], packed[:, chans:]], axis=0)
-    for b in range(3):
-        for dz in range(3):
-            first = (b * 3 + dz) * chans
-            block = recv_ref[pl.ds(first, chans)].astype(F32)
-            k = (2 - b) * 3 + dz
-            conv_ref[k] = block[:, :chans] * conv_scale
-            conv_ref[9 + k] = block[:, chans:] * conv_scale
-            conv_ref[18 + k] = column[first : first + chans] * conv_scale
+    copies = []
+    for dx in range(3):
+        for b in range(3):
+            for dz in range(3):
+                at = (b * 3 + dz) * chans
+                if dx < 2:
+                    block = recv_ref[pl.ds(at, chans)].astype(F32)[:, dx * chans : (dx + 1) * chans]
+                else:
+                    block = column[at : at + chans]
+                conv_ref[dx * 9 + (2 - b) * 3 + dz] = block * conv_scale
+        part = pl.ds(dx * third, third)
+        copies.append(pltpu.make_async_copy(conv_ref.at[part], conv_far.at[part], sems.at[dx]))
+        copies[-1].start()
     width = recv_ref.shape[1]
     terms = recv_ref[pl.ds(rows + half, 2 * chans)].astype(F32)
     terms = terms.reshape(2 * chans // share, 2, share // 2, width)
     proj_ref[...] = jnp.sum(terms, axis=1).reshape(chans, width) * proj_scale
+    for copy in copies:
+        copy.wait()
 
 
 def local(particles, send_counts, cell_lists, base_field, proj_weight, conv_weight, cotangent):
@@ -435,6 +457,7 @@
             pltpu.SemaphoreType.DMA((4,)),
         ),
         far=range(4),
+        limit=ALL,
     )
     west, east = move(plane, 1, 0), move(plane, -1, 0)
     (payload,) = call(same_kernel, [payload], (payload,), 0, far=(0,), far_out=(0,), aliases={0: 0})
@@ -487,19 +510,27 @@
             pltpu.VMEM((9 * chans, rows), F32),
             pltpu.VMEM((ndev, share, feats), BF16),
             pltpu.VMEM((ndev, 2 * cap, feats), BF16),
-            pltpu.SemaphoreType.DMA((2,)),
+            pltpu.SemaphoreType.DMA((3,)),
         ),
         far_out=(1,),
     )
+    (payload,) = call(same_kernel, [payload], (payload,), 0, far=(0,), far_out=(0,), aliases={0: 0})
     payload = payload.reshape(-1, feats)
-    recv = exchange(payload, ndev)
+    recv = exchange(payload, ndev).reshape(ndev, share + 2 * cap, feats)
     index = (lax.axis_index("gx") * ngy + lax.axis_index("gy")).astype(I32).reshape(1, 1)
-    row_grads, sums = call(
+    (sums,) = call(
+        functools.partial(sums_kernel, chans, cap),
+        [shape((ndev, share, feats), BF16)],
+        (recv, index),
+        1000,
+    )
+    (row_grads,) = call(
         functools.partial(rows_kernel, ngx, ngy, cap, chans),
-        [shape((nrows, feats), F32), shape((ndev * share, feats), BF16)],
-        (recv, index, send_counts, proj_t),
+        [shape((nrows, feats), F32)],
+        (recv, send_counts, proj_t),
         2 * nrows * slots * chans,
     )
+    sums = sums.reshape(-1, feats)
     recv = exchange(sums, ndev)
     conv_grad, proj_grad = call(
         functools.partial(
@@ -508,6 +539,8 @@
         [shape((27, chans, chans), F32), shape((chans, feats), F32)],
         (recv,),
         1000,
+        (pltpu.VMEM((27, chans, chans), F32), pltpu.SemaphoreType.DMA((3,))),
+        far_out=(0,),
     )
     out_field = jnp.concatenate([out_edge[:1], out_rows[1 : cy - 1], out_edge[1:]], axis=0)
     return (out_field.transpose(1, 0, 2)[:, None], row_grads, conv_grad, proj_grad.T)

time: 71.8 us -> 70.7 us (0.985)
  local copies, waits for them, and re-layouts: 9.49 us -> 5.8 us
  Pallas kernels: 14.6 us -> 17.5 us
    pallas_call x7 -> x9, Pallas kernels: 14.6 us -> 17.5 us  [call(): pl.pallas_call(kernel, out_shape=[jax.ShapeDtypeStruct(o.shape, o.dtype)...]
    unnamed x16, local copies, waits for them, and re-layouts: 5.52 us -> 3.33 us
    reshape x2, local copies, waits for them, and re-layouts: 1.65 us -> 0.55 us  [local(): wf = taps.transpose(1, 2, 3, 0, 4).reshape(9 * chans, rows)]
    ppermute x4, waiting for transfers between devices: 0.79 us -> 0.01 us  [send(): return lax.ppermute(block, AXES, pairs)]
  transfers between devices with their start and end apart: 7 -> 7, of which waited for: 4 -> 3; matrix products, arithmetic and copies ran while one was open for 9% -> 5% of each run, Pallas kernels for 13% -> 15%
where the time goes in v5:
time: 70.7 us; the launch traced here: 70.3 us
  waiting for transfers between devices  25.9 us (37%)
  starting transfers between devices  20.2 us (29%)
  Pallas kernels  17.5 us (25%)
  local copies, waits for them, and re-layouts  5.8 us (8%)
  between operations  0.84 us (1%)
    all_to_all x3, waiting for transfers between devices, exchange(): lax.all_to_all(payload.reshape(ndev, rows // ndev, width), AXES, split_ax...  25.9 us
    pallas_call x9, Pallas kernels, call(): pl.pallas_call(kernel, out_shape=[jax.ShapeDtypeStruct(o.shape, o.dtype)...  17.5 us
    all_to_all x3, starting transfers between devices, exchange(): lax.all_to_all(payload.reshape(ndev, rows // ndev, width), AXES, split_ax...  12.8 us
    ppermute x4, starting transfers between devices, send(): return lax.ppermute(block, AXES, pairs)  7.33 us
    unnamed x16, local copies, waits for them, and re-layouts  3.33 us
  transfers between devices with their start and end apart: 7, of which 3 were waited for; matrix products, arithmetic and copies ran while one was open for 5% of the time, Pallas kernels for 15%

profile of v5, /device:TPU:0, one launch (start us, length us, event | category | flops | bytes accessed | tf_op | source)
XLA Modules:
  0.0 70.3 jit_solution(10714575230461755293)
XLA Ops:
  0.6 0.0 copy-start.5
  0.6 2.2 %shard_map.102 = (bf16[1040,256]{1,0:T(8,128)(2,1)}, bf16[768,128]{1,0:T(8,128)(2,1)}) custom-call(bf16[64,16,256]{2,1,0:T(8,128)(2,1)} %bitcast.40, s32[1,256]{1,0:T(1,128)} %cells_far.1, bf16[128,128]{1,0:T(8,128)(2,1)} %rows_far.1, s32[1,32]{1,0:T(1,128)} %counts_ref.1), custom_call_target="tpu_custom_call" | custom-call | flops 8388608 | bytes 1287296 | tf_op jit(solution)/shard_map/pallas_call | solution.py:27
  2.9 0.5 collective-permute-start
  3.4 2.9 %collective-permute-start.1 = (bf16[1040,256]{1,0:T(8,128)(2,1)}, bf16[1040,256]{1,0:T(8,128)(2,1)S(1)}, u32[]{:S(2)}, u32[]{:S(2)}) collective-permute-start(bf16[1040,256]{1,0:T(8,128)(2,1)} %get-tuple-element.18.own_ref), channel_id=1, source_target_pairs={{0,28},{1,29},{2,30},{3,31},{4,0},{5,1},{6,2},{7,3},{8,4},{9,5},{1... | collective-permute-start | bytes 1597448 | tf_op jit(solution)/shard_map/ppermute | solution.py:48
  6.3 0.0 copy-start.1
  6.3 0.9 %copy-done.1 = bf16[768,128]{1,0:T(8,128)(2,1)S(1)} copy-done((bf16[768,128]{1,0:T(8,128)(2,1)S(1)}, bf16[768,128]{1,0:T(8,128)(2,1)}, u32[]{:S(2)}) %copy-start.1) | copy-done | bytes 196632
  7.2 0.0 copy-start.2
  7.2 0.7 copy-done.2
  7.9 5.6 %all-to-all-start = ((bf16[32,24,128]{2,1,0:T(8,128)(2,1)}), bf16[32,24,128]{2,1,0:T(8,128)(2,1)S(1)}, u32[]{:S(2)}, u32[]{:S(2)}) async-start(bf16[32,24,128]{2,1,0:T(8,128)(2,1)} %bitcast.32), calls=%async_computation | async-start | bytes 393216 | tf_op jit(solution)/shard_map/all_to_all | solution.py:53
  13.6 0.0 copy-done.5
  13.6 0.9 %copy.18 = bf16[3,3,3,64,64]{3,2,1,4,0:T(4,128)(2,1)S(1)} copy(bf16[3,3,3,64,64]{4,3,2,1,0:T(8,128)(2,1)S(1)} %bitcast.38) | data formatting | bytes 442368 | tf_op jit(solution)/shard_map/reshape | solution.py:467
  14.5 0.4 copy.27
  14.9 0.4 reshape.36
  15.3 0.2 copy.20.wf_ref
  15.5 0.0 copy-start.6
  15.5 0.4 reshape.37
  15.9 0.2 copy.21.wb_ref
  16.1 0.5 copy-done.6
  16.5 0.0 copy-start
  16.5 0.0 copy-start.3
  16.5 0.2 copy.28
  16.7 6.2 %all-to-all-done = bf16[32,24,128]{2,1,0:T(8,128)(2,1)S(1)} async-done(((bf16[32,24,128]{2,1,0:T(8,128)(2,1)}), bf16[32,24,128]{2,1,0:T(8,128)(2,1)S(1)}, u32[]{:S(2)}, u32[]{:S(2)}) %all-to-all-start) | async-done | bytes 196640 | tf_op jit(solution)/shard_map/all_to_all | solution.py:53
  22.9 0.0 collective-permute-done.west_ref
  22.9 0.0 collective-permute-done.1.east_ref
  22.9 0.0 copy-done
  22.9 0.0 copy-done.3
  22.9 0.6 shard_map.105
  23.5 0.6 collective-permute-start.2
  24.2 3.2 %collective-permute-start.3 = (bf16[448,256]{1,0:T(8,128)(2,1)S(1)}, bf16[448,256]{1,0:T(8,128)(2,1)S(1)}, u32[]{:S(2)}, u32[]{:S(2)}) collective-permute-start(bf16[448,256]{1,0:T(8,128)(2,1)S(1)} %get-tuple-element.24.first_ref), channel_id=1, source_target_pairs={{0,3},{1,0},{2,1},{3,2},{4,7},{5,4},{6,5},{7,6},{8,11},{9,8},{10,9... | collective-permute-start | bytes 688136 | tf_op jit(solution)/shard_map/ppermute | solution.py:48
  27.4 9.2 %shard_map.104 = (bf16[16,64,256]{2,1,0:T(8,128)(2,1)S(1)}, f32[576,192]{1,0:T(8,128)S(1)}, f32[4,192,256]{2,1,0:T(8,128)S(1)}, f32[4,192,256]{2,1,0:T(8,128)S(1)}, f32[3,64,256]{2,1,0:T(8,128)S(1)}) custom-call(bf16[768,128]{1,0:T(8,128)(2,1)S(1)} %bitcast.29, bf16[64,128]{1,0:T(8,128)(2,1)S(1)} %bitcast.34, bf16[16,64,256]{2,1,0:T(8,128)(2,1)S(1)} %bitcast.26, ...), custom_call_target="tpu_custom_call" | custom-call | flops 2717908992 | bytes 5513216 | tf_op jit(solution)/shard_map/pallas_call | solution.py:27
  36.6 0.0 collective-permute-done.2.north_ref
  36.6 0.0 collective-permute-done.3.south_ref
  36.6 2.0 %shard_map.106 = (bf16[2,64,256]{2,1,0:T(8,128)(2,1)S(1)}, bf16[32,48,128]{2,1,0:T(8,128)(2,1)}) custom-call(f32[4,192,256]{2,1,0:T(8,128)S(1)} %get-tuple-element.19.pre_ref, f32[4,192,256]{2,1,0:T(8,128)S(1)} %get-tuple-element.20.slot_ref, f32[3,64,256]{2,1,0:T(8,128)S(1)} %get-tuple-element.21.sums_ref, f32[576,192]{1,0:T(8,128)S(1)} %get-tuple-element.22.total_ref, ...), custom_call_target="tpu_custom_call" | custom-call | flops 226492416 | bytes 6348800 | tf_op jit(solution)/shard_map/pallas_call | solution.py:27
  38.6 3.3 %all-to-all-start.1 = ((bf16[32,48,128]{2,1,0:T(8,128)(2,1)}), bf16[32,48,128]{2,1,0:T(8,128)(2,1)S(1)}, u32[]{:S(2)}, u32[]{:S(2)}) async-start(bf16[32,48,128]{2,1,0:T(8,128)(2,1)} %shard_map.107), calls=%async_computation.1 | async-start | bytes 786432 | tf_op jit(solution)/shard_map/all_to_all | solution.py:53
  42.0 11.8 %all-to-all-done.1.recv_ref = bf16[32,48,128]{2,1,0:T(8,128)(2,1)S(1)} async-done(((bf16[32,48,128]{2,1,0:T(8,128)(2,1)}), bf16[32,48,128]{2,1,0:T(8,128)(2,1)S(1)}, u32[]{:S(2)}, u32[]{:S(2)}) %all-to-all-start.1) | async-done | bytes 393248 | tf_op jit(solution)/shard_map/all_to_all | solution.py:53
  53.8 0.8 %shard_map.109 = bf16[32,32,128]{2,1,0:T(8,128)(2,1)} custom-call(bf16[32,48,128]{2,1,0:T(8,128)(2,1)S(1)} %all-to-all-done.1.recv_ref, s32[1,1]{1,0:T(1,128)} %bitcast.12.index_ref), custom_call_target="tpu_custom_call" | custom-call | flops 1000 | bytes 655364 | tf_op jit(solution)/shard_map/pallas_call | solution.py:27
  54.6 3.9 %all-to-all-start.2 = ((bf16[32,32,128]{2,1,0:T(8,128)(2,1)}), bf16[32,32,128]{2,1,0:T(8,128)(2,1)S(1)}, u32[]{:S(2)}, u32[]{:S(2)}) async-start(bf16[32,32,128]{2,1,0:T(8,128)(2,1)} %shard_map.109), calls=%async_computation.2 | async-start | bytes 524288 | tf_op jit(solution)/shard_map/all_to_all | solution.py:53
  58.5 0.1 maximum_bitcast_fusion
  58.6 0.0 copy-start.4
  58.6 1.1 %copy.24 = bf16[64,1,16,256]{3,2,1,0:T(8,128)(2,1)} copy(bf16[64,1,16,256]{3,0,2,1:T(8,128)(2,1)S(1)} %maximum_bitcast_fusion) | data formatting | bytes 1048576
  59.7 0.0 copy-done.4
  59.7 1.1 %shard_map.108 = f32[128,128]{1,0:T(8,128)} custom-call(bf16[32,48,128]{2,1,0:T(8,128)(2,1)S(1)} %all-to-all-done.1.recv_ref, s32[1,32]{1,0:T(1,128)S(1)} %copy-done.4, bf16[64,128]{1,0:T(8,128)(2,1)S(1)} %bitcast.35), custom_call_target="tpu_custom_call" | custom-call | flops 4194304 | bytes 475264 | tf_op jit(solution)/shard_map/pallas_call | solution.py:27
  60.8 7.8 %all-to-all-done.2 = bf16[32,32,128]{2,1,0:T(8,128)(2,1)S(1)} async-done(((bf16[32,32,128]{2,1,0:T(8,128)(2,1)}), bf16[32,32,128]{2,1,0:T(8,128)(2,1)S(1)}, u32[]{:S(2)}, u32[]{:S(2)}) %all-to-all-start.2) | async-done | bytes 262176 | tf_op jit(solution)/shard_map/all_to_all | solution.py:53
  68.7 1.6 %shard_map.110 = (f32[27,64,64]{2,1,0:T(8,128)}, f32[64,128]{1,0:T(8,128)}) custom-call(bf16[1024,128]{1,0:T(8,128)(2,1)S(1)} %bitcast.31), custom_call_target="tpu_custom_call" | custom-call | flops 1000 | bytes 737280 | tf_op jit(solution)/shard_map/pallas_call | solution.py:27
  (4 shorter events, 0.0 us)
Async XLA Ops:
  0.6 12.9 %copy-start.5 = (bf16[27,64,64]{2,1,0:T(8,128)(2,1)S(1)}, bf16[27,64,64]{2,1,0:T(8,128)(2,1)}, u32[]{:S(2)}) copy-start(bf16[27,64,64]{2,1,0:T(8,128)(2,1)} %param.12) | copy-start | bytes 663556
  2.9 20.0 %collective-permute-start = (bf16[1040,256]{1,0:T(8,128)(2,1)}, bf16[1040,256]{1,0:T(8,128)(2,1)S(1)}, u32[]{:S(2)}, u32[]{:S(2)}) collective-permute-start(bf16[1040,256]{1,0:T(8,128)(2,1)} %get-tuple-element.18.own_ref), channel_id=1, source_target_pairs={{0,4},{1,5},{2,6},{3,7},{4,8},{5,9},{6,10},{7,11},{8,12},{9,13},{1... | collective-permute-start | bytes 1597448 | tf_op jit(solution)/shard_map/ppermute | solution.py:48
  3.4 19.5 %collective-permute-start.1 = (bf16[1040,256]{1,0:T(8,128)(2,1)}, bf16[1040,256]{1,0:T(8,128)(2,1)S(1)}, u32[]{:S(2)}, u32[]{:S(2)}) collective-permute-start(bf16[1040,256]{1,0:T(8,128)(2,1)} %get-tuple-element.18.own_ref), channel_id=1, source_target_pairs={{0,28},{1,29},{2,30},{3,31},{4,0},{5,1},{6,2},{7,3},{8,4},{9,5},{1... | collective-permute-start | bytes 1597448 | tf_op jit(solution)/shard_map/ppermute | solution.py:48
  6.3 0.9 %copy-start.1 = (bf16[768,128]{1,0:T(8,128)(2,1)S(1)}, bf16[768,128]{1,0:T(8,128)(2,1)}, u32[]{:S(2)}) copy-start(bf16[768,128]{1,0:T(8,128)(2,1)} %get-tuple-element.17.in_ref) | copy-start | bytes 589828
  7.2 0.7 copy-start.2
  7.9 15.0 %all-to-all-start = ((bf16[32,24,128]{2,1,0:T(8,128)(2,1)}), bf16[32,24,128]{2,1,0:T(8,128)(2,1)S(1)}, u32[]{:S(2)}, u32[]{:S(2)}) async-start(bf16[32,24,128]{2,1,0:T(8,128)(2,1)} %bitcast.32), calls=%async_computation | async-start | bytes 393216 | tf_op jit(solution)/shard_map/all_to_all | solution.py:53
  15.5 1.0 %copy-start.6 = (bf16[64,1,16,256]{3,2,1,0:T(8,128)(2,1)S(1)}, bf16[64,1,16,256]{3,2,1,0:T(8,128)(2,1)}, u32[]{:S(2)}) copy-start(bf16[64,1,16,256]{3,2,1,0:T(8,128)(2,1)} %param.13) | copy-start | bytes 1572868
  16.5 6.4 %copy-start = (bf16[1040,256]{1,0:T(8,128)(2,1)S(1)}, bf16[1040,256]{1,0:T(8,128)(2,1)}, u32[]{:S(2)}) copy-start(bf16[1040,256]{1,0:T(8,128)(2,1)} %get-tuple-element.18.own_ref) | copy-start | bytes 1597444
  16.5 6.4 %copy-start.3 = (bf16[128,64]{0,1:T(8,128)(2,1)S(1)}, bf16[128,64]{0,1:T(8,128)(2,1)}, u32[]{:S(2)}) copy-start(bf16[128,64]{0,1:T(8,128)(2,1)} %param.11) | copy-start | bytes 49156
  23.5 13.1 %collective-permute-start.2 = (bf16[448,256]{1,0:T(8,128)(2,1)S(1)}, bf16[448,256]{1,0:T(8,128)(2,1)S(1)}, u32[]{:S(2)}, u32[]{:S(2)}) collective-permute-start(bf16[448,256]{1,0:T(8,128)(2,1)S(1)} %get-tuple-element.23.last_ref), channel_id=1, source_target_pairs={{0,1},{1,2},{2,3},{3,0},{4,5},{5,6},{6,7},{7,4},{8,9},{9,10},{10,1... | collective-permute-start | bytes 688136 | tf_op jit(solution)/shard_map/ppermute | solution.py:48
  24.2 12.4 %collective-permute-start.3 = (bf16[448,256]{1,0:T(8,128)(2,1)S(1)}, bf16[448,256]{1,0:T(8,128)(2,1)S(1)}, u32[]{:S(2)}, u32[]{:S(2)}) collective-permute-start(bf16[448,256]{1,0:T(8,128)(2,1)S(1)} %get-tuple-element.24.first_ref), channel_id=1, source_target_pairs={{0,3},{1,0},{2,1},{3,2},{4,7},{5,4},{6,5},{7,6},{8,11},{9,8},{10,9... | collective-permute-start | bytes 688136 | tf_op jit(solution)/shard_map/ppermute | solution.py:48
  38.6 15.2 %all-to-all-start.1 = ((bf16[32,48,128]{2,1,0:T(8,128)(2,1)}), bf16[32,48,128]{2,1,0:T(8,128)(2,1)S(1)}, u32[]{:S(2)}, u32[]{:S(2)}) async-start(bf16[32,48,128]{2,1,0:T(8,128)(2,1)} %shard_map.107), calls=%async_computation.1 | async-start | bytes 786432 | tf_op jit(solution)/shard_map/all_to_all | solution.py:53
  54.6 14.1 %all-to-all-start.2 = ((bf16[32,32,128]{2,1,0:T(8,128)(2,1)}), bf16[32,32,128]{2,1,0:T(8,128)(2,1)S(1)}, u32[]{:S(2)}, u32[]{:S(2)}) async-start(bf16[32,32,128]{2,1,0:T(8,128)(2,1)} %shard_map.109), calls=%async_computation.2 | async-start | bytes 524288 | tf_op jit(solution)/shard_map/all_to_all | solution.py:53
  58.6 1.1 %copy-start.4 = (s32[1,32]{1,0:T(1,128)S(1)}, s32[1,32]{1,0:T(1,128)}, u32[]{:S(2)}) copy-start(s32[1,32]{1,0:T(1,128)} %counts_ref.1) | copy-start | bytes 388

commit v6 on v5

--- a/solution.py
+++ b/solution.py
@@ -68,13 +68,6 @@
     return x
 
 
-def widths(nl, slots, block):
-    block = block.astype(F32)
-    y = jnp.concatenate([block[n : n + 1] for n in range(nl)], axis=1)[:, :slots]
-    z = jnp.concatenate([block[nl + n : nl + n + 1] for n in range(nl)], axis=1)[:, :slots]
-    return y.astype(I32), z.astype(I32)
-
-
 def picked_depth(z, nz):
     depth = lax.broadcasted_iota(I32, (nz, z.shape[1]), 0)
     return jnp.where(depth == z, 1.0, 0.0).astype(BF16)
@@ -105,35 +98,17 @@
 
 
 def first_kernel(
-    ngx, ngy, cap, base_far, cells_far, rows_far, counts_far,
-    out_ref, send_ref, base_ref, cells_ref, rows_ref, counts_ref, sems,
+    ngx, ngy, cap, rows_far, counts_far, send_ref, rows_ref, counts_ref, sems
 ):
-    pairs = (
-        (rows_far, rows_ref), (counts_far, counts_ref), (cells_far, cells_ref), (base_far, base_ref)
-    )
-    copies = [pltpu.make_async_copy(src, dst, sems.at[n]) for n, (src, dst) in enumerate(pairs)]
+    copies = [
+        pltpu.make_async_copy(rows_far, rows_ref, sems.at[0]),
+        pltpu.make_async_copy(counts_far, counts_ref, sems.at[1]),
+    ]
     for copy in copies:
         copy.start()
-    chans, cy, nz = base_ref.shape
-    for copy in copies[:3]:
+    for copy in copies:
         copy.wait()
     pick(ngx, ngy, cap, counts_ref, rows_ref, send_ref)
-    cells = cells_ref[...]
-    slots = cells.shape[1]
-    nl = -(-slots // nz)
-    tail = out_ref.shape[0] - cy * chans
-    lines = []
-    for values in (cells // nz, cells % nz):
-        values = values.astype(F32)
-        if nl * nz > slots:
-            values = jnp.concatenate([values, jnp.zeros((1, nl * nz - slots), F32)], axis=1)
-        lines += [values[:, n * nz : (n + 1) * nz] for n in range(nl)]
-    if tail > 2 * nl:
-        lines.append(jnp.zeros((tail - 2 * nl, nz), F32))
-    out_ref[pl.ds(cy * chans, tail)] = jnp.concatenate(lines, axis=0).astype(BF16)
-    copies[3].wait()
-    turned = jnp.swapaxes(base_ref[...].astype(F32), 0, 1)
-    out_ref[pl.ds(0, cy * chans)] = turned.reshape(cy * chans, nz).astype(BF16)
 
 
 def same_kernel(in_ref, out_ref):
@@ -167,45 +142,50 @@
 
 
 def outer_kernel(
-    ndev, cap, chans, cy, recv_ref, own_ref, west_ref, east_ref, proj_t_ref, cot_ref,
-    first_ref, last_ref, masked,
+    ndev, cap, recv_ref, own_ref, west_ref, east_ref, own_cells, west_cells, east_cells,
+    proj_t_ref, cot_ref, first_ref, last_ref, masked,
 ):
-    slots = ndev * cap
-    nz = own_ref.shape[1]
+    chans, cy, nz = own_ref.shape
     raws = rows_in(recv_ref, ndev, cap)
     ns = (0, 1, cy - 2, cy - 1)
-    for dx, ref in enumerate((west_ref, own_ref, east_ref)):
+    planes = ((west_ref, west_cells), (own_ref, own_cells), (east_ref, east_cells))
+    for dx, (ref, cells_ref) in enumerate(planes):
         values = mm(proj_t_ref[...], raws[dx], NT).astype(BF16)
-        painted = painted_rows(values, list_of(ref, cy, chans, slots), nz, ns, masked)
+        painted = painted_rows(values, place(cells_ref, nz), nz, ns, masked)
+        base = turned(ref)
         for n, row in enumerate(ns):
             part = painted[n * chans : (n + 1) * chans]
-            field = (ref[pl.ds(row * chans, chans)].astype(F32) + part).astype(BF16)
+            field = (base[row] + part).astype(BF16)
             target = first_ref if n < 2 else last_ref
             target[pl.ds((3 * (n % 2) + dx) * chans, chans)] = field
     first_ref[pl.ds(6 * chans, chans)] = cot_ref[0]
     last_ref[pl.ds(6 * chans, chans)] = cot_ref[cy - 1]
 
 
-def list_of(ref, cy, chans, slots):
-    tail = ref.shape[0] - cy * chans
-    return widths(-(-slots // ref.shape[1]), slots, ref[pl.ds(cy * chans, tail)])
+def place(cells_ref, nz):
+    cells = cells_ref[...]
+    return cells // nz, cells % nz
+
+
+def turned(ref):
+    return jnp.swapaxes(ref[...].astype(F32), 0, 1)
 
 
 def conv_kernel(
-    ndev, cap, chans, cy, recv_ref, proj_t_ref, cot_ref, wf_ref, wb_ref, own_ref, west_ref, east_ref,
+    ndev, cap, recv_ref, proj_t_ref, cot_ref, wf_ref, wb_ref,
+    own_ref, west_ref, east_ref, own_cells, west_cells, east_cells,
     out_ref, total_ref, pre_ref, slot_ref, sums_ref, x_ref, acc, grads, back, plane, masked,
 ):
+    chans, cy, nz = own_ref.shape
     rows = 3 * chans
-    nz = x_ref.shape[2]
     slots = ndev * cap
     raws = rows_in(recv_ref, ndev, cap)
-    for dx, ref in enumerate((west_ref, own_ref, east_ref)):
+    planes = ((west_ref, west_cells), (own_ref, own_cells), (east_ref, east_cells))
+    for dx, (ref, cells_ref) in enumerate(planes):
         values = mm(proj_t_ref[...], raws[dx], NT).astype(BF16)
-        painted = painted_rows(values, list_of(ref, cy, chans, slots), nz, range(cy), masked)
-        for n in range(cy):
-            part = painted[n * chans : (n + 1) * chans]
-            field = ref[pl.ds(n * chans, chans)].astype(F32) + part
-            x_ref[n, pl.ds(dx * chans, chans)] = field.astype(BF16)
+        painted = painted_rows(values, place(cells_ref, nz), nz, range(cy), masked)
+        field = turned(ref) + painted.reshape(cy, chans, nz)
+        x_ref[:, pl.ds(dx * chans, chans)] = field.astype(BF16)
     own = pl.ds(chans, chans)
     zeros = jnp.zeros((rows, nz), BF16)
     for t in (0, 1, cy, cy + 1):
@@ -268,8 +248,8 @@
     slot_ref[2] = back[cy - 2]
     slot_ref[3] = back[cy - 1]
     zero = jnp.zeros((chans, slots), F32)
-    for dx, ref in enumerate((west_ref, own_ref, east_ref)):
-        sums_ref[dx] = at_slots(plane[dx], list_of(ref, cy, chans, slots), range(2, cy - 2), zero)
+    for dx, (_, cells_ref) in enumerate(planes):
+        sums_ref[dx] = at_slots(plane[dx], place(cells_ref, nz), range(2, cy - 2), zero)
 
 
 def at_slots(part, cells, first, total):
@@ -282,13 +262,13 @@
 
 
 def edge_kernel(
-    ndev, cap, chans, cy,
+    ndev, cap,
     pre_ref, slot_ref, sums_ref, total_ref, north_ref, south_ref, first_ref, last_ref,
-    wf_ref, wb_ref, cot_ref, own_ref, west_ref, east_ref, recv_ref,
+    wf_ref, wb_ref, cot_ref, own_cells, west_cells, east_cells, recv_ref,
     out_ref, send_far, total, sums_send, slots_send, sems,
 ):
+    cy, chans, nz = cot_ref.shape
     rows = 3 * chans
-    slots = ndev * cap
     own = slice(chans, 2 * chans)
     fields = [ref[pl.ds(n * rows, rows)] for ref in (north_ref, first_ref, last_ref, south_ref) for n in (0, 1)]
     cots = [ref[pl.ds(2 * rows, chans)] for ref in (north_ref, first_ref, last_ref, south_ref)]
@@ -322,13 +302,13 @@
     third = slot_ref[2] + inner[:rows]
     bottom = slot_ref[3] + inner[rows:] + mm(wb_ref[pl.ds(0, rows)], grads[3])
     found = []
-    for dx, ref in enumerate((west_ref, own_ref, east_ref)):
+    for dx, cells_ref in enumerate((west_cells, own_cells, east_cells)):
         parts = [value[dx * chans : (dx + 1) * chans] for value in (top, second, third, bottom)]
         if dx == 1:
             inner = (cots[1], cot_ref[1], cot_ref[cy - 2], cots[2])
             parts = [part + cot.astype(F32) for part, cot in zip(parts, inner)]
         part = jnp.concatenate(parts, axis=0).astype(BF16)
-        cells = list_of(ref, cy, chans, slots)
+        cells = place(cells_ref, nz)
         found.append(at_slots(part, cells, (0, 1, cy - 2, cy - 1), sums_ref[dx]))
     raws = rows_in(recv_ref, ndev, cap)
     proj = sum(mm(found[dx].astype(BF16), raws[dx]) for dx in range(3))
@@ -400,32 +380,24 @@
     rows_ref[...] = mm(sides, both) + mm(middle, both)
 
 
-def finish_kernel(conv_scale, proj_scale, share, recv_ref, conv_far, proj_ref, conv_ref, sems):
+def finish_kernel(conv_scale, proj_scale, share, recv_ref, conv_ref, proj_ref):
     taps, chans, _ = conv_ref.shape
     rows = 9 * chans
     half = rows // 2
-    third = taps // 3
     packed = recv_ref[pl.ds(rows, half)].astype(F32)
     column = jnp.concatenate([packed[:, :chans], packed[:, chans:]], axis=0)
-    copies = []
-    for dx in range(3):
-        for b in range(3):
-            for dz in range(3):
-                at = (b * 3 + dz) * chans
-                if dx < 2:
-                    block = recv_ref[pl.ds(at, chans)].astype(F32)[:, dx * chans : (dx + 1) * chans]
-                else:
-                    block = column[at : at + chans]
-                conv_ref[dx * 9 + (2 - b) * 3 + dz] = block * conv_scale
-        part = pl.ds(dx * third, third)
-        copies.append(pltpu.make_async_copy(conv_ref.at[part], conv_far.at[part], sems.at[dx]))
-        copies[-1].start()
+    for b in range(3):
+        for dz in range(3):
+            first = (b * 3 + dz) * chans
+            block = recv_ref[pl.ds(first, chans)].astype(F32)
+            k = (2 - b) * 3 + dz
+            conv_ref[k] = block[:, :chans] * conv_scale
+            conv_ref[9 + k] = block[:, chans:] * conv_scale
+            conv_ref[18 + k] = column[first : first + chans] * conv_scale
     width = recv_ref.shape[1]
     terms = recv_ref[pl.ds(rows + half, 2 * chans)].astype(F32)
     terms = terms.reshape(2 * chans // share, 2, share // 2, width)
     proj_ref[...] = jnp.sum(terms, axis=1).reshape(chans, width) * proj_scale
-    for copy in copies:
-        copy.wait()
 
 
 def local(particles, send_counts, cell_lists, base_field, proj_weight, conv_weight, cotangent):
@@ -442,25 +414,23 @@
     rows = 3 * chans
     one = 2 * rows * rows * nz
 
-    tail = -(-2 * -(-slots // nz) // 16) * 16
     base = base_field.reshape(chans, cy, nz)
-    plane, payload = call(
+    west, east = move(base_field, 1, 0), move(base_field, -1, 0)
+    planes = (base, west.reshape(base.shape), east.reshape(base.shape))
+    lists = (cell_lists, move(cell_lists, 1, 0), move(cell_lists, -1, 0))
+    (payload,) = call(
         functools.partial(first_kernel, ngx, ngy, cap),
-        [shape((cy * chans + tail, nz), BF16), shape((ndev * 3 * cap, feats), BF16)],
-        (base, cell_lists, particles, send_counts),
+        [shape((ndev * 3 * cap, feats), BF16)],
+        (particles, send_counts),
         2 * slots * nrows * feats,
         (
-            pltpu.VMEM(base.shape, BF16),
-            pltpu.VMEM(cell_lists.shape, I32),
             pltpu.VMEM(particles.shape, BF16),
             pltpu.VMEM(send_counts.shape, I32),
-            pltpu.SemaphoreType.DMA((4,)),
+            pltpu.SemaphoreType.DMA((2,)),
         ),
-        far=range(4),
+        far=range(2),
         limit=ALL,
     )
-    west, east = move(plane, 1, 0), move(plane, -1, 0)
-    (payload,) = call(same_kernel, [payload], (payload,), 0, far=(0,), far_out=(0,), aliases={0: 0})
     recv = exchange(payload, ndev)
 
     cot = cotangent[:, 0].transpose(1, 0, 2)
@@ -469,15 +439,15 @@
     wb = taps.transpose(1, 0, 4, 2, 3).reshape(9 * chans, rows)
 
     first, last = call(
-        functools.partial(outer_kernel, ndev, cap, chans, cy),
+        functools.partial(outer_kernel, ndev, cap),
         [shape((2 * rows + chans, nz), BF16)] * 2,
-        (recv, plane, west, east, proj_t, cot),
+        (recv, *planes, *lists, proj_t, cot),
         2 * slots * count * chans,
         (pltpu.VMEM((4 * chans, slots), BF16),),
     )
     north, south = move(last, 0, 1), move(first, 0, -1)
     out_rows, total, pre_edge, slot_edge, sums = call(
-        functools.partial(conv_kernel, ndev, cap, chans, cy),
+        functools.partial(conv_kernel, ndev, cap),
         [
             shape((cy, chans, nz), BF16),
             shape((9 * chans, rows), F32),
@@ -485,7 +455,7 @@
             shape((4, rows, nz), F32),
             shape((3, chans, slots), F32),
         ],
-        (recv, proj_t, cot, wf, wb, plane, west, east),
+        (recv, proj_t, cot, wf, wb, *planes, *lists),
         3 * cy * 3 * one,
         (
             pltpu.VMEM((cy, rows, nz), BF16),
@@ -499,11 +469,11 @@
     grad_rows = 27 * chans * chans // feats
     share = -(-(grad_rows + 2 * chans) // (16 * ndev)) * 16
     out_edge, payload = call(
-        functools.partial(edge_kernel, ndev, cap, chans, cy),
+        functools.partial(edge_kernel, ndev, cap),
         [shape((2, chans, nz), BF16), shape((ndev, share + 2 * cap, feats), BF16)],
         (
             pre_edge, slot_edge, sums, total, north, south, first, last,
-            wf, wb, cot, plane, west, east, recv,
+            wf, wb, cot, *lists, recv,
         ),
         12 * one,
         (
@@ -539,8 +509,6 @@
         [shape((27, chans, chans), F32), shape((chans, feats), F32)],
         (recv,),
         1000,
-        (pltpu.VMEM((27, chans, chans), F32), pltpu.SemaphoreType.DMA((3,))),
-        far_out=(0,),
     )
     out_field = jnp.concatenate([out_edge[:1], out_rows[1 : cy - 1], out_edge[1:]], axis=0)
     return (out_field.transpose(1, 0, 2)[:, None], row_grads, conv_grad, proj_grad.T)

time: 70.7 us -> 67.9 us (0.960)
  waiting for transfers between devices: 25.9 us -> 22.5 us
  starting transfers between devices: 20.2 us -> 22.1 us
  local copies, waits for them, and re-layouts: 5.8 us -> 4.82 us
    all_to_all x3, waiting for transfers between devices: 25.9 us -> 22.5 us  [exchange(): lax.all_to_all(payload.reshape(ndev, rows // ndev, width), AXES, split_ax...]
    ppermute x4 -> x6, starting transfers between devices: 7.33 us -> 10 us  [send(): return lax.ppermute(block, AXES, pairs)]
    unnamed x16 -> x12, local copies, waits for them, and re-layouts: 3.33 us -> 2.37 us
    all_to_all x3, starting transfers between devices: 12.8 us -> 12.1 us  [exchange(): lax.all_to_all(payload.reshape(ndev, rows // ndev, width), AXES, split_ax...]
    pallas_call x9 -> x8, Pallas kernels: 17.5 us -> 17.1 us  [call(): pl.pallas_call(kernel, out_shape=[jax.ShapeDtypeStruct(o.shape, o.dtype)...]
  transfers between devices with their start and end apart: 7 -> 9, of which waited for: 3 -> 3; matrix products, arithmetic and copies ran while one was open for 5% -> 7% of each run, Pallas kernels for 15% -> 19%
where the time goes in v6:
time: 67.9 us; the launch traced here: 67.5 us
  waiting for transfers between devices  22.5 us (33%)
  starting transfers between devices  22.1 us (33%)
  Pallas kernels  17.1 us (25%)
  local copies, waits for them, and re-layouts  4.82 us (7%)
  between operations  0.86 us (1%)
    all_to_all x3, waiting for transfers between devices, exchange(): lax.all_to_all(payload.reshape(ndev, rows // ndev, width), AXES, split_ax...  22.5 us
    pallas_call x8, Pallas kernels, call(): pl.pallas_call(kernel, out_shape=[jax.ShapeDtypeStruct(o.shape, o.dtype)...  17.1 us
    all_to_all x3, starting transfers between devices, exchange(): lax.all_to_all(payload.reshape(ndev, rows // ndev, width), AXES, split_ax...  12.1 us
    ppermute x6, starting transfers between devices, send(): return lax.ppermute(block, AXES, pairs)  10 us
    unnamed x12, local copies, waits for them, and re-layouts  2.37 us
  transfers between devices with their start and end apart: 9, of which 3 were waited for; matrix products, arithmetic and copies ran while one was open for 7% of the time, Pallas kernels for 19%

profile of v6, /device:TPU:0, one launch (start us, length us, event | category | flops | bytes accessed | tf_op | source)
XLA Modules:
  0.0 67.5 jit_solution(117762214645585337)
XLA Ops:
  0.6 0.0 copy-start.4
  0.6 0.5 collective-permute-start
  1.1 2.9 %collective-permute-start.1 = (bf16[64,1,16,256]{3,2,0,1:T(8,128)(2,1)}, bf16[64,1,16,256]{3,2,0,1:T(8,128)(2,1)S(1)}, u32[]{:S(2)}, u32[]{:S(2)}) collective-permute-start(bf16[64,1,16,256]{3,2,0,1:T(8,128)(2,1)} %bitcast.36), channel_id=1, source_target_pairs={{0,28},{1,29},{2,30},{3,31},{4,0},{5,1},{6,2},{7,3},{8,4},{9,5},{1... | collective-permute-start | bytes 1572872 | tf_op jit(solution)/shard_map/ppermute | solution.py:48
  4.1 1.7 %shard_map.102 = bf16[768,128]{1,0:T(8,128)(2,1)} custom-call(bf16[128,128]{1,0:T(8,128)(2,1)} %rows_far.1, s32[1,32]{1,0:T(1,128)} %counts_ref.1), custom_call_target="tpu_custom_call" | custom-call | flops 8388608 | bytes 229504 | tf_op jit(solution)/shard_map/pallas_call | solution.py:27
  5.8 0.0 copy-start.2
  5.8 5.6 %all-to-all-start = ((bf16[32,24,128]{2,1,0:T(8,128)(2,1)}), bf16[32,24,128]{2,1,0:T(8,128)(2,1)S(1)}, u32[]{:S(2)}, u32[]{:S(2)}) async-start(bf16[32,24,128]{2,1,0:T(8,128)(2,1)} %bitcast.50), calls=%async_computation | async-start | bytes 393216 | tf_op jit(solution)/shard_map/all_to_all | solution.py:53
  11.5 0.0 copy-done.2
  11.5 0.3 collective-permute-start.2
  11.8 2.4 %collective-permute-start.3 = (s32[1,256]{1,0:T(1,128)S(1)}, s32[1,256]{1,0:T(1,128)S(1)}, u32[]{:S(2)}, u32[]{:S(2)}) collective-permute-start(s32[1,256]{1,0:T(1,128)S(1)} %copy-done.2), channel_id=1, source_target_pairs={{0,28},{1,29},{2,30},{3,31},{4,0},{5,1},{6,2},{7,3},{8,4},{9,5},{1... | collective-permute-start | bytes 3080 | tf_op jit(solution)/shard_map/ppermute | solution.py:48
  14.2 0.0 copy-done.4
  14.2 0.9 %copy.19 = bf16[3,3,3,64,64]{3,2,1,4,0:T(4,128)(2,1)S(1)} copy(bf16[3,3,3,64,64]{4,3,2,1,0:T(8,128)(2,1)S(1)} %bitcast.48) | data formatting | bytes 442368 | tf_op jit(solution)/shard_map/reshape | solution.py:437
  15.1 0.4 copy.30
  15.5 0.4 reshape.41
  15.9 0.2 copy.23.wf_ref
  16.1 0.4 reshape.42
  16.5 0.2 copy.24.wb_ref
  16.6 0.0 copy-start
  16.7 0.0 copy-start.1
  16.7 1.3 %copy.31 = bf16[64,1,16,256]{3,0,2,1:T(8,128)(2,1)S(1)} copy(bf16[64,1,16,256]{3,2,1,0:T(8,128)(2,1)} %param.13) | data formatting | bytes 1048576 | tf_op args[6]
  17.9 0.0 collective-permute-done.2.west_cells
  17.9 0.0 collective-permute-done.3.east_cells
  18.0 2.9 %all-to-all-done = bf16[32,24,128]{2,1,0:T(8,128)(2,1)S(1)} async-done(((bf16[32,24,128]{2,1,0:T(8,128)(2,1)}), bf16[32,24,128]{2,1,0:T(8,128)(2,1)S(1)}, u32[]{:S(2)}, u32[]{:S(2)}) %all-to-all-start) | async-done | bytes 196640 | tf_op jit(solution)/shard_map/all_to_all | solution.py:53
  20.8 0.0 collective-permute-done
  20.8 0.0 collective-permute-done.1
  20.8 0.0 copy-done
  20.8 0.0 copy-done.1
  20.8 0.6 shard_map.104
  21.5 0.3 collective-permute-start.4
  21.7 3.6 %collective-permute-start.5 = (bf16[448,256]{1,0:T(8,128)(2,1)S(1)}, bf16[448,256]{1,0:T(8,128)(2,1)S(1)}, u32[]{:S(2)}, u32[]{:S(2)}) collective-permute-start(bf16[448,256]{1,0:T(8,128)(2,1)S(1)} %get-tuple-element.20.first_ref), channel_id=1, source_target_pairs={{0,3},{1,0},{2,1},{3,2},{4,7},{5,4},{6,5},{7,6},{8,11},{9,8},{10,9... | collective-permute-start | bytes 688136 | tf_op jit(solution)/shard_map/ppermute | solution.py:48
  25.4 9.7 %shard_map.103 = (bf16[16,64,256]{2,1,0:T(8,128)(2,1)S(1)}, f32[576,192]{1,0:T(8,128)S(1)}, f32[4,192,256]{2,1,0:T(8,128)S(1)}, f32[4,192,256]{2,1,0:T(8,128)S(1)}, f32[3,64,256]{2,1,0:T(8,128)S(1)}) custom-call(bf16[768,128]{1,0:T(8,128)(2,1)S(1)} %bitcast.32, bf16[64,128]{1,0:T(8,128)(2,1)S(1)} %bitcast.44, bf16[16,64,256]{2,1,0:T(8,128)(2,1)S(1)} %bitcast.29, ...), custom_call_target="tpu_custom_call" | custom-call | flops 2717908992 | bytes 5491712 | tf_op jit(solution)/shard_map/pallas_call | solution.py:27
  35.1 0.0 collective-permute-done.4.north_ref
  35.1 0.0 collective-permute-done.5.south_ref
  35.1 2.0 %shard_map.105 = (bf16[2,64,256]{2,1,0:T(8,128)(2,1)S(1)}, bf16[32,48,128]{2,1,0:T(8,128)(2,1)}) custom-call(f32[4,192,256]{2,1,0:T(8,128)S(1)} %get-tuple-element.15.pre_ref, f32[4,192,256]{2,1,0:T(8,128)S(1)} %get-tuple-element.16.slot_ref, f32[3,64,256]{2,1,0:T(8,128)S(1)} %get-tuple-element.17.sums_ref, f32[576,192]{1,0:T(8,128)S(1)} %get-tuple-element.18.total_ref, ...), custom_call_target="tpu_custom_call" | custom-call | flops 226492416 | bytes 4754432 | tf_op jit(solution)/shard_map/pallas_call | solution.py:27
  37.1 2.6 %all-to-all-start.1 = ((bf16[32,48,128]{2,1,0:T(8,128)(2,1)}), bf16[32,48,128]{2,1,0:T(8,128)(2,1)S(1)}, u32[]{:S(2)}, u32[]{:S(2)}) async-start(bf16[32,48,128]{2,1,0:T(8,128)(2,1)} %shard_map.106), calls=%async_computation.1 | async-start | bytes 786432 | tf_op jit(solution)/shard_map/all_to_all | solution.py:53
  39.7 11.8 %all-to-all-done.1.recv_ref = bf16[32,48,128]{2,1,0:T(8,128)(2,1)S(1)} async-done(((bf16[32,48,128]{2,1,0:T(8,128)(2,1)}), bf16[32,48,128]{2,1,0:T(8,128)(2,1)S(1)}, u32[]{:S(2)}, u32[]{:S(2)}) %all-to-all-start.1) | async-done | bytes 393248 | tf_op jit(solution)/shard_map/all_to_all | solution.py:53
  51.6 0.8 %shard_map.108 = bf16[32,32,128]{2,1,0:T(8,128)(2,1)} custom-call(bf16[32,48,128]{2,1,0:T(8,128)(2,1)S(1)} %all-to-all-done.1.recv_ref, s32[1,1]{1,0:T(1,128)} %bitcast.15.index_ref), custom_call_target="tpu_custom_call" | custom-call | flops 1000 | bytes 655364 | tf_op jit(solution)/shard_map/pallas_call | solution.py:27
  52.4 3.8 %all-to-all-start.2 = ((bf16[32,32,128]{2,1,0:T(8,128)(2,1)}), bf16[32,32,128]{2,1,0:T(8,128)(2,1)S(1)}, u32[]{:S(2)}, u32[]{:S(2)}) async-start(bf16[32,32,128]{2,1,0:T(8,128)(2,1)} %shard_map.108), calls=%async_computation.2 | async-start | bytes 524288 | tf_op jit(solution)/shard_map/all_to_all | solution.py:53
  56.2 0.1 maximum_bitcast_fusion
  56.3 0.0 copy-start.3
  56.3 1.1 %copy.27 = bf16[64,1,16,256]{3,2,1,0:T(8,128)(2,1)} copy(bf16[64,1,16,256]{3,0,2,1:T(8,128)(2,1)S(1)} %maximum_bitcast_fusion) | data formatting | bytes 1048576
  57.4 0.0 copy-done.3
  57.4 1.1 %shard_map.107 = f32[128,128]{1,0:T(8,128)} custom-call(bf16[32,48,128]{2,1,0:T(8,128)(2,1)S(1)} %all-to-all-done.1.recv_ref, s32[1,32]{1,0:T(1,128)S(1)} %copy-done.3, bf16[64,128]{1,0:T(8,128)(2,1)S(1)} %bitcast.45), custom_call_target="tpu_custom_call" | custom-call | flops 4194304 | bytes 475264 | tf_op jit(solution)/shard_map/pallas_call | solution.py:27
  58.6 7.8 %all-to-all-done.2 = bf16[32,32,128]{2,1,0:T(8,128)(2,1)S(1)} async-done(((bf16[32,32,128]{2,1,0:T(8,128)(2,1)}), bf16[32,32,128]{2,1,0:T(8,128)(2,1)S(1)}, u32[]{:S(2)}, u32[]{:S(2)}) %all-to-all-start.2) | async-done | bytes 262176 | tf_op jit(solution)/shard_map/all_to_all | solution.py:53
  66.4 1.1 %shard_map.109 = (f32[27,64,64]{2,1,0:T(8,128)}, f32[64,128]{1,0:T(8,128)}) custom-call(bf16[1024,128]{1,0:T(8,128)(2,1)S(1)} %bitcast.34), custom_call_target="tpu_custom_call" | custom-call | flops 1000 | bytes 737280 | tf_op jit(solution)/shard_map/pallas_call | solution.py:27
  (3 shorter events, 0.0 us)
Async XLA Ops:
  0.6 13.6 %copy-start.4 = (bf16[27,64,64]{2,1,0:T(8,128)(2,1)S(1)}, bf16[27,64,64]{2,1,0:T(8,128)(2,1)}, u32[]{:S(2)}) copy-start(bf16[27,64,64]{2,1,0:T(8,128)(2,1)} %param.12) | copy-start | bytes 663556
  0.6 20.2 %collective-permute-start = (bf16[64,1,16,256]{3,2,0,1:T(8,128)(2,1)}, bf16[64,1,16,256]{3,2,0,1:T(8,128)(2,1)S(1)}, u32[]{:S(2)}, u32[]{:S(2)}) collective-permute-start(bf16[64,1,16,256]{3,2,0,1:T(8,128)(2,1)} %bitcast.35), channel_id=1, source_target_pairs={{0,4},{1,5},{2,6},{3,7},{4,8},{5,9},{6,10},{7,11},{8,12},{9,13},{1... | collective-permute-start | bytes 1572872 | tf_op jit(solution)/shard_map/ppermute | solution.py:48
  1.1 19.7 %collective-permute-start.1 = (bf16[64,1,16,256]{3,2,0,1:T(8,128)(2,1)}, bf16[64,1,16,256]{3,2,0,1:T(8,128)(2,1)S(1)}, u32[]{:S(2)}, u32[]{:S(2)}) collective-permute-start(bf16[64,1,16,256]{3,2,0,1:T(8,128)(2,1)} %bitcast.36), channel_id=1, source_target_pairs={{0,28},{1,29},{2,30},{3,31},{4,0},{5,1},{6,2},{7,3},{8,4},{9,5},{1... | collective-permute-start | bytes 1572872 | tf_op jit(solution)/shard_map/ppermute | solution.py:48
  5.8 5.7 %copy-start.2 = (s32[1,256]{1,0:T(1,128)S(1)}, s32[1,256]{1,0:T(1,128)}, u32[]{:S(2)}) copy-start(s32[1,256]{1,0:T(1,128)} %own_cells.5) | copy-start | bytes 3076
  5.8 15.0 %all-to-all-start = ((bf16[32,24,128]{2,1,0:T(8,128)(2,1)}), bf16[32,24,128]{2,1,0:T(8,128)(2,1)S(1)}, u32[]{:S(2)}, u32[]{:S(2)}) async-start(bf16[32,24,128]{2,1,0:T(8,128)(2,1)} %bitcast.50), calls=%async_computation | async-start | bytes 393216 | tf_op jit(solution)/shard_map/all_to_all | solution.py:53
  11.5 6.4 %collective-permute-start.2 = (s32[1,256]{1,0:T(1,128)S(1)}, s32[1,256]{1,0:T(1,128)S(1)}, u32[]{:S(2)}, u32[]{:S(2)}) collective-permute-start(s32[1,256]{1,0:T(1,128)S(1)} %copy-done.2), channel_id=1, source_target_pairs={{0,4},{1,5},{2,6},{3,7},{4,8},{5,9},{6,10},{7,11},{8,12},{9,13},{1... | collective-permute-start | bytes 3080 | tf_op jit(solution)/shard_map/ppermute | solution.py:48
  11.8 6.1 %collective-permute-start.3 = (s32[1,256]{1,0:T(1,128)S(1)}, s32[1,256]{1,0:T(1,128)S(1)}, u32[]{:S(2)}, u32[]{:S(2)}) collective-permute-start(s32[1,256]{1,0:T(1,128)S(1)} %copy-done.2), channel_id=1, source_target_pairs={{0,28},{1,29},{2,30},{3,31},{4,0},{5,1},{6,2},{7,3},{8,4},{9,5},{1... | collective-permute-start | bytes 3080 | tf_op jit(solution)/shard_map/ppermute | solution.py:48
  16.6 4.2 %copy-start = (bf16[64,1,16,256]{3,2,1,0:T(8,128)(2,1)S(1)}, bf16[64,1,16,256]{3,2,1,0:T(8,128)(2,1)}, u32[]{:S(2)}) copy-start(bf16[64,1,16,256]{3,2,1,0:T(8,128)(2,1)} %param.10) | copy-start | bytes 1572868
  16.7 4.2 %copy-start.1 = (bf16[128,64]{0,1:T(8,128)(2,1)S(1)}, bf16[128,64]{0,1:T(8,128)(2,1)}, u32[]{:S(2)}) copy-start(bf16[128,64]{0,1:T(8,128)(2,1)} %param.11) | copy-start | bytes 49156
  21.5 13.6 %collective-permute-start.4 = (bf16[448,256]{1,0:T(8,128)(2,1)S(1)}, bf16[448,256]{1,0:T(8,128)(2,1)S(1)}, u32[]{:S(2)}, u32[]{:S(2)}) collective-permute-start(bf16[448,256]{1,0:T(8,128)(2,1)S(1)} %get-tuple-element.19.last_ref), channel_id=1, source_target_pairs={{0,1},{1,2},{2,3},{3,0},{4,5},{5,6},{6,7},{7,4},{8,9},{9,10},{10,1... | collective-permute-start | bytes 688136 | tf_op jit(solution)/shard_map/ppermute | solution.py:48
  21.7 13.3 %collective-permute-start.5 = (bf16[448,256]{1,0:T(8,128)(2,1)S(1)}, bf16[448,256]{1,0:T(8,128)(2,1)S(1)}, u32[]{:S(2)}, u32[]{:S(2)}) collective-permute-start(bf16[448,256]{1,0:T(8,128)(2,1)S(1)} %get-tuple-element.20.first_ref), channel_id=1, source_target_pairs={{0,3},{1,0},{2,1},{3,2},{4,7},{5,4},{6,5},{7,6},{8,11},{9,8},{10,9... | collective-permute-start | bytes 688136 | tf_op jit(solution)/shard_map/ppermute | solution.py:48
  37.1 14.4 %all-to-all-start.1 = ((bf16[32,48,128]{2,1,0:T(8,128)(2,1)}), bf16[32,48,128]{2,1,0:T(8,128)(2,1)S(1)}, u32[]{:S(2)}, u32[]{:S(2)}) async-start(bf16[32,48,128]{2,1,0:T(8,128)(2,1)} %shard_map.106), calls=%async_computation.1 | async-start | bytes 786432 | tf_op jit(solution)/shard_map/all_to_all | solution.py:53
  52.4 14.0 %all-to-all-start.2 = ((bf16[32,32,128]{2,1,0:T(8,128)(2,1)}), bf16[32,32,128]{2,1,0:T(8,128)(2,1)S(1)}, u32[]{:S(2)}, u32[]{:S(2)}) async-start(bf16[32,32,128]{2,1,0:T(8,128)(2,1)} %shard_map.108), calls=%async_computation.2 | async-start | bytes 524288 | tf_op jit(solution)/shard_map/all_to_all | solution.py:53
  56.3 1.1 %copy-start.3 = (s32[1,32]{1,0:T(1,128)S(1)}, s32[1,32]{1,0:T(1,128)}, u32[]{:S(2)}) copy-start(s32[1,32]{1,0:T(1,128)} %counts_ref.1) | copy-start | bytes 388

commit v7 on v6

--- a/solution.py
+++ b/solution.py
@@ -87,10 +87,13 @@
     ).astype(BF16)
 
 
-def finish_row(acc, field, cot):
-    chans, nz = field.shape
-    pre = acc[chans : 2 * chans]
-    pre = pre + pltpu.roll(acc[:chans], 1, 1) + pltpu.roll(acc[2 * chans :], nz - 1, 1)
+def over_depth(acc):
+    chans, nz = acc.shape[0] // 3, acc.shape[1]
+    total = acc[chans : 2 * chans] + pltpu.roll(acc[:chans], 1, 1)
+    return total + pltpu.roll(acc[2 * chans :], nz - 1, 1)
+
+
+def finish_row(pre, field, cot):
     sig = jax.nn.sigmoid(pre)
     out = field.astype(F32) + pre * sig
     grad = cot.astype(F32) * sig * (1.0 + pre * (1.0 - sig))
@@ -120,12 +123,11 @@
     nrows, feats = rows_ref.shape
     slots = ndev * cap
     counts = counts_ref[...].astype(F32)
-    slot = lax.broadcasted_iota(I32, (slots, ndev), 0)
+    owner = lax.broadcasted_iota(I32, (ndev, cap, ndev), 0).reshape(slots, ndev)
     lane = lax.broadcasted_iota(I32, (slots, ndev), 1)
-    owner = slot // cap
     start = jnp.sum(jnp.where(lane < owner, counts, 0.0), axis=1, keepdims=True)
     held = jnp.sum(jnp.where(lane == owner, counts, 0.0), axis=1, keepdims=True)
-    place = (lax.broadcasted_iota(I32, (slots, nrows), 0) % cap).astype(F32)
+    place = lax.broadcasted_iota(I32, (ndev, cap, nrows), 1).reshape(slots, nrows).astype(F32)
     row = lax.broadcasted_iota(I32, (slots, nrows), 1).astype(F32)
     onehot = jnp.where((row == place + start) & (place < held), 1.0, 0.0).astype(BF16)
     raw = mm(onehot, rows_ref[...]).reshape(ngx, ngy, cap, feats)
@@ -143,9 +145,10 @@
 
 def outer_kernel(
     ndev, cap, recv_ref, own_ref, west_ref, east_ref, own_cells, west_cells, east_cells,
-    proj_t_ref, cot_ref, first_ref, last_ref, masked,
+    proj_t_ref, cot_ref, wf_ref, first_ref, last_ref, field_ref, masked,
 ):
     chans, cy, nz = own_ref.shape
+    rows = 3 * chans
     raws = rows_in(recv_ref, ndev, cap)
     ns = (0, 1, cy - 2, cy - 1)
     planes = ((west_ref, west_cells), (own_ref, own_cells), (east_ref, east_cells))
@@ -155,11 +158,17 @@
         base = turned(ref)
         for n, row in enumerate(ns):
             part = painted[n * chans : (n + 1) * chans]
-            field = (base[row] + part).astype(BF16)
-            target = first_ref if n < 2 else last_ref
-            target[pl.ds((3 * (n % 2) + dx) * chans, chans)] = field
-    first_ref[pl.ds(6 * chans, chans)] = cot_ref[0]
-    last_ref[pl.ds(6 * chans, chans)] = cot_ref[cy - 1]
+            field_ref[n, pl.ds(dx * chans, chans)] = (base[row] + part).astype(BF16)
+    near = mm(wf_ref[pl.ds(0, 2 * rows)], field_ref[3])
+    far = mm(wf_ref[pl.ds(0, rows)], field_ref[2])
+    last_ref[pl.ds(0, chans)] = over_depth(near[:rows]).astype(BF16)
+    last_ref[pl.ds(chans, chans)] = over_depth(near[rows:] + far).astype(BF16)
+    last_ref[pl.ds(2 * chans, chans)] = cot_ref[cy - 1]
+    near = mm(wf_ref[pl.ds(rows, 2 * rows)], field_ref[0])
+    far = mm(wf_ref[pl.ds(2 * rows, rows)], field_ref[1])
+    first_ref[pl.ds(0, chans)] = over_depth(near[rows:]).astype(BF16)
+    first_ref[pl.ds(chans, chans)] = over_depth(near[:rows] + far).astype(BF16)
+    first_ref[pl.ds(2 * chans, chans)] = cot_ref[0]
 
 
 def place(cells_ref, nz):
@@ -200,20 +209,20 @@
         acc[n] += terms[rows : 2 * rows]
         return terms[2 * rows :]
 
-    pre_ref[0] = spread(0)
-    pre_ref[1] = acc[0] + spread(1)
-
-    def forward(n, carry):
+    pre_ref[0] = over_depth(spread(0))
+    pre_ref[1] = over_depth(acc[0] + spread(1))
+
+    def forward(n):
         done = spread(n) + acc[n - 1]
         y = n - 1
-        out, grad = finish_row(done, x_ref[y, own], cot_ref[y])
+        out, grad = finish_row(over_depth(done), x_ref[y, own], cot_ref[y])
         out_ref[y] = out
         grads[y + 1] = stacked(grad)
-        return carry
-
-    lax.fori_loop(2, cy, forward, 0, unroll=2)
-    pre_ref[2] = acc[cy - 1]
-    pre_ref[3] = acc[cy]
+
+    for n in range(2, cy):
+        forward(n)
+    pre_ref[2] = over_depth(acc[cy - 1])
+    pre_ref[3] = over_depth(acc[cy])
     total_ref[...] = jnp.zeros_like(total_ref)
     back[0] = jnp.zeros((rows, nz), F32)
     back[1] = jnp.zeros((rows, nz), F32)
@@ -228,7 +237,7 @@
         back[n] += terms[rows : 2 * rows]
         return terms[:rows]
 
-    def backward(n, carry):
+    def backward(n):
         taps(n)
         value = spread_back(n) + back[n - 1]
         for dx in range(3):
@@ -236,14 +245,14 @@
             if dx == 1:
                 part = part + cot_ref[n - 1].astype(F32)
             plane[dx, pl.ds((n - 3) * chans, chans)] = part.astype(BF16)
-        return carry
 
     taps(0)
     taps(1)
     slot_ref[0] = spread_back(1)
     taps(2)
     slot_ref[1] = spread_back(2) + back[1]
-    lax.fori_loop(3, cy - 1, backward, 0, unroll=2)
+    for n in range(3, cy - 1):
+        backward(n)
     taps(cy - 1)
     slot_ref[2] = back[cy - 2]
     slot_ref[3] = back[cy - 1]
@@ -263,26 +272,26 @@
 
 def edge_kernel(
     ndev, cap,
-    pre_ref, slot_ref, sums_ref, total_ref, north_ref, south_ref, first_ref, last_ref,
-    wf_ref, wb_ref, cot_ref, own_cells, west_cells, east_cells, recv_ref,
+    pre_ref, slot_ref, sums_ref, total_ref, north_ref, south_ref, field_ref, wb_ref, cot_ref,
+    own_cells, west_cells, east_cells, recv_ref,
     out_ref, send_far, total, sums_send, slots_send, sems,
 ):
     cy, chans, nz = cot_ref.shape
     rows = 3 * chans
-    own = slice(chans, 2 * chans)
-    fields = [ref[pl.ds(n * rows, rows)] for ref in (north_ref, first_ref, last_ref, south_ref) for n in (0, 1)]
-    cots = [ref[pl.ds(2 * rows, chans)] for ref in (north_ref, first_ref, last_ref, south_ref)]
-    near = mm(wf_ref[pl.ds(0, 2 * rows)], fields[1])
-    pre = [pre_ref[0] + near[rows:] + mm(wf_ref[pl.ds(0, rows)], fields[0]), pre_ref[1] + near[:rows]]
-    near = mm(wf_ref[pl.ds(rows, 2 * rows)], fields[6])
-    pre += [pre_ref[2] + near[rows:], pre_ref[3] + near[:rows] + mm(wf_ref[pl.ds(2 * rows, rows)], fields[7])]
-    at = (1, 2, 5, 6)
-    ends = [finish_row(pre[n], fields[at[n]][own], cots[n]) for n in range(4)]
+    own = pl.ds(chans, chans)
+    cots = (north_ref[pl.ds(2 * chans, chans)], cot_ref[0], cot_ref[cy - 1], south_ref[pl.ds(2 * chans, chans)])
+    added = [ref[pl.ds(n * chans, chans)].astype(F32) for ref, n in ((north_ref, 1), (north_ref, 0), (south_ref, 0), (south_ref, 1))]
+    ends = [
+        finish_row(pre_ref[n] + added[n], field_ref[0 if n < 2 else 3, own], cots[n]) for n in range(4)
+    ]
     out_ref[0], out_ref[1] = ends[1][0], ends[2][0]
     grads = [stacked(grad) for _, grad in ends]
-    for n in range(3):
-        here = pl.ds(n * rows, rows)
-        total[here] = total_ref[here] + (mm(grads[1], fields[3 - n], NT) + mm(grads[2], fields[6 - n], NT))
+    top = mm(jnp.concatenate([grads[0], grads[1]], axis=0), field_ref[0], NT)
+    bottom = mm(jnp.concatenate([grads[2], grads[3]], axis=0), field_ref[3], NT)
+    here = [pl.ds(n * rows, rows) for n in range(3)]
+    total[here[0]] = total_ref[here[0]] + (top[:rows] + mm(grads[1], field_ref[1], NT))
+    total[here[1]] = total_ref[here[1]] + (top[rows:] + bottom[:rows])
+    total[here[2]] = total_ref[here[2]] + (bottom[rows:] + mm(grads[2], field_ref[2], NT))
     width = send_far.shape[2]
     share = send_far.shape[1] - 2 * cap
     half = 3 * rows // 2
@@ -438,10 +447,10 @@
     wf = taps.transpose(1, 2, 3, 0, 4).reshape(9 * chans, rows)
     wb = taps.transpose(1, 0, 4, 2, 3).reshape(9 * chans, rows)
 
-    first, last = call(
+    first, last, outer = call(
         functools.partial(outer_kernel, ndev, cap),
-        [shape((2 * rows + chans, nz), BF16)] * 2,
-        (recv, *planes, *lists, proj_t, cot),
+        [shape((rows, nz), BF16)] * 2 + [shape((4, rows, nz), BF16)],
+        (recv, *planes, *lists, proj_t, cot, wf),
         2 * slots * count * chans,
         (pltpu.VMEM((4 * chans, slots), BF16),),
     )
@@ -451,7 +460,7 @@
         [
             shape((cy, chans, nz), BF16),
             shape((9 * chans, rows), F32),
-            shape((4, rows, nz), F32),
+            shape((4, chans, nz), F32),
             shape((4, rows, nz), F32),
             shape((3, chans, slots), F32),
         ],
@@ -472,8 +481,7 @@
         functools.partial(edge_kernel, ndev, cap),
         [shape((2, chans, nz), BF16), shape((ndev, share + 2 * cap, feats), BF16)],
         (
-            pre_edge, slot_edge, sums, total, north, south, first, last,
-            wf, wb, cot, *lists, recv,
+            pre_edge, slot_edge, sums, total, north, south, outer, wb, cot, *lists, recv,
         ),
         12 * one,
         (

time: 67.9 us -> 63.8 us (0.940)
  Pallas kernels: 17.1 us -> 13 us
    pallas_call x8, Pallas kernels: 17.1 us -> 13 us  [call(): pl.pallas_call(kernel, out_shape=[jax.ShapeDtypeStruct(o.shape, o.dtype)...]
    unnamed x12 -> x14, local copies, waits for them, and re-layouts: 2.37 us -> 2.14 us
  transfers between devices with their start and end apart: 9 -> 9, of which waited for: 3 -> 3; matrix products, arithmetic and copies ran while one was open for 7% -> 6% of each run, Pallas kernels for 19% -> 13%
where the time goes in v7:
time: 63.8 us; the launch traced here: 63.3 us
  waiting for transfers between devices  22.8 us (36%)
  starting transfers between devices  22.1 us (35%)
  Pallas kernels  13 us (20%)
  local copies, waits for them, and re-layouts  4.58 us (7%)
  between operations  0.86 us (1%)
    all_to_all x3, waiting for transfers between devices, exchange(): lax.all_to_all(payload.reshape(ndev, rows // ndev, width), AXES, split_ax...  22.7 us
    pallas_call x8, Pallas kernels, call(): pl.pallas_call(kernel, out_shape=[jax.ShapeDtypeStruct(o.shape, o.dtype)...  13 us
    all_to_all x3, starting transfers between devices, exchange(): lax.all_to_all(payload.reshape(ndev, rows // ndev, width), AXES, split_ax...  12.1 us
    ppermute x6, starting transfers between devices, send(): return lax.ppermute(block, AXES, pairs)  10 us
    unnamed x14, local copies, waits for them, and re-layouts  2.14 us
    reshape x2, local copies, waits for them, and re-layouts, local(): taps = conv_weight.reshape(3, 3, 3, chans, chans)  1.3 us
  transfers between devices with their start and end apart: 9, of which 3 were waited for; matrix products, arithmetic and copies ran while one was open for 6% of the time, Pallas kernels for 13%

profile of v7, /device:TPU:0, one launch (start us, length us, event | category | flops | bytes accessed | tf_op | source)
XLA Modules:
  0.0 63.3 jit_solution(13574819328201753927)
XLA Ops:
  0.6 0.0 copy-start.4
  0.6 0.5 collective-permute-start
  1.1 2.9 %collective-permute-start.1 = (bf16[64,1,16,256]{3,2,0,1:T(8,128)(2,1)}, bf16[64,1,16,256]{3,2,0,1:T(8,128)(2,1)S(1)}, u32[]{:S(2)}, u32[]{:S(2)}) collective-permute-start(bf16[64,1,16,256]{3,2,0,1:T(8,128)(2,1)} %bitcast.36), channel_id=1, source_target_pairs={{0,28},{1,29},{2,30},{3,31},{4,0},{5,1},{6,2},{7,3},{8,4},{9,5},{1... | collective-permute-start | bytes 1572872 | tf_op jit(solution)/shard_map/ppermute | solution.py:48
  4.1 1.7 %shard_map.102 = bf16[768,128]{1,0:T(8,128)(2,1)} custom-call(bf16[128,128]{1,0:T(8,128)(2,1)} %rows_far.1, s32[1,32]{1,0:T(1,128)} %counts_ref.1), custom_call_target="tpu_custom_call" | custom-call | flops 8388608 | bytes 229504 | tf_op jit(solution)/shard_map/pallas_call | solution.py:27
  5.8 0.0 copy-start.2
  5.8 5.6 %all-to-all-start = ((bf16[32,24,128]{2,1,0:T(8,128)(2,1)}), bf16[32,24,128]{2,1,0:T(8,128)(2,1)S(1)}, u32[]{:S(2)}, u32[]{:S(2)}) async-start(bf16[32,24,128]{2,1,0:T(8,128)(2,1)} %bitcast.50), calls=%async_computation | async-start | bytes 393216 | tf_op jit(solution)/shard_map/all_to_all | solution.py:53
  11.5 0.0 copy-done.2
  11.5 0.3 collective-permute-start.2
  11.8 2.4 %collective-permute-start.3 = (s32[1,256]{1,0:T(1,128)S(1)}, s32[1,256]{1,0:T(1,128)S(1)}, u32[]{:S(2)}, u32[]{:S(2)}) collective-permute-start(s32[1,256]{1,0:T(1,128)S(1)} %copy-done.2), channel_id=1, source_target_pairs={{0,28},{1,29},{2,30},{3,31},{4,0},{5,1},{6,2},{7,3},{8,4},{9,5},{1... | collective-permute-start | bytes 3080 | tf_op jit(solution)/shard_map/ppermute | solution.py:48
  14.2 0.0 copy-done.4
  14.2 0.9 %copy.19 = bf16[3,3,3,64,64]{3,2,1,4,0:T(4,128)(2,1)S(1)} copy(bf16[3,3,3,64,64]{4,3,2,1,0:T(8,128)(2,1)S(1)} %bitcast.48) | data formatting | bytes 442368 | tf_op jit(solution)/shard_map/reshape | solution.py:446
  15.1 0.4 copy.30
  15.5 0.4 reshape.41
  15.9 0.2 copy.23.wf_ref
  16.1 0.4 reshape.42
  16.5 0.0 copy-start.5
  16.5 0.2 copy.24.wb_ref
  16.7 0.9 %copy-done.5 = bf16[64,1,16,256]{3,2,1,0:T(8,128)(2,1)S(1)} copy-done((bf16[64,1,16,256]{3,2,1,0:T(8,128)(2,1)S(1)}, bf16[64,1,16,256]{3,2,1,0:T(8,128)(2,1)}, u32[]{:S(2)}) %copy-start.5) | copy-done | bytes 524312
  17.5 0.0 copy-start
  17.5 0.0 copy-start.1
  17.5 0.2 copy.31
  17.7 0.0 collective-permute-done.2.west_cells
  17.7 0.0 collective-permute-done.3.east_cells
  17.7 3.1 %all-to-all-done = bf16[32,24,128]{2,1,0:T(8,128)(2,1)S(1)} async-done(((bf16[32,24,128]{2,1,0:T(8,128)(2,1)}), bf16[32,24,128]{2,1,0:T(8,128)(2,1)S(1)}, u32[]{:S(2)}, u32[]{:S(2)}) %all-to-all-start) | async-done | bytes 196640 | tf_op jit(solution)/shard_map/all_to_all | solution.py:53
  20.8 0.0 collective-permute-done
  20.8 0.0 collective-permute-done.1
  20.8 0.0 copy-done
  20.8 0.0 copy-done.1
  20.8 1.0 %shard_map.104 = (bf16[192,256]{1,0:T(8,128)(2,1)S(1)}, bf16[192,256]{1,0:T(8,128)(2,1)S(1)}, bf16[4,192,256]{2,1,0:T(8,128)(2,1)S(1)}) custom-call(bf16[768,128]{1,0:T(8,128)(2,1)S(1)} %bitcast.31, bf16[64,16,256]{2,1,0:T(8,128)(2,1)S(1)} %bitcast.37, bf16[64,16,256]{2,1,0:T(8,128)(2,1)S(1)} %bitcast.39, bf16[64,16,256]{2,1,0:T(8,128)(2,1)S(1)} %bitcast.41, ...), custom_call_target="tpu_custom_call" | custom-call | flops 134217728 | bytes 3124224 | tf_op jit(solution)/shard_map/pallas_call | solution.py:27
  21.8 0.3 collective-permute-start.4
  22.1 3.6 %collective-permute-start.5 = (bf16[192,256]{1,0:T(8,128)(2,1)S(1)}, bf16[192,256]{1,0:T(8,128)(2,1)S(1)}, u32[]{:S(2)}, u32[]{:S(2)}) collective-permute-start(bf16[192,256]{1,0:T(8,128)(2,1)S(1)} %get-tuple-element.21), channel_id=1, source_target_pairs={{0,3},{1,0},{2,1},{3,2},{4,7},{5,4},{6,5},{7,6},{8,11},{9,8},{10,9... | collective-permute-start | bytes 294920 | tf_op jit(solution)/shard_map/ppermute | solution.py:48
  25.7 5.6 %shard_map.103 = (bf16[16,64,256]{2,1,0:T(8,128)(2,1)S(1)}, f32[576,192]{1,0:T(8,128)S(1)}, f32[4,64,256]{2,1,0:T(8,128)S(1)}, f32[4,192,256]{2,1,0:T(8,128)S(1)}, f32[3,64,256]{2,1,0:T(8,128)S(1)}) custom-call(bf16[768,128]{1,0:T(8,128)(2,1)S(1)} %bitcast.32, bf16[64,128]{1,0:T(8,128)(2,1)S(1)} %bitcast.44, bf16[16,64,256]{2,1,0:T(8,128)(2,1)S(1)} %bitcast.29, ...), custom_call_target="tpu_custom_call" | custom-call | flops 2717908992 | bytes 4967424 | tf_op jit(solution)/shard_map/pallas_call | solution.py:27
  31.3 0.0 collective-permute-done.4.north_ref
  31.4 0.0 collective-permute-done.5.south_ref
  31.4 1.6 %shard_map.105 = (bf16[2,64,256]{2,1,0:T(8,128)(2,1)S(1)}, bf16[32,48,128]{2,1,0:T(8,128)(2,1)}) custom-call(f32[4,64,256]{2,1,0:T(8,128)S(1)} %get-tuple-element.16.pre_ref, f32[4,192,256]{2,1,0:T(8,128)S(1)} %get-tuple-element.17.slot_ref, f32[3,64,256]{2,1,0:T(8,128)S(1)} %get-tuple-element.18.sums_ref, f32[576,192]{1,0:T(8,128)S(1)} %get-tuple-element.19.total_ref, ...), custom_call_target="tpu_custom_call" | custom-call | flops 226492416 | bytes 3681280 | tf_op jit(solution)/shard_map/pallas_call | solution.py:27
  33.0 2.6 %all-to-all-start.1 = ((bf16[32,48,128]{2,1,0:T(8,128)(2,1)}), bf16[32,48,128]{2,1,0:T(8,128)(2,1)S(1)}, u32[]{:S(2)}, u32[]{:S(2)}) async-start(bf16[32,48,128]{2,1,0:T(8,128)(2,1)} %shard_map.106), calls=%async_computation.1 | async-start | bytes 786432 | tf_op jit(solution)/shard_map/all_to_all | solution.py:53
  35.6 11.8 %all-to-all-done.1.recv_ref = bf16[32,48,128]{2,1,0:T(8,128)(2,1)S(1)} async-done(((bf16[32,48,128]{2,1,0:T(8,128)(2,1)}), bf16[32,48,128]{2,1,0:T(8,128)(2,1)S(1)}, u32[]{:S(2)}, u32[]{:S(2)}) %all-to-all-start.1) | async-done | bytes 393248 | tf_op jit(solution)/shard_map/all_to_all | solution.py:53
  47.4 0.8 %shard_map.108 = bf16[32,32,128]{2,1,0:T(8,128)(2,1)} custom-call(bf16[32,48,128]{2,1,0:T(8,128)(2,1)S(1)} %all-to-all-done.1.recv_ref, s32[1,1]{1,0:T(1,128)} %bitcast.15.index_ref), custom_call_target="tpu_custom_call" | custom-call | flops 1000 | bytes 655364 | tf_op jit(solution)/shard_map/pallas_call | solution.py:27
  48.2 3.8 %all-to-all-start.2 = ((bf16[32,32,128]{2,1,0:T(8,128)(2,1)}), bf16[32,32,128]{2,1,0:T(8,128)(2,1)S(1)}, u32[]{:S(2)}, u32[]{:S(2)}) async-start(bf16[32,32,128]{2,1,0:T(8,128)(2,1)} %shard_map.108), calls=%async_computation.2 | async-start | bytes 524288 | tf_op jit(solution)/shard_map/all_to_all | solution.py:53
  52.1 0.1 maximum_bitcast_fusion
  52.2 0.0 copy-start.3
  52.2 1.1 %copy.27 = bf16[64,1,16,256]{3,2,1,0:T(8,128)(2,1)} copy(bf16[64,1,16,256]{3,0,2,1:T(8,128)(2,1)S(1)} %maximum_bitcast_fusion) | data formatting | bytes 1048576
  53.3 0.0 copy-done.3
  53.3 1.1 %shard_map.107 = f32[128,128]{1,0:T(8,128)} custom-call(bf16[32,48,128]{2,1,0:T(8,128)(2,1)S(1)} %all-to-all-done.1.recv_ref, s32[1,32]{1,0:T(1,128)S(1)} %copy-done.3, bf16[64,128]{1,0:T(8,128)(2,1)S(1)} %bitcast.45), custom_call_target="tpu_custom_call" | custom-call | flops 4194304 | bytes 475264 | tf_op jit(solution)/shard_map/pallas_call | solution.py:27
  54.4 7.8 %all-to-all-done.2 = bf16[32,32,128]{2,1,0:T(8,128)(2,1)S(1)} async-done(((bf16[32,32,128]{2,1,0:T(8,128)(2,1)}), bf16[32,32,128]{2,1,0:T(8,128)(2,1)S(1)}, u32[]{:S(2)}, u32[]{:S(2)}) %all-to-all-start.2) | async-done | bytes 262176 | tf_op jit(solution)/shard_map/all_to_all | solution.py:53
  62.3 1.1 %shard_map.109 = (f32[27,64,64]{2,1,0:T(8,128)}, f32[64,128]{1,0:T(8,128)}) custom-call(bf16[1024,128]{1,0:T(8,128)(2,1)S(1)} %bitcast.34), custom_call_target="tpu_custom_call" | custom-call | flops 1000 | bytes 737280 | tf_op jit(solution)/shard_map/pallas_call | solution.py:27
  (3 shorter events, 0.0 us)
Async XLA Ops:
  0.6 13.6 %copy-start.4 = (bf16[27,64,64]{2,1,0:T(8,128)(2,1)S(1)}, bf16[27,64,64]{2,1,0:T(8,128)(2,1)}, u32[]{:S(2)}) copy-start(bf16[27,64,64]{2,1,0:T(8,128)(2,1)} %param.12) | copy-start | bytes 663556
  0.6 20.2 %collective-permute-start = (bf16[64,1,16,256]{3,2,0,1:T(8,128)(2,1)}, bf16[64,1,16,256]{3,2,0,1:T(8,128)(2,1)S(1)}, u32[]{:S(2)}, u32[]{:S(2)}) collective-permute-start(bf16[64,1,16,256]{3,2,0,1:T(8,128)(2,1)} %bitcast.35), channel_id=1, source_target_pairs={{0,4},{1,5},{2,6},{3,7},{4,8},{5,9},{6,10},{7,11},{8,12},{9,13},{1... | collective-permute-start | bytes 1572872 | tf_op jit(solution)/shard_map/ppermute | solution.py:48
  1.1 19.7 %collective-permute-start.1 = (bf16[64,1,16,256]{3,2,0,1:T(8,128)(2,1)}, bf16[64,1,16,256]{3,2,0,1:T(8,128)(2,1)S(1)}, u32[]{:S(2)}, u32[]{:S(2)}) collective-permute-start(bf16[64,1,16,256]{3,2,0,1:T(8,128)(2,1)} %bitcast.36), channel_id=1, source_target_pairs={{0,28},{1,29},{2,30},{3,31},{4,0},{5,1},{6,2},{7,3},{8,4},{9,5},{1... | collective-permute-start | bytes 1572872 | tf_op jit(solution)/shard_map/ppermute | solution.py:48
  5.8 5.7 %copy-start.2 = (s32[1,256]{1,0:T(1,128)S(1)}, s32[1,256]{1,0:T(1,128)}, u32[]{:S(2)}) copy-start(s32[1,256]{1,0:T(1,128)} %own_cells.5) | copy-start | bytes 3076
  5.8 15.0 %all-to-all-start = ((bf16[32,24,128]{2,1,0:T(8,128)(2,1)}), bf16[32,24,128]{2,1,0:T(8,128)(2,1)S(1)}, u32[]{:S(2)}, u32[]{:S(2)}) async-start(bf16[32,24,128]{2,1,0:T(8,128)(2,1)} %bitcast.50), calls=%async_computation | async-start | bytes 393216 | tf_op jit(solution)/shard_map/all_to_all | solution.py:53
  11.5 6.2 %collective-permute-start.2 = (s32[1,256]{1,0:T(1,128)S(1)}, s32[1,256]{1,0:T(1,128)S(1)}, u32[]{:S(2)}, u32[]{:S(2)}) collective-permute-start(s32[1,256]{1,0:T(1,128)S(1)} %copy-done.2), channel_id=1, source_target_pairs={{0,4},{1,5},{2,6},{3,7},{4,8},{5,9},{6,10},{7,11},{8,12},{9,13},{1... | collective-permute-start | bytes 3080 | tf_op jit(solution)/shard_map/ppermute | solution.py:48
  11.8 5.9 %collective-permute-start.3 = (s32[1,256]{1,0:T(1,128)S(1)}, s32[1,256]{1,0:T(1,128)S(1)}, u32[]{:S(2)}, u32[]{:S(2)}) collective-permute-start(s32[1,256]{1,0:T(1,128)S(1)} %copy-done.2), channel_id=1, source_target_pairs={{0,28},{1,29},{2,30},{3,31},{4,0},{5,1},{6,2},{7,3},{8,4},{9,5},{1... | collective-permute-start | bytes 3080 | tf_op jit(solution)/shard_map/ppermute | solution.py:48
  16.5 1.0 %copy-start.5 = (bf16[64,1,16,256]{3,2,1,0:T(8,128)(2,1)S(1)}, bf16[64,1,16,256]{3,2,1,0:T(8,128)(2,1)}, u32[]{:S(2)}) copy-start(bf16[64,1,16,256]{3,2,1,0:T(8,128)(2,1)} %param.13) | copy-start | bytes 1572868
  17.5 3.3 %copy-start = (bf16[64,1,16,256]{3,2,1,0:T(8,128)(2,1)S(1)}, bf16[64,1,16,256]{3,2,1,0:T(8,128)(2,1)}, u32[]{:S(2)}) copy-start(bf16[64,1,16,256]{3,2,1,0:T(8,128)(2,1)} %param.10) | copy-start | bytes 1572868
  17.5 3.3 %copy-start.1 = (bf16[128,64]{0,1:T(8,128)(2,1)S(1)}, bf16[128,64]{0,1:T(8,128)(2,1)}, u32[]{:S(2)}) copy-start(bf16[128,64]{0,1:T(8,128)(2,1)} %param.11) | copy-start | bytes 49156
  21.8 9.5 %collective-permute-start.4 = (bf16[192,256]{1,0:T(8,128)(2,1)S(1)}, bf16[192,256]{1,0:T(8,128)(2,1)S(1)}, u32[]{:S(2)}, u32[]{:S(2)}) collective-permute-start(bf16[192,256]{1,0:T(8,128)(2,1)S(1)} %get-tuple-element.20), channel_id=1, source_target_pairs={{0,1},{1,2},{2,3},{3,0},{4,5},{5,6},{6,7},{7,4},{8,9},{9,10},{10,1... | collective-permute-start | bytes 294920 | tf_op jit(solution)/shard_map/ppermute | solution.py:48
  22.1 9.3 %collective-permute-start.5 = (bf16[192,256]{1,0:T(8,128)(2,1)S(1)}, bf16[192,256]{1,0:T(8,128)(2,1)S(1)}, u32[]{:S(2)}, u32[]{:S(2)}) collective-permute-start(bf16[192,256]{1,0:T(8,128)(2,1)S(1)} %get-tuple-element.21), channel_id=1, source_target_pairs={{0,3},{1,0},{2,1},{3,2},{4,7},{5,4},{6,5},{7,6},{8,11},{9,8},{10,9... | collective-permute-start | bytes 294920 | tf_op jit(solution)/shard_map/ppermute | solution.py:48
  33.0 14.4 %all-to-all-start.1 = ((bf16[32,48,128]{2,1,0:T(8,128)(2,1)}), bf16[32,48,128]{2,1,0:T(8,128)(2,1)S(1)}, u32[]{:S(2)}, u32[]{:S(2)}) async-start(bf16[32,48,128]{2,1,0:T(8,128)(2,1)} %shard_map.106), calls=%async_computation.1 | async-start | bytes 786432 | tf_op jit(solution)/shard_map/all_to_all | solution.py:53
  48.2 14.0 %all-to-all-start.2 = ((bf16[32,32,128]{2,1,0:T(8,128)(2,1)}), bf16[32,32,128]{2,1,0:T(8,128)(2,1)S(1)}, u32[]{:S(2)}, u32[]{:S(2)}) async-start(bf16[32,32,128]{2,1,0:T(8,128)(2,1)} %shard_map.108), calls=%async_computation.2 | async-start | bytes 524288 | tf_op jit(solution)/shard_map/all_to_all | solution.py:53
  52.2 1.1 %copy-start.3 = (s32[1,32]{1,0:T(1,128)S(1)}, s32[1,32]{1,0:T(1,128)}, u32[]{:S(2)}) copy-start(s32[1,32]{1,0:T(1,128)} %counts_ref.1) | copy-start | bytes 388

commit v8 on v7

--- a/solution.py
+++ b/solution.py
@@ -20,14 +20,17 @@
     return lax.dot_general(a, b, dims, preferred_element_type=F32)
 
 
-def call(kernel, outs, args, flops, scratch=(), far=(), far_out=(), aliases=None, limit=LIMIT):
+def call(kernel, outs, args, flops, scratch=(), far=(), far_out=(), aliases=None, limit=LIMIT, scalar=()):
     traffic = sum(math.prod(a.shape) * a.dtype.itemsize for a in (*args, *outs))
     near = pl.BlockSpec(memory_space=pltpu.VMEM)
     there = pl.BlockSpec(memory_space=pltpu.HBM)
     return pl.pallas_call(
         kernel,
         out_shape=[jax.ShapeDtypeStruct(o.shape, o.dtype) for o in outs],
-        in_specs=[there if n in far else near for n in range(len(args))],
+        in_specs=[
+            pl.BlockSpec(memory_space=pltpu.SMEM) if n in scalar else there if n in far else near
+            for n in range(len(args))
+        ],
         out_specs=[there if n in far_out else near for n in range(len(outs))],
         scratch_shapes=list(scratch),
         input_output_aliases=aliases or {},
@@ -46,6 +49,10 @@
         for j in range(ngy):
             pairs.append((i * ngy + j, ((i + di) % ngx) * ngy + (j + dj) % ngy))
     return lax.ppermute(block, AXES, pairs)
+
+
+def swap(block):
+    return lax.ppermute(block, "gx", [(i, i ^ 1) for i in range(lax.axis_size("gx"))])
 
 
 def exchange(payload, ndev):
@@ -271,92 +278,103 @@
 
 
 def edge_kernel(
-    ndev, cap,
-    pre_ref, slot_ref, sums_ref, total_ref, north_ref, south_ref, field_ref, wb_ref, cot_ref,
-    own_cells, west_cells, east_cells, recv_ref,
-    out_ref, send_far, total, sums_send, slots_send, sems,
+    part, parity_ref, pre_ref, total_ref, north_ref, south_ref, field_ref, cot_ref,
+    out_ref, grads_ref, keep_ref, give_ref, total, sums,
 ):
     cy, chans, nz = cot_ref.shape
     rows = 3 * chans
     own = pl.ds(chans, chans)
-    cots = (north_ref[pl.ds(2 * chans, chans)], cot_ref[0], cot_ref[cy - 1], south_ref[pl.ds(2 * chans, chans)])
-    added = [ref[pl.ds(n * chans, chans)].astype(F32) for ref, n in ((north_ref, 1), (north_ref, 0), (south_ref, 0), (south_ref, 1))]
-    ends = [
-        finish_row(pre_ref[n] + added[n], field_ref[0 if n < 2 else 3, own], cots[n]) for n in range(4)
-    ]
+    last = pl.ds(2 * chans, chans)
+    cots = (north_ref[last], cot_ref[0], cot_ref[cy - 1], south_ref[last])
+    sides = ((north_ref, 1), (north_ref, 0), (south_ref, 0), (south_ref, 1))
+    ends = []
+    for n, (ref, at) in enumerate(sides):
+        pre = pre_ref[n] + ref[pl.ds(at * chans, chans)].astype(F32)
+        ends.append(finish_row(pre, field_ref[0 if n < 2 else 3, own], cots[n]))
     out_ref[0], out_ref[1] = ends[1][0], ends[2][0]
     grads = [stacked(grad) for _, grad in ends]
+    for n in range(4):
+        grads_ref[n] = grads[n]
     top = mm(jnp.concatenate([grads[0], grads[1]], axis=0), field_ref[0], NT)
     bottom = mm(jnp.concatenate([grads[2], grads[3]], axis=0), field_ref[3], NT)
     here = [pl.ds(n * rows, rows) for n in range(3)]
     total[here[0]] = total_ref[here[0]] + (top[:rows] + mm(grads[1], field_ref[1], NT))
     total[here[1]] = total_ref[here[1]] + (top[rows:] + bottom[:rows])
     total[here[2]] = total_ref[here[2]] + (bottom[rows:] + mm(grads[2], field_ref[2], NT))
-    width = send_far.shape[2]
-    share = send_far.shape[1] - 2 * cap
+    full, _, width = keep_ref.shape
     half = 3 * rows // 2
-    taps = total[:, 2 * chans :]
-    taps = jnp.concatenate([taps[:half], taps[half:]], axis=1)
-    taps = jnp.concatenate([total[:, : 2 * chans], taps], axis=0)
-    full = taps.shape[0] // share
-    sums_send[pl.ds(0, full)] = taps.reshape(full, share, width).astype(BF16)
-    early = pltpu.make_async_copy(
-        sums_send.at[pl.ds(0, full)], send_far.at[pl.ds(0, full), pl.ds(0, share)], sems.at[0]
-    )
-    early.start()
-    inner = mm(wb_ref[pl.ds(rows, 2 * rows)], grads[1])
-    top = slot_ref[0] + inner[:rows] + mm(wb_ref[pl.ds(2 * rows, rows)], grads[0])
+    split = 3 * rows // (2 * part)
+    sums[pl.ds(0, split)] = total[:, :width].reshape(split, 2, part, width)
+    taps = jnp.concatenate([total[pl.ds(0, half), width:], total[pl.ds(half, half), width:]], axis=1)
+    sums[pl.ds(split, full - split)] = taps.reshape(full - split, 2, part, width)
+    parity = parity_ref[0]
+    keep_ref[...] = sums[:, parity]
+    give_ref[...] = sums[:, 1 - parity]
+
+
+def slots_kernel(
+    ndev, cap, part, full, slot_ref, sums_ref, grads_ref, wb_ref, cot_ref,
+    own_cells, west_cells, east_cells, recv_ref, send_far, slots_send, proj_send, sems,
+):
+    cy, chans, nz = cot_ref.shape
+    rows = 3 * chans
+    inner = mm(wb_ref[pl.ds(rows, 2 * rows)], grads_ref[1])
+    top = slot_ref[0] + inner[:rows] + mm(wb_ref[pl.ds(2 * rows, rows)], grads_ref[0])
     second = slot_ref[1] + inner[rows:]
-    inner = mm(wb_ref[pl.ds(0, 2 * rows)], grads[2])
+    inner = mm(wb_ref[pl.ds(0, 2 * rows)], grads_ref[2])
     third = slot_ref[2] + inner[:rows]
-    bottom = slot_ref[3] + inner[rows:] + mm(wb_ref[pl.ds(0, rows)], grads[3])
+    bottom = slot_ref[3] + inner[rows:] + mm(wb_ref[pl.ds(0, rows)], grads_ref[3])
+    at = (0, 1, cy - 2, cy - 1)
     found = []
     for dx, cells_ref in enumerate((west_cells, own_cells, east_cells)):
         parts = [value[dx * chans : (dx + 1) * chans] for value in (top, second, third, bottom)]
         if dx == 1:
-            inner = (cots[1], cot_ref[1], cot_ref[cy - 2], cots[2])
-            parts = [part + cot.astype(F32) for part, cot in zip(parts, inner)]
-        part = jnp.concatenate(parts, axis=0).astype(BF16)
-        cells = place(cells_ref, nz)
-        found.append(at_slots(part, cells, (0, 1, cy - 2, cy - 1), sums_ref[dx]))
+            parts = [value + cot_ref[n].astype(F32) for value, n in zip(parts, at)]
+        terms = jnp.concatenate(parts, axis=0).astype(BF16)
+        found.append(at_slots(terms, place(cells_ref, nz), at, sums_ref[dx]))
+    sides = jnp.concatenate([found[0], found[2]], axis=0).T
+    middle = jnp.concatenate([found[1], jnp.zeros_like(found[1])], axis=0).T
+    width = send_far.shape[2]
+    back = [sides.reshape(ndev, cap, width), middle.reshape(ndev, cap, width)]
+    slots_send[...] = jnp.concatenate(back, axis=1).astype(BF16)
+    copies = [pltpu.make_async_copy(slots_send, send_far.at[:, pl.ds(part, 2 * cap)], sems.at[0])]
+    copies[0].start()
     raws = rows_in(recv_ref, ndev, cap)
     proj = sum(mm(found[dx].astype(BF16), raws[dx]) for dx in range(3))
-    proj_high = proj.astype(BF16).astype(F32)
-    sides = jnp.concatenate([found[0], found[2]], axis=0).T
-    middle = jnp.concatenate([found[1], jnp.zeros_like(found[1])], axis=0).T
-    halves = [v.reshape(2 * chans // share, share // 2, width) for v in (proj_high, proj - proj_high)]
-    proj = jnp.stack(halves, axis=1).reshape(2 * chans // share * 2, share // 2, width)
     rest = ndev - full
-    pad = jnp.zeros(((rest * 2 - proj.shape[0]), share // 2, width), F32)
-    proj = jnp.concatenate([proj, pad], axis=0).reshape(rest, share, width)
-    sums_send[pl.ds(full, rest)] = proj.astype(BF16)
-    back = [sides.reshape(ndev, cap, width), middle.reshape(ndev, cap, width)]
-    slots_send[...] = jnp.concatenate(back, axis=1).astype(BF16)
-    copies = [
-        pltpu.make_async_copy(
-            sums_send.at[pl.ds(full, rest)], send_far.at[pl.ds(full, rest), pl.ds(0, share)], sems.at[1]
-        ),
-        pltpu.make_async_copy(slots_send, send_far.at[:, pl.ds(share, 2 * cap)], sems.at[2]),
-    ]
-    for copy in copies:
-        copy.start()
-    early.wait()
+    pad = jnp.zeros((rest * part - chans, width), F32)
+    proj = jnp.concatenate([proj, pad], axis=0).reshape(rest, part, width)
+    proj_send[...] = proj.astype(BF16)
+    copies.append(
+        pltpu.make_async_copy(proj_send, send_far.at[pl.ds(full, rest), pl.ds(0, part)], sems.at[1])
+    )
+    copies[1].start()
     for copy in copies:
         copy.wait()
 
 
-def sums_kernel(chans, cap, recv_ref, index_ref, sums_ref):
+def pair_kernel(keep_ref, got_ref, same_far, send_far, sums_send, sem):
+    full, part, _ = keep_ref.shape
+    sums_send[...] = (keep_ref[...] + got_ref[...]).astype(BF16)
+    copy = pltpu.make_async_copy(sums_send, send_far.at[pl.ds(0, full), pl.ds(0, part)], sem)
+    copy.start()
+    copy.wait()
+
+
+def sums_kernel(ngx, ngy, full, cap, recv_ref, index_ref, sums_ref):
     ndev, each, width = recv_ref.shape
-    share = each - 2 * cap
-    sums = jnp.sum(recv_ref[:, pl.ds(0, share)].astype(F32), axis=0)
-    half = share // 2
-    whole = sums[:half] + sums[half:]
+    part = each - 2 * cap
+    terms = recv_ref[:, pl.ds(0, part)].astype(F32).reshape(ngx // 2, 2, ngy, part, width)
+    sums = jnp.sum(terms, axis=(0, 2))
+    whole = sums[0] + sums[1]
     high = whole.astype(BF16).astype(F32)
-    split = jnp.concatenate([high, whole - high], axis=0)
-    device = jnp.broadcast_to(index_ref[...], sums.shape)
-    sums = jnp.where(device * share >= 27 * chans * chans // width, split, sums).astype(BF16)
+    last = jnp.broadcast_to(index_ref[...], whole.shape) >= full
+    sums = [
+        jnp.where(last, high, sums[0]).astype(BF16),
+        jnp.where(last, whole - high, sums[1]).astype(BF16),
+    ]
     for n in range(ndev):
-        sums_ref[n] = sums
+        sums_ref[n] = sums[(n // ngy) % 2]
 
 
 def rows_kernel(ngx, ngy, cap, chans, recv_ref, counts_ref, proj_t_ref, rows_ref):
@@ -389,23 +407,26 @@
     rows_ref[...] = mm(sides, both) + mm(middle, both)
 
 
-def finish_kernel(conv_scale, proj_scale, share, recv_ref, conv_ref, proj_ref):
+def finish_kernel(conv_scale, proj_scale, parity_ref, mine_ref, other_ref, conv_ref, proj_ref, both):
+    ndev, part, width = mine_ref.shape
+    parity = parity_ref[0]
+    both[:, parity] = mine_ref[...]
+    both[:, 1 - parity] = other_ref[...]
+    sums = both[...].astype(F32).reshape(ndev * 2 * part, width)
     taps, chans, _ = conv_ref.shape
     rows = 9 * chans
     half = rows // 2
-    packed = recv_ref[pl.ds(rows, half)].astype(F32)
+    packed = sums[rows : rows + half]
     column = jnp.concatenate([packed[:, :chans], packed[:, chans:]], axis=0)
     for b in range(3):
         for dz in range(3):
             first = (b * 3 + dz) * chans
-            block = recv_ref[pl.ds(first, chans)].astype(F32)
+            block = sums[first : first + chans]
             k = (2 - b) * 3 + dz
             conv_ref[k] = block[:, :chans] * conv_scale
             conv_ref[9 + k] = block[:, chans:] * conv_scale
             conv_ref[18 + k] = column[first : first + chans] * conv_scale
-    width = recv_ref.shape[1]
-    terms = recv_ref[pl.ds(rows + half, 2 * chans)].astype(F32)
-    terms = terms.reshape(2 * chans // share, 2, share // 2, width)
+    terms = sums[rows + half : rows + half + 2 * chans].reshape(chans // part, 2, part, width)
     proj_ref[...] = jnp.sum(terms, axis=1).reshape(chans, width) * proj_scale
 
 
@@ -454,7 +475,7 @@
         2 * slots * count * chans,
         (pltpu.VMEM((4 * chans, slots), BF16),),
     )
-    north, south = move(last, 0, 1), move(first, 0, -1)
+    south, north = move(first, 0, -1), move(last, 0, 1)
     out_rows, total, pre_edge, slot_edge, sums = call(
         functools.partial(conv_kernel, ndev, cap),
         [
@@ -476,29 +497,52 @@
         ),
     )
     grad_rows = 27 * chans * chans // feats
-    share = -(-(grad_rows + 2 * chans) // (16 * ndev)) * 16
-    out_edge, payload = call(
-        functools.partial(edge_kernel, ndev, cap),
-        [shape((2, chans, nz), BF16), shape((ndev, share + 2 * cap, feats), BF16)],
+    part = -(-(grad_rows + 2 * chans) // (32 * ndev)) * 16
+    full = grad_rows // (2 * part)
+    assert ngx % 2 == 0 and full * 2 * part == grad_rows
+    row = lax.axis_index("gx")
+    parity = (row % 2).astype(I32).reshape(1)
+    out_edge, grads, keep, give = call(
+        functools.partial(edge_kernel, part),
+        [
+            shape((2, chans, nz), BF16),
+            shape((4, rows, nz), BF16),
+            shape((full, part, feats), F32),
+            shape((full, part, feats), F32),
+        ],
+        (parity, pre_edge, total, north, south, outer, cot),
+        6 * one,
+        (pltpu.VMEM((9 * chans, rows), F32), pltpu.VMEM((full, 2, part, feats), F32)),
+        scalar=(0,),
+    )
+    got = swap(give)
+    (payload,) = call(
+        functools.partial(slots_kernel, ndev, cap, part, full),
+        [shape((ndev, part + 2 * cap, feats), BF16)],
+        (slot_edge, sums, grads, wb, cot, *lists, recv),
+        6 * one,
         (
-            pre_edge, slot_edge, sums, total, north, south, outer, wb, cot, *lists, recv,
+            pltpu.VMEM((ndev, 2 * cap, feats), BF16),
+            pltpu.VMEM((ndev - full, part, feats), BF16),
+            pltpu.SemaphoreType.DMA((2,)),
         ),
-        12 * one,
-        (
-            pltpu.VMEM((9 * chans, rows), F32),
-            pltpu.VMEM((ndev, share, feats), BF16),
-            pltpu.VMEM((ndev, 2 * cap, feats), BF16),
-            pltpu.SemaphoreType.DMA((3,)),
-        ),
-        far_out=(1,),
-    )
-    (payload,) = call(same_kernel, [payload], (payload,), 0, far=(0,), far_out=(0,), aliases={0: 0})
-    payload = payload.reshape(-1, feats)
-    recv = exchange(payload, ndev).reshape(ndev, share + 2 * cap, feats)
-    index = (lax.axis_index("gx") * ngy + lax.axis_index("gy")).astype(I32).reshape(1, 1)
+        far_out=(0,),
+    )
+    (payload,) = call(
+        pair_kernel,
+        [payload],
+        (keep, got, payload),
+        1000,
+        (pltpu.VMEM((full, part, feats), BF16), pltpu.SemaphoreType.DMA),
+        far=(2,),
+        far_out=(0,),
+        aliases={2: 0},
+    )
+    recv = exchange(payload.reshape(-1, feats), ndev).reshape(payload.shape)
+    index = (row * ngy + lax.axis_index("gy")).astype(I32).reshape(1, 1)
     (sums,) = call(
-        functools.partial(sums_kernel, chans, cap),
-        [shape((ndev, share, feats), BF16)],
+        functools.partial(sums_kernel, ngx, ngy, full, cap),
+        [shape((ndev, part, feats), BF16)],
         (recv, index),
         1000,
     )
@@ -508,15 +552,17 @@
         (recv, send_counts, proj_t),
         2 * nrows * slots * chans,
     )
-    sums = sums.reshape(-1, feats)
-    recv = exchange(sums, ndev)
+    mine = exchange(sums.reshape(-1, feats), ndev).reshape(sums.shape)
+    other = swap(mine)
     conv_grad, proj_grad = call(
         functools.partial(
-            finish_kernel, 1.0 / math.sqrt(count * ndev), 1.0 / math.sqrt(nrows * ndev), share
+            finish_kernel, 1.0 / math.sqrt(count * ndev), 1.0 / math.sqrt(nrows * ndev)
         ),
         [shape((27, chans, chans), F32), shape((chans, feats), F32)],
-        (recv,),
+        (parity, mine, other),
         1000,
+        (pltpu.VMEM((ndev, 2, part, feats), BF16),),
+        scalar=(0,),
     )
     out_field = jnp.concatenate([out_edge[:1], out_rows[1 : cy - 1], out_edge[1:]], axis=0)
     return (out_field.transpose(1, 0, 2)[:, None], row_grads, conv_grad, proj_grad.T)

time: 63.8 us -> 63 us (0.987)
  waiting for transfers between devices: 22.8 us -> 21.3 us
  starting transfers between devices: 22.1 us -> 21.1 us
  Pallas kernels: 13 us -> 13.8 us
  local copies, waits for them, and re-layouts: 4.58 us -> 5.3 us
    all_to_all x3, waiting for transfers between devices: 22.7 us -> 20.7 us  [exchange(): lax.all_to_all(payload.reshape(ndev, rows // ndev, width), AXES, split_ax...]
    reshape x2, local copies, waits for them, and re-layouts: 0.56 us -> 1.7 us  [local(): wf = taps.transpose(1, 2, 3, 0, 4).reshape(9 * chans, rows)]
    pallas_call x8 -> x9, Pallas kernels: 13 us -> 13.8 us  [call(): pl.pallas_call(kernel, out_shape=[jax.ShapeDtypeStruct(o.shape, o.dtype)...]
    unnamed x14, local copies, waits for them, and re-layouts: 2.14 us -> 1.28 us
    all_to_all x3, starting transfers between devices: 12.1 us -> 11.3 us  [exchange(): lax.all_to_all(payload.reshape(ndev, rows // ndev, width), AXES, split_ax...]
  transfers between devices with their start and end apart: 9 -> 11, of which waited for: 3 -> 5; matrix products, arithmetic and copies ran while one was open for 6% -> 9% of each run, Pallas kernels for 13% -> 16%
where the time goes in v8:
time: 63 us; the launch traced here: 62.6 us
  waiting for transfers between devices  21.3 us (34%)
  starting transfers between devices  21.1 us (33%)
  Pallas kernels  13.8 us (22%)
  local copies, waits for them, and re-layouts  5.3 us (8%)
  between operations  0.89 us (1%)
    all_to_all x3, waiting for transfers between devices, exchange(): lax.all_to_all(payload.reshape(ndev, rows // ndev, width), AXES, split_ax...  20.7 us
    pallas_call x9, Pallas kernels, call(): pl.pallas_call(kernel, out_shape=[jax.ShapeDtypeStruct(o.shape, o.dtype)...  13.8 us
    all_to_all x3, starting transfers between devices, exchange(): lax.all_to_all(payload.reshape(ndev, rows // ndev, width), AXES, split_ax...  11.3 us
    ppermute x6, starting transfers between devices, send(): return lax.ppermute(block, AXES, pairs)  9.73 us
    reshape x2, local copies, waits for them, and re-layouts, local(): taps = conv_weight.reshape(3, 3, 3, chans, chans)  1.72 us
    reshape x2, local copies, waits for them, and re-layouts, local(): wf = taps.transpose(1, 2, 3, 0, 4).reshape(9 * chans, rows)  1.7 us
    unnamed x14, local copies, waits for them, and re-layouts  1.28 us
  transfers between devices with their start and end apart: 11, of which 5 were waited for; matrix products, arithmetic and copies ran while one was open for 9% of the time, Pallas kernels for 16%

profile of v8, /device:TPU:0, one launch (start us, length us, event | category | flops | bytes accessed | tf_op | source)
XLA Modules:
  0.0 62.6 jit_solution(12636339214962765921)
XLA Ops:
  0.6 0.0 copy-start.4
  0.6 3.4 %collective-permute-start.1 = (bf16[64,1,16,256]{3,2,0,1:T(8,128)(2,1)}, bf16[64,1,16,256]{3,2,0,1:T(8,128)(2,1)S(1)}, u32[]{:S(2)}, u32[]{:S(2)}) collective-permute-start(bf16[64,1,16,256]{3,2,0,1:T(8,128)(2,1)} %bitcast.35), channel_id=1, source_target_pairs={{0,28},{1,29},{2,30},{3,31},{4,0},{5,1},{6,2},{7,3},{8,4},{9,5},{1... | collective-permute-start | bytes 1572872 | tf_op jit(solution)/shard_map/ppermute | solution.py:51
  4.0 0.0 collective-permute-start
  4.0 1.7 %shard_map.102 = bf16[768,128]{1,0:T(8,128)(2,1)} custom-call(bf16[128,128]{1,0:T(8,128)(2,1)} %rows_far.1, s32[1,32]{1,0:T(1,128)} %counts_ref.1), custom_call_target="tpu_custom_call" | custom-call | flops 8388608 | bytes 229504 | tf_op jit(solution)/shard_map/pallas_call | solution.py:27
  5.8 0.0 copy-start.2
  5.8 6.1 %all-to-all-start = ((bf16[32,24,128]{2,1,0:T(8,128)(2,1)}), bf16[32,24,128]{2,1,0:T(8,128)(2,1)S(1)}, u32[]{:S(2)}, u32[]{:S(2)}) async-start(bf16[32,24,128]{2,1,0:T(8,128)(2,1)} %bitcast.50), calls=%async_computation | async-start | bytes 393216 | tf_op jit(solution)/shard_map/all_to_all | solution.py:60
  11.8 0.0 copy-done.2
  11.8 2.5 %collective-permute-start.3 = (s32[1,256]{1,0:T(1,128)S(1)}, s32[1,256]{1,0:T(1,128)S(1)}, u32[]{:S(2)}, u32[]{:S(2)}) collective-permute-start(s32[1,256]{1,0:T(1,128)S(1)} %copy-done.2), channel_id=1, source_target_pairs={{0,28},{1,29},{2,30},{3,31},{4,0},{5,1},{6,2},{7,3},{8,4},{9,5},{1... | collective-permute-start | bytes 3080 | tf_op jit(solution)/shard_map/ppermute | solution.py:51
  14.3 0.0 collective-permute-start.2
  14.3 0.0 copy-done.4
  14.3 0.4 copy.30
  14.7 0.0 copy-start.5
  14.7 1.3 %copy.19 = bf16[3,3,3,64,64]{3,2,1,4,0:T(4,128)(2,1)} copy(bf16[3,3,3,64,64]{4,3,2,1,0:T(8,128)(2,1)S(1)} %bitcast.49) | data formatting | bytes 442368 | tf_op jit(solution)/shard_map/reshape | solution.py:467
  16.1 0.0 copy-done.5
  16.1 0.2 copy.31
  16.2 0.4 reshape.43
  16.6 0.2 copy.24.wb_ref
  16.8 0.0 copy-start
  16.8 1.5 %reshape.42 = bf16[576,192]{0,1:T(8,128)(2,1)S(1)} reshape(bf16[3,3,64,3,64]{2,1,0,4,3:T(4,128)(2,1)} %bitcast.46) | data formatting | bytes 442368 | tf_op jit(solution)/shard_map/reshape | solution.py:468
  18.3 0.0 copy-start.1
  18.4 0.2 copy.23.wf_ref
  18.5 0.0 collective-permute-done.3.east_cells
  18.5 0.5 collective-permute-done.2.west_cells
  19.1 2.1 %all-to-all-done = bf16[32,24,128]{2,1,0:T(8,128)(2,1)S(1)} async-done(((bf16[32,24,128]{2,1,0:T(8,128)(2,1)}), bf16[32,24,128]{2,1,0:T(8,128)(2,1)S(1)}, u32[]{:S(2)}, u32[]{:S(2)}) %all-to-all-start) | async-done | bytes 196640 | tf_op jit(solution)/shard_map/all_to_all | solution.py:60
  21.2 0.0 collective-permute-done.1
  21.2 0.0 collective-permute-done
  21.2 0.0 copy-done
  21.2 0.0 copy-done.1
  21.2 1.0 %shard_map.104 = (bf16[192,256]{1,0:T(8,128)(2,1)S(1)}, bf16[192,256]{1,0:T(8,128)(2,1)S(1)}, bf16[4,192,256]{2,1,0:T(8,128)(2,1)S(1)}) custom-call(bf16[768,128]{1,0:T(8,128)(2,1)S(1)} %bitcast.32, bf16[64,16,256]{2,1,0:T(8,128)(2,1)S(1)} %bitcast.37, bf16[64,16,256]{2,1,0:T(8,128)(2,1)S(1)} %bitcast.41, bf16[64,16,256]{2,1,0:T(8,128)(2,1)S(1)} %bitcast.39, ...), custom_call_target="tpu_custom_call" | custom-call | flops 134217728 | bytes 3124224 | tf_op jit(solution)/shard_map/pallas_call | solution.py:27
  22.2 0.1 collective-permute-start.4
  22.2 3.8 %collective-permute-start.5 = (bf16[192,256]{1,0:T(8,128)(2,1)S(1)}, bf16[192,256]{1,0:T(8,128)(2,1)S(1)}, u32[]{:S(2)}, u32[]{:S(2)}) collective-permute-start(bf16[192,256]{1,0:T(8,128)(2,1)S(1)} %get-tuple-element.21), channel_id=1, source_target_pairs={{0,3},{1,0},{2,1},{3,2},{4,7},{5,4},{6,5},{7,6},{8,11},{9,8},{10,9... | collective-permute-start | bytes 294920 | tf_op jit(solution)/shard_map/ppermute | solution.py:51
  26.1 5.6 %shard_map.103 = (bf16[16,64,256]{2,1,0:T(8,128)(2,1)S(1)}, f32[576,192]{1,0:T(8,128)S(1)}, f32[4,64,256]{2,1,0:T(8,128)S(1)}, f32[4,192,256]{2,1,0:T(8,128)S(1)}, f32[3,64,256]{2,1,0:T(8,128)S(1)}) custom-call(bf16[768,128]{1,0:T(8,128)(2,1)S(1)} %bitcast.33, bf16[64,128]{1,0:T(8,128)(2,1)S(1)} %bitcast.44, bf16[16,64,256]{2,1,0:T(8,128)(2,1)S(1)} %bitcast.29, ...), custom_call_target="tpu_custom_call" | custom-call | flops 2717908992 | bytes 4967424 | tf_op jit(solution)/shard_map/pallas_call | solution.py:27
  31.7 0.0 collective-permute-done.4.north_ref
  31.7 0.0 collective-permute-done.5.south_ref
  31.7 0.6 shard_map.105
  32.3 0.1 collective-permute-start.6
  32.3 1.3 %shard_map.106.same_far = bf16[32,32,128]{2,1,0:T(8,128)(2,1)} custom-call(f32[4,192,256]{2,1,0:T(8,128)S(1)} %get-tuple-element.27.slot_ref, f32[3,64,256]{2,1,0:T(8,128)S(1)} %get-tuple-element.28.sums_ref, bf16[4,192,256]{2,1,0:T(8,128)(2,1)S(1)} %get-tuple-element.29.grads_ref, bf16[576,192]{1,0:T(8,128)(2,1)S(1)} %copy.24.wb_ref, ...), custom_call_target="tpu_custom_call" | custom-call | flops 113246208 | bytes 2583552 | tf_op jit(solution)/shard_map/pallas_call | solution.py:27
  33.6 0.2 collective-permute-done.6.got_ref
  33.8 0.7 %shard_map.107 = bf16[32,32,128]{2,1,0:T(8,128)(2,1)} custom-call(f32[27,16,128]{2,1,0:T(8,128)S(1)} %get-tuple-element.25.keep_ref, f32[27,16,128]{2,1,0:T(8,128)S(1)} %collective-permute-done.6.got_ref, bf16[32,32,128]{2,1,0:T(8,128)(2,1)} %shard_map.106.same_far), custom_call_target="tpu_custom_call", output_to_operand_aliasing={{}: (2, {})} | custom-call | flops 1000 | bytes 966656 | tf_op jit(solution)/shard_map/pallas_call | solution.py:27
  34.5 2.6 %all-to-all-start.1 = ((bf16[32,32,128]{2,1,0:T(8,128)(2,1)}), bf16[32,32,128]{2,1,0:T(8,128)(2,1)S(1)}, u32[]{:S(2)}, u32[]{:S(2)}) async-start(bf16[32,32,128]{2,1,0:T(8,128)(2,1)} %shard_map.107), calls=%async_computation.1 | async-start | bytes 524288 | tf_op jit(solution)/shard_map/all_to_all | solution.py:60
  37.1 10.2 %all-to-all-done.1.recv_ref = bf16[32,32,128]{2,1,0:T(8,128)(2,1)S(1)} async-done(((bf16[32,32,128]{2,1,0:T(8,128)(2,1)}), bf16[32,32,128]{2,1,0:T(8,128)(2,1)S(1)}, u32[]{:S(2)}, u32[]{:S(2)}) %all-to-all-start.1) | async-done | bytes 262176 | tf_op jit(solution)/shard_map/all_to_all | solution.py:60
  47.3 0.7 %shard_map.109 = bf16[32,16,128]{2,1,0:T(8,128)(2,1)} custom-call(bf16[32,32,128]{2,1,0:T(8,128)(2,1)S(1)} %all-to-all-done.1.recv_ref, s32[1,1]{1,0:T(1,128)} %bitcast.16.index_ref), custom_call_target="tpu_custom_call" | custom-call | flops 1000 | bytes 393220 | tf_op jit(solution)/shard_map/pallas_call | solution.py:27
  48.0 2.7 %all-to-all-start.2 = ((bf16[32,16,128]{2,1,0:T(8,128)(2,1)}), bf16[32,16,128]{2,1,0:T(8,128)(2,1)S(1)}, u32[]{:S(2)}, u32[]{:S(2)}) async-start(bf16[32,16,128]{2,1,0:T(8,128)(2,1)} %shard_map.109), calls=%async_computation.2 | async-start | bytes 262144 | tf_op jit(solution)/shard_map/all_to_all | solution.py:60
  50.8 8.4 %all-to-all-done.2.mine_ref = bf16[32,16,128]{2,1,0:T(8,128)(2,1)S(1)} async-done(((bf16[32,16,128]{2,1,0:T(8,128)(2,1)}), bf16[32,16,128]{2,1,0:T(8,128)(2,1)S(1)}, u32[]{:S(2)}, u32[]{:S(2)}) %all-to-all-start.2) | async-done | bytes 131104 | tf_op jit(solution)/shard_map/all_to_all | solution.py:60
  59.1 0.0 collective-permute-start.7
  59.2 0.1 maximum_bitcast_fusion
  59.2 0.0 copy-start.3
  59.2 1.1 %copy.27 = bf16[64,1,16,256]{3,2,1,0:T(8,128)(2,1)} copy(bf16[64,1,16,256]{3,0,2,1:T(8,128)(2,1)S(1)} %maximum_bitcast_fusion) | data formatting | bytes 1048576
  60.3 0.0 copy-done.3
  60.3 1.1 %shard_map.108 = f32[128,128]{1,0:T(8,128)} custom-call(bf16[32,32,128]{2,1,0:T(8,128)(2,1)S(1)} %all-to-all-done.1.recv_ref, s32[1,32]{1,0:T(1,128)S(1)} %copy-done.3, bf16[64,128]{1,0:T(8,128)(2,1)S(1)} %bitcast.45), custom_call_target="tpu_custom_call" | custom-call | flops 4194304 | bytes 344192 | tf_op jit(solution)/shard_map/pallas_call | solution.py:27
  61.5 0.0 collective-permute-done.7.other_ref
  61.5 1.1 %shard_map.110 = (f32[27,64,64]{2,1,0:T(8,128)}, f32[64,128]{1,0:T(8,128)}) custom-call(s32[1]{0:T(128)} %bitcast.parity_ref, bf16[32,16,128]{2,1,0:T(8,128)(2,1)S(1)} %all-to-all-done.2.mine_ref, bf16[32,16,128]{2,1,0:T(8,128)(2,1)S(1)} %collective-permute-done.7.other_ref), custom_call_target="tpu_custom_call" | custom-call | flops 1000 | bytes 737284 | tf_op jit(solution)/shard_map/pallas_call | solution.py:27
  (2 shorter events, 0.0 us)
Async XLA Ops:
  0.6 13.7 %copy-start.4 = (bf16[27,64,64]{2,1,0:T(8,128)(2,1)S(1)}, bf16[27,64,64]{2,1,0:T(8,128)(2,1)}, u32[]{:S(2)}) copy-start(bf16[27,64,64]{2,1,0:T(8,128)(2,1)} %param.12) | copy-start | bytes 663556
  0.6 20.5 %collective-permute-start.1 = (bf16[64,1,16,256]{3,2,0,1:T(8,128)(2,1)}, bf16[64,1,16,256]{3,2,0,1:T(8,128)(2,1)S(1)}, u32[]{:S(2)}, u32[]{:S(2)}) collective-permute-start(bf16[64,1,16,256]{3,2,0,1:T(8,128)(2,1)} %bitcast.35), channel_id=1, source_target_pairs={{0,28},{1,29},{2,30},{3,31},{4,0},{5,1},{6,2},{7,3},{8,4},{9,5},{1... | collective-permute-start | bytes 1572872 | tf_op jit(solution)/shard_map/ppermute | solution.py:51
  4.0 17.1 %collective-permute-start = (bf16[64,1,16,256]{3,2,0,1:T(8,128)(2,1)}, bf16[64,1,16,256]{3,2,0,1:T(8,128)(2,1)S(1)}, u32[]{:S(2)}, u32[]{:S(2)}) collective-permute-start(bf16[64,1,16,256]{3,2,0,1:T(8,128)(2,1)} %bitcast.36), channel_id=1, source_target_pairs={{0,4},{1,5},{2,6},{3,7},{4,8},{5,9},{6,10},{7,11},{8,12},{9,13},{1... | collective-permute-start | bytes 1572872 | tf_op jit(solution)/shard_map/ppermute | solution.py:51
  5.8 6.1 %copy-start.2 = (s32[1,256]{1,0:T(1,128)S(1)}, s32[1,256]{1,0:T(1,128)}, u32[]{:S(2)}) copy-start(s32[1,256]{1,0:T(1,128)} %own_cells.5) | copy-start | bytes 3076
  5.8 15.4 %all-to-all-start = ((bf16[32,24,128]{2,1,0:T(8,128)(2,1)}), bf16[32,24,128]{2,1,0:T(8,128)(2,1)S(1)}, u32[]{:S(2)}, u32[]{:S(2)}) async-start(bf16[32,24,128]{2,1,0:T(8,128)(2,1)} %bitcast.50), calls=%async_computation | async-start | bytes 393216 | tf_op jit(solution)/shard_map/all_to_all | solution.py:60
  11.8 6.7 %collective-permute-start.3 = (s32[1,256]{1,0:T(1,128)S(1)}, s32[1,256]{1,0:T(1,128)S(1)}, u32[]{:S(2)}, u32[]{:S(2)}) collective-permute-start(s32[1,256]{1,0:T(1,128)S(1)} %copy-done.2), channel_id=1, source_target_pairs={{0,28},{1,29},{2,30},{3,31},{4,0},{5,1},{6,2},{7,3},{8,4},{9,5},{1... | collective-permute-start | bytes 3080 | tf_op jit(solution)/shard_map/ppermute | solution.py:51
  14.3 4.7 %collective-permute-start.2 = (s32[1,256]{1,0:T(1,128)S(1)}, s32[1,256]{1,0:T(1,128)S(1)}, u32[]{:S(2)}, u32[]{:S(2)}) collective-permute-start(s32[1,256]{1,0:T(1,128)S(1)} %copy-done.2), channel_id=1, source_target_pairs={{0,4},{1,5},{2,6},{3,7},{4,8},{5,9},{6,10},{7,11},{8,12},{9,13},{1... | collective-permute-start | bytes 3080 | tf_op jit(solution)/shard_map/ppermute | solution.py:51
  14.7 1.4 %copy-start.5 = (bf16[64,1,16,256]{3,2,1,0:T(8,128)(2,1)S(1)}, bf16[64,1,16,256]{3,2,1,0:T(8,128)(2,1)}, u32[]{:S(2)}) copy-start(bf16[64,1,16,256]{3,2,1,0:T(8,128)(2,1)} %param.13) | copy-start | bytes 1572868
  16.8 4.4 %copy-start = (bf16[64,1,16,256]{3,2,1,0:T(8,128)(2,1)S(1)}, bf16[64,1,16,256]{3,2,1,0:T(8,128)(2,1)}, u32[]{:S(2)}) copy-start(bf16[64,1,16,256]{3,2,1,0:T(8,128)(2,1)} %param.10) | copy-start | bytes 1572868
  18.3 2.8 %copy-start.1 = (bf16[128,64]{0,1:T(8,128)(2,1)S(1)}, bf16[128,64]{0,1:T(8,128)(2,1)}, u32[]{:S(2)}) copy-start(bf16[128,64]{0,1:T(8,128)(2,1)} %param.11) | copy-start | bytes 49156
  22.2 9.5 %collective-permute-start.4 = (bf16[192,256]{1,0:T(8,128)(2,1)S(1)}, bf16[192,256]{1,0:T(8,128)(2,1)S(1)}, u32[]{:S(2)}, u32[]{:S(2)}) collective-permute-start(bf16[192,256]{1,0:T(8,128)(2,1)S(1)} %get-tuple-element.20), channel_id=1, source_target_pairs={{0,1},{1,2},{2,3},{3,0},{4,5},{5,6},{6,7},{7,4},{8,9},{9,10},{10,1... | collective-permute-start | bytes 294920 | tf_op jit(solution)/shard_map/ppermute | solution.py:51
  22.2 9.4 %collective-permute-start.5 = (bf16[192,256]{1,0:T(8,128)(2,1)S(1)}, bf16[192,256]{1,0:T(8,128)(2,1)S(1)}, u32[]{:S(2)}, u32[]{:S(2)}) collective-permute-start(bf16[192,256]{1,0:T(8,128)(2,1)S(1)} %get-tuple-element.21), channel_id=1, source_target_pairs={{0,3},{1,0},{2,1},{3,2},{4,7},{5,4},{6,5},{7,6},{8,11},{9,8},{10,9... | collective-permute-start | bytes 294920 | tf_op jit(solution)/shard_map/ppermute | solution.py:51
  32.3 1.5 %collective-permute-start.6 = (f32[27,16,128]{2,1,0:T(8,128)S(1)}, f32[27,16,128]{2,1,0:T(8,128)S(1)}, u32[]{:S(2)}, u32[]{:S(2)}) collective-permute-start(f32[27,16,128]{2,1,0:T(8,128)S(1)} %get-tuple-element.26), channel_id=1, source_target_pairs={{0,4},{4,0},{8,12},{12,8},{16,20},{20,16},{24,28},{28,24},{1,5},{5... | collective-permute-start | bytes 663560 | tf_op jit(solution)/shard_map/ppermute | solution.py:55
  34.5 12.8 %all-to-all-start.1 = ((bf16[32,32,128]{2,1,0:T(8,128)(2,1)}), bf16[32,32,128]{2,1,0:T(8,128)(2,1)S(1)}, u32[]{:S(2)}, u32[]{:S(2)}) async-start(bf16[32,32,128]{2,1,0:T(8,128)(2,1)} %shard_map.107), calls=%async_computation.1 | async-start | bytes 524288 | tf_op jit(solution)/shard_map/all_to_all | solution.py:60
  48.0 11.1 %all-to-all-start.2 = ((bf16[32,16,128]{2,1,0:T(8,128)(2,1)}), bf16[32,16,128]{2,1,0:T(8,128)(2,1)S(1)}, u32[]{:S(2)}, u32[]{:S(2)}) async-start(bf16[32,16,128]{2,1,0:T(8,128)(2,1)} %shard_map.109), calls=%async_computation.2 | async-start | bytes 262144 | tf_op jit(solution)/shard_map/all_to_all | solution.py:60
  59.1 2.3 %collective-permute-start.7 = (bf16[32,16,128]{2,1,0:T(8,128)(2,1)S(1)}, bf16[32,16,128]{2,1,0:T(8,128)(2,1)S(1)}, u32[]{:S(2)}, u32[]{:S(2)}) collective-permute-start(bf16[32,16,128]{2,1,0:T(8,128)(2,1)S(1)} %all-to-all-done.2.mine_ref), channel_id=1, source_target_pairs={{0,4},{4,0},{8,12},{12,8},{16,20},{20,16},{24,28},{28,24},{1,5},{5... | collective-permute-start | bytes 393224 | tf_op jit(solution)/shard_map/ppermute | solution.py:55
  59.2 1.1 %copy-start.3 = (s32[1,32]{1,0:T(1,128)S(1)}, s32[1,32]{1,0:T(1,128)}, u32[]{:S(2)}) copy-start(s32[1,32]{1,0:T(1,128)} %counts_ref.1) | copy-start | bytes 388

commit v9 on v8

--- a/solution.py
+++ b/solution.py
@@ -150,51 +150,40 @@
     return mm(masked[pl.ds(0, len(ns) * chans)], picked_depth(z, nz), NT)
 
 
+def add_to_rows(near, far, cot, rows, back, out_ref):
+    chans = cot.shape[0]
+    at, over = (rows, 0) if back else (0, rows)
+    out_ref[pl.ds(0, chans)] = over_depth(near[at : at + rows]).astype(BF16)
+    out_ref[pl.ds(chans, chans)] = over_depth(near[over : over + rows] + far).astype(BF16)
+    out_ref[pl.ds(2 * chans, chans)] = cot
+
+
 def outer_kernel(
     ndev, cap, recv_ref, own_ref, west_ref, east_ref, own_cells, west_cells, east_cells,
-    proj_t_ref, cot_ref, wf_ref, first_ref, last_ref, field_ref, masked,
+    proj_t_ref, cot_ref, wf_ref, first_ref, masked, field,
 ):
     chans, cy, nz = own_ref.shape
     rows = 3 * chans
     raws = rows_in(recv_ref, ndev, cap)
-    ns = (0, 1, cy - 2, cy - 1)
     planes = ((west_ref, west_cells), (own_ref, own_cells), (east_ref, east_cells))
     for dx, (ref, cells_ref) in enumerate(planes):
         values = mm(proj_t_ref[...], raws[dx], NT).astype(BF16)
-        painted = painted_rows(values, place(cells_ref, nz), nz, ns, masked)
+        painted = painted_rows(values, place(cells_ref, nz), nz, (0, 1), masked)
         base = turned(ref)
-        for n, row in enumerate(ns):
+        for n in range(2):
             part = painted[n * chans : (n + 1) * chans]
-            field_ref[n, pl.ds(dx * chans, chans)] = (base[row] + part).astype(BF16)
-    near = mm(wf_ref[pl.ds(0, 2 * rows)], field_ref[3])
-    far = mm(wf_ref[pl.ds(0, rows)], field_ref[2])
-    last_ref[pl.ds(0, chans)] = over_depth(near[:rows]).astype(BF16)
-    last_ref[pl.ds(chans, chans)] = over_depth(near[rows:] + far).astype(BF16)
-    last_ref[pl.ds(2 * chans, chans)] = cot_ref[cy - 1]
-    near = mm(wf_ref[pl.ds(rows, 2 * rows)], field_ref[0])
-    far = mm(wf_ref[pl.ds(2 * rows, rows)], field_ref[1])
-    first_ref[pl.ds(0, chans)] = over_depth(near[rows:]).astype(BF16)
-    first_ref[pl.ds(chans, chans)] = over_depth(near[:rows] + far).astype(BF16)
-    first_ref[pl.ds(2 * chans, chans)] = cot_ref[0]
-
-
-def place(cells_ref, nz):
-    cells = cells_ref[...]
-    return cells // nz, cells % nz
-
-
-def turned(ref):
-    return jnp.swapaxes(ref[...].astype(F32), 0, 1)
-
-
-def conv_kernel(
-    ndev, cap, recv_ref, proj_t_ref, cot_ref, wf_ref, wb_ref,
-    own_ref, west_ref, east_ref, own_cells, west_cells, east_cells,
-    out_ref, total_ref, pre_ref, slot_ref, sums_ref, x_ref, acc, grads, back, plane, masked,
+            field[n, pl.ds(dx * chans, chans)] = (base[n] + part).astype(BF16)
+    near = mm(wf_ref[pl.ds(rows, 2 * rows)], field[0])
+    far = mm(wf_ref[pl.ds(2 * rows, rows)], field[1])
+    add_to_rows(near, far, cot_ref[0], rows, True, first_ref)
+
+
+def field_kernel(
+    ndev, cap, recv_ref, own_ref, west_ref, east_ref, own_cells, west_cells, east_cells,
+    proj_t_ref, cot_ref, wf_ref, x_ref, last_ref, masked,
 ):
     chans, cy, nz = own_ref.shape
     rows = 3 * chans
-    slots = ndev * cap
     raws = rows_in(recv_ref, ndev, cap)
     planes = ((west_ref, west_cells), (own_ref, own_cells), (east_ref, east_cells))
     for dx, (ref, cells_ref) in enumerate(planes):
@@ -202,6 +191,27 @@
         painted = painted_rows(values, place(cells_ref, nz), nz, range(cy), masked)
         field = turned(ref) + painted.reshape(cy, chans, nz)
         x_ref[:, pl.ds(dx * chans, chans)] = field.astype(BF16)
+    near = mm(wf_ref[pl.ds(0, 2 * rows)], x_ref[cy - 1])
+    far = mm(wf_ref[pl.ds(0, rows)], x_ref[cy - 2])
+    add_to_rows(near, far, cot_ref[cy - 1], rows, False, last_ref)
+
+
+def place(cells_ref, nz):
+    cells = cells_ref[...]
+    return cells // nz, cells % nz
+
+
+def turned(ref):
+    return jnp.swapaxes(ref[...].astype(F32), 0, 1)
+
+
+def conv_kernel(
+    x_ref, cot_ref, wf_ref, wb_ref, own_cells, west_cells, east_cells,
+    out_ref, total_ref, pre_ref, slot_ref, sums_ref, acc, grads, back, plane,
+):
+    cy, chans, nz = cot_ref.shape
+    rows = 3 * chans
+    slots = own_cells.shape[1]
     own = pl.ds(chans, chans)
     zeros = jnp.zeros((rows, nz), BF16)
     for t in (0, 1, cy, cy + 1):
@@ -264,7 +274,7 @@
     slot_ref[2] = back[cy - 2]
     slot_ref[3] = back[cy - 1]
     zero = jnp.zeros((chans, slots), F32)
-    for dx, (_, cells_ref) in enumerate(planes):
+    for dx, cells_ref in enumerate((west_cells, own_cells, east_cells)):
         sums_ref[dx] = at_slots(plane[dx], place(cells_ref, nz), range(2, cy - 2), zero)
 
 
@@ -278,7 +288,7 @@
 
 
 def edge_kernel(
-    part, parity_ref, pre_ref, total_ref, north_ref, south_ref, field_ref, cot_ref,
+    part, parity_ref, pre_ref, total_ref, north_ref, south_ref, x_ref, cot_ref,
     out_ref, grads_ref, keep_ref, give_ref, total, sums,
 ):
     cy, chans, nz = cot_ref.shape
@@ -290,17 +300,17 @@
     ends = []
     for n, (ref, at) in enumerate(sides):
         pre = pre_ref[n] + ref[pl.ds(at * chans, chans)].astype(F32)
-        ends.append(finish_row(pre, field_ref[0 if n < 2 else 3, own], cots[n]))
+        ends.append(finish_row(pre, x_ref[0 if n < 2 else cy - 1, own], cots[n]))
     out_ref[0], out_ref[1] = ends[1][0], ends[2][0]
     grads = [stacked(grad) for _, grad in ends]
     for n in range(4):
         grads_ref[n] = grads[n]
-    top = mm(jnp.concatenate([grads[0], grads[1]], axis=0), field_ref[0], NT)
-    bottom = mm(jnp.concatenate([grads[2], grads[3]], axis=0), field_ref[3], NT)
+    top = mm(jnp.concatenate([grads[0], grads[1]], axis=0), x_ref[0], NT)
+    bottom = mm(jnp.concatenate([grads[2], grads[3]], axis=0), x_ref[cy - 1], NT)
     here = [pl.ds(n * rows, rows) for n in range(3)]
-    total[here[0]] = total_ref[here[0]] + (top[:rows] + mm(grads[1], field_ref[1], NT))
+    total[here[0]] = total_ref[here[0]] + (top[:rows] + mm(grads[1], x_ref[1], NT))
     total[here[1]] = total_ref[here[1]] + (top[rows:] + bottom[:rows])
-    total[here[2]] = total_ref[here[2]] + (bottom[rows:] + mm(grads[2], field_ref[2], NT))
+    total[here[2]] = total_ref[here[2]] + (bottom[rows:] + mm(grads[2], x_ref[cy - 2], NT))
     full, _, width = keep_ref.shape
     half = 3 * rows // 2
     split = 3 * rows // (2 * part)
@@ -309,12 +319,12 @@
     sums[pl.ds(split, full - split)] = taps.reshape(full - split, 2, part, width)
     parity = parity_ref[0]
     keep_ref[...] = sums[:, parity]
-    give_ref[...] = sums[:, 1 - parity]
+    give_ref[...] = sums[:, 1 - parity].astype(BF16)
 
 
 def slots_kernel(
     ndev, cap, part, full, slot_ref, sums_ref, grads_ref, wb_ref, cot_ref,
-    own_cells, west_cells, east_cells, recv_ref, send_far, slots_send, proj_send, sems,
+    own_cells, west_cells, east_cells, recv_ref, slots_ref, proj_ref,
 ):
     cy, chans, nz = cot_ref.shape
     rows = 3 * chans
@@ -334,31 +344,32 @@
         found.append(at_slots(terms, place(cells_ref, nz), at, sums_ref[dx]))
     sides = jnp.concatenate([found[0], found[2]], axis=0).T
     middle = jnp.concatenate([found[1], jnp.zeros_like(found[1])], axis=0).T
-    width = send_far.shape[2]
+    width = recv_ref.shape[1]
     back = [sides.reshape(ndev, cap, width), middle.reshape(ndev, cap, width)]
-    slots_send[...] = jnp.concatenate(back, axis=1).astype(BF16)
-    copies = [pltpu.make_async_copy(slots_send, send_far.at[:, pl.ds(part, 2 * cap)], sems.at[0])]
-    copies[0].start()
+    slots_ref[...] = jnp.concatenate(back, axis=1).astype(BF16)
     raws = rows_in(recv_ref, ndev, cap)
     proj = sum(mm(found[dx].astype(BF16), raws[dx]) for dx in range(3))
     rest = ndev - full
     pad = jnp.zeros((rest * part - chans, width), F32)
     proj = jnp.concatenate([proj, pad], axis=0).reshape(rest, part, width)
-    proj_send[...] = proj.astype(BF16)
-    copies.append(
-        pltpu.make_async_copy(proj_send, send_far.at[pl.ds(full, rest), pl.ds(0, part)], sems.at[1])
-    )
+    proj_ref[...] = proj.astype(BF16)
+
+
+def pair_kernel(keep_ref, got_ref, slots_ref, proj_ref, send_far, sums_send, sems):
+    full, part, _ = keep_ref.shape
+    ndev, back, _ = slots_ref.shape
+    pieces = (
+        (slots_ref, send_far.at[:, pl.ds(part, back)]),
+        (proj_ref, send_far.at[pl.ds(full, ndev - full), pl.ds(0, part)]),
+        (sums_send, send_far.at[pl.ds(0, full), pl.ds(0, part)]),
+    )
+    copies = [pltpu.make_async_copy(src, dst, sems.at[n]) for n, (src, dst) in enumerate(pieces)]
+    copies[0].start()
     copies[1].start()
+    sums_send[...] = (keep_ref[...] + got_ref[...].astype(F32)).astype(BF16)
+    copies[2].start()
     for copy in copies:
         copy.wait()
-
-
-def pair_kernel(keep_ref, got_ref, same_far, send_far, sums_send, sem):
-    full, part, _ = keep_ref.shape
-    sums_send[...] = (keep_ref[...] + got_ref[...]).astype(BF16)
-    copy = pltpu.make_async_copy(sums_send, send_far.at[pl.ds(0, full), pl.ds(0, part)], sem)
-    copy.start()
-    copy.wait()
 
 
 def sums_kernel(ngx, ngy, full, cap, recv_ref, index_ref, sums_ref):
@@ -377,7 +388,9 @@
         sums_ref[n] = sums[(n // ngy) % 2]
 
 
-def rows_kernel(ngx, ngy, cap, chans, recv_ref, counts_ref, proj_t_ref, rows_ref):
+def rows_kernel(
+    ngx, ngy, cap, chans, recv_ref, counts_ref, proj_t_ref, inner_ref, ends_ref, rows_ref, out_ref
+):
     ndev = ngx * ngy
     nrows = rows_ref.shape[0]
     width = recv_ref.shape[2]
@@ -405,6 +418,9 @@
     sides = mm(onehot, sides.astype(BF16)).astype(BF16)
     middle = mm(onehot, middle.astype(BF16)).astype(BF16)
     rows_ref[...] = mm(sides, both) + mm(middle, both)
+    cy = inner_ref.shape[0]
+    field = jnp.concatenate([ends_ref[:1], inner_ref[1 : cy - 1], ends_ref[1:]], axis=0)
+    out_ref[...] = jnp.swapaxes(field.astype(F32), 0, 1).astype(BF16)
 
 
 def finish_kernel(conv_scale, proj_scale, parity_ref, mine_ref, other_ref, conv_ref, proj_ref, both):
@@ -468,16 +484,25 @@
     wf = taps.transpose(1, 2, 3, 0, 4).reshape(9 * chans, rows)
     wb = taps.transpose(1, 0, 4, 2, 3).reshape(9 * chans, rows)
 
-    first, last, outer = call(
+    inputs = (recv, *planes, *lists, proj_t, cot, wf)
+    (first,) = call(
         functools.partial(outer_kernel, ndev, cap),
-        [shape((rows, nz), BF16)] * 2 + [shape((4, rows, nz), BF16)],
-        (recv, *planes, *lists, proj_t, cot, wf),
-        2 * slots * count * chans,
-        (pltpu.VMEM((4 * chans, slots), BF16),),
-    )
-    south, north = move(first, 0, -1), move(last, 0, 1)
+        [shape((rows, nz), BF16)],
+        inputs,
+        2 * one,
+        (pltpu.VMEM((2 * chans, slots), BF16), pltpu.VMEM((2, rows, nz), BF16)),
+    )
+    south = move(first, 0, -1)
+    x_all, last = call(
+        functools.partial(field_kernel, ndev, cap),
+        [shape((cy, rows, nz), BF16), shape((rows, nz), BF16)],
+        inputs,
+        6 * slots * count * chans,
+        (pltpu.VMEM((cy * chans, slots), BF16),),
+    )
+    north = move(last, 0, 1)
     out_rows, total, pre_edge, slot_edge, sums = call(
-        functools.partial(conv_kernel, ndev, cap),
+        conv_kernel,
         [
             shape((cy, chans, nz), BF16),
             shape((9 * chans, rows), F32),
@@ -485,15 +510,13 @@
             shape((4, rows, nz), F32),
             shape((3, chans, slots), F32),
         ],
-        (recv, proj_t, cot, wf, wb, *planes, *lists),
+        (x_all, cot, wf, wb, *lists),
         3 * cy * 3 * one,
         (
-            pltpu.VMEM((cy, rows, nz), BF16),
             pltpu.VMEM((cy + 1, rows, nz), F32),
             pltpu.VMEM((cy + 2, rows, nz), BF16),
             pltpu.VMEM((cy, rows, nz), F32),
             pltpu.VMEM((3, (cy - 4) * chans, nz), BF16),
-            pltpu.VMEM((cy * chans, slots), BF16),
         ),
     )
     grad_rows = 27 * chans * chans // feats
@@ -508,36 +531,29 @@
             shape((2, chans, nz), BF16),
             shape((4, rows, nz), BF16),
             shape((full, part, feats), F32),
-            shape((full, part, feats), F32),
+            shape((full, part, feats), BF16),
         ],
-        (parity, pre_edge, total, north, south, outer, cot),
+        (parity, pre_edge, total, north, south, x_all, cot),
         6 * one,
         (pltpu.VMEM((9 * chans, rows), F32), pltpu.VMEM((full, 2, part, feats), F32)),
         scalar=(0,),
     )
     got = swap(give)
-    (payload,) = call(
+    back, proj = call(
         functools.partial(slots_kernel, ndev, cap, part, full),
-        [shape((ndev, part + 2 * cap, feats), BF16)],
+        [shape((ndev, 2 * cap, feats), BF16), shape((ndev - full, part, feats), BF16)],
         (slot_edge, sums, grads, wb, cot, *lists, recv),
         6 * one,
-        (
-            pltpu.VMEM((ndev, 2 * cap, feats), BF16),
-            pltpu.VMEM((ndev - full, part, feats), BF16),
-            pltpu.SemaphoreType.DMA((2,)),
-        ),
-        far_out=(0,),
     )
     (payload,) = call(
         pair_kernel,
-        [payload],
-        (keep, got, payload),
+        [shape((ndev, part + 2 * cap, feats), BF16)],
+        (keep, got, back, proj),
         1000,
-        (pltpu.VMEM((full, part, feats), BF16), pltpu.SemaphoreType.DMA),
-        far=(2,),
+        (pltpu.VMEM((full, part, feats), BF16), pltpu.SemaphoreType.DMA((3,))),
         far_out=(0,),
-        aliases={2: 0},
-    )
+    )
+    (payload,) = call(same_kernel, [payload], (payload,), 0, far=(0,), far_out=(0,), aliases={0: 0})
     recv = exchange(payload.reshape(-1, feats), ndev).reshape(payload.shape)
     index = (row * ngy + lax.axis_index("gy")).astype(I32).reshape(1, 1)
     (sums,) = call(
@@ -546,13 +562,14 @@
         (recv, index),
         1000,
     )
-    (row_grads,) = call(
+    row_grads, out_field = call(
         functools.partial(rows_kernel, ngx, ngy, cap, chans),
-        [shape((nrows, feats), F32)],
-        (recv, send_counts, proj_t),
+        [shape((nrows, feats), F32), shape((chans, cy, nz), BF16)],
+        (recv, send_counts, proj_t, out_rows, out_edge),
         2 * nrows * slots * chans,
     )
     mine = exchange(sums.reshape(-1, feats), ndev).reshape(sums.shape)
+    mine, row_grads, out_field = lax.optimization_barrier((mine, row_grads, out_field))
     other = swap(mine)
     conv_grad, proj_grad = call(
         functools.partial(
@@ -564,8 +581,7 @@
         (pltpu.VMEM((ndev, 2, part, feats), BF16),),
         scalar=(0,),
     )
-    out_field = jnp.concatenate([out_edge[:1], out_rows[1 : cy - 1], out_edge[1:]], axis=0)
-    return (out_field.transpose(1, 0, 2)[:, None], row_grads, conv_grad, proj_grad.T)
+    return (out_field[:, None], row_grads, conv_grad, proj_grad.T)
 
 
 def solution(mesh):

time: 63 us -> 64.1 us (1.017)
  waiting for transfers between devices: 21.3 us -> 22 us
    all_to_all x3, waiting for transfers between devices: 20.7 us -> 18.3 us  [exchange(): lax.all_to_all(payload.reshape(ndev, rows // ndev, width), AXES, split_ax...]
    ppermute x2, waiting for transfers between devices: 0.17 us -> 1.99 us  [swap(): lax.ppermute(block, 'gx', [(i, i ^ 1) for i in range(lax.axis_size('gx'))])]
    ppermute x6, starting transfers between devices: 9.73 us -> 8.17 us  [send(): return lax.ppermute(block, AXES, pairs)]
    all_to_all x3, starting transfers between devices: 11.3 us -> 12.8 us  [exchange(): lax.all_to_all(payload.reshape(ndev, rows // ndev, width), AXES, split_ax...]
    reshape x2, local copies, waits for them, and re-layouts: 1.72 us -> 3.13 us  [local(): taps = conv_weight.reshape(3, 3, 3, chans, chans)]
    ppermute x6, waiting for transfers between devices: 0.52 us -> 1.72 us  [send(): return lax.ppermute(block, AXES, pairs)]
    reshape x2, local copies, waits for them, and re-layouts: 1.7 us -> 0.55 us  [local(): wf = taps.transpose(1, 2, 3, 0, 4).reshape(9 * chans, rows)]
    reshape x2, local copies, waits for them, and re-layouts: 0.55 us -> 1.7 us  [local(): wb = taps.transpose(1, 0, 4, 2, 3).reshape(9 * chans, rows)]
  transfers between devices with their start and end apart: 11 -> 11, of which waited for: 5 -> 6; matrix products, arithmetic and copies ran while one was open for 9% -> 9% of each run, Pallas kernels for 16% -> 16%
where the time goes in v9:
time: 64.1 us; the launch traced here: 63.7 us
  waiting for transfers between devices  22 us (34%)
  starting transfers between devices  21.1 us (33%)
  Pallas kernels  14.1 us (22%)
  local copies, waits for them, and re-layouts  5.57 us (9%)
  between operations  0.9 us (1%)
    all_to_all x3, waiting for transfers between devices, exchange(): lax.all_to_all(payload.reshape(ndev, rows // ndev, width), AXES, split_ax...  18.3 us
    pallas_call x11, Pallas kernels, call(): pl.pallas_call(kernel, out_shape=[jax.ShapeDtypeStruct(o.shape, o.dtype)...  14.1 us
    all_to_all x3, starting transfers between devices, exchange(): lax.all_to_all(payload.reshape(ndev, rows // ndev, width), AXES, split_ax...  12.8 us
    ppermute x6, starting transfers between devices, send(): return lax.ppermute(block, AXES, pairs)  8.17 us
    reshape x2, local copies, waits for them, and re-layouts, local(): taps = conv_weight.reshape(3, 3, 3, chans, chans)  3.13 us
    ppermute x2, waiting for transfers between devices, swap(): lax.ppermute(block, 'gx', [(i, i ^ 1) for i in range(lax.axis_size('gx'))])  1.99 us
    ppermute x6, waiting for transfers between devices, send(): return lax.ppermute(block, AXES, pairs)  1.72 us
    reshape x2, local copies, waits for them, and re-layouts, local(): wb = taps.transpose(1, 0, 4, 2, 3).reshape(9 * chans, rows)  1.7 us
  transfers between devices with their start and end apart: 11, of which 6 were waited for; matrix products, arithmetic and copies ran while one was open for 9% of the time, Pallas kernels for 16%

profile of v9, /device:TPU:0, one launch (start us, length us, event | category | flops | bytes accessed | tf_op | source)
XLA Modules:
  0.0 63.7 jit_solution(6588688691621826030)
XLA Ops:
  0.6 0.0 copy-start.4
  0.6 0.0 copy-start.5
  0.7 3.4 %collective-permute-start.1 = (bf16[64,1,16,256]{3,2,0,1:T(8,128)(2,1)}, bf16[64,1,16,256]{3,2,0,1:T(8,128)(2,1)S(1)}, u32[]{:S(2)}, u32[]{:S(2)}) collective-permute-start(bf16[64,1,16,256]{3,2,0,1:T(8,128)(2,1)} %bitcast.35), channel_id=1, source_target_pairs={{0,28},{1,29},{2,30},{3,31},{4,0},{5,1},{6,2},{7,3},{8,4},{9,5},{1... | collective-permute-start | bytes 1572872 | tf_op jit(solution)/shard_map/ppermute | solution.py:51
  4.0 0.0 collective-permute-start
  4.0 1.7 %shard_map.102 = bf16[768,128]{1,0:T(8,128)(2,1)} custom-call(bf16[128,128]{1,0:T(8,128)(2,1)} %rows_far.1, s32[1,32]{1,0:T(1,128)} %counts_ref.1), custom_call_target="tpu_custom_call" | custom-call | flops 8388608 | bytes 229504 | tf_op jit(solution)/shard_map/pallas_call | solution.py:27
  5.8 6.1 %all-to-all-start = ((bf16[32,24,128]{2,1,0:T(8,128)(2,1)}), bf16[32,24,128]{2,1,0:T(8,128)(2,1)S(1)}, u32[]{:S(2)}, u32[]{:S(2)}) async-start(bf16[32,24,128]{2,1,0:T(8,128)(2,1)} %bitcast.50), calls=%async_computation | async-start | bytes 393216 | tf_op jit(solution)/shard_map/all_to_all | solution.py:60
  11.8 2.5 %collective-permute-start.3 = (s32[1,256]{1,0:T(1,128)}, s32[1,256]{1,0:T(1,128)S(1)}, u32[]{:S(2)}, u32[]{:S(2)}) collective-permute-start(s32[1,256]{1,0:T(1,128)} %own_cells.7), channel_id=1, source_target_pairs={{0,28},{1,29},{2,30},{3,31},{4,0},{5,1},{6,2},{7,3},{8,4},{9,5},{1... | collective-permute-start | bytes 3080 | tf_op jit(solution)/shard_map/ppermute | solution.py:51
  14.3 0.0 collective-permute-start.2
  14.3 2.2 %copy.31 = bf16[3,3,3,64,64]{4,0,1,3,2:T(4,128)(2,1)} copy(bf16[3,3,3,64,64]{4,3,2,1,0:T(8,128)(2,1)} %bitcast.48) | data formatting | bytes 442368 | tf_op jit(solution)/shard_map/reshape | solution.py:483
  16.5 0.0 copy-done.4
  16.5 0.9 %copy.21 = bf16[3,3,3,64,64]{3,2,1,4,0:T(4,128)(2,1)S(1)} copy(bf16[3,3,3,64,64]{4,3,2,1,0:T(8,128)(2,1)S(1)} %bitcast.49) | data formatting | bytes 442368 | tf_op jit(solution)/shard_map/reshape | solution.py:483
  17.4 0.0 copy-done.5
  17.4 0.2 copy.32
  17.6 0.0 copy-start
  17.6 0.0 copy-start.1
  17.6 0.0 copy-start.2
  17.7 1.5 %reshape.46 = bf16[576,192]{0,1:T(8,128)(2,1)S(1)} reshape(bf16[3,3,64,3,64]{2,1,0,4,3:T(4,128)(2,1)} %bitcast.47) | data formatting | bytes 442368 | tf_op jit(solution)/shard_map/reshape | solution.py:485
  19.2 0.2 copy.25.wb_ref
  19.4 0.4 reshape.45
  19.8 0.2 copy.22.wf_ref
  19.9 0.0 collective-permute-done.3.east_cells
  19.9 0.0 collective-permute-done.2.west_cells
  20.0 1.2 %all-to-all-done = bf16[32,24,128]{2,1,0:T(8,128)(2,1)S(1)} async-done(((bf16[32,24,128]{2,1,0:T(8,128)(2,1)}), bf16[32,24,128]{2,1,0:T(8,128)(2,1)S(1)}, u32[]{:S(2)}, u32[]{:S(2)}) %all-to-all-start) | async-done | bytes 196640 | tf_op jit(solution)/shard_map/all_to_all | solution.py:60
  21.2 0.0 collective-permute-done.1
  21.2 0.0 collective-permute-done
  21.2 0.0 copy-done
  21.2 0.0 copy-done.1
  21.2 0.0 copy-done.2
  21.2 0.7 %shard_map.105 = bf16[192,256]{1,0:T(8,128)(2,1)S(1)} custom-call(bf16[768,128]{1,0:T(8,128)(2,1)S(1)} %bitcast.32, bf16[64,16,256]{2,1,0:T(8,128)(2,1)S(1)} %bitcast.37, bf16[64,16,256]{2,1,0:T(8,128)(2,1)S(1)} %bitcast.41, bf16[64,16,256]{2,1,0:T(8,128)(2,1)S(1)} %bitcast.39, s32[1,256]{1,0:T(1,128)S(1)} %copy-done.2, ...), custom_call_target="tpu_custom_call" | custom-call | flops 37748736 | bytes 2632704 | tf_op jit(solution)/shard_map/pallas_call | solution.py:27
  21.9 2.2 %collective-permute-start.5 = (bf16[192,256]{1,0:T(8,128)(2,1)S(1)}, bf16[192,256]{1,0:T(8,128)(2,1)S(1)}, u32[]{:S(2)}, u32[]{:S(2)}) collective-permute-start(bf16[192,256]{1,0:T(8,128)(2,1)S(1)} %shard_map.105), channel_id=1, source_target_pairs={{0,3},{1,0},{2,1},{3,2},{4,7},{5,4},{6,5},{7,6},{8,11},{9,8},{10,9... | collective-permute-start | bytes 294920 | tf_op jit(solution)/shard_map/ppermute | solution.py:51
  24.2 1.7 %shard_map.103 = (bf16[16,192,256]{2,1,0:T(8,128)(2,1)S(1)}, bf16[192,256]{1,0:T(8,128)(2,1)S(1)}) custom-call(bf16[768,128]{1,0:T(8,128)(2,1)S(1)} %bitcast.33, bf16[64,16,256]{2,1,0:T(8,128)(2,1)S(1)} %bitcast.38, bf16[64,16,256]{2,1,0:T(8,128)(2,1)S(1)} %bitcast.42, bf16[64,16,256]{2,1,0:T(8,128)(2,1)S(1)} %bitcast.40, s32[1,256]{1,0:T(1,128)S(1)} %copy-done.2, ...), custom_call_target="tpu_custom_call" | custom-call | flops 402653184 | bytes 4205568 | tf_op jit(solution)/shard_map/pallas_call | solution.py:27
  25.9 0.1 collective-permute-start.4
  26.0 4.7 %shard_map.104 = (bf16[16,64,256]{2,1,0:T(8,128)(2,1)S(1)}, f32[576,192]{1,0:T(8,128)S(1)}, f32[4,64,256]{2,1,0:T(8,128)S(1)}, f32[4,192,256]{2,1,0:T(8,128)S(1)}, f32[3,64,256]{2,1,0:T(8,128)S(1)}) custom-call(bf16[16,192,256]{2,1,0:T(8,128)(2,1)S(1)} %get-tuple-element.24.x_ref, bf16[16,64,256]{2,1,0:T(8,128)(2,1)S(1)} %bitcast.29, ...), custom_call_target="tpu_custom_call" | custom-call | flops 2717908992 | bytes 4754432 | tf_op jit(solution)/shard_map/pallas_call | solution.py:27
  30.7 0.0 collective-permute-done.5.south_ref
  30.7 1.7 %collective-permute-done.4.north_ref = bf16[192,256]{1,0:T(8,128)(2,1)S(1)} collective-permute-done((bf16[192,256]{1,0:T(8,128)(2,1)S(1)}, bf16[192,256]{1,0:T(8,128)(2,1)S(1)}, u32[]{:S(2)}, u32[]{:S(2)}) %collective-permute-start.4) | collective-permute-done | bytes 98336 | tf_op jit(solution)/shard_map/ppermute | solution.py:51
  32.4 0.6 shard_map.106
  32.9 0.1 collective-permute-start.6
  33.0 0.6 %shard_map.107 = (bf16[32,16,128]{2,1,0:T(8,128)(2,1)S(1)}, bf16[5,16,128]{2,1,0:T(8,128)(2,1)S(1)}) custom-call(f32[4,192,256]{2,1,0:T(8,128)S(1)} %get-tuple-element.30.slot_ref, f32[3,64,256]{2,1,0:T(8,128)S(1)} %get-tuple-element.31.sums_ref, bf16[4,192,256]{2,1,0:T(8,128)(2,1)S(1)} %get-tuple-element.32.grads_ref, bf16[576,192]{1,0:T(8,128)(2,1)S(1)} %copy.25.wb_ref, ...), custom_call_target="tpu_custom_call" | custom-call | flops 113246208 | bytes 2472960 | tf_op jit(solution)/shard_map/pallas_call | solution.py:27
  33.7 0.0 copy-start.3
  33.7 0.6 %collective-permute-done.6.got_ref = bf16[27,16,128]{2,1,0:T(8,128)(2,1)S(1)} collective-permute-done((bf16[27,16,128]{2,1,0:T(8,128)(2,1)S(1)}, bf16[27,16,128]{2,1,0:T(8,128)(2,1)S(1)}, u32[]{:S(2)}, u32[]{:S(2)}) %collective-permute-start.6) | collective-permute-done | bytes 110624 | tf_op jit(solution)/shard_map/ppermute | solution.py:55
  34.3 0.7 %shard_map.108.in_ref = bf16[32,32,128]{2,1,0:T(8,128)(2,1)} custom-call(f32[27,16,128]{2,1,0:T(8,128)S(1)} %get-tuple-element.28.keep_ref, bf16[27,16,128]{2,1,0:T(8,128)(2,1)S(1)} %collective-permute-done.6.got_ref, bf16[32,16,128]{2,1,0:T(8,128)(2,1)S(1)} %get-tuple-element.33.slots_ref, bf16[5,16,128]{2,1,0:T(8,128)(2,1)S(1)} %get-tuple-element.34.proj_ref), custom_call_target="tpu_custom_call" | custom-call | flops 1000 | bytes 745472 | tf_op jit(solution)/shard_map/pallas_call | solution.py:27
  35.1 4.1 %all-to-all-start.1 = ((bf16[32,32,128]{2,1,0:T(8,128)(2,1)}), bf16[32,32,128]{2,1,0:T(8,128)(2,1)S(1)}, u32[]{:S(2)}, u32[]{:S(2)}) async-start(bf16[32,32,128]{2,1,0:T(8,128)(2,1)} %shard_map.109), calls=%async_computation.1 | async-start | bytes 524288 | tf_op jit(solution)/shard_map/all_to_all | solution.py:60
  39.1 10.2 %all-to-all-done.1.recv_ref = bf16[32,32,128]{2,1,0:T(8,128)(2,1)S(1)} async-done(((bf16[32,32,128]{2,1,0:T(8,128)(2,1)}), bf16[32,32,128]{2,1,0:T(8,128)(2,1)S(1)}, u32[]{:S(2)}, u32[]{:S(2)}) %all-to-all-start.1) | async-done | bytes 262176 | tf_op jit(solution)/shard_map/all_to_all | solution.py:60
  49.3 0.7 %shard_map.110 = bf16[32,16,128]{2,1,0:T(8,128)(2,1)} custom-call(bf16[32,32,128]{2,1,0:T(8,128)(2,1)S(1)} %all-to-all-done.1.recv_ref, s32[1,1]{1,0:T(1,128)} %bitcast.14.index_ref), custom_call_target="tpu_custom_call" | custom-call | flops 1000 | bytes 393220 | tf_op jit(solution)/shard_map/pallas_call | solution.py:27
  50.1 2.7 %all-to-all-start.2 = ((bf16[32,16,128]{2,1,0:T(8,128)(2,1)}), bf16[32,16,128]{2,1,0:T(8,128)(2,1)S(1)}, u32[]{:S(2)}, u32[]{:S(2)}) async-start(bf16[32,16,128]{2,1,0:T(8,128)(2,1)} %shard_map.110), calls=%async_computation.2 | async-start | bytes 262144 | tf_op jit(solution)/shard_map/all_to_all | solution.py:60
  52.8 0.0 copy-done.3
  52.8 1.5 %shard_map.111 = (f32[128,128]{1,0:T(8,128)}, bf16[64,16,256]{2,1,0:T(8,128)(2,1)}) custom-call(bf16[32,32,128]{2,1,0:T(8,128)(2,1)S(1)} %all-to-all-done.1.recv_ref, s32[1,32]{1,0:T(1,128)S(1)} %copy-done.3, bf16[64,128]{1,0:T(8,128)(2,1)S(1)} %bitcast.45, bf16[16,64,256]{2,1,0:T(8,128)(2,1)S(1)} %get-tuple-element.35.inner_ref, ...), custom_call_target="tpu_custom_call" | custom-call | flops 4194304 | bytes 1458304 | tf_op jit(solution)/shard_map/pallas_call | solution.py:27
  54.3 6.9 %all-to-all-done.2.mine_ref = bf16[32,16,128]{2,1,0:T(8,128)(2,1)S(1)} async-done(((bf16[32,16,128]{2,1,0:T(8,128)(2,1)}), bf16[32,16,128]{2,1,0:T(8,128)(2,1)S(1)}, u32[]{:S(2)}, u32[]{:S(2)}) %all-to-all-start.2) | async-done | bytes 131104 | tf_op jit(solution)/shard_map/all_to_all | solution.py:60
  61.2 0.0 collective-permute-start.7
  61.2 1.3 %collective-permute-done.7.other_ref = bf16[32,16,128]{2,1,0:T(8,128)(2,1)S(1)} collective-permute-done((bf16[32,16,128]{2,1,0:T(8,128)(2,1)S(1)}, bf16[32,16,128]{2,1,0:T(8,128)(2,1)S(1)}, u32[]{:S(2)}, u32[]{:S(2)}) %collective-permute-start.7) | collective-permute-done | bytes 131104 | tf_op jit(solution)/shard_map/ppermute | solution.py:55
  62.6 1.1 %shard_map.112 = (f32[27,64,64]{2,1,0:T(8,128)}, f32[64,128]{1,0:T(8,128)}) custom-call(s32[1]{0:T(128)} %bitcast.parity_ref, bf16[32,16,128]{2,1,0:T(8,128)(2,1)S(1)} %all-to-all-done.2.mine_ref, bf16[32,16,128]{2,1,0:T(8,128)(2,1)S(1)} %collective-permute-done.7.other_ref), custom_call_target="tpu_custom_call" | custom-call | flops 1000 | bytes 737284 | tf_op jit(solution)/shard_map/pallas_call | solution.py:27
  (1 shorter events, 0.0 us)
Async XLA Ops:
  0.6 15.9 %copy-start.4 = (bf16[27,64,64]{2,1,0:T(8,128)(2,1)S(1)}, bf16[27,64,64]{2,1,0:T(8,128)(2,1)}, u32[]{:S(2)}) copy-start(bf16[27,64,64]{2,1,0:T(8,128)(2,1)} %param.12) | copy-start | bytes 663556
  0.6 16.8 %copy-start.5 = (bf16[64,1,16,256]{3,2,1,0:T(8,128)(2,1)S(1)}, bf16[64,1,16,256]{3,2,1,0:T(8,128)(2,1)}, u32[]{:S(2)}) copy-start(bf16[64,1,16,256]{3,2,1,0:T(8,128)(2,1)} %param.13) | copy-start | bytes 1572868
  0.7 20.5 %collective-permute-start.1 = (bf16[64,1,16,256]{3,2,0,1:T(8,128)(2,1)}, bf16[64,1,16,256]{3,2,0,1:T(8,128)(2,1)S(1)}, u32[]{:S(2)}, u32[]{:S(2)}) collective-permute-start(bf16[64,1,16,256]{3,2,0,1:T(8,128)(2,1)} %bitcast.35), channel_id=1, source_target_pairs={{0,28},{1,29},{2,30},{3,31},{4,0},{5,1},{6,2},{7,3},{8,4},{9,5},{1... | collective-permute-start | bytes 1572872 | tf_op jit(solution)/shard_map/ppermute | solution.py:51
  4.0 17.1 %collective-permute-start = (bf16[64,1,16,256]{3,2,0,1:T(8,128)(2,1)}, bf16[64,1,16,256]{3,2,0,1:T(8,128)(2,1)S(1)}, u32[]{:S(2)}, u32[]{:S(2)}) collective-permute-start(bf16[64,1,16,256]{3,2,0,1:T(8,128)(2,1)} %bitcast.36), channel_id=1, source_target_pairs={{0,4},{1,5},{2,6},{3,7},{4,8},{5,9},{6,10},{7,11},{8,12},{9,13},{1... | collective-permute-start | bytes 1572872 | tf_op jit(solution)/shard_map/ppermute | solution.py:51
  5.8 15.4 %all-to-all-start = ((bf16[32,24,128]{2,1,0:T(8,128)(2,1)}), bf16[32,24,128]{2,1,0:T(8,128)(2,1)S(1)}, u32[]{:S(2)}, u32[]{:S(2)}) async-start(bf16[32,24,128]{2,1,0:T(8,128)(2,1)} %bitcast.50), calls=%async_computation | async-start | bytes 393216 | tf_op jit(solution)/shard_map/all_to_all | solution.py:60
  11.8 8.1 %collective-permute-start.3 = (s32[1,256]{1,0:T(1,128)}, s32[1,256]{1,0:T(1,128)S(1)}, u32[]{:S(2)}, u32[]{:S(2)}) collective-permute-start(s32[1,256]{1,0:T(1,128)} %own_cells.7), channel_id=1, source_target_pairs={{0,28},{1,29},{2,30},{3,31},{4,0},{5,1},{6,2},{7,3},{8,4},{9,5},{1... | collective-permute-start | bytes 3080 | tf_op jit(solution)/shard_map/ppermute | solution.py:51
  14.3 5.7 %collective-permute-start.2 = (s32[1,256]{1,0:T(1,128)}, s32[1,256]{1,0:T(1,128)S(1)}, u32[]{:S(2)}, u32[]{:S(2)}) collective-permute-start(s32[1,256]{1,0:T(1,128)} %own_cells.7), channel_id=1, source_target_pairs={{0,4},{1,5},{2,6},{3,7},{4,8},{5,9},{6,10},{7,11},{8,12},{9,13},{1... | collective-permute-start | bytes 3080 | tf_op jit(solution)/shard_map/ppermute | solution.py:51
  17.6 3.5 %copy-start = (bf16[64,1,16,256]{3,2,1,0:T(8,128)(2,1)S(1)}, bf16[64,1,16,256]{3,2,1,0:T(8,128)(2,1)}, u32[]{:S(2)}) copy-start(bf16[64,1,16,256]{3,2,1,0:T(8,128)(2,1)} %param.10) | copy-start | bytes 1572868
  17.6 3.5 %copy-start.1 = (bf16[128,64]{0,1:T(8,128)(2,1)S(1)}, bf16[128,64]{0,1:T(8,128)(2,1)}, u32[]{:S(2)}) copy-start(bf16[128,64]{0,1:T(8,128)(2,1)} %param.11) | copy-start | bytes 49156
  17.6 3.5 %copy-start.2 = (s32[1,256]{1,0:T(1,128)S(1)}, s32[1,256]{1,0:T(1,128)}, u32[]{:S(2)}) copy-start(s32[1,256]{1,0:T(1,128)} %own_cells.7) | copy-start | bytes 3076
  21.9 8.7 %collective-permute-start.5 = (bf16[192,256]{1,0:T(8,128)(2,1)S(1)}, bf16[192,256]{1,0:T(8,128)(2,1)S(1)}, u32[]{:S(2)}, u32[]{:S(2)}) collective-permute-start(bf16[192,256]{1,0:T(8,128)(2,1)S(1)} %shard_map.105), channel_id=1, source_target_pairs={{0,3},{1,0},{2,1},{3,2},{4,7},{5,4},{6,5},{7,6},{8,11},{9,8},{10,9... | collective-permute-start | bytes 294920 | tf_op jit(solution)/shard_map/ppermute | solution.py:51
  25.9 6.5 %collective-permute-start.4 = (bf16[192,256]{1,0:T(8,128)(2,1)S(1)}, bf16[192,256]{1,0:T(8,128)(2,1)S(1)}, u32[]{:S(2)}, u32[]{:S(2)}) collective-permute-start(bf16[192,256]{1,0:T(8,128)(2,1)S(1)} %get-tuple-element.27), channel_id=1, source_target_pairs={{0,1},{1,2},{2,3},{3,0},{4,5},{5,6},{6,7},{7,4},{8,9},{9,10},{10,1... | collective-permute-start | bytes 294920 | tf_op jit(solution)/shard_map/ppermute | solution.py:51
  32.9 1.4 %collective-permute-start.6 = (bf16[27,16,128]{2,1,0:T(8,128)(2,1)S(1)}, bf16[27,16,128]{2,1,0:T(8,128)(2,1)S(1)}, u32[]{:S(2)}, u32[]{:S(2)}) collective-permute-start(bf16[27,16,128]{2,1,0:T(8,128)(2,1)S(1)} %get-tuple-element.29), channel_id=1, source_target_pairs={{0,4},{4,0},{8,12},{12,8},{16,20},{20,16},{24,28},{28,24},{1,5},{5... | collective-permute-start | bytes 331784 | tf_op jit(solution)/shard_map/ppermute | solution.py:55
  33.7 19.1 %copy-start.3 = (s32[1,32]{1,0:T(1,128)S(1)}, s32[1,32]{1,0:T(1,128)}, u32[]{:S(2)}) copy-start(s32[1,32]{1,0:T(1,128)} %counts_ref.1) | copy-start | bytes 388
  35.1 14.3 %all-to-all-start.1 = ((bf16[32,32,128]{2,1,0:T(8,128)(2,1)}), bf16[32,32,128]{2,1,0:T(8,128)(2,1)S(1)}, u32[]{:S(2)}, u32[]{:S(2)}) async-start(bf16[32,32,128]{2,1,0:T(8,128)(2,1)} %shard_map.109), calls=%async_computation.1 | async-start | bytes 524288 | tf_op jit(solution)/shard_map/all_to_all | solution.py:60
  50.1 11.1 %all-to-all-start.2 = ((bf16[32,16,128]{2,1,0:T(8,128)(2,1)}), bf16[32,16,128]{2,1,0:T(8,128)(2,1)S(1)}, u32[]{:S(2)}, u32[]{:S(2)}) async-start(bf16[32,16,128]{2,1,0:T(8,128)(2,1)} %shard_map.110), calls=%async_computation.2 | async-start | bytes 262144 | tf_op jit(solution)/shard_map/all_to_all | solution.py:60
  61.2 1.3 %collective-permute-start.7 = (bf16[32,16,128]{2,1,0:T(8,128)(2,1)S(1)}, bf16[32,16,128]{2,1,0:T(8,128)(2,1)S(1)}, u32[]{:S(2)}, u32[]{:S(2)}) collective-permute-start(bf16[32,16,128]{2,1,0:T(8,128)(2,1)S(1)} %all-to-all-done.2.mine_ref), channel_id=1, source_target_pairs={{0,4},{4,0},{8,12},{12,8},{16,20},{20,16},{24,28},{28,24},{1,5},{5... | collective-permute-start | bytes 393224 | tf_op jit(solution)/shard_map/ppermute | solution.py:55

commit v10 on v9

--- a/solution.py
+++ b/solution.py
@@ -142,16 +142,16 @@
     out_ref[...] = jnp.stack(parts, axis=1).reshape(out_ref.shape).astype(BF16)
 
 
-def painted_rows(values, cells, nz, ns, masked):
+def painted_rows(values, y, onehot, ns, masked):
     chans = values.shape[0]
-    y, z = cells
     for n, row in enumerate(ns):
         masked[pl.ds(n * chans, chans)] = values * jnp.where(y == row, 1.0, 0.0).astype(BF16)
-    return mm(masked[pl.ds(0, len(ns) * chans)], picked_depth(z, nz), NT)
-
-
-def add_to_rows(near, far, cot, rows, back, out_ref):
+    return mm(masked[pl.ds(0, len(ns) * chans)], onehot, NT)
+
+
+def add_to_rows(near, far, cot, back, out_ref):
     chans = cot.shape[0]
+    rows = 3 * chans
     at, over = (rows, 0) if back else (0, rows)
     out_ref[pl.ds(0, chans)] = over_depth(near[at : at + rows]).astype(BF16)
     out_ref[pl.ds(chans, chans)] = over_depth(near[over : over + rows] + far).astype(BF16)
@@ -160,40 +160,28 @@
 
 def outer_kernel(
     ndev, cap, recv_ref, own_ref, west_ref, east_ref, own_cells, west_cells, east_cells,
-    proj_t_ref, cot_ref, wf_ref, first_ref, masked, field,
+    proj_t_ref, cot_ref, wf_ref, first_ref, last_ref, values_ref, hot_ref, masked, field,
 ):
     chans, cy, nz = own_ref.shape
     rows = 3 * chans
     raws = rows_in(recv_ref, ndev, cap)
+    ns = (0, 1, cy - 2, cy - 1)
     planes = ((west_ref, west_cells), (own_ref, own_cells), (east_ref, east_cells))
     for dx, (ref, cells_ref) in enumerate(planes):
         values = mm(proj_t_ref[...], raws[dx], NT).astype(BF16)
-        painted = painted_rows(values, place(cells_ref, nz), nz, (0, 1), masked)
+        y, z = place(cells_ref, nz)
+        onehot = picked_depth(z, nz)
+        values_ref[dx] = values
+        hot_ref[dx] = onehot
+        painted = painted_rows(values, y, onehot, ns, masked)
         base = turned(ref)
-        for n in range(2):
+        for n, row in enumerate(ns):
             part = painted[n * chans : (n + 1) * chans]
-            field[n, pl.ds(dx * chans, chans)] = (base[n] + part).astype(BF16)
+            field[n, pl.ds(dx * chans, chans)] = (base[row] + part).astype(BF16)
+    near = mm(wf_ref[pl.ds(0, 2 * rows)], field[3])
+    add_to_rows(near, mm(wf_ref[pl.ds(0, rows)], field[2]), cot_ref[cy - 1], False, last_ref)
     near = mm(wf_ref[pl.ds(rows, 2 * rows)], field[0])
-    far = mm(wf_ref[pl.ds(2 * rows, rows)], field[1])
-    add_to_rows(near, far, cot_ref[0], rows, True, first_ref)
-
-
-def field_kernel(
-    ndev, cap, recv_ref, own_ref, west_ref, east_ref, own_cells, west_cells, east_cells,
-    proj_t_ref, cot_ref, wf_ref, x_ref, last_ref, masked,
-):
-    chans, cy, nz = own_ref.shape
-    rows = 3 * chans
-    raws = rows_in(recv_ref, ndev, cap)
-    planes = ((west_ref, west_cells), (own_ref, own_cells), (east_ref, east_cells))
-    for dx, (ref, cells_ref) in enumerate(planes):
-        values = mm(proj_t_ref[...], raws[dx], NT).astype(BF16)
-        painted = painted_rows(values, place(cells_ref, nz), nz, range(cy), masked)
-        field = turned(ref) + painted.reshape(cy, chans, nz)
-        x_ref[:, pl.ds(dx * chans, chans)] = field.astype(BF16)
-    near = mm(wf_ref[pl.ds(0, 2 * rows)], x_ref[cy - 1])
-    far = mm(wf_ref[pl.ds(0, rows)], x_ref[cy - 2])
-    add_to_rows(near, far, cot_ref[cy - 1], rows, False, last_ref)
+    add_to_rows(near, mm(wf_ref[pl.ds(2 * rows, rows)], field[1]), cot_ref[0], True, first_ref)
 
 
 def place(cells_ref, nz):
@@ -206,12 +194,18 @@
 
 
 def conv_kernel(
-    x_ref, cot_ref, wf_ref, wb_ref, own_cells, west_cells, east_cells,
-    out_ref, total_ref, pre_ref, slot_ref, sums_ref, acc, grads, back, plane,
+    values_ref, hot_ref, own_ref, west_ref, east_ref, own_cells, west_cells, east_cells,
+    cot_ref, wf_ref, wb_ref,
+    x_ref, out_ref, total_ref, pre_ref, slot_ref, plane, acc, grads, back, masked,
 ):
     cy, chans, nz = cot_ref.shape
     rows = 3 * chans
-    slots = own_cells.shape[1]
+    planes = ((west_ref, west_cells), (own_ref, own_cells), (east_ref, east_cells))
+    for dx, (ref, cells_ref) in enumerate(planes):
+        y, _ = place(cells_ref, nz)
+        painted = painted_rows(values_ref[dx], y, hot_ref[dx], range(cy), masked)
+        field = turned(ref) + painted.reshape(cy, chans, nz)
+        x_ref[:, pl.ds(dx * chans, chans)] = field.astype(BF16)
     own = pl.ds(chans, chans)
     zeros = jnp.zeros((rows, nz), BF16)
     for t in (0, 1, cy, cy + 1):
@@ -273,15 +267,12 @@
     taps(cy - 1)
     slot_ref[2] = back[cy - 2]
     slot_ref[3] = back[cy - 1]
-    zero = jnp.zeros((chans, slots), F32)
-    for dx, cells_ref in enumerate((west_cells, own_cells, east_cells)):
-        sums_ref[dx] = at_slots(plane[dx], place(cells_ref, nz), range(2, cy - 2), zero)
-
-
-def at_slots(part, cells, first, total):
-    chans = total.shape[0]
-    y, z = cells
-    found = mm(part, picked_depth(z, part.shape[1]))
+
+
+def at_slots(part, y, onehot, first):
+    found = mm(part, onehot)
+    chans = found.shape[0] // len(first)
+    total = jnp.zeros((chans, found.shape[1]), F32)
     for n, row in enumerate(first):
         total = total + jnp.where(y == row, found[n * chans : (n + 1) * chans], 0.0)
     return total
@@ -323,7 +314,7 @@
 
 
 def slots_kernel(
-    ndev, cap, part, full, slot_ref, sums_ref, grads_ref, wb_ref, cot_ref,
+    ndev, cap, part, full, slot_ref, plane_ref, hot_ref, grads_ref, wb_ref, cot_ref,
     own_cells, west_cells, east_cells, recv_ref, slots_ref, proj_ref,
 ):
     cy, chans, nz = cot_ref.shape
@@ -340,8 +331,10 @@
         parts = [value[dx * chans : (dx + 1) * chans] for value in (top, second, third, bottom)]
         if dx == 1:
             parts = [value + cot_ref[n].astype(F32) for value, n in zip(parts, at)]
-        terms = jnp.concatenate(parts, axis=0).astype(BF16)
-        found.append(at_slots(terms, place(cells_ref, nz), at, sums_ref[dx]))
+        parts = [value.astype(BF16) for value in parts]
+        terms = jnp.concatenate([plane_ref[dx], *parts], axis=0)
+        y, _ = place(cells_ref, nz)
+        found.append(at_slots(terms, y, hot_ref[dx], (*range(2, cy - 2), *at)))
     sides = jnp.concatenate([found[0], found[2]], axis=0).T
     middle = jnp.concatenate([found[1], jnp.zeros_like(found[1])], axis=0).T
     width = recv_ref.shape[1]
@@ -484,39 +477,32 @@
     wf = taps.transpose(1, 2, 3, 0, 4).reshape(9 * chans, rows)
     wb = taps.transpose(1, 0, 4, 2, 3).reshape(9 * chans, rows)
 
-    inputs = (recv, *planes, *lists, proj_t, cot, wf)
-    (first,) = call(
+    first, last, values, hots = call(
         functools.partial(outer_kernel, ndev, cap),
-        [shape((rows, nz), BF16)],
-        inputs,
-        2 * one,
-        (pltpu.VMEM((2 * chans, slots), BF16), pltpu.VMEM((2, rows, nz), BF16)),
-    )
-    south = move(first, 0, -1)
-    x_all, last = call(
-        functools.partial(field_kernel, ndev, cap),
-        [shape((cy, rows, nz), BF16), shape((rows, nz), BF16)],
-        inputs,
-        6 * slots * count * chans,
-        (pltpu.VMEM((cy * chans, slots), BF16),),
-    )
-    north = move(last, 0, 1)
-    out_rows, total, pre_edge, slot_edge, sums = call(
+        [shape((rows, nz), BF16)] * 2
+        + [shape((3, chans, slots), BF16), shape((3, nz, slots), BF16)],
+        (recv, *planes, *lists, proj_t, cot, wf),
+        4 * one,
+        (pltpu.VMEM((4 * chans, slots), BF16), pltpu.VMEM((4, rows, nz), BF16)),
+    )
+    south, north = move(first, 0, -1), move(last, 0, 1)
+    x_all, out_rows, total, pre_edge, slot_edge, plane = call(
         conv_kernel,
         [
+            shape((cy, rows, nz), BF16),
             shape((cy, chans, nz), BF16),
             shape((9 * chans, rows), F32),
             shape((4, chans, nz), F32),
             shape((4, rows, nz), F32),
-            shape((3, chans, slots), F32),
+            shape((3, (cy - 4) * chans, nz), BF16),
         ],
-        (x_all, cot, wf, wb, *lists),
+        (values, hots, *planes, *lists, cot, wf, wb),
         3 * cy * 3 * one,
         (
             pltpu.VMEM((cy + 1, rows, nz), F32),
             pltpu.VMEM((cy + 2, rows, nz), BF16),
             pltpu.VMEM((cy, rows, nz), F32),
-            pltpu.VMEM((3, (cy - 4) * chans, nz), BF16),
+            pltpu.VMEM((cy * chans, slots), BF16),
         ),
     )
     grad_rows = 27 * chans * chans // feats
@@ -542,7 +528,7 @@
     back, proj = call(
         functools.partial(slots_kernel, ndev, cap, part, full),
         [shape((ndev, 2 * cap, feats), BF16), shape((ndev - full, part, feats), BF16)],
-        (slot_edge, sums, grads, wb, cot, *lists, recv),
+        (slot_edge, plane, hots, grads, wb, cot, *lists, recv),
         6 * one,
     )
     (payload,) = call(

time: 64.1 us -> 61.6 us (0.961)
  waiting for transfers between devices: 22 us -> 20.5 us
    ppermute x6, waiting for transfers between devices: 1.72 us -> 0.02 us  [send(): return lax.ppermute(block, AXES, pairs)]
    ppermute x6, starting transfers between devices: 8.17 us -> 9.73 us  [send(): return lax.ppermute(block, AXES, pairs)]
    all_to_all x3, starting transfers between devices: 12.8 us -> 11.3 us  [exchange(): lax.all_to_all(payload.reshape(ndev, rows // ndev, width), AXES, split_ax...]
    reshape x2, local copies, waits for them, and re-layouts: 1.7 us -> 0.55 us  [local(): wb = taps.transpose(1, 0, 4, 2, 3).reshape(9 * chans, rows)]
    reshape x2, local copies, waits for them, and re-layouts: 0.55 us -> 1.65 us  [local(): wf = taps.transpose(1, 2, 3, 0, 4).reshape(9 * chans, rows)]
    pallas_call x11 -> x10, Pallas kernels: 14.1 us -> 13.5 us  [call(): pl.pallas_call(kernel, out_shape=[jax.ShapeDtypeStruct(o.shape, o.dtype)...]
  transfers between devices with their start and end apart: 11 -> 11, of which waited for: 6 -> 5; matrix products, arithmetic and copies ran while one was open for 9% -> 8% of each run, Pallas kernels for 16% -> 15%
where the time goes in v10:
time: 61.6 us; the launch traced here: 61.2 us
  starting transfers between devices  21.1 us (34%)
  waiting for transfers between devices  20.5 us (33%)
  Pallas kernels  13.5 us (22%)
  local copies, waits for them, and re-layouts  5.13 us (8%)
  between operations  0.89 us (1%)
    all_to_all x3, waiting for transfers between devices, exchange(): lax.all_to_all(payload.reshape(ndev, rows // ndev, width), AXES, split_ax...  18.7 us
    pallas_call x10, Pallas kernels, call(): pl.pallas_call(kernel, out_shape=[jax.ShapeDtypeStruct(o.shape, o.dtype)...  13.5 us
    all_to_all x3, starting transfers between devices, exchange(): lax.all_to_all(payload.reshape(ndev, rows // ndev, width), AXES, split_ax...  11.3 us
    ppermute x6, starting transfers between devices, send(): return lax.ppermute(block, AXES, pairs)  9.73 us
    reshape x2, local copies, waits for them, and re-layouts, local(): taps = conv_weight.reshape(3, 3, 3, chans, chans)  2.74 us
    ppermute x2, waiting for transfers between devices, swap(): lax.ppermute(block, 'gx', [(i, i ^ 1) for i in range(lax.axis_size('gx'))])  1.74 us
    reshape x2, local copies, waits for them, and re-layouts, local(): wf = taps.transpose(1, 2, 3, 0, 4).reshape(9 * chans, rows)  1.65 us
  transfers between devices with their start and end apart: 11, of which 5 were waited for; matrix products, arithmetic and copies ran while one was open for 8% of the time, Pallas kernels for 15%

profile of v10, /device:TPU:0, one launch (start us, length us, event | category | flops | bytes accessed | tf_op | source)
XLA Modules:
  0.0 61.2 jit_solution(13050263407097229230)
XLA Ops:
  0.6 0.0 copy-start.4
  0.6 0.0 copy-start.5
  0.7 3.4 %collective-permute-start.1 = (bf16[64,1,16,256]{3,2,0,1:T(8,128)(2,1)}, bf16[64,1,16,256]{3,2,0,1:T(8,128)(2,1)S(1)}, u32[]{:S(2)}, u32[]{:S(2)}) collective-permute-start(bf16[64,1,16,256]{3,2,0,1:T(8,128)(2,1)} %bitcast.33), channel_id=1, source_target_pairs={{0,28},{1,29},{2,30},{3,31},{4,0},{5,1},{6,2},{7,3},{8,4},{9,5},{1... | collective-permute-start | bytes 1572872 | tf_op jit(solution)/shard_map/ppermute | solution.py:51
  4.0 0.0 collective-permute-start
  4.0 1.7 %shard_map.102 = bf16[768,128]{1,0:T(8,128)(2,1)} custom-call(bf16[128,128]{1,0:T(8,128)(2,1)} %rows_far.1, s32[1,32]{1,0:T(1,128)} %counts_ref.1), custom_call_target="tpu_custom_call" | custom-call | flops 8388608 | bytes 229504 | tf_op jit(solution)/shard_map/pallas_call | solution.py:27
  5.8 6.1 %all-to-all-start = ((bf16[32,24,128]{2,1,0:T(8,128)(2,1)}), bf16[32,24,128]{2,1,0:T(8,128)(2,1)S(1)}, u32[]{:S(2)}, u32[]{:S(2)}) async-start(bf16[32,24,128]{2,1,0:T(8,128)(2,1)} %bitcast.47), calls=%async_computation | async-start | bytes 393216 | tf_op jit(solution)/shard_map/all_to_all | solution.py:60
  11.8 2.5 %collective-permute-start.3 = (s32[1,256]{1,0:T(1,128)}, s32[1,256]{1,0:T(1,128)S(1)}, u32[]{:S(2)}, u32[]{:S(2)}) collective-permute-start(s32[1,256]{1,0:T(1,128)} %own_cells.5), channel_id=1, source_target_pairs={{0,28},{1,29},{2,30},{3,31},{4,0},{5,1},{6,2},{7,3},{8,4},{9,5},{1... | collective-permute-start | bytes 3080 | tf_op jit(solution)/shard_map/ppermute | solution.py:51
  14.3 0.0 collective-permute-start.2
  14.3 1.4 %copy.30 = bf16[3,3,3,64,64]{4,0,1,3,2:T(4,128)(2,1)S(1)} copy(bf16[3,3,3,64,64]{4,3,2,1,0:T(8,128)(2,1)} %bitcast.45) | data formatting | bytes 442368 | tf_op jit(solution)/shard_map/reshape | solution.py:476
  15.7 0.0 copy-done.4
  15.7 1.3 %copy.21 = bf16[3,3,3,64,64]{3,2,1,4,0:T(4,128)(2,1)} copy(bf16[3,3,3,64,64]{4,3,2,1,0:T(8,128)(2,1)S(1)} %bitcast.46) | data formatting | bytes 442368 | tf_op jit(solution)/shard_map/reshape | solution.py:476
  17.1 0.0 copy-done.5
  17.1 0.2 copy.31
  17.2 0.0 copy-start
  17.2 0.0 copy-start.1
  17.2 0.0 copy-start.2
  17.3 0.4 reshape.46
  17.7 0.2 copy.25.wb_ref
  17.8 1.5 %reshape.45 = bf16[576,192]{0,1:T(8,128)(2,1)S(1)} reshape(bf16[3,3,64,3,64]{2,1,0,4,3:T(4,128)(2,1)} %bitcast.43) | data formatting | bytes 442368 | tf_op jit(solution)/shard_map/reshape | solution.py:477
  19.3 0.2 copy.22.wf_ref
  19.5 0.0 collective-permute-done.3.east_cells
  19.5 0.0 collective-permute-done.2.west_cells
  19.5 1.6 %all-to-all-done = bf16[32,24,128]{2,1,0:T(8,128)(2,1)S(1)} async-done(((bf16[32,24,128]{2,1,0:T(8,128)(2,1)}), bf16[32,24,128]{2,1,0:T(8,128)(2,1)S(1)}, u32[]{:S(2)}, u32[]{:S(2)}) %all-to-all-start) | async-done | bytes 196640 | tf_op jit(solution)/shard_map/all_to_all | solution.py:60
  21.2 0.0 collective-permute-done.1
  21.2 0.0 collective-permute-done
  21.2 0.0 copy-done
  21.2 0.0 copy-done.1
  21.2 0.0 copy-done.2
  21.2 1.0 %shard_map.103 = (bf16[192,256]{1,0:T(8,128)(2,1)S(1)}, bf16[192,256]{1,0:T(8,128)(2,1)S(1)}, bf16[3,64,256]{2,1,0:T(8,128)(2,1)S(1)}, bf16[3,256,256]{2,1,0:T(8,128)(2,1)S(1)}) custom-call(bf16[768,128]{1,0:T(8,128)(2,1)S(1)} %bitcast.31, bf16[64,16,256]{2,1,0:T(8,128)(2,1)S(1)} %bitcast.35, bf16[64,16,256]{2,1,0:T(8,128)(2,1)S(1)} %bitcast.39, ...), custom_call_target="tpu_custom_call" | custom-call | flops 75497472 | bytes 3222528 | tf_op jit(solution)/shard_map/pallas_call | solution.py:27
  22.2 0.1 collective-permute-start.4
  22.3 3.8 %collective-permute-start.5 = (bf16[192,256]{1,0:T(8,128)(2,1)S(1)}, bf16[192,256]{1,0:T(8,128)(2,1)S(1)}, u32[]{:S(2)}, u32[]{:S(2)}) collective-permute-start(bf16[192,256]{1,0:T(8,128)(2,1)S(1)} %get-tuple-element.32), channel_id=1, source_target_pairs={{0,3},{1,0},{2,1},{3,2},{4,7},{5,4},{6,5},{7,6},{8,11},{9,8},{10,9... | collective-permute-start | bytes 294920 | tf_op jit(solution)/shard_map/ppermute | solution.py:51
  26.1 5.3 %shard_map.104 = (bf16[16,192,256]{2,1,0:T(8,128)(2,1)S(1)}, bf16[16,64,256]{2,1,0:T(8,128)(2,1)S(1)}, f32[576,192]{1,0:T(8,128)S(1)}, f32[4,64,256]{2,1,0:T(8,1...) custom-call(bf16[3,64,256]{2,1,0:T(8,128)(2,1)S(1)} %get-tuple-element.27.values_ref, ...), custom_call_target="tpu_custom_call" | custom-call | flops 2717908992 | bytes 7801856 | tf_op jit(solution)/shard_map/pallas_call | solution.py:27
  31.4 0.0 collective-permute-done.4.north_ref
  31.4 0.0 collective-permute-done.5.south_ref
  31.4 0.6 shard_map.105
  32.0 0.1 collective-permute-start.6
  32.0 0.9 %shard_map.106 = (bf16[32,16,128]{2,1,0:T(8,128)(2,1)S(1)}, bf16[5,16,128]{2,1,0:T(8,128)(2,1)S(1)}) custom-call(f32[4,192,256]{2,1,0:T(8,128)S(1)} %get-tuple-element.36.slot_ref, bf16[3,768,256]{2,1,0:T(8,128)(2,1)S(1)} %get-tuple-element.37.plane_ref, bf16[3,256,256]{2,1,0:T(8,128)(2,1)S(1)} %get-tuple-element.28.hot_ref, ...), custom_call_target="tpu_custom_call" | custom-call | flops 113246208 | bytes 3849216 | tf_op jit(solution)/shard_map/pallas_call | solution.py:27
  32.9 0.0 copy-start.3
  32.9 0.4 collective-permute-done.6.got_ref
  33.3 0.7 %shard_map.107.in_ref = bf16[32,32,128]{2,1,0:T(8,128)(2,1)} custom-call(f32[27,16,128]{2,1,0:T(8,128)S(1)} %get-tuple-element.34.keep_ref, bf16[27,16,128]{2,1,0:T(8,128)(2,1)S(1)} %collective-permute-done.6.got_ref, bf16[32,16,128]{2,1,0:T(8,128)(2,1)S(1)} %get-tuple-element.39.slots_ref, bf16[5,16,128]{2,1,0:T(8,128)(2,1)S(1)} %get-tuple-element.40.proj_ref), custom_call_target="tpu_custom_call" | custom-call | flops 1000 | bytes 745472 | tf_op jit(solution)/shard_map/pallas_call | solution.py:27
  34.1 2.6 %all-to-all-start.1 = ((bf16[32,32,128]{2,1,0:T(8,128)(2,1)}), bf16[32,32,128]{2,1,0:T(8,128)(2,1)S(1)}, u32[]{:S(2)}, u32[]{:S(2)}) async-start(bf16[32,32,128]{2,1,0:T(8,128)(2,1)} %shard_map.108), calls=%async_computation.1 | async-start | bytes 524288 | tf_op jit(solution)/shard_map/all_to_all | solution.py:60
  36.7 10.2 %all-to-all-done.1.recv_ref = bf16[32,32,128]{2,1,0:T(8,128)(2,1)S(1)} async-done(((bf16[32,32,128]{2,1,0:T(8,128)(2,1)}), bf16[32,32,128]{2,1,0:T(8,128)(2,1)S(1)}, u32[]{:S(2)}, u32[]{:S(2)}) %all-to-all-start.1) | async-done | bytes 262176 | tf_op jit(solution)/shard_map/all_to_all | solution.py:60
  46.9 0.7 %shard_map.109 = bf16[32,16,128]{2,1,0:T(8,128)(2,1)} custom-call(bf16[32,32,128]{2,1,0:T(8,128)(2,1)S(1)} %all-to-all-done.1.recv_ref, s32[1,1]{1,0:T(1,128)} %bitcast.14.index_ref), custom_call_target="tpu_custom_call" | custom-call | flops 1000 | bytes 393220 | tf_op jit(solution)/shard_map/pallas_call | solution.py:27
  47.6 2.7 %all-to-all-start.2 = ((bf16[32,16,128]{2,1,0:T(8,128)(2,1)}), bf16[32,16,128]{2,1,0:T(8,128)(2,1)S(1)}, u32[]{:S(2)}, u32[]{:S(2)}) async-start(bf16[32,16,128]{2,1,0:T(8,128)(2,1)} %shard_map.109), calls=%async_computation.2 | async-start | bytes 262144 | tf_op jit(solution)/shard_map/all_to_all | solution.py:60
  50.3 0.0 copy-done.3
  50.3 1.5 %shard_map.110 = (f32[128,128]{1,0:T(8,128)}, bf16[64,16,256]{2,1,0:T(8,128)(2,1)}) custom-call(bf16[32,32,128]{2,1,0:T(8,128)(2,1)S(1)} %all-to-all-done.1.recv_ref, s32[1,32]{1,0:T(1,128)S(1)} %copy-done.3, bf16[64,128]{1,0:T(8,128)(2,1)S(1)} %bitcast.42, bf16[16,64,256]{2,1,0:T(8,128)(2,1)S(1)} %get-tuple-element.41.inner_ref, ...), custom_call_target="tpu_custom_call" | custom-call | flops 4194304 | bytes 1458304 | tf_op jit(solution)/shard_map/pallas_call | solution.py:27
  51.9 6.9 %all-to-all-done.2.mine_ref = bf16[32,16,128]{2,1,0:T(8,128)(2,1)S(1)} async-done(((bf16[32,16,128]{2,1,0:T(8,128)(2,1)}), bf16[32,16,128]{2,1,0:T(8,128)(2,1)S(1)}, u32[]{:S(2)}, u32[]{:S(2)}) %all-to-all-start.2) | async-done | bytes 131104 | tf_op jit(solution)/shard_map/all_to_all | solution.py:60
  58.7 0.0 collective-permute-start.7
  58.7 1.3 %collective-permute-done.7.other_ref = bf16[32,16,128]{2,1,0:T(8,128)(2,1)S(1)} collective-permute-done((bf16[32,16,128]{2,1,0:T(8,128)(2,1)S(1)}, bf16[32,16,128]{2,1,0:T(8,128)(2,1)S(1)}, u32[]{:S(2)}, u32[]{:S(2)}) %collective-permute-start.7) | collective-permute-done | bytes 131104 | tf_op jit(solution)/shard_map/ppermute | solution.py:55
  60.1 1.1 %shard_map.111 = (f32[27,64,64]{2,1,0:T(8,128)}, f32[64,128]{1,0:T(8,128)}) custom-call(s32[1]{0:T(128)} %bitcast.parity_ref, bf16[32,16,128]{2,1,0:T(8,128)(2,1)S(1)} %all-to-all-done.2.mine_ref, bf16[32,16,128]{2,1,0:T(8,128)(2,1)S(1)} %collective-permute-done.7.other_ref), custom_call_target="tpu_custom_call" | custom-call | flops 1000 | bytes 737284 | tf_op jit(solution)/shard_map/pallas_call | solution.py:27
  (1 shorter events, 0.0 us)
Async XLA Ops:
  0.6 15.1 %copy-start.4 = (bf16[27,64,64]{2,1,0:T(8,128)(2,1)S(1)}, bf16[27,64,64]{2,1,0:T(8,128)(2,1)}, u32[]{:S(2)}) copy-start(bf16[27,64,64]{2,1,0:T(8,128)(2,1)} %param.12) | copy-start | bytes 663556
  0.6 16.4 %copy-start.5 = (bf16[64,1,16,256]{3,2,1,0:T(8,128)(2,1)S(1)}, bf16[64,1,16,256]{3,2,1,0:T(8,128)(2,1)}, u32[]{:S(2)}) copy-start(bf16[64,1,16,256]{3,2,1,0:T(8,128)(2,1)} %param.13) | copy-start | bytes 1572868
  0.7 20.5 %collective-permute-start.1 = (bf16[64,1,16,256]{3,2,0,1:T(8,128)(2,1)}, bf16[64,1,16,256]{3,2,0,1:T(8,128)(2,1)S(1)}, u32[]{:S(2)}, u32[]{:S(2)}) collective-permute-start(bf16[64,1,16,256]{3,2,0,1:T(8,128)(2,1)} %bitcast.33), channel_id=1, source_target_pairs={{0,28},{1,29},{2,30},{3,31},{4,0},{5,1},{6,2},{7,3},{8,4},{9,5},{1... | collective-permute-start | bytes 1572872 | tf_op jit(solution)/shard_map/ppermute | solution.py:51
  4.0 17.1 %collective-permute-start = (bf16[64,1,16,256]{3,2,0,1:T(8,128)(2,1)}, bf16[64,1,16,256]{3,2,0,1:T(8,128)(2,1)S(1)}, u32[]{:S(2)}, u32[]{:S(2)}) collective-permute-start(bf16[64,1,16,256]{3,2,0,1:T(8,128)(2,1)} %bitcast.34), channel_id=1, source_target_pairs={{0,4},{1,5},{2,6},{3,7},{4,8},{5,9},{6,10},{7,11},{8,12},{9,13},{1... | collective-permute-start | bytes 1572872 | tf_op jit(solution)/shard_map/ppermute | solution.py:51
  5.8 15.4 %all-to-all-start = ((bf16[32,24,128]{2,1,0:T(8,128)(2,1)}), bf16[32,24,128]{2,1,0:T(8,128)(2,1)S(1)}, u32[]{:S(2)}, u32[]{:S(2)}) async-start(bf16[32,24,128]{2,1,0:T(8,128)(2,1)} %bitcast.47), calls=%async_computation | async-start | bytes 393216 | tf_op jit(solution)/shard_map/all_to_all | solution.py:60
  11.8 7.7 %collective-permute-start.3 = (s32[1,256]{1,0:T(1,128)}, s32[1,256]{1,0:T(1,128)S(1)}, u32[]{:S(2)}, u32[]{:S(2)}) collective-permute-start(s32[1,256]{1,0:T(1,128)} %own_cells.5), channel_id=1, source_target_pairs={{0,28},{1,29},{2,30},{3,31},{4,0},{5,1},{6,2},{7,3},{8,4},{9,5},{1... | collective-permute-start | bytes 3080 | tf_op jit(solution)/shard_map/ppermute | solution.py:51
  14.3 5.2 %collective-permute-start.2 = (s32[1,256]{1,0:T(1,128)}, s32[1,256]{1,0:T(1,128)S(1)}, u32[]{:S(2)}, u32[]{:S(2)}) collective-permute-start(s32[1,256]{1,0:T(1,128)} %own_cells.5), channel_id=1, source_target_pairs={{0,4},{1,5},{2,6},{3,7},{4,8},{5,9},{6,10},{7,11},{8,12},{9,13},{1... | collective-permute-start | bytes 3080 | tf_op jit(solution)/shard_map/ppermute | solution.py:51
  17.2 3.9 %copy-start = (bf16[64,1,16,256]{3,2,1,0:T(8,128)(2,1)S(1)}, bf16[64,1,16,256]{3,2,1,0:T(8,128)(2,1)}, u32[]{:S(2)}) copy-start(bf16[64,1,16,256]{3,2,1,0:T(8,128)(2,1)} %param.10) | copy-start | bytes 1572868
  17.2 3.9 %copy-start.1 = (bf16[128,64]{0,1:T(8,128)(2,1)S(1)}, bf16[128,64]{0,1:T(8,128)(2,1)}, u32[]{:S(2)}) copy-start(bf16[128,64]{0,1:T(8,128)(2,1)} %param.11) | copy-start | bytes 49156
  17.2 3.9 %copy-start.2 = (s32[1,256]{1,0:T(1,128)S(1)}, s32[1,256]{1,0:T(1,128)}, u32[]{:S(2)}) copy-start(s32[1,256]{1,0:T(1,128)} %own_cells.5) | copy-start | bytes 3076
  22.2 9.2 %collective-permute-start.4 = (bf16[192,256]{1,0:T(8,128)(2,1)S(1)}, bf16[192,256]{1,0:T(8,128)(2,1)S(1)}, u32[]{:S(2)}, u32[]{:S(2)}) collective-permute-start(bf16[192,256]{1,0:T(8,128)(2,1)S(1)} %get-tuple-element.31), channel_id=1, source_target_pairs={{0,1},{1,2},{2,3},{3,0},{4,5},{5,6},{6,7},{7,4},{8,9},{9,10},{10,1... | collective-permute-start | bytes 294920 | tf_op jit(solution)/shard_map/ppermute | solution.py:51
  22.3 9.1 %collective-permute-start.5 = (bf16[192,256]{1,0:T(8,128)(2,1)S(1)}, bf16[192,256]{1,0:T(8,128)(2,1)S(1)}, u32[]{:S(2)}, u32[]{:S(2)}) collective-permute-start(bf16[192,256]{1,0:T(8,128)(2,1)S(1)} %get-tuple-element.32), channel_id=1, source_target_pairs={{0,3},{1,0},{2,1},{3,2},{4,7},{5,4},{6,5},{7,6},{8,11},{9,8},{10,9... | collective-permute-start | bytes 294920 | tf_op jit(solution)/shard_map/ppermute | solution.py:51
  32.0 1.4 %collective-permute-start.6 = (bf16[27,16,128]{2,1,0:T(8,128)(2,1)S(1)}, bf16[27,16,128]{2,1,0:T(8,128)(2,1)S(1)}, u32[]{:S(2)}, u32[]{:S(2)}) collective-permute-start(bf16[27,16,128]{2,1,0:T(8,128)(2,1)S(1)} %get-tuple-element.35), channel_id=1, source_target_pairs={{0,4},{4,0},{8,12},{12,8},{16,20},{20,16},{24,28},{28,24},{1,5},{5... | collective-permute-start | bytes 331784 | tf_op jit(solution)/shard_map/ppermute | solution.py:55
  32.9 17.4 %copy-start.3 = (s32[1,32]{1,0:T(1,128)S(1)}, s32[1,32]{1,0:T(1,128)}, u32[]{:S(2)}) copy-start(s32[1,32]{1,0:T(1,128)} %counts_ref.1) | copy-start | bytes 388
  34.1 12.8 %all-to-all-start.1 = ((bf16[32,32,128]{2,1,0:T(8,128)(2,1)}), bf16[32,32,128]{2,1,0:T(8,128)(2,1)S(1)}, u32[]{:S(2)}, u32[]{:S(2)}) async-start(bf16[32,32,128]{2,1,0:T(8,128)(2,1)} %shard_map.108), calls=%async_computation.1 | async-start | bytes 524288 | tf_op jit(solution)/shard_map/all_to_all | solution.py:60
  47.6 11.1 %all-to-all-start.2 = ((bf16[32,16,128]{2,1,0:T(8,128)(2,1)}), bf16[32,16,128]{2,1,0:T(8,128)(2,1)S(1)}, u32[]{:S(2)}, u32[]{:S(2)}) async-start(bf16[32,16,128]{2,1,0:T(8,128)(2,1)} %shard_map.109), calls=%async_computation.2 | async-start | bytes 262144 | tf_op jit(solution)/shard_map/all_to_all | solution.py:60
  58.7 1.3 %collective-permute-start.7 = (bf16[32,16,128]{2,1,0:T(8,128)(2,1)S(1)}, bf16[32,16,128]{2,1,0:T(8,128)(2,1)S(1)}, u32[]{:S(2)}, u32[]{:S(2)}) collective-permute-start(bf16[32,16,128]{2,1,0:T(8,128)(2,1)S(1)} %all-to-all-done.2.mine_ref), channel_id=1, source_target_pairs={{0,4},{4,0},{8,12},{12,8},{16,20},{20,16},{24,28},{28,24},{1,5},{5... | collective-permute-start | bytes 393224 | tf_op jit(solution)/shard_map/ppermute | solution.py:55

commit v11 on v10

--- a/solution.py
+++ b/solution.py
@@ -314,8 +314,8 @@
 
 
 def slots_kernel(
-    ndev, cap, part, full, slot_ref, plane_ref, hot_ref, grads_ref, wb_ref, cot_ref,
-    own_cells, west_cells, east_cells, recv_ref, slots_ref, proj_ref,
+    parity_ref, slot_ref, plane_ref, hot_ref, grads_ref, wb_ref, cot_ref,
+    own_cells, west_cells, east_cells, terms_ref, give_ref,
 ):
     cy, chans, nz = cot_ref.shape
     rows = 3 * chans
@@ -326,7 +326,6 @@
     third = slot_ref[2] + inner[:rows]
     bottom = slot_ref[3] + inner[rows:] + mm(wb_ref[pl.ds(0, rows)], grads_ref[3])
     at = (0, 1, cy - 2, cy - 1)
-    found = []
     for dx, cells_ref in enumerate((west_cells, own_cells, east_cells)):
         parts = [value[dx * chans : (dx + 1) * chans] for value in (top, second, third, bottom)]
         if dx == 1:
@@ -334,32 +333,37 @@
         parts = [value.astype(BF16) for value in parts]
         terms = jnp.concatenate([plane_ref[dx], *parts], axis=0)
         y, _ = place(cells_ref, nz)
-        found.append(at_slots(terms, y, hot_ref[dx], (*range(2, cy - 2), *at)))
-    sides = jnp.concatenate([found[0], found[2]], axis=0).T
-    middle = jnp.concatenate([found[1], jnp.zeros_like(found[1])], axis=0).T
-    width = recv_ref.shape[1]
-    back = [sides.reshape(ndev, cap, width), middle.reshape(ndev, cap, width)]
-    slots_ref[...] = jnp.concatenate(back, axis=1).astype(BF16)
+        terms_ref[dx] = at_slots(terms, y, hot_ref[dx], (*range(2, cy - 2), *at))
+    give_ref[...] = terms_ref[2 - 2 * parity_ref[0]].astype(BF16)
+
+
+def proj_kernel(ndev, cap, parity_ref, terms_ref, recv_ref, proj_ref, outer_ref):
     raws = rows_in(recv_ref, ndev, cap)
-    proj = sum(mm(found[dx].astype(BF16), raws[dx]) for dx in range(3))
-    rest = ndev - full
-    pad = jnp.zeros((rest * part - chans, width), F32)
+    proj = sum(mm(terms_ref[dx].astype(BF16), raws[dx]) for dx in range(3))
+    rest, part, width = proj_ref.shape
+    pad = jnp.zeros((rest * part - proj.shape[0], width), F32)
     proj = jnp.concatenate([proj, pad], axis=0).reshape(rest, part, width)
     proj_ref[...] = proj.astype(BF16)
-
-
-def pair_kernel(keep_ref, got_ref, slots_ref, proj_ref, send_far, sums_send, sems):
-    full, part, _ = keep_ref.shape
-    ndev, back, _ = slots_ref.shape
+    outer_ref[...] = terms_ref[2 * parity_ref[0]]
+
+
+def pair_kernel(
+    keep_ref, got_ref, terms_ref, got_terms_ref, outer_ref, proj_ref, send_far, sums_send, slots_send, sems
+):
+    full, part, width = keep_ref.shape
+    ndev, back, _ = slots_send.shape
     pieces = (
-        (slots_ref, send_far.at[:, pl.ds(part, back)]),
         (proj_ref, send_far.at[pl.ds(full, ndev - full), pl.ds(0, part)]),
         (sums_send, send_far.at[pl.ds(0, full), pl.ds(0, part)]),
+        (slots_send, send_far.at[:, pl.ds(part, back)]),
     )
     copies = [pltpu.make_async_copy(src, dst, sems.at[n]) for n, (src, dst) in enumerate(pieces)]
     copies[0].start()
+    sums_send[...] = (keep_ref[...] + got_ref[...].astype(F32)).astype(BF16)
     copies[1].start()
-    sums_send[...] = (keep_ref[...] + got_ref[...].astype(F32)).astype(BF16)
+    own = terms_ref[1] + got_terms_ref[...].astype(F32)
+    terms = jnp.concatenate([own, outer_ref[...]], axis=0).T
+    slots_send[...] = terms.reshape(slots_send.shape).astype(BF16)
     copies[2].start()
     for copy in copies:
         copy.wait()
@@ -367,7 +371,7 @@
 
 def sums_kernel(ngx, ngy, full, cap, recv_ref, index_ref, sums_ref):
     ndev, each, width = recv_ref.shape
-    part = each - 2 * cap
+    part = each - cap
     terms = recv_ref[:, pl.ds(0, part)].astype(F32).reshape(ngx // 2, 2, ngy, part, width)
     sums = jnp.sum(terms, axis=(0, 2))
     whole = sums[0] + sums[1]
@@ -388,12 +392,11 @@
     nrows = rows_ref.shape[0]
     width = recv_ref.shape[2]
     slots = ndev * cap
-    share = recv_ref.shape[1] - 2 * cap
-    arrived = recv_ref[:, pl.ds(share, 2 * cap)].astype(F32)
-    sides = arrived[:, :cap].reshape(ngx, ngy, cap, width)
-    left = lax.broadcasted_iota(I32, sides.shape, 3) < chans
-    sides = jnp.where(left, rolled(sides, 1, 0), rolled(sides, -1, 0)).reshape(slots, width)
-    middle = arrived[:, cap:].reshape(slots, width)
+    part = recv_ref.shape[1] - cap
+    arrived = recv_ref[:, pl.ds(part, cap)].astype(F32).reshape(ngx, ngy, cap, width)
+    outer = [arrived[(i - 1) % ngx if i % 2 == 0 else (i + 1) % ngx] for i in range(ngx)]
+    left = lax.broadcasted_iota(I32, arrived.shape, 3) < chans
+    terms = jnp.where(left, arrived, jnp.stack(outer, axis=0)).reshape(slots, width)
     counts = counts_ref[...].astype(F32)
     place = lax.broadcasted_iota(I32, (nrows, ndev), 0).astype(F32)
     lane = lax.broadcasted_iota(I32, (ndev, ndev), 1)
@@ -408,9 +411,8 @@
     ).astype(BF16)
     proj_t = proj_t_ref[...]
     both = jnp.concatenate([proj_t, proj_t], axis=0)
-    sides = mm(onehot, sides.astype(BF16)).astype(BF16)
-    middle = mm(onehot, middle.astype(BF16)).astype(BF16)
-    rows_ref[...] = mm(sides, both) + mm(middle, both)
+    picked = mm(onehot, terms.astype(BF16)).astype(BF16)
+    rows_ref[...] = mm(picked, both)
     cy = inner_ref.shape[0]
     field = jnp.concatenate([ends_ref[:1], inner_ref[1 : cy - 1], ends_ref[1:]], axis=0)
     out_ref[...] = jnp.swapaxes(field.astype(F32), 0, 1).astype(BF16)
@@ -525,18 +527,31 @@
         scalar=(0,),
     )
     got = swap(give)
-    back, proj = call(
-        functools.partial(slots_kernel, ndev, cap, part, full),
-        [shape((ndev, 2 * cap, feats), BF16), shape((ndev - full, part, feats), BF16)],
-        (slot_edge, plane, hots, grads, wb, cot, *lists, recv),
+    terms, give = call(
+        slots_kernel,
+        [shape((3, chans, slots), F32), shape((chans, slots), BF16)],
+        (parity, slot_edge, plane, hots, grads, wb, cot, *lists),
         6 * one,
+        scalar=(0,),
+    )
+    got_terms = swap(give)
+    proj, outer = call(
+        functools.partial(proj_kernel, ndev, cap),
+        [shape((ndev - full, part, feats), BF16), shape((chans, slots), F32)],
+        (parity, terms, recv),
+        one,
+        scalar=(0,),
     )
     (payload,) = call(
         pair_kernel,
-        [shape((ndev, part + 2 * cap, feats), BF16)],
-        (keep, got, back, proj),
+        [shape((ndev, part + cap, feats), BF16)],
+        (keep, got, terms, got_terms, outer, proj),
         1000,
-        (pltpu.VMEM((full, part, feats), BF16), pltpu.SemaphoreType.DMA((3,))),
+        (
+            pltpu.VMEM((full, part, feats), BF16),
+            pltpu.VMEM((ndev, cap, feats), BF16),
+            pltpu.SemaphoreType.DMA((3,)),
+        ),
         far_out=(0,),
     )
     (payload,) = call(same_kernel, [payload], (payload,), 0, far=(0,), far_out=(0,), aliases={0: 0})

time: 61.6 us -> 64.7 us (1.050)
  local copies, waits for them, and re-layouts: 5.13 us -> 8.76 us
  waiting for transfers between devices: 20.5 us -> 18.3 us
  starting transfers between devices: 21.1 us -> 22.7 us
    reshape x2, local copies, waits for them, and re-layouts: 0.55 us -> 3.25 us  [local(): wb = taps.transpose(1, 0, 4, 2, 3).reshape(9 * chans, rows)]
    all_to_all x3, waiting for transfers between devices: 18.7 us -> 16.2 us  [exchange(): lax.all_to_all(payload.reshape(ndev, rows // ndev, width), AXES, split_ax...]
    all_to_all x3, starting transfers between devices: 11.3 us -> 12.3 us  [exchange(): lax.all_to_all(payload.reshape(ndev, rows // ndev, width), AXES, split_ax...]
    ppermute x2 -> x3, waiting for transfers between devices: 1.74 us -> 2.04 us  [swap(): lax.ppermute(block, 'gx', [(i, i ^ 1) for i in range(lax.axis_size('gx'))])]
    pallas_call x10 -> x11, Pallas kernels: 13.5 us -> 13.6 us  [call(): pl.pallas_call(kernel, out_shape=[jax.ShapeDtypeStruct(o.shape, o.dtype)...]
  transfers between devices with their start and end apart: 11 -> 12, of which waited for: 5 -> 4; matrix products, arithmetic and copies ran while one was open for 8% -> 14% of each run, Pallas kernels for 15% -> 15%
where the time goes in v11:
time: 64.7 us; the launch traced here: 64.2 us
  starting transfers between devices  22.7 us (35%)
  waiting for transfers between devices  18.3 us (28%)
  Pallas kernels  13.6 us (21%)
  local copies, waits for them, and re-layouts  8.76 us (14%)
  between operations  0.91 us (1%)
    all_to_all x3, waiting for transfers between devices, exchange(): lax.all_to_all(payload.reshape(ndev, rows // ndev, width), AXES, split_ax...  16.2 us
    pallas_call x11, Pallas kernels, call(): pl.pallas_call(kernel, out_shape=[jax.ShapeDtypeStruct(o.shape, o.dtype)...  13.6 us
    all_to_all x3, starting transfers between devices, exchange(): lax.all_to_all(payload.reshape(ndev, rows // ndev, width), AXES, split_ax...  12.3 us
    ppermute x6, starting transfers between devices, send(): return lax.ppermute(block, AXES, pairs)  9.74 us
    reshape x2, local copies, waits for them, and re-layouts, local(): wb = taps.transpose(1, 0, 4, 2, 3).reshape(9 * chans, rows)  3.25 us
    reshape x2, local copies, waits for them, and re-layouts, local(): taps = conv_weight.reshape(3, 3, 3, chans, chans)  3.13 us
    reshape x2, local copies, waits for them, and re-layouts, local(): wf = taps.transpose(1, 2, 3, 0, 4).reshape(9 * chans, rows)  2.19 us
    ppermute x3, waiting for transfers between devices, swap(): lax.ppermute(block, 'gx', [(i, i ^ 1) for i in range(lax.axis_size('gx'))])  2.04 us
  transfers between devices with their start and end apart: 12, of which 4 were waited for; matrix products, arithmetic and copies ran while one was open for 14% of the time, Pallas kernels for 15%

profile of v11, /device:TPU:0, one launch (start us, length us, event | category | flops | bytes accessed | tf_op | source)
XLA Modules:
  0.0 64.2 jit_solution(10359310991230734416)
XLA Ops:
  0.6 0.0 copy-start.4
  0.6 0.0 copy-start.5
  0.7 3.4 %collective-permute-start.1 = (bf16[64,1,16,256]{3,2,0,1:T(8,128)(2,1)}, bf16[64,1,16,256]{3,2,0,1:T(8,128)(2,1)S(1)}, u32[]{:S(2)}, u32[]{:S(2)}) collective-permute-start(bf16[64,1,16,256]{3,2,0,1:T(8,128)(2,1)} %bitcast.33), channel_id=1, source_target_pairs={{0,28},{1,29},{2,30},{3,31},{4,0},{5,1},{6,2},{7,3},{8,4},{9,5},{1... | collective-permute-start | bytes 1572872 | tf_op jit(solution)/shard_map/ppermute | solution.py:51
  4.0 0.0 collective-permute-start
  4.0 1.7 %shard_map.102 = bf16[768,128]{1,0:T(8,128)(2,1)} custom-call(bf16[128,128]{1,0:T(8,128)(2,1)} %rows_far.1, s32[1,32]{1,0:T(1,128)} %counts_ref.1), custom_call_target="tpu_custom_call" | custom-call | flops 8388608 | bytes 229504 | tf_op jit(solution)/shard_map/pallas_call | solution.py:27
  5.8 6.1 %all-to-all-start = ((bf16[32,24,128]{2,1,0:T(8,128)(2,1)}), bf16[32,24,128]{2,1,0:T(8,128)(2,1)S(1)}, u32[]{:S(2)}, u32[]{:S(2)}) async-start(bf16[32,24,128]{2,1,0:T(8,128)(2,1)} %bitcast.47), calls=%async_computation | async-start | bytes 393216 | tf_op jit(solution)/shard_map/all_to_all | solution.py:60
  11.8 2.5 %collective-permute-start.3 = (s32[1,256]{1,0:T(1,128)}, s32[1,256]{1,0:T(1,128)S(1)}, u32[]{:S(2)}, u32[]{:S(2)}) collective-permute-start(s32[1,256]{1,0:T(1,128)} %own_cells.5), channel_id=1, source_target_pairs={{0,28},{1,29},{2,30},{3,31},{4,0},{5,1},{6,2},{7,3},{8,4},{9,5},{1... | collective-permute-start | bytes 3080 | tf_op jit(solution)/shard_map/ppermute | solution.py:51
  14.3 0.0 collective-permute-start.2
  14.3 2.2 %copy.30 = bf16[3,3,3,64,64]{4,0,1,3,2:T(4,128)(2,1)} copy(bf16[3,3,3,64,64]{4,3,2,1,0:T(8,128)(2,1)} %bitcast.45) | data formatting | bytes 442368 | tf_op jit(solution)/shard_map/reshape | solution.py:478
  16.5 0.0 copy-done.4
  16.5 0.9 %copy.21 = bf16[3,3,3,64,64]{3,2,1,4,0:T(4,128)(2,1)S(1)} copy(bf16[3,3,3,64,64]{4,3,2,1,0:T(8,128)(2,1)S(1)} %bitcast.46) | data formatting | bytes 442368 | tf_op jit(solution)/shard_map/reshape | solution.py:478
  17.4 0.0 copy-done.5
  17.4 0.2 copy.31
  17.6 0.0 copy-start
  17.6 0.0 copy-start.1
  17.6 0.0 copy-start.2
  17.6 2.2 %reshape.46 = bf16[576,192]{0,1:T(8,128)(2,1)} reshape(bf16[3,3,64,3,64]{2,1,0,4,3:T(4,128)(2,1)} %bitcast.44) | data formatting | bytes 442368 | tf_op jit(solution)/shard_map/reshape | solution.py:480
  19.8 1.1 %copy.25.wb_ref = bf16[576,192]{1,0:T(8,128)(2,1)S(1)} copy(bf16[576,192]{0,1:T(8,128)(2,1)} %reshape.46) | data formatting | bytes 442368 | tf_op jit(solution)/shard_map/reshape | solution.py:480
  20.9 1.1 %reshape.45 = bf16[576,192]{0,1:T(8,128)(2,1)} reshape(bf16[3,3,64,3,64]{2,1,0,4,3:T(4,128)(2,1)S(1)} %bitcast.43) | data formatting | bytes 442368 | tf_op jit(solution)/shard_map/reshape | solution.py:479
  22.0 1.1 %copy.22.wf_ref = bf16[576,192]{1,0:T(8,128)(2,1)S(1)} copy(bf16[576,192]{0,1:T(8,128)(2,1)} %reshape.45) | data formatting | bytes 442368 | tf_op jit(solution)/shard_map/reshape | solution.py:479
  23.1 0.0 collective-permute-done.3.east_cells
  23.1 0.0 collective-permute-done.2.west_cells
  23.1 0.0 all-to-all-done
  23.1 0.0 collective-permute-done.1
  23.1 0.0 collective-permute-done
  23.2 0.0 copy-done
  23.2 0.0 copy-done.1
  23.2 0.0 copy-done.2
  23.2 1.0 %shard_map.103 = (bf16[192,256]{1,0:T(8,128)(2,1)S(1)}, bf16[192,256]{1,0:T(8,128)(2,1)S(1)}, bf16[3,64,256]{2,1,0:T(8,128)(2,1)S(1)}, bf16[3,256,256]{2,1,0:T(8,128)(2,1)S(1)}) custom-call(bf16[768,128]{1,0:T(8,128)(2,1)S(1)} %bitcast.31, bf16[64,16,256]{2,1,0:T(8,128)(2,1)S(1)} %bitcast.35, bf16[64,16,256]{2,1,0:T(8,128)(2,1)S(1)} %bitcast.39, ...), custom_call_target="tpu_custom_call" | custom-call | flops 75497472 | bytes 3222528 | tf_op jit(solution)/shard_map/pallas_call | solution.py:27
  24.2 1.5 %collective-permute-start.4 = (bf16[192,256]{1,0:T(8,128)(2,1)S(1)}, bf16[192,256]{1,0:T(8,128)(2,1)S(1)}, u32[]{:S(2)}, u32[]{:S(2)}) collective-permute-start(bf16[192,256]{1,0:T(8,128)(2,1)S(1)} %get-tuple-element.33), channel_id=1, source_target_pairs={{0,1},{1,2},{2,3},{3,0},{4,5},{5,6},{6,7},{7,4},{8,9},{9,10},{10,1... | collective-permute-start | bytes 294920 | tf_op jit(solution)/shard_map/ppermute | solution.py:51
  25.7 2.4 %collective-permute-start.5 = (bf16[192,256]{1,0:T(8,128)(2,1)S(1)}, bf16[192,256]{1,0:T(8,128)(2,1)S(1)}, u32[]{:S(2)}, u32[]{:S(2)}) collective-permute-start(bf16[192,256]{1,0:T(8,128)(2,1)S(1)} %get-tuple-element.34), channel_id=1, source_target_pairs={{0,3},{1,0},{2,1},{3,2},{4,7},{5,4},{6,5},{7,6},{8,11},{9,8},{10,9... | collective-permute-start | bytes 294920 | tf_op jit(solution)/shard_map/ppermute | solution.py:51
  28.1 5.3 %shard_map.104 = (bf16[16,192,256]{2,1,0:T(8,128)(2,1)S(1)}, bf16[16,64,256]{2,1,0:T(8,128)(2,1)S(1)}, f32[576,192]{1,0:T(8,128)S(1)}, f32[4,64,256]{2,1,0:T(8,1...) custom-call(bf16[3,64,256]{2,1,0:T(8,128)(2,1)S(1)} %get-tuple-element.29.values_ref, ...), custom_call_target="tpu_custom_call" | custom-call | flops 2717908992 | bytes 7801856 | tf_op jit(solution)/shard_map/pallas_call | solution.py:27
  33.4 0.0 collective-permute-done.4.north_ref
  33.4 0.0 collective-permute-done.5.south_ref
  33.4 0.6 shard_map.105
  34.0 0.1 collective-permute-start.6
  34.0 0.8 %shard_map.106 = (f32[3,64,256]{2,1,0:T(8,128)S(1)}, bf16[64,256]{1,0:T(8,128)(2,1)S(1)}) custom-call(s32[1]{0:T(128)} %bitcast.parity_ref, f32[4,192,256]{2,1,0:T(8,128)S(1)} %get-tuple-element.38.slot_ref, bf16[3,768,256]{2,1,0:T(8,128)(2,1)S(1)} %get-tuple-element.39.plane_ref, bf16[3,256,256]{2,1,0:T(8,128)(2,1)S(1)} %get-tuple-element.30.hot_ref, ...), custom_call_target="tpu_custom_call" | custom-call | flops 113246208 | bytes 3730436 | tf_op jit(solution)/shard_map/pallas_call | solution.py:27
  34.8 0.0 copy-start.3
  34.8 0.6 collective-permute-start.7
  35.4 0.2 shard_map.107
  35.6 0.7 %collective-permute-done.7.got_terms_ref = bf16[64,256]{1,0:T(8,128)(2,1)S(1)} collective-permute-done((bf16[64,256]{1,0:T(8,128)(2,1)S(1)}, bf16[64,256]{1,0:T(8,128)(2,1)S(1)}, u32[]{:S(2)}, u32[]{:S(2)}) %collective-permute-start.7) | collective-permute-done | bytes 32800 | tf_op jit(solution)/shard_map/ppermute | solution.py:55
  36.2 0.0 collective-permute-done.6.got_ref
  36.2 0.8 %shard_map.108.in_ref = bf16[32,24,128]{2,1,0:T(8,128)(2,1)} custom-call(f32[27,16,128]{2,1,0:T(8,128)S(1)} %get-tuple-element.36.keep_ref, bf16[27,16,128]{2,1,0:T(8,128)(2,1)S(1)} %collective-permute-done.6.got_ref, f32[3,64,256]{2,1,0:T(8,128)S(1)} %get-tuple-element.41.terms_ref, bf16[64,256]{1,0:T(8,128)(2,1)S(1)} %collective-permute-done.7.got_terms_ref, ...), custom_call_target="tpu_custom_call" | custom-call | flops 1000 | bytes 843776 | tf_op jit(solution)/shard_map/pallas_call | solution.py:27
  37.0 3.7 %all-to-all-start.1 = ((bf16[32,24,128]{2,1,0:T(8,128)(2,1)}), bf16[32,24,128]{2,1,0:T(8,128)(2,1)S(1)}, u32[]{:S(2)}, u32[]{:S(2)}) async-start(bf16[32,24,128]{2,1,0:T(8,128)(2,1)} %shard_map.109), calls=%async_computation.1 | async-start | bytes 393216 | tf_op jit(solution)/shard_map/all_to_all | solution.py:60
  40.7 9.3 %all-to-all-done.1.recv_ref = bf16[32,24,128]{2,1,0:T(8,128)(2,1)S(1)} async-done(((bf16[32,24,128]{2,1,0:T(8,128)(2,1)}), bf16[32,24,128]{2,1,0:T(8,128)(2,1)S(1)}, u32[]{:S(2)}, u32[]{:S(2)}) %all-to-all-start.1) | async-done | bytes 196640 | tf_op jit(solution)/shard_map/all_to_all | solution.py:60
  50.1 0.7 %shard_map.110 = bf16[32,16,128]{2,1,0:T(8,128)(2,1)} custom-call(bf16[32,24,128]{2,1,0:T(8,128)(2,1)S(1)} %all-to-all-done.1.recv_ref, s32[1,1]{1,0:T(1,128)} %bitcast.14.index_ref), custom_call_target="tpu_custom_call" | custom-call | flops 1000 | bytes 327684 | tf_op jit(solution)/shard_map/pallas_call | solution.py:27
  50.8 2.6 %all-to-all-start.2 = ((bf16[32,16,128]{2,1,0:T(8,128)(2,1)}), bf16[32,16,128]{2,1,0:T(8,128)(2,1)S(1)}, u32[]{:S(2)}, u32[]{:S(2)}) async-start(bf16[32,16,128]{2,1,0:T(8,128)(2,1)} %shard_map.110), calls=%async_computation.2 | async-start | bytes 262144 | tf_op jit(solution)/shard_map/all_to_all | solution.py:60
  53.4 0.0 copy-done.3
  53.4 1.5 %shard_map.111 = (f32[128,128]{1,0:T(8,128)}, bf16[64,16,256]{2,1,0:T(8,128)(2,1)}) custom-call(bf16[32,24,128]{2,1,0:T(8,128)(2,1)S(1)} %all-to-all-done.1.recv_ref, s32[1,32]{1,0:T(1,128)S(1)} %copy-done.3, bf16[64,128]{1,0:T(8,128)(2,1)S(1)} %bitcast.42, bf16[16,64,256]{2,1,0:T(8,128)(2,1)S(1)} %get-tuple-element.45.inner_ref, ...), custom_call_target="tpu_custom_call" | custom-call | flops 4194304 | bytes 1392768 | tf_op jit(solution)/shard_map/pallas_call | solution.py:27
  54.9 6.9 %all-to-all-done.2.mine_ref = bf16[32,16,128]{2,1,0:T(8,128)(2,1)S(1)} async-done(((bf16[32,16,128]{2,1,0:T(8,128)(2,1)}), bf16[32,16,128]{2,1,0:T(8,128)(2,1)S(1)}, u32[]{:S(2)}, u32[]{:S(2)}) %all-to-all-start.2) | async-done | bytes 131104 | tf_op jit(solution)/shard_map/all_to_all | solution.py:60
  61.8 0.0 collective-permute-start.8
  61.8 1.3 %collective-permute-done.8.other_ref = bf16[32,16,128]{2,1,0:T(8,128)(2,1)S(1)} collective-permute-done((bf16[32,16,128]{2,1,0:T(8,128)(2,1)S(1)}, bf16[32,16,128]{2,1,0:T(8,128)(2,1)S(1)}, u32[]{:S(2)}, u32[]{:S(2)}) %collective-permute-start.8) | collective-permute-done | bytes 131104 | tf_op jit(solution)/shard_map/ppermute | solution.py:55
  63.1 1.1 %shard_map.112 = (f32[27,64,64]{2,1,0:T(8,128)}, f32[64,128]{1,0:T(8,128)}) custom-call(s32[1]{0:T(128)} %bitcast.parity_ref, bf16[32,16,128]{2,1,0:T(8,128)(2,1)S(1)} %all-to-all-done.2.mine_ref, bf16[32,16,128]{2,1,0:T(8,128)(2,1)S(1)} %collective-permute-done.8.other_ref), custom_call_target="tpu_custom_call" | custom-call | flops 1000 | bytes 737284 | tf_op jit(solution)/shard_map/pallas_call | solution.py:27
  (1 shorter events, 0.0 us)
Async XLA Ops:
  0.6 15.9 %copy-start.4 = (bf16[27,64,64]{2,1,0:T(8,128)(2,1)S(1)}, bf16[27,64,64]{2,1,0:T(8,128)(2,1)}, u32[]{:S(2)}) copy-start(bf16[27,64,64]{2,1,0:T(8,128)(2,1)} %param.12) | copy-start | bytes 663556
  0.6 16.8 %copy-start.5 = (bf16[64,1,16,256]{3,2,1,0:T(8,128)(2,1)S(1)}, bf16[64,1,16,256]{3,2,1,0:T(8,128)(2,1)}, u32[]{:S(2)}) copy-start(bf16[64,1,16,256]{3,2,1,0:T(8,128)(2,1)} %param.13) | copy-start | bytes 1572868
  0.7 22.5 %collective-permute-start.1 = (bf16[64,1,16,256]{3,2,0,1:T(8,128)(2,1)}, bf16[64,1,16,256]{3,2,0,1:T(8,128)(2,1)S(1)}, u32[]{:S(2)}, u32[]{:S(2)}) collective-permute-start(bf16[64,1,16,256]{3,2,0,1:T(8,128)(2,1)} %bitcast.33), channel_id=1, source_target_pairs={{0,28},{1,29},{2,30},{3,31},{4,0},{5,1},{6,2},{7,3},{8,4},{9,5},{1... | collective-permute-start | bytes 1572872 | tf_op jit(solution)/shard_map/ppermute | solution.py:51
  4.0 19.1 %collective-permute-start = (bf16[64,1,16,256]{3,2,0,1:T(8,128)(2,1)}, bf16[64,1,16,256]{3,2,0,1:T(8,128)(2,1)S(1)}, u32[]{:S(2)}, u32[]{:S(2)}) collective-permute-start(bf16[64,1,16,256]{3,2,0,1:T(8,128)(2,1)} %bitcast.34), channel_id=1, source_target_pairs={{0,4},{1,5},{2,6},{3,7},{4,8},{5,9},{6,10},{7,11},{8,12},{9,13},{1... | collective-permute-start | bytes 1572872 | tf_op jit(solution)/shard_map/ppermute | solution.py:51
  5.8 17.4 %all-to-all-start = ((bf16[32,24,128]{2,1,0:T(8,128)(2,1)}), bf16[32,24,128]{2,1,0:T(8,128)(2,1)S(1)}, u32[]{:S(2)}, u32[]{:S(2)}) async-start(bf16[32,24,128]{2,1,0:T(8,128)(2,1)} %bitcast.47), calls=%async_computation | async-start | bytes 393216 | tf_op jit(solution)/shard_map/all_to_all | solution.py:60
  11.8 11.3 %collective-permute-start.3 = (s32[1,256]{1,0:T(1,128)}, s32[1,256]{1,0:T(1,128)S(1)}, u32[]{:S(2)}, u32[]{:S(2)}) collective-permute-start(s32[1,256]{1,0:T(1,128)} %own_cells.5), channel_id=1, source_target_pairs={{0,28},{1,29},{2,30},{3,31},{4,0},{5,1},{6,2},{7,3},{8,4},{9,5},{1... | collective-permute-start | bytes 3080 | tf_op jit(solution)/shard_map/ppermute | solution.py:51
  14.3 8.8 %collective-permute-start.2 = (s32[1,256]{1,0:T(1,128)}, s32[1,256]{1,0:T(1,128)S(1)}, u32[]{:S(2)}, u32[]{:S(2)}) collective-permute-start(s32[1,256]{1,0:T(1,128)} %own_cells.5), channel_id=1, source_target_pairs={{0,4},{1,5},{2,6},{3,7},{4,8},{5,9},{6,10},{7,11},{8,12},{9,13},{1... | collective-permute-start | bytes 3080 | tf_op jit(solution)/shard_map/ppermute | solution.py:51
  17.6 5.5 %copy-start = (bf16[64,1,16,256]{3,2,1,0:T(8,128)(2,1)S(1)}, bf16[64,1,16,256]{3,2,1,0:T(8,128)(2,1)}, u32[]{:S(2)}) copy-start(bf16[64,1,16,256]{3,2,1,0:T(8,128)(2,1)} %param.10) | copy-start | bytes 1572868
  17.6 5.5 %copy-start.1 = (bf16[128,64]{0,1:T(8,128)(2,1)S(1)}, bf16[128,64]{0,1:T(8,128)(2,1)}, u32[]{:S(2)}) copy-start(bf16[128,64]{0,1:T(8,128)(2,1)} %param.11) | copy-start | bytes 49156
  17.6 5.5 %copy-start.2 = (s32[1,256]{1,0:T(1,128)S(1)}, s32[1,256]{1,0:T(1,128)}, u32[]{:S(2)}) copy-start(s32[1,256]{1,0:T(1,128)} %own_cells.5) | copy-start | bytes 3076
  24.2 9.2 %collective-permute-start.4 = (bf16[192,256]{1,0:T(8,128)(2,1)S(1)}, bf16[192,256]{1,0:T(8,128)(2,1)S(1)}, u32[]{:S(2)}, u32[]{:S(2)}) collective-permute-start(bf16[192,256]{1,0:T(8,128)(2,1)S(1)} %get-tuple-element.33), channel_id=1, source_target_pairs={{0,1},{1,2},{2,3},{3,0},{4,5},{5,6},{6,7},{7,4},{8,9},{9,10},{10,1... | collective-permute-start | bytes 294920 | tf_op jit(solution)/shard_map/ppermute | solution.py:51
  25.7 7.7 %collective-permute-start.5 = (bf16[192,256]{1,0:T(8,128)(2,1)S(1)}, bf16[192,256]{1,0:T(8,128)(2,1)S(1)}, u32[]{:S(2)}, u32[]{:S(2)}) collective-permute-start(bf16[192,256]{1,0:T(8,128)(2,1)S(1)} %get-tuple-element.34), channel_id=1, source_target_pairs={{0,3},{1,0},{2,1},{3,2},{4,7},{5,4},{6,5},{7,6},{8,11},{9,8},{10,9... | collective-permute-start | bytes 294920 | tf_op jit(solution)/shard_map/ppermute | solution.py:51
  34.0 2.3 %collective-permute-start.6 = (bf16[27,16,128]{2,1,0:T(8,128)(2,1)S(1)}, bf16[27,16,128]{2,1,0:T(8,128)(2,1)S(1)}, u32[]{:S(2)}, u32[]{:S(2)}) collective-permute-start(bf16[27,16,128]{2,1,0:T(8,128)(2,1)S(1)} %get-tuple-element.37), channel_id=1, source_target_pairs={{0,4},{4,0},{8,12},{12,8},{16,20},{20,16},{24,28},{28,24},{1,5},{5... | collective-permute-start | bytes 331784 | tf_op jit(solution)/shard_map/ppermute | solution.py:55
  34.8 18.6 %copy-start.3 = (s32[1,32]{1,0:T(1,128)S(1)}, s32[1,32]{1,0:T(1,128)}, u32[]{:S(2)}) copy-start(s32[1,32]{1,0:T(1,128)} %counts_ref.1) | copy-start | bytes 388
  34.8 1.4 %collective-permute-start.7 = (bf16[64,256]{1,0:T(8,128)(2,1)S(1)}, bf16[64,256]{1,0:T(8,128)(2,1)S(1)}, u32[]{:S(2)}, u32[]{:S(2)}) collective-permute-start(bf16[64,256]{1,0:T(8,128)(2,1)S(1)} %get-tuple-element.42), channel_id=1, source_target_pairs={{0,4},{4,0},{8,12},{12,8},{16,20},{20,16},{24,28},{28,24},{1,5},{5... | collective-permute-start | bytes 98312 | tf_op jit(solution)/shard_map/ppermute | solution.py:55
  37.0 13.0 %all-to-all-start.1 = ((bf16[32,24,128]{2,1,0:T(8,128)(2,1)}), bf16[32,24,128]{2,1,0:T(8,128)(2,1)S(1)}, u32[]{:S(2)}, u32[]{:S(2)}) async-start(bf16[32,24,128]{2,1,0:T(8,128)(2,1)} %shard_map.109), calls=%async_computation.1 | async-start | bytes 393216 | tf_op jit(solution)/shard_map/all_to_all | solution.py:60
  50.8 11.0 %all-to-all-start.2 = ((bf16[32,16,128]{2,1,0:T(8,128)(2,1)}), bf16[32,16,128]{2,1,0:T(8,128)(2,1)S(1)}, u32[]{:S(2)}, u32[]{:S(2)}) async-start(bf16[32,16,128]{2,1,0:T(8,128)(2,1)} %shard_map.110), calls=%async_computation.2 | async-start | bytes 262144 | tf_op jit(solution)/shard_map/all_to_all | solution.py:60
  61.8 1.3 %collective-permute-start.8 = (bf16[32,16,128]{2,1,0:T(8,128)(2,1)S(1)}, bf16[32,16,128]{2,1,0:T(8,128)(2,1)S(1)}, u32[]{:S(2)}, u32[]{:S(2)}) collective-permute-start(bf16[32,16,128]{2,1,0:T(8,128)(2,1)S(1)} %all-to-all-done.2.mine_ref), channel_id=1, source_target_pairs={{0,4},{4,0},{8,12},{12,8},{16,20},{20,16},{24,28},{28,24},{1,5},{5... | collective-permute-start | bytes 393224 | tf_op jit(solution)/shard_map/ppermute | solution.py:55

commit v12 on v10

--- a/solution.py
+++ b/solution.py
@@ -43,6 +43,14 @@
     return jax.ShapeDtypeStruct(dims, dtype)
 
 
+def beside(block, step):
+    count = lax.axis_size("gy")
+    if step == 0:
+        return lax.ppermute(block, "gy", [(0, count - 1), (count - 1, 0)])
+    starts = range(count - 1) if step > 0 else range(1, count)
+    return lax.ppermute(block, "gy", [(j, j + step) for j in starts])
+
+
 def send(block, di, dj, ngx, ngy):
     pairs = []
     for i in range(ngx):
@@ -122,6 +130,10 @@
 
 
 def same_kernel(in_ref, out_ref):
+    pass
+
+
+def both_kernel(first_ref, last_ref, first_out, last_out):
     pass
 
 
@@ -159,8 +171,8 @@
 
 
 def outer_kernel(
-    ndev, cap, recv_ref, own_ref, west_ref, east_ref, own_cells, west_cells, east_cells,
-    proj_t_ref, cot_ref, wf_ref, first_ref, last_ref, values_ref, hot_ref, masked, field,
+    ndev, cap, spot_ref, recv_ref, own_ref, west_ref, east_ref, own_cells, west_cells, east_cells,
+    proj_t_ref, cot_ref, wf_ref, first_ref, last_ref, wrap_ref, values_ref, hot_ref, masked, field,
 ):
     chans, cy, nz = own_ref.shape
     rows = 3 * chans
@@ -183,6 +195,14 @@
     near = mm(wf_ref[pl.ds(rows, 2 * rows)], field[0])
     add_to_rows(near, mm(wf_ref[pl.ds(2 * rows, rows)], field[1]), cot_ref[0], True, first_ref)
 
+    @pl.when(spot_ref[1] == 1)
+    def _():
+        wrap_ref[...] = first_ref[...]
+
+    @pl.when(spot_ref[1] != 1)
+    def _():
+        wrap_ref[...] = last_ref[...]
+
 
 def place(cells_ref, nz):
     cells = cells_ref[...]
@@ -279,18 +299,19 @@
 
 
 def edge_kernel(
-    part, parity_ref, pre_ref, total_ref, north_ref, south_ref, x_ref, cot_ref,
+    part, spot_ref, pre_ref, total_ref, north_ref, south_ref, wrap_ref, x_ref, cot_ref,
     out_ref, grads_ref, keep_ref, give_ref, total, sums,
 ):
     cy, chans, nz = cot_ref.shape
     rows = 3 * chans
     own = pl.ds(chans, chans)
-    last = pl.ds(2 * chans, chans)
-    cots = (north_ref[last], cot_ref[0], cot_ref[cy - 1], south_ref[last])
-    sides = ((north_ref, 1), (north_ref, 0), (south_ref, 0), (south_ref, 1))
+    wrap = wrap_ref[...].astype(F32)
+    north = jnp.where(spot_ref[1] == 1, wrap, north_ref[...].astype(F32))
+    south = jnp.where(spot_ref[2] == 1, wrap, south_ref[...].astype(F32))
+    cots = (north[2 * chans :], cot_ref[0], cot_ref[cy - 1], south[2 * chans :])
     ends = []
-    for n, (ref, at) in enumerate(sides):
-        pre = pre_ref[n] + ref[pl.ds(at * chans, chans)].astype(F32)
+    for n, (side, at) in enumerate(((north, 1), (north, 0), (south, 0), (south, 1))):
+        pre = pre_ref[n] + side[at * chans : (at + 1) * chans]
         ends.append(finish_row(pre, x_ref[0 if n < 2 else cy - 1, own], cots[n]))
     out_ref[0], out_ref[1] = ends[1][0], ends[2][0]
     grads = [stacked(grad) for _, grad in ends]
@@ -308,7 +329,7 @@
     sums[pl.ds(0, split)] = total[:, :width].reshape(split, 2, part, width)
     taps = jnp.concatenate([total[pl.ds(0, half), width:], total[pl.ds(half, half), width:]], axis=1)
     sums[pl.ds(split, full - split)] = taps.reshape(full - split, 2, part, width)
-    parity = parity_ref[0]
+    parity = spot_ref[0]
     keep_ref[...] = sums[:, parity]
     give_ref[...] = sums[:, 1 - parity].astype(BF16)
 
@@ -477,15 +498,20 @@
     wf = taps.transpose(1, 2, 3, 0, 4).reshape(9 * chans, rows)
     wb = taps.transpose(1, 0, 4, 2, 3).reshape(9 * chans, rows)
 
-    first, last, values, hots = call(
+    row, column = lax.axis_index("gx"), lax.axis_index("gy")
+    spot = jnp.stack([row % 2, column == 0, column == ngy - 1]).astype(I32)
+    first, last, wrap, values, hots = call(
         functools.partial(outer_kernel, ndev, cap),
-        [shape((rows, nz), BF16)] * 2
+        [shape((rows, nz), BF16)] * 3
         + [shape((3, chans, slots), BF16), shape((3, nz, slots), BF16)],
-        (recv, *planes, *lists, proj_t, cot, wf),
+        (spot, recv, *planes, *lists, proj_t, cot, wf),
         4 * one,
         (pltpu.VMEM((4 * chans, slots), BF16), pltpu.VMEM((4, rows, nz), BF16)),
-    )
-    south, north = move(first, 0, -1), move(last, 0, 1)
+        scalar=(0,),
+    )
+    wrap = beside(wrap, 0)
+    first, last = call(both_kernel, [first, last], (first, last), 0, aliases={0: 0, 1: 1})
+    south, north = beside(first, -1), beside(last, 1)
     x_all, out_rows, total, pre_edge, slot_edge, plane = call(
         conv_kernel,
         [
@@ -508,9 +534,7 @@
     grad_rows = 27 * chans * chans // feats
     part = -(-(grad_rows + 2 * chans) // (32 * ndev)) * 16
     full = grad_rows // (2 * part)
-    assert ngx % 2 == 0 and full * 2 * part == grad_rows
-    row = lax.axis_index("gx")
-    parity = (row % 2).astype(I32).reshape(1)
+    assert ngx % 2 == 0 and ngy > 1 and full * 2 * part == grad_rows
     out_edge, grads, keep, give = call(
         functools.partial(edge_kernel, part),
         [
@@ -519,7 +543,7 @@
             shape((full, part, feats), F32),
             shape((full, part, feats), BF16),
         ],
-        (parity, pre_edge, total, north, south, x_all, cot),
+        (spot, pre_edge, total, north, south, wrap, x_all, cot),
         6 * one,
         (pltpu.VMEM((9 * chans, rows), F32), pltpu.VMEM((full, 2, part, feats), F32)),
         scalar=(0,),
@@ -541,7 +565,7 @@
     )
     (payload,) = call(same_kernel, [payload], (payload,), 0, far=(0,), far_out=(0,), aliases={0: 0})
     recv = exchange(payload.reshape(-1, feats), ndev).reshape(payload.shape)
-    index = (row * ngy + lax.axis_index("gy")).astype(I32).reshape(1, 1)
+    index = (row * ngy + column).astype(I32).reshape(1, 1)
     (sums,) = call(
         functools.partial(sums_kernel, ngx, ngy, full, cap),
         [shape((ndev, part, feats), BF16)],
@@ -562,7 +586,7 @@
             finish_kernel, 1.0 / math.sqrt(count * ndev), 1.0 / math.sqrt(nrows * ndev)
         ),
         [shape((27, chans, chans), F32), shape((chans, feats), F32)],
-        (parity, mine, other),
+        (spot, mine, other),
         1000,
         (pltpu.VMEM((ndev, 2, part, feats), BF16),),
         scalar=(0,),

time: 61.6 us -> 69.2 us (1.12)
  starting transfers between devices: 21.1 us -> 27 us
  Pallas kernels: 13.5 us -> 15.2 us
    ppermute x0 -> x3, starting transfers between devices: none -> 6.66 us  [the longest x1 4.07 us: beside(): return lax.ppermute(block, 'gy', [(0, count - 1), (count - 1, 0)])]
    ppermute x6 -> x4, starting transfers between devices: 9.73 us -> 5.87 us  [send(): return lax.ppermute(block, AXES, pairs)]
    all_to_all x3, starting transfers between devices: 11.3 us -> 14.4 us  [exchange(): lax.all_to_all(payload.reshape(ndev, rows // ndev, width), AXES, split_ax...]
    pallas_call x10 -> x11, Pallas kernels: 13.5 us -> 15.2 us  [call(): pl.pallas_call(kernel, out_shape=[jax.ShapeDtypeStruct(o.shape, o.dtype)...]
  transfers between devices with their start and end apart: 11 -> 12, of which waited for: 5 -> 5; matrix products, arithmetic and copies ran while one was open for 8% -> 8% of each run, Pallas kernels for 15% -> 14%
where the time goes in v12:
time: 69.2 us; the launch traced here: 68.7 us
  starting transfers between devices  27 us (39%)
  waiting for transfers between devices  20.4 us (29%)
  Pallas kernels  15.2 us (22%)
  local copies, waits for them, and re-layouts  5.13 us (7%)
  between operations  0.92 us (1%)
    all_to_all x3, waiting for transfers between devices, exchange(): lax.all_to_all(payload.reshape(ndev, rows // ndev, width), AXES, split_ax...  18.6 us
    pallas_call x11, Pallas kernels, call(): pl.pallas_call(kernel, out_shape=[jax.ShapeDtypeStruct(o.shape, o.dtype)...  15.2 us
    all_to_all x3, starting transfers between devices, exchange(): lax.all_to_all(payload.reshape(ndev, rows // ndev, width), AXES, split_ax...  14.4 us
    ppermute x4, starting transfers between devices, send(): return lax.ppermute(block, AXES, pairs)  5.87 us
    ppermute x1, starting transfers between devices, beside(): return lax.ppermute(block, 'gy', [(0, count - 1), (count - 1, 0)])  4.07 us
    reshape x2, local copies, waits for them, and re-layouts, local(): taps = conv_weight.reshape(3, 3, 3, chans, chans)  2.74 us
    ppermute x2, starting transfers between devices, beside(): return lax.ppermute(block, 'gy', [(j, j + step) for j in starts])  2.59 us
    ppermute x2, waiting for transfers between devices, swap(): lax.ppermute(block, 'gx', [(i, i ^ 1) for i in range(lax.axis_size('gx'))])  1.73 us
  transfers between devices with their start and end apart: 12, of which 5 were waited for; matrix products, arithmetic and copies ran while one was open for 8% of the time, Pallas kernels for 14%

profile of v12, /device:TPU:0, one launch (start us, length us, event | category | flops | bytes accessed | tf_op | source)
XLA Modules:
  0.0 68.7 jit_solution(5595160289561327138)
XLA Ops:
  0.6 0.0 copy-start.4
  0.6 0.0 copy-start.5
  0.7 3.4 %collective-permute-start.1 = (bf16[64,1,16,256]{3,2,0,1:T(8,128)(2,1)}, bf16[64,1,16,256]{3,2,0,1:T(8,128)(2,1)S(1)}, u32[]{:S(2)}, u32[]{:S(2)}) collective-permute-start(bf16[64,1,16,256]{3,2,0,1:T(8,128)(2,1)} %bitcast.35), channel_id=1, source_target_pairs={{0,28},{1,29},{2,30},{3,31},{4,0},{5,1},{6,2},{7,3},{8,4},{9,5},{1... | collective-permute-start | bytes 1572872 | tf_op jit(solution)/shard_map/ppermute | solution.py:59
  4.0 0.0 collective-permute-start
  4.0 1.7 %shard_map.102 = bf16[768,128]{1,0:T(8,128)(2,1)} custom-call(bf16[128,128]{1,0:T(8,128)(2,1)} %rows_far.1, s32[1,32]{1,0:T(1,128)} %counts_ref.1), custom_call_target="tpu_custom_call" | custom-call | flops 8388608 | bytes 229504 | tf_op jit(solution)/shard_map/pallas_call | solution.py:27
  5.8 6.1 %all-to-all-start = ((bf16[32,24,128]{2,1,0:T(8,128)(2,1)}), bf16[32,24,128]{2,1,0:T(8,128)(2,1)S(1)}, u32[]{:S(2)}, u32[]{:S(2)}) async-start(bf16[32,24,128]{2,1,0:T(8,128)(2,1)} %bitcast.49), calls=%async_computation | async-start | bytes 393216 | tf_op jit(solution)/shard_map/all_to_all | solution.py:68
  11.8 2.5 %collective-permute-start.3 = (s32[1,256]{1,0:T(1,128)}, s32[1,256]{1,0:T(1,128)S(1)}, u32[]{:S(2)}, u32[]{:S(2)}) collective-permute-start(s32[1,256]{1,0:T(1,128)} %own_cells.5), channel_id=1, source_target_pairs={{0,28},{1,29},{2,30},{3,31},{4,0},{5,1},{6,2},{7,3},{8,4},{9,5},{1... | collective-permute-start | bytes 3080 | tf_op jit(solution)/shard_map/ppermute | solution.py:59
  14.3 0.0 collective-permute-start.2
  14.3 0.1 pad_add_fusion.spot_ref.parity_ref
  14.4 1.4 %copy.32 = bf16[3,3,3,64,64]{4,0,1,3,2:T(4,128)(2,1)S(1)} copy(bf16[3,3,3,64,64]{4,3,2,1,0:T(8,128)(2,1)} %bitcast.47) | data formatting | bytes 442368 | tf_op jit(solution)/shard_map/reshape | solution.py:497
  15.8 0.0 copy-done.4
  15.8 1.3 %copy.23 = bf16[3,3,3,64,64]{3,2,1,4,0:T(4,128)(2,1)} copy(bf16[3,3,3,64,64]{4,3,2,1,0:T(8,128)(2,1)S(1)} %bitcast.48) | data formatting | bytes 442368 | tf_op jit(solution)/shard_map/reshape | solution.py:497
  17.1 0.0 copy-done.5
  17.1 0.2 copy.33
  17.3 0.0 copy-start
  17.3 0.0 copy-start.1
  17.3 0.0 copy-start.2
  17.3 0.4 reshape.42
  17.7 0.2 copy.27.wb_ref
  17.9 1.5 %reshape.41 = bf16[576,192]{0,1:T(8,128)(2,1)S(1)} reshape(bf16[3,3,64,3,64]{2,1,0,4,3:T(4,128)(2,1)} %bitcast.45) | data formatting | bytes 442368 | tf_op jit(solution)/shard_map/reshape | solution.py:498
  19.4 0.2 copy.24.wf_ref
  19.6 0.0 collective-permute-done.3.east_cells
  19.6 0.0 collective-permute-done.2.west_cells
  19.6 1.6 %all-to-all-done = bf16[32,24,128]{2,1,0:T(8,128)(2,1)S(1)} async-done(((bf16[32,24,128]{2,1,0:T(8,128)(2,1)}), bf16[32,24,128]{2,1,0:T(8,128)(2,1)S(1)}, u32[]{:S(2)}, u32[]{:S(2)}) %all-to-all-start) | async-done | bytes 196640 | tf_op jit(solution)/shard_map/all_to_all | solution.py:68
  21.2 0.0 collective-permute-done.1
  21.2 0.0 collective-permute-done
  21.2 0.0 copy-done
  21.2 0.0 copy-done.1
  21.2 0.0 copy-done.2
  21.2 1.6 %shard_map.103 = (bf16[192,256]{1,0:T(8,128)(2,1)S(1)}, bf16[192,256]{1,0:T(8,128)(2,1)S(1)}, bf16[192,256]{1,0:T(8,128)(2,1)S(1)}, bf16[3,64,256]{2,1,0:T(8,128)(2,1)S(1)}, bf16[3,256,256]{2,1,0:T(8,128)(2,1)S(1)}) custom-call(s32[3]{0:T(128)S(1)} %pad_add_fusion.spot_ref.parity_ref, bf16[768,128]{1,0:T(8,128)(2,1)S(1)} %bitcast.33, ...), custom_call_target="tpu_custom_call" | custom-call | flops 75497472 | bytes 3320844 | tf_op jit(solution)/shard_map/pallas_call | solution.py:27
  22.7 4.1 %collective-permute-start.6 = (bf16[192,256]{1,0:T(8,128)(2,1)S(1)}, bf16[192,256]{1,0:T(8,128)(2,1)S(1)}, u32[]{:S(2)}, u32[]{:S(2)}) collective-permute-start(bf16[192,256]{1,0:T(8,128)(2,1)S(1)} %get-tuple-element.38), channel_id=1, source_target_pairs={{0,3},{3,0},{4,7},{7,4},{8,11},{11,8},{12,15},{15,12},{16,19},{19,... | collective-permute-start | bytes 294920 | tf_op jit(solution)/shard_map/ppermute | solution.py:49
  26.8 1.3 %collective-permute-start.4 = (bf16[192,256]{1,0:T(8,128)(2,1)S(1)}, bf16[192,256]{1,0:T(8,128)(2,1)S(1)}, u32[]{:S(2)}, u32[]{:S(2)}) collective-permute-start(bf16[192,256]{1,0:T(8,128)(2,1)S(1)} %get-tuple-element.36), channel_id=1, source_target_pairs={{0,1},{1,2},{2,3},{4,5},{5,6},{6,7},{8,9},{9,10},{10,11},{12,13},{... | collective-permute-start | bytes 294920 | tf_op jit(solution)/shard_map/ppermute | solution.py:51
  28.1 1.3 %collective-permute-start.5 = (bf16[192,256]{1,0:T(8,128)(2,1)S(1)}, bf16[192,256]{1,0:T(8,128)(2,1)S(1)}, u32[]{:S(2)}, u32[]{:S(2)}) collective-permute-start(bf16[192,256]{1,0:T(8,128)(2,1)S(1)} %get-tuple-element.37), channel_id=1, source_target_pairs={{1,0},{2,1},{3,2},{5,4},{6,5},{7,6},{9,8},{10,9},{11,10},{13,12},{... | collective-permute-start | bytes 294920 | tf_op jit(solution)/shard_map/ppermute | solution.py:51
  29.4 5.3 %shard_map.104 = (bf16[16,192,256]{2,1,0:T(8,128)(2,1)S(1)}, bf16[16,64,256]{2,1,0:T(8,128)(2,1)S(1)}, f32[576,192]{1,0:T(8,128)S(1)}, f32[4,64,256]{2,1,0:T(8,1...) custom-call(bf16[3,64,256]{2,1,0:T(8,128)(2,1)S(1)} %get-tuple-element.30.values_ref, ...), custom_call_target="tpu_custom_call" | custom-call | flops 2717908992 | bytes 7801856 | tf_op jit(solution)/shard_map/pallas_call | solution.py:27
  34.8 0.0 collective-permute-done.6.wrap_ref
  34.8 0.0 collective-permute-done.4.north_ref
  34.8 0.0 collective-permute-done.5.south_ref
  34.8 1.1 %shard_map.106 = (bf16[2,64,256]{2,1,0:T(8,128)(2,1)S(1)}, bf16[4,192,256]{2,1,0:T(8,128)(2,1)S(1)}, f32[27,16,128]{2,1,0:T(8,128)S(1)}, bf16[27,16,128]{2,1,0:T(8,128)(2,1)S(1)}) custom-call(s32[3]{0:T(128)S(1)} %pad_add_fusion.spot_ref.parity_ref, f32[4,64,256]{2,1,0:T(8,128)S(1)} %get-tuple-element.32.pre_ref, ...), custom_call_target="tpu_custom_call" | custom-call | flops 113246208 | bytes 3887116 | tf_op jit(solution)/shard_map/pallas_call | solution.py:27
  35.9 0.1 collective-permute-start.7
  36.0 0.9 %shard_map.107 = (bf16[32,16,128]{2,1,0:T(8,128)(2,1)S(1)}, bf16[5,16,128]{2,1,0:T(8,128)(2,1)S(1)}) custom-call(f32[4,192,256]{2,1,0:T(8,128)S(1)} %get-tuple-element.42.slot_ref, bf16[3,768,256]{2,1,0:T(8,128)(2,1)S(1)} %get-tuple-element.43.plane_ref, bf16[3,256,256]{2,1,0:T(8,128)(2,1)S(1)} %get-tuple-element.31.hot_ref, ...), custom_call_target="tpu_custom_call" | custom-call | flops 113246208 | bytes 3849216 | tf_op jit(solution)/shard_map/pallas_call | solution.py:27
  36.9 0.0 copy-start.3
  36.9 0.4 collective-permute-done.7.got_ref
  37.3 0.7 %shard_map.108.in_ref = bf16[32,32,128]{2,1,0:T(8,128)(2,1)} custom-call(f32[27,16,128]{2,1,0:T(8,128)S(1)} %get-tuple-element.40.keep_ref, bf16[27,16,128]{2,1,0:T(8,128)(2,1)S(1)} %collective-permute-done.7.got_ref, bf16[32,16,128]{2,1,0:T(8,128)(2,1)S(1)} %get-tuple-element.45.slots_ref, bf16[5,16,128]{2,1,0:T(8,128)(2,1)S(1)} %get-tuple-element.46.proj_ref), custom_call_target="tpu_custom_call" | custom-call | flops 1000 | bytes 745472 | tf_op jit(solution)/shard_map/pallas_call | solution.py:27
  38.0 5.6 %all-to-all-start.1 = ((bf16[32,32,128]{2,1,0:T(8,128)(2,1)}), bf16[32,32,128]{2,1,0:T(8,128)(2,1)S(1)}, u32[]{:S(2)}, u32[]{:S(2)}) async-start(bf16[32,32,128]{2,1,0:T(8,128)(2,1)} %shard_map.109), calls=%async_computation.1 | async-start | bytes 524288 | tf_op jit(solution)/shard_map/all_to_all | solution.py:68
  43.7 10.2 %all-to-all-done.1.recv_ref = bf16[32,32,128]{2,1,0:T(8,128)(2,1)S(1)} async-done(((bf16[32,32,128]{2,1,0:T(8,128)(2,1)}), bf16[32,32,128]{2,1,0:T(8,128)(2,1)S(1)}, u32[]{:S(2)}, u32[]{:S(2)}) %all-to-all-start.1) | async-done | bytes 262176 | tf_op jit(solution)/shard_map/all_to_all | solution.py:68
  53.9 0.7 %shard_map.110 = bf16[32,16,128]{2,1,0:T(8,128)(2,1)} custom-call(bf16[32,32,128]{2,1,0:T(8,128)(2,1)S(1)} %all-to-all-done.1.recv_ref, s32[1,1]{1,0:T(1,128)} %bitcast.16.index_ref), custom_call_target="tpu_custom_call" | custom-call | flops 1000 | bytes 393220 | tf_op jit(solution)/shard_map/pallas_call | solution.py:27
  54.6 2.7 %all-to-all-start.2 = ((bf16[32,16,128]{2,1,0:T(8,128)(2,1)}), bf16[32,16,128]{2,1,0:T(8,128)(2,1)S(1)}, u32[]{:S(2)}, u32[]{:S(2)}) async-start(bf16[32,16,128]{2,1,0:T(8,128)(2,1)} %shard_map.110), calls=%async_computation.2 | async-start | bytes 262144 | tf_op jit(solution)/shard_map/all_to_all | solution.py:68
  57.4 0.0 copy-done.3
  57.4 1.5 %shard_map.111 = (f32[128,128]{1,0:T(8,128)}, bf16[64,16,256]{2,1,0:T(8,128)(2,1)}) custom-call(bf16[32,32,128]{2,1,0:T(8,128)(2,1)S(1)} %all-to-all-done.1.recv_ref, s32[1,32]{1,0:T(1,128)S(1)} %copy-done.3, bf16[64,128]{1,0:T(8,128)(2,1)S(1)} %bitcast.44, bf16[16,64,256]{2,1,0:T(8,128)(2,1)S(1)} %get-tuple-element.47.inner_ref, ...), custom_call_target="tpu_custom_call" | custom-call | flops 4194304 | bytes 1458304 | tf_op jit(solution)/shard_map/pallas_call | solution.py:27
  58.9 6.9 %all-to-all-done.2.mine_ref = bf16[32,16,128]{2,1,0:T(8,128)(2,1)S(1)} async-done(((bf16[32,16,128]{2,1,0:T(8,128)(2,1)}), bf16[32,16,128]{2,1,0:T(8,128)(2,1)S(1)}, u32[]{:S(2)}, u32[]{:S(2)}) %all-to-all-start.2) | async-done | bytes 131104 | tf_op jit(solution)/shard_map/all_to_all | solution.py:68
  65.8 0.0 collective-permute-start.8
  65.8 1.3 %collective-permute-done.8.other_ref = bf16[32,16,128]{2,1,0:T(8,128)(2,1)S(1)} collective-permute-done((bf16[32,16,128]{2,1,0:T(8,128)(2,1)S(1)}, bf16[32,16,128]{2,1,0:T(8,128)(2,1)S(1)}, u32[]{:S(2)}, u32[]{:S(2)}) %collective-permute-start.8) | collective-permute-done | bytes 131104 | tf_op jit(solution)/shard_map/ppermute | solution.py:63
  67.1 1.6 %shard_map.112 = (f32[27,64,64]{2,1,0:T(8,128)}, f32[64,128]{1,0:T(8,128)}) custom-call(s32[3]{0:T(128)S(1)} %pad_add_fusion.spot_ref.parity_ref, bf16[32,16,128]{2,1,0:T(8,128)(2,1)S(1)} %all-to-all-done.2.mine_ref, bf16[32,16,128]{2,1,0:T(8,128)(2,1)S(1)} %collective-permute-done.8.other_ref), custom_call_target="tpu_custom_call" | custom-call | flops 1000 | bytes 737292 | tf_op jit(solution)/shard_map/pallas_call | solution.py:27
  (2 shorter events, 0.0 us)
Async XLA Ops:
  0.6 15.1 %copy-start.4 = (bf16[27,64,64]{2,1,0:T(8,128)(2,1)S(1)}, bf16[27,64,64]{2,1,0:T(8,128)(2,1)}, u32[]{:S(2)}) copy-start(bf16[27,64,64]{2,1,0:T(8,128)(2,1)} %param.12) | copy-start | bytes 663556
  0.6 16.5 %copy-start.5 = (bf16[64,1,16,256]{3,2,1,0:T(8,128)(2,1)S(1)}, bf16[64,1,16,256]{3,2,1,0:T(8,128)(2,1)}, u32[]{:S(2)}) copy-start(bf16[64,1,16,256]{3,2,1,0:T(8,128)(2,1)} %param.13) | copy-start | bytes 1572868
  0.7 20.5 %collective-permute-start.1 = (bf16[64,1,16,256]{3,2,0,1:T(8,128)(2,1)}, bf16[64,1,16,256]{3,2,0,1:T(8,128)(2,1)S(1)}, u32[]{:S(2)}, u32[]{:S(2)}) collective-permute-start(bf16[64,1,16,256]{3,2,0,1:T(8,128)(2,1)} %bitcast.35), channel_id=1, source_target_pairs={{0,28},{1,29},{2,30},{3,31},{4,0},{5,1},{6,2},{7,3},{8,4},{9,5},{1... | collective-permute-start | bytes 1572872 | tf_op jit(solution)/shard_map/ppermute | solution.py:59
  4.0 17.1 %collective-permute-start = (bf16[64,1,16,256]{3,2,0,1:T(8,128)(2,1)}, bf16[64,1,16,256]{3,2,0,1:T(8,128)(2,1)S(1)}, u32[]{:S(2)}, u32[]{:S(2)}) collective-permute-start(bf16[64,1,16,256]{3,2,0,1:T(8,128)(2,1)} %bitcast.36), channel_id=1, source_target_pairs={{0,4},{1,5},{2,6},{3,7},{4,8},{5,9},{6,10},{7,11},{8,12},{9,13},{1... | collective-permute-start | bytes 1572872 | tf_op jit(solution)/shard_map/ppermute | solution.py:59
  5.8 15.4 %all-to-all-start = ((bf16[32,24,128]{2,1,0:T(8,128)(2,1)}), bf16[32,24,128]{2,1,0:T(8,128)(2,1)S(1)}, u32[]{:S(2)}, u32[]{:S(2)}) async-start(bf16[32,24,128]{2,1,0:T(8,128)(2,1)} %bitcast.49), calls=%async_computation | async-start | bytes 393216 | tf_op jit(solution)/shard_map/all_to_all | solution.py:68
  11.8 7.7 %collective-permute-start.3 = (s32[1,256]{1,0:T(1,128)}, s32[1,256]{1,0:T(1,128)S(1)}, u32[]{:S(2)}, u32[]{:S(2)}) collective-permute-start(s32[1,256]{1,0:T(1,128)} %own_cells.5), channel_id=1, source_target_pairs={{0,28},{1,29},{2,30},{3,31},{4,0},{5,1},{6,2},{7,3},{8,4},{9,5},{1... | collective-permute-start | bytes 3080 | tf_op jit(solution)/shard_map/ppermute | solution.py:59
  14.3 5.3 %collective-permute-start.2 = (s32[1,256]{1,0:T(1,128)}, s32[1,256]{1,0:T(1,128)S(1)}, u32[]{:S(2)}, u32[]{:S(2)}) collective-permute-start(s32[1,256]{1,0:T(1,128)} %own_cells.5), channel_id=1, source_target_pairs={{0,4},{1,5},{2,6},{3,7},{4,8},{5,9},{6,10},{7,11},{8,12},{9,13},{1... | collective-permute-start | bytes 3080 | tf_op jit(solution)/shard_map/ppermute | solution.py:59
  17.3 3.9 %copy-start = (bf16[64,1,16,256]{3,2,1,0:T(8,128)(2,1)S(1)}, bf16[64,1,16,256]{3,2,1,0:T(8,128)(2,1)}, u32[]{:S(2)}) copy-start(bf16[64,1,16,256]{3,2,1,0:T(8,128)(2,1)} %param.10) | copy-start | bytes 1572868
  17.3 3.9 %copy-start.1 = (bf16[128,64]{0,1:T(8,128)(2,1)S(1)}, bf16[128,64]{0,1:T(8,128)(2,1)}, u32[]{:S(2)}) copy-start(bf16[128,64]{0,1:T(8,128)(2,1)} %param.11) | copy-start | bytes 49156
  17.3 3.9 %copy-start.2 = (s32[1,256]{1,0:T(1,128)S(1)}, s32[1,256]{1,0:T(1,128)}, u32[]{:S(2)}) copy-start(s32[1,256]{1,0:T(1,128)} %own_cells.5) | copy-start | bytes 3076
  22.7 12.0 %collective-permute-start.6 = (bf16[192,256]{1,0:T(8,128)(2,1)S(1)}, bf16[192,256]{1,0:T(8,128)(2,1)S(1)}, u32[]{:S(2)}, u32[]{:S(2)}) collective-permute-start(bf16[192,256]{1,0:T(8,128)(2,1)S(1)} %get-tuple-element.38), channel_id=1, source_target_pairs={{0,3},{3,0},{4,7},{7,4},{8,11},{11,8},{12,15},{15,12},{16,19},{19,... | collective-permute-start | bytes 294920 | tf_op jit(solution)/shard_map/ppermute | solution.py:49
  26.8 7.9 %collective-permute-start.4 = (bf16[192,256]{1,0:T(8,128)(2,1)S(1)}, bf16[192,256]{1,0:T(8,128)(2,1)S(1)}, u32[]{:S(2)}, u32[]{:S(2)}) collective-permute-start(bf16[192,256]{1,0:T(8,128)(2,1)S(1)} %get-tuple-element.36), channel_id=1, source_target_pairs={{0,1},{1,2},{2,3},{4,5},{5,6},{6,7},{8,9},{9,10},{10,11},{12,13},{... | collective-permute-start | bytes 294920 | tf_op jit(solution)/shard_map/ppermute | solution.py:51
  28.1 6.6 %collective-permute-start.5 = (bf16[192,256]{1,0:T(8,128)(2,1)S(1)}, bf16[192,256]{1,0:T(8,128)(2,1)S(1)}, u32[]{:S(2)}, u32[]{:S(2)}) collective-permute-start(bf16[192,256]{1,0:T(8,128)(2,1)S(1)} %get-tuple-element.37), channel_id=1, source_target_pairs={{1,0},{2,1},{3,2},{5,4},{6,5},{7,6},{9,8},{10,9},{11,10},{13,12},{... | collective-permute-start | bytes 294920 | tf_op jit(solution)/shard_map/ppermute | solution.py:51
  35.9 1.4 %collective-permute-start.7 = (bf16[27,16,128]{2,1,0:T(8,128)(2,1)S(1)}, bf16[27,16,128]{2,1,0:T(8,128)(2,1)S(1)}, u32[]{:S(2)}, u32[]{:S(2)}) collective-permute-start(bf16[27,16,128]{2,1,0:T(8,128)(2,1)S(1)} %get-tuple-element.41), channel_id=1, source_target_pairs={{0,4},{4,0},{8,12},{12,8},{16,20},{20,16},{24,28},{28,24},{1,5},{5... | collective-permute-start | bytes 331784 | tf_op jit(solution)/shard_map/ppermute | solution.py:63
  36.9 20.4 %copy-start.3 = (s32[1,32]{1,0:T(1,128)S(1)}, s32[1,32]{1,0:T(1,128)}, u32[]{:S(2)}) copy-start(s32[1,32]{1,0:T(1,128)} %counts_ref.1) | copy-start | bytes 388
  38.0 15.8 %all-to-all-start.1 = ((bf16[32,32,128]{2,1,0:T(8,128)(2,1)}), bf16[32,32,128]{2,1,0:T(8,128)(2,1)S(1)}, u32[]{:S(2)}, u32[]{:S(2)}) async-start(bf16[32,32,128]{2,1,0:T(8,128)(2,1)} %shard_map.109), calls=%async_computation.1 | async-start | bytes 524288 | tf_op jit(solution)/shard_map/all_to_all | solution.py:68
  54.6 11.1 %all-to-all-start.2 = ((bf16[32,16,128]{2,1,0:T(8,128)(2,1)}), bf16[32,16,128]{2,1,0:T(8,128)(2,1)S(1)}, u32[]{:S(2)}, u32[]{:S(2)}) async-start(bf16[32,16,128]{2,1,0:T(8,128)(2,1)} %shard_map.110), calls=%async_computation.2 | async-start | bytes 262144 | tf_op jit(solution)/shard_map/all_to_all | solution.py:68
  65.8 1.3 %collective-permute-start.8 = (bf16[32,16,128]{2,1,0:T(8,128)(2,1)S(1)}, bf16[32,16,128]{2,1,0:T(8,128)(2,1)S(1)}, u32[]{:S(2)}, u32[]{:S(2)}) collective-permute-start(bf16[32,16,128]{2,1,0:T(8,128)(2,1)S(1)} %all-to-all-done.2.mine_ref), channel_id=1, source_target_pairs={{0,4},{4,0},{8,12},{12,8},{16,20},{20,16},{24,28},{28,24},{1,5},{5... | collective-permute-start | bytes 393224 | tf_op jit(solution)/shard_map/ppermute | solution.py:63

commit v13 on v10

--- a/solution.py
+++ b/solution.py
@@ -190,7 +190,7 @@
 
 
 def turned(ref):
-    return jnp.swapaxes(ref[...].astype(F32), 0, 1)
+    return jnp.swapaxes(ref[...], 0, 1).astype(F32)
 
 
 def conv_kernel(
@@ -413,7 +413,7 @@
     rows_ref[...] = mm(sides, both) + mm(middle, both)
     cy = inner_ref.shape[0]
     field = jnp.concatenate([ends_ref[:1], inner_ref[1 : cy - 1], ends_ref[1:]], axis=0)
-    out_ref[...] = jnp.swapaxes(field.astype(F32), 0, 1).astype(BF16)
+    out_ref[...] = jnp.swapaxes(field, 0, 1)
 
 
 def finish_kernel(conv_scale, proj_scale, parity_ref, mine_ref, other_ref, conv_ref, proj_ref, both):

time: 61.6 us -> 61.3 us (level)
  no operation moved by 1% of the time
where the time goes in v13:
time: 61.3 us; the launch traced here: 60.9 us
  starting transfers between devices  21.1 us (34%)
  waiting for transfers between devices  20.6 us (34%)
  Pallas kernels  13.1 us (21%)
  local copies, waits for them, and re-layouts  5.13 us (8%)
  between operations  0.89 us (1%)
    all_to_all x3, waiting for transfers between devices, exchange(): lax.all_to_all(payload.reshape(ndev, rows // ndev, width), AXES, split_ax...  18.9 us
    pallas_call x10, Pallas kernels, call(): pl.pallas_call(kernel, out_shape=[jax.ShapeDtypeStruct(o.shape, o.dtype)...  13.1 us
    all_to_all x3, starting transfers between devices, exchange(): lax.all_to_all(payload.reshape(ndev, rows // ndev, width), AXES, split_ax...  11.3 us
    ppermute x6, starting transfers between devices, send(): return lax.ppermute(block, AXES, pairs)  9.73 us
    reshape x2, local copies, waits for them, and re-layouts, local(): taps = conv_weight.reshape(3, 3, 3, chans, chans)  2.74 us
    ppermute x2, waiting for transfers between devices, swap(): lax.ppermute(block, 'gx', [(i, i ^ 1) for i in range(lax.axis_size('gx'))])  1.74 us
    reshape x2, local copies, waits for them, and re-layouts, local(): wf = taps.transpose(1, 2, 3, 0, 4).reshape(9 * chans, rows)  1.65 us
  transfers between devices with their start and end apart: 11, of which 5 were waited for; matrix products, arithmetic and copies ran while one was open for 8% of the time, Pallas kernels for 15%

profile of v13, /device:TPU:0, one launch (start us, length us, event | category | flops | bytes accessed | tf_op | source)
XLA Modules:
  0.0 60.9 jit_solution(16476870587723466484)
XLA Ops:
  0.6 0.0 copy-start.4
  0.6 0.0 copy-start.5
  0.7 3.4 %collective-permute-start.1 = (bf16[64,1,16,256]{3,2,0,1:T(8,128)(2,1)}, bf16[64,1,16,256]{3,2,0,1:T(8,128)(2,1)S(1)}, u32[]{:S(2)}, u32[]{:S(2)}) collective-permute-start(bf16[64,1,16,256]{3,2,0,1:T(8,128)(2,1)} %bitcast.33), channel_id=1, source_target_pairs={{0,28},{1,29},{2,30},{3,31},{4,0},{5,1},{6,2},{7,3},{8,4},{9,5},{1... | collective-permute-start | bytes 1572872 | tf_op jit(solution)/shard_map/ppermute | solution.py:51
  4.0 0.0 collective-permute-start
  4.0 1.7 %shard_map.102 = bf16[768,128]{1,0:T(8,128)(2,1)} custom-call(bf16[128,128]{1,0:T(8,128)(2,1)} %rows_far.1, s32[1,32]{1,0:T(1,128)} %counts_ref.1), custom_call_target="tpu_custom_call" | custom-call | flops 8388608 | bytes 229504 | tf_op jit(solution)/shard_map/pallas_call | solution.py:27
  5.8 6.1 %all-to-all-start = ((bf16[32,24,128]{2,1,0:T(8,128)(2,1)}), bf16[32,24,128]{2,1,0:T(8,128)(2,1)S(1)}, u32[]{:S(2)}, u32[]{:S(2)}) async-start(bf16[32,24,128]{2,1,0:T(8,128)(2,1)} %bitcast.47), calls=%async_computation | async-start | bytes 393216 | tf_op jit(solution)/shard_map/all_to_all | solution.py:60
  11.8 2.5 %collective-permute-start.3 = (s32[1,256]{1,0:T(1,128)}, s32[1,256]{1,0:T(1,128)S(1)}, u32[]{:S(2)}, u32[]{:S(2)}) collective-permute-start(s32[1,256]{1,0:T(1,128)} %own_cells.5), channel_id=1, source_target_pairs={{0,28},{1,29},{2,30},{3,31},{4,0},{5,1},{6,2},{7,3},{8,4},{9,5},{1... | collective-permute-start | bytes 3080 | tf_op jit(solution)/shard_map/ppermute | solution.py:51
  14.3 0.0 collective-permute-start.2
  14.3 1.4 %copy.30 = bf16[3,3,3,64,64]{4,0,1,3,2:T(4,128)(2,1)S(1)} copy(bf16[3,3,3,64,64]{4,3,2,1,0:T(8,128)(2,1)} %bitcast.45) | data formatting | bytes 442368 | tf_op jit(solution)/shard_map/reshape | solution.py:476
  15.7 0.0 copy-done.4
  15.7 1.3 %copy.21 = bf16[3,3,3,64,64]{3,2,1,4,0:T(4,128)(2,1)} copy(bf16[3,3,3,64,64]{4,3,2,1,0:T(8,128)(2,1)S(1)} %bitcast.46) | data formatting | bytes 442368 | tf_op jit(solution)/shard_map/reshape | solution.py:476
  17.1 0.0 copy-done.5
  17.1 0.2 copy.31
  17.2 0.0 copy-start
  17.2 0.0 copy-start.1
  17.2 0.0 copy-start.2
  17.3 0.4 reshape.46
  17.7 0.2 copy.25.wb_ref
  17.8 1.5 %reshape.45 = bf16[576,192]{0,1:T(8,128)(2,1)S(1)} reshape(bf16[3,3,64,3,64]{2,1,0,4,3:T(4,128)(2,1)} %bitcast.43) | data formatting | bytes 442368 | tf_op jit(solution)/shard_map/reshape | solution.py:477
  19.3 0.2 copy.22.wf_ref
  19.5 0.0 collective-permute-done.3.east_cells
  19.5 0.0 collective-permute-done.2.west_cells
  19.5 1.6 %all-to-all-done = bf16[32,24,128]{2,1,0:T(8,128)(2,1)S(1)} async-done(((bf16[32,24,128]{2,1,0:T(8,128)(2,1)}), bf16[32,24,128]{2,1,0:T(8,128)(2,1)S(1)}, u32[]{:S(2)}, u32[]{:S(2)}) %all-to-all-start) | async-done | bytes 196640 | tf_op jit(solution)/shard_map/all_to_all | solution.py:60
  21.2 0.0 collective-permute-done.1
  21.2 0.0 collective-permute-done
  21.2 0.0 copy-done
  21.2 0.0 copy-done.1
  21.2 0.0 copy-done.2
  21.2 1.0 %shard_map.103 = (bf16[192,256]{1,0:T(8,128)(2,1)S(1)}, bf16[192,256]{1,0:T(8,128)(2,1)S(1)}, bf16[3,64,256]{2,1,0:T(8,128)(2,1)S(1)}, bf16[3,256,256]{2,1,0:T(8,128)(2,1)S(1)}) custom-call(bf16[768,128]{1,0:T(8,128)(2,1)S(1)} %bitcast.31, bf16[64,16,256]{2,1,0:T(8,128)(2,1)S(1)} %bitcast.35, bf16[64,16,256]{2,1,0:T(8,128)(2,1)S(1)} %bitcast.39, ...), custom_call_target="tpu_custom_call" | custom-call | flops 75497472 | bytes 3222528 | tf_op jit(solution)/shard_map/pallas_call | solution.py:27
  22.2 0.1 collective-permute-start.4
  22.2 3.8 %collective-permute-start.5 = (bf16[192,256]{1,0:T(8,128)(2,1)S(1)}, bf16[192,256]{1,0:T(8,128)(2,1)S(1)}, u32[]{:S(2)}, u32[]{:S(2)}) collective-permute-start(bf16[192,256]{1,0:T(8,128)(2,1)S(1)} %get-tuple-element.32), channel_id=1, source_target_pairs={{0,3},{1,0},{2,1},{3,2},{4,7},{5,4},{6,5},{7,6},{8,11},{9,8},{10,9... | collective-permute-start | bytes 294920 | tf_op jit(solution)/shard_map/ppermute | solution.py:51
  26.0 5.1 %shard_map.104 = (bf16[16,192,256]{2,1,0:T(8,128)(2,1)S(1)}, bf16[16,64,256]{2,1,0:T(8,128)(2,1)S(1)}, f32[576,192]{1,0:T(8,128)S(1)}, f32[4,64,256]{2,1,0:T(8,1...) custom-call(bf16[3,64,256]{2,1,0:T(8,128)(2,1)S(1)} %get-tuple-element.27.values_ref, ...), custom_call_target="tpu_custom_call" | custom-call | flops 2717908992 | bytes 7801856 | tf_op jit(solution)/shard_map/pallas_call | solution.py:27
  31.1 0.0 collective-permute-done.4.north_ref
  31.1 0.0 collective-permute-done.5.south_ref
  31.1 0.6 shard_map.105
  31.7 0.1 collective-permute-start.6
  31.8 0.9 %shard_map.106 = (bf16[32,16,128]{2,1,0:T(8,128)(2,1)S(1)}, bf16[5,16,128]{2,1,0:T(8,128)(2,1)S(1)}) custom-call(f32[4,192,256]{2,1,0:T(8,128)S(1)} %get-tuple-element.36.slot_ref, bf16[3,768,256]{2,1,0:T(8,128)(2,1)S(1)} %get-tuple-element.37.plane_ref, bf16[3,256,256]{2,1,0:T(8,128)(2,1)S(1)} %get-tuple-element.28.hot_ref, ...), custom_call_target="tpu_custom_call" | custom-call | flops 113246208 | bytes 3849216 | tf_op jit(solution)/shard_map/pallas_call | solution.py:27
  32.7 0.0 copy-start.3
  32.7 0.4 collective-permute-done.6.got_ref
  33.1 0.7 %shard_map.107.in_ref = bf16[32,32,128]{2,1,0:T(8,128)(2,1)} custom-call(f32[27,16,128]{2,1,0:T(8,128)S(1)} %get-tuple-element.34.keep_ref, bf16[27,16,128]{2,1,0:T(8,128)(2,1)S(1)} %collective-permute-done.6.got_ref, bf16[32,16,128]{2,1,0:T(8,128)(2,1)S(1)} %get-tuple-element.39.slots_ref, bf16[5,16,128]{2,1,0:T(8,128)(2,1)S(1)} %get-tuple-element.40.proj_ref), custom_call_target="tpu_custom_call" | custom-call | flops 1000 | bytes 745472 | tf_op jit(solution)/shard_map/pallas_call | solution.py:27
  33.8 2.6 %all-to-all-start.1 = ((bf16[32,32,128]{2,1,0:T(8,128)(2,1)}), bf16[32,32,128]{2,1,0:T(8,128)(2,1)S(1)}, u32[]{:S(2)}, u32[]{:S(2)}) async-start(bf16[32,32,128]{2,1,0:T(8,128)(2,1)} %shard_map.108), calls=%async_computation.1 | async-start | bytes 524288 | tf_op jit(solution)/shard_map/all_to_all | solution.py:60
  36.4 10.2 %all-to-all-done.1.recv_ref = bf16[32,32,128]{2,1,0:T(8,128)(2,1)S(1)} async-done(((bf16[32,32,128]{2,1,0:T(8,128)(2,1)}), bf16[32,32,128]{2,1,0:T(8,128)(2,1)S(1)}, u32[]{:S(2)}, u32[]{:S(2)}) %all-to-all-start.1) | async-done | bytes 262176 | tf_op jit(solution)/shard_map/all_to_all | solution.py:60
  46.6 0.7 %shard_map.109 = bf16[32,16,128]{2,1,0:T(8,128)(2,1)} custom-call(bf16[32,32,128]{2,1,0:T(8,128)(2,1)S(1)} %all-to-all-done.1.recv_ref, s32[1,1]{1,0:T(1,128)} %bitcast.14.index_ref), custom_call_target="tpu_custom_call" | custom-call | flops 1000 | bytes 393220 | tf_op jit(solution)/shard_map/pallas_call | solution.py:27
  47.4 2.7 %all-to-all-start.2 = ((bf16[32,16,128]{2,1,0:T(8,128)(2,1)}), bf16[32,16,128]{2,1,0:T(8,128)(2,1)S(1)}, u32[]{:S(2)}, u32[]{:S(2)}) async-start(bf16[32,16,128]{2,1,0:T(8,128)(2,1)} %shard_map.109), calls=%async_computation.2 | async-start | bytes 262144 | tf_op jit(solution)/shard_map/all_to_all | solution.py:60
  50.1 0.0 copy-done.3
  50.1 1.4 %shard_map.110 = (f32[128,128]{1,0:T(8,128)}, bf16[64,16,256]{2,1,0:T(8,128)(2,1)}) custom-call(bf16[32,32,128]{2,1,0:T(8,128)(2,1)S(1)} %all-to-all-done.1.recv_ref, s32[1,32]{1,0:T(1,128)S(1)} %copy-done.3, bf16[64,128]{1,0:T(8,128)(2,1)S(1)} %bitcast.42, bf16[16,64,256]{2,1,0:T(8,128)(2,1)S(1)} %get-tuple-element.41.inner_ref, ...), custom_call_target="tpu_custom_call" | custom-call | flops 4194304 | bytes 1458304 | tf_op jit(solution)/shard_map/pallas_call | solution.py:27
  51.4 7.0 %all-to-all-done.2.mine_ref = bf16[32,16,128]{2,1,0:T(8,128)(2,1)S(1)} async-done(((bf16[32,16,128]{2,1,0:T(8,128)(2,1)}), bf16[32,16,128]{2,1,0:T(8,128)(2,1)S(1)}, u32[]{:S(2)}, u32[]{:S(2)}) %all-to-all-start.2) | async-done | bytes 131104 | tf_op jit(solution)/shard_map/all_to_all | solution.py:60
  58.5 0.0 collective-permute-start.7
  58.5 1.3 %collective-permute-done.7.other_ref = bf16[32,16,128]{2,1,0:T(8,128)(2,1)S(1)} collective-permute-done((bf16[32,16,128]{2,1,0:T(8,128)(2,1)S(1)}, bf16[32,16,128]{2,1,0:T(8,128)(2,1)S(1)}, u32[]{:S(2)}, u32[]{:S(2)}) %collective-permute-start.7) | collective-permute-done | bytes 131104 | tf_op jit(solution)/shard_map/ppermute | solution.py:55
  59.8 1.1 %shard_map.111 = (f32[27,64,64]{2,1,0:T(8,128)}, f32[64,128]{1,0:T(8,128)}) custom-call(s32[1]{0:T(128)} %bitcast.parity_ref, bf16[32,16,128]{2,1,0:T(8,128)(2,1)S(1)} %all-to-all-done.2.mine_ref, bf16[32,16,128]{2,1,0:T(8,128)(2,1)S(1)} %collective-permute-done.7.other_ref), custom_call_target="tpu_custom_call" | custom-call | flops 1000 | bytes 737284 | tf_op jit(solution)/shard_map/pallas_call | solution.py:27
  (1 shorter events, 0.0 us)
Async XLA Ops:
  0.6 15.1 %copy-start.4 = (bf16[27,64,64]{2,1,0:T(8,128)(2,1)S(1)}, bf16[27,64,64]{2,1,0:T(8,128)(2,1)}, u32[]{:S(2)}) copy-start(bf16[27,64,64]{2,1,0:T(8,128)(2,1)} %param.12) | copy-start | bytes 663556
  0.6 16.4 %copy-start.5 = (bf16[64,1,16,256]{3,2,1,0:T(8,128)(2,1)S(1)}, bf16[64,1,16,256]{3,2,1,0:T(8,128)(2,1)}, u32[]{:S(2)}) copy-start(bf16[64,1,16,256]{3,2,1,0:T(8,128)(2,1)} %param.13) | copy-start | bytes 1572868
  0.7 20.5 %collective-permute-start.1 = (bf16[64,1,16,256]{3,2,0,1:T(8,128)(2,1)}, bf16[64,1,16,256]{3,2,0,1:T(8,128)(2,1)S(1)}, u32[]{:S(2)}, u32[]{:S(2)}) collective-permute-start(bf16[64,1,16,256]{3,2,0,1:T(8,128)(2,1)} %bitcast.33), channel_id=1, source_target_pairs={{0,28},{1,29},{2,30},{3,31},{4,0},{5,1},{6,2},{7,3},{8,4},{9,5},{1... | collective-permute-start | bytes 1572872 | tf_op jit(solution)/shard_map/ppermute | solution.py:51
  4.0 17.1 %collective-permute-start = (bf16[64,1,16,256]{3,2,0,1:T(8,128)(2,1)}, bf16[64,1,16,256]{3,2,0,1:T(8,128)(2,1)S(1)}, u32[]{:S(2)}, u32[]{:S(2)}) collective-permute-start(bf16[64,1,16,256]{3,2,0,1:T(8,128)(2,1)} %bitcast.34), channel_id=1, source_target_pairs={{0,4},{1,5},{2,6},{3,7},{4,8},{5,9},{6,10},{7,11},{8,12},{9,13},{1... | collective-permute-start | bytes 1572872 | tf_op jit(solution)/shard_map/ppermute | solution.py:51
  5.8 15.4 %all-to-all-start = ((bf16[32,24,128]{2,1,0:T(8,128)(2,1)}), bf16[32,24,128]{2,1,0:T(8,128)(2,1)S(1)}, u32[]{:S(2)}, u32[]{:S(2)}) async-start(bf16[32,24,128]{2,1,0:T(8,128)(2,1)} %bitcast.47), calls=%async_computation | async-start | bytes 393216 | tf_op jit(solution)/shard_map/all_to_all | solution.py:60
  11.8 7.7 %collective-permute-start.3 = (s32[1,256]{1,0:T(1,128)}, s32[1,256]{1,0:T(1,128)S(1)}, u32[]{:S(2)}, u32[]{:S(2)}) collective-permute-start(s32[1,256]{1,0:T(1,128)} %own_cells.5), channel_id=1, source_target_pairs={{0,28},{1,29},{2,30},{3,31},{4,0},{5,1},{6,2},{7,3},{8,4},{9,5},{1... | collective-permute-start | bytes 3080 | tf_op jit(solution)/shard_map/ppermute | solution.py:51
  14.3 5.2 %collective-permute-start.2 = (s32[1,256]{1,0:T(1,128)}, s32[1,256]{1,0:T(1,128)S(1)}, u32[]{:S(2)}, u32[]{:S(2)}) collective-permute-start(s32[1,256]{1,0:T(1,128)} %own_cells.5), channel_id=1, source_target_pairs={{0,4},{1,5},{2,6},{3,7},{4,8},{5,9},{6,10},{7,11},{8,12},{9,13},{1... | collective-permute-start | bytes 3080 | tf_op jit(solution)/shard_map/ppermute | solution.py:51
  17.2 3.9 %copy-start = (bf16[64,1,16,256]{3,2,1,0:T(8,128)(2,1)S(1)}, bf16[64,1,16,256]{3,2,1,0:T(8,128)(2,1)}, u32[]{:S(2)}) copy-start(bf16[64,1,16,256]{3,2,1,0:T(8,128)(2,1)} %param.10) | copy-start | bytes 1572868
  17.2 3.9 %copy-start.1 = (bf16[128,64]{0,1:T(8,128)(2,1)S(1)}, bf16[128,64]{0,1:T(8,128)(2,1)}, u32[]{:S(2)}) copy-start(bf16[128,64]{0,1:T(8,128)(2,1)} %param.11) | copy-start | bytes 49156
  17.2 3.9 %copy-start.2 = (s32[1,256]{1,0:T(1,128)S(1)}, s32[1,256]{1,0:T(1,128)}, u32[]{:S(2)}) copy-start(s32[1,256]{1,0:T(1,128)} %own_cells.5) | copy-start | bytes 3076
  22.2 9.0 %collective-permute-start.4 = (bf16[192,256]{1,0:T(8,128)(2,1)S(1)}, bf16[192,256]{1,0:T(8,128)(2,1)S(1)}, u32[]{:S(2)}, u32[]{:S(2)}) collective-permute-start(bf16[192,256]{1,0:T(8,128)(2,1)S(1)} %get-tuple-element.31), channel_id=1, source_target_pairs={{0,1},{1,2},{2,3},{3,0},{4,5},{5,6},{6,7},{7,4},{8,9},{9,10},{10,1... | collective-permute-start | bytes 294920 | tf_op jit(solution)/shard_map/ppermute | solution.py:51
  22.2 8.9 %collective-permute-start.5 = (bf16[192,256]{1,0:T(8,128)(2,1)S(1)}, bf16[192,256]{1,0:T(8,128)(2,1)S(1)}, u32[]{:S(2)}, u32[]{:S(2)}) collective-permute-start(bf16[192,256]{1,0:T(8,128)(2,1)S(1)} %get-tuple-element.32), channel_id=1, source_target_pairs={{0,3},{1,0},{2,1},{3,2},{4,7},{5,4},{6,5},{7,6},{8,11},{9,8},{10,9... | collective-permute-start | bytes 294920 | tf_op jit(solution)/shard_map/ppermute | solution.py:51
  31.7 1.4 %collective-permute-start.6 = (bf16[27,16,128]{2,1,0:T(8,128)(2,1)S(1)}, bf16[27,16,128]{2,1,0:T(8,128)(2,1)S(1)}, u32[]{:S(2)}, u32[]{:S(2)}) collective-permute-start(bf16[27,16,128]{2,1,0:T(8,128)(2,1)S(1)} %get-tuple-element.35), channel_id=1, source_target_pairs={{0,4},{4,0},{8,12},{12,8},{16,20},{20,16},{24,28},{28,24},{1,5},{5... | collective-permute-start | bytes 331784 | tf_op jit(solution)/shard_map/ppermute | solution.py:55
  32.7 17.4 %copy-start.3 = (s32[1,32]{1,0:T(1,128)S(1)}, s32[1,32]{1,0:T(1,128)}, u32[]{:S(2)}) copy-start(s32[1,32]{1,0:T(1,128)} %counts_ref.1) | copy-start | bytes 388
  33.8 12.8 %all-to-all-start.1 = ((bf16[32,32,128]{2,1,0:T(8,128)(2,1)}), bf16[32,32,128]{2,1,0:T(8,128)(2,1)S(1)}, u32[]{:S(2)}, u32[]{:S(2)}) async-start(bf16[32,32,128]{2,1,0:T(8,128)(2,1)} %shard_map.108), calls=%async_computation.1 | async-start | bytes 524288 | tf_op jit(solution)/shard_map/all_to_all | solution.py:60
  47.4 11.1 %all-to-all-start.2 = ((bf16[32,16,128]{2,1,0:T(8,128)(2,1)}), bf16[32,16,128]{2,1,0:T(8,128)(2,1)S(1)}, u32[]{:S(2)}, u32[]{:S(2)}) async-start(bf16[32,16,128]{2,1,0:T(8,128)(2,1)} %shard_map.109), calls=%async_computation.2 | async-start | bytes 262144 | tf_op jit(solution)/shard_map/all_to_all | solution.py:60
  58.5 1.3 %collective-permute-start.7 = (bf16[32,16,128]{2,1,0:T(8,128)(2,1)S(1)}, bf16[32,16,128]{2,1,0:T(8,128)(2,1)S(1)}, u32[]{:S(2)}, u32[]{:S(2)}) collective-permute-start(bf16[32,16,128]{2,1,0:T(8,128)(2,1)S(1)} %all-to-all-done.2.mine_ref), channel_id=1, source_target_pairs={{0,4},{4,0},{8,12},{12,8},{16,20},{20,16},{24,28},{28,24},{1,5},{5... | collective-permute-start | bytes 393224 | tf_op jit(solution)/shard_map/ppermute | solution.py:55

commit v14 on v13

--- a/solution.py
+++ b/solution.py
@@ -11,7 +11,6 @@
 AXES = ("gx", "gy")
 F32, BF16, I32 = jnp.float32, jnp.bfloat16, jnp.int32
 LIMIT = 40 * 1024 * 1024
-ALL = 60 * 1024 * 1024
 NT = (((1,), (1,)), ((), ()))
 NN = (((1,), (0,)), ((), ()))
 
@@ -20,7 +19,7 @@
     return lax.dot_general(a, b, dims, preferred_element_type=F32)
 
 
-def call(kernel, outs, args, flops, scratch=(), far=(), far_out=(), aliases=None, limit=LIMIT, scalar=()):
+def call(kernel, outs, args, flops, scratch=(), far=(), far_out=(), aliases=None, scalar=()):
     traffic = sum(math.prod(a.shape) * a.dtype.itemsize for a in (*args, *outs))
     near = pl.BlockSpec(memory_space=pltpu.VMEM)
     there = pl.BlockSpec(memory_space=pltpu.HBM)
@@ -34,7 +33,7 @@
         out_specs=[there if n in far_out else near for n in range(len(outs))],
         scratch_shapes=list(scratch),
         input_output_aliases=aliases or {},
-        compiler_params=pltpu.CompilerParams(vmem_limit_bytes=limit),
+        compiler_params=pltpu.CompilerParams(vmem_limit_bytes=LIMIT),
         cost_estimate=pl.CostEstimate(flops=flops, bytes_accessed=traffic, transcendentals=0),
     )(*args)
 
@@ -105,20 +104,6 @@
     out = field.astype(F32) + pre * sig
     grad = cot.astype(F32) * sig * (1.0 + pre * (1.0 - sig))
     return out.astype(BF16), grad.astype(BF16)
-
-
-def first_kernel(
-    ngx, ngy, cap, rows_far, counts_far, send_ref, rows_ref, counts_ref, sems
-):
-    copies = [
-        pltpu.make_async_copy(rows_far, rows_ref, sems.at[0]),
-        pltpu.make_async_copy(counts_far, counts_ref, sems.at[1]),
-    ]
-    for copy in copies:
-        copy.start()
-    for copy in copies:
-        copy.wait()
-    pick(ngx, ngy, cap, counts_ref, rows_ref, send_ref)
 
 
 def same_kernel(in_ref, out_ref):
@@ -458,17 +443,10 @@
     planes = (base, west.reshape(base.shape), east.reshape(base.shape))
     lists = (cell_lists, move(cell_lists, 1, 0), move(cell_lists, -1, 0))
     (payload,) = call(
-        functools.partial(first_kernel, ngx, ngy, cap),
+        functools.partial(pick, ngx, ngy, cap),
         [shape((ndev * 3 * cap, feats), BF16)],
-        (particles, send_counts),
+        (send_counts, particles),
         2 * slots * nrows * feats,
-        (
-            pltpu.VMEM(particles.shape, BF16),
-            pltpu.VMEM(send_counts.shape, I32),
-            pltpu.SemaphoreType.DMA((2,)),
-        ),
-        far=range(2),
-        limit=ALL,
     )
     recv = exchange(payload, ndev)
 

time: 61.3 us -> 62 us (1.011)
  local copies, waits for them, and re-layouts: 5.13 us -> 6.54 us
  Pallas kernels: 13.1 us -> 12.4 us
    unnamed x13 -> x17, local copies, waits for them, and re-layouts: 0.19 us -> 1.6 us
    pallas_call x10, Pallas kernels: 13.1 us -> 12.4 us  [call(): pl.pallas_call(kernel, out_shape=[jax.ShapeDtypeStruct(o.shape, o.dtype)...]
  transfers between devices with their start and end apart: 11 -> 11, of which waited for: 5 -> 5; matrix products, arithmetic and copies ran while one was open for 8% -> 8% of each run, Pallas kernels for 15% -> 13%
where the time goes in v14:
time: 62 us; the launch traced here: 61.5 us
  starting transfers between devices  21.1 us (34%)
  waiting for transfers between devices  20.6 us (33%)
  Pallas kernels  12.4 us (20%)
  local copies, waits for them, and re-layouts  6.54 us (11%)
  between operations  0.87 us (1%)
    all_to_all x3, waiting for transfers between devices, exchange(): lax.all_to_all(payload.reshape(ndev, rows // ndev, width), AXES, split_ax...  18.9 us
    pallas_call x10, Pallas kernels, call(): pl.pallas_call(kernel, out_shape=[jax.ShapeDtypeStruct(o.shape, o.dtype)...  12.4 us
    all_to_all x3, starting transfers between devices, exchange(): lax.all_to_all(payload.reshape(ndev, rows // ndev, width), AXES, split_ax...  11.3 us
    ppermute x6, starting transfers between devices, send(): return lax.ppermute(block, AXES, pairs)  9.73 us
    reshape x2, local copies, waits for them, and re-layouts, local(): taps = conv_weight.reshape(3, 3, 3, chans, chans)  2.74 us
    ppermute x2, waiting for transfers between devices, swap(): lax.ppermute(block, 'gx', [(i, i ^ 1) for i in range(lax.axis_size('gx'))])  1.73 us
    reshape x2, local copies, waits for them, and re-layouts, local(): wf = taps.transpose(1, 2, 3, 0, 4).reshape(9 * chans, rows)  1.65 us
    unnamed x17, local copies, waits for them, and re-layouts  1.6 us
  transfers between devices with their start and end apart: 11, of which 5 were waited for; matrix products, arithmetic and copies ran while one was open for 8% of the time, Pallas kernels for 13%

profile of v14, /device:TPU:0, one launch (start us, length us, event | category | flops | bytes accessed | tf_op | source)
XLA Modules:
  0.0 61.5 jit_solution(11975636995068963363)
XLA Ops:
  0.6 3.4 %collective-permute-start.1 = (bf16[64,1,16,256]{3,2,0,1:T(8,128)(2,1)}, bf16[64,1,16,256]{3,2,0,1:T(8,128)(2,1)S(1)}, u32[]{:S(2)}, u32[]{:S(2)}) collective-permute-start(bf16[64,1,16,256]{3,2,0,1:T(8,128)(2,1)} %bitcast.33), channel_id=1, source_target_pairs={{0,28},{1,29},{2,30},{3,31},{4,0},{5,1},{6,2},{7,3},{8,4},{9,5},{1... | collective-permute-start | bytes 1572872 | tf_op jit(solution)/shard_map/ppermute | solution.py:50
  4.0 0.0 collective-permute-start
  4.0 0.0 copy-start.2
  4.0 0.8 %copy-done.2 = bf16[128,128]{1,0:T(8,128)(2,1)S(1)} copy-done((bf16[128,128]{1,0:T(8,128)(2,1)S(1)}, bf16[128,128]{1,0:T(8,128)(2,1)}, u32[]{:S(2)}) %copy-start.2) | copy-done | bytes 32792
  4.8 0.0 copy-start.4
  4.8 0.7 %copy-done.4 = s32[1,32]{1,0:T(1,128)S(1)} copy-done((s32[1,32]{1,0:T(1,128)S(1)}, s32[1,32]{1,0:T(1,128)}, u32[]{:S(2)}) %copy-start.4) | copy-done | bytes 152
  5.4 0.0 copy-start.6
  5.4 0.0 copy-start.7
  5.4 0.9 %shard_map.102 = bf16[768,128]{1,0:T(8,128)(2,1)} custom-call(s32[1,32]{1,0:T(1,128)S(1)} %copy-done.4, bf16[128,128]{1,0:T(8,128)(2,1)S(1)} %copy-done.2), custom_call_target="tpu_custom_call" | custom-call | flops 8388608 | bytes 229504 | tf_op jit(solution)/shard_map/pallas_call | solution.py:26
  6.4 6.0 %all-to-all-start = ((bf16[32,24,128]{2,1,0:T(8,128)(2,1)}), bf16[32,24,128]{2,1,0:T(8,128)(2,1)S(1)}, u32[]{:S(2)}, u32[]{:S(2)}) async-start(bf16[32,24,128]{2,1,0:T(8,128)(2,1)} %bitcast.1), calls=%async_computation | async-start | bytes 393216 | tf_op jit(solution)/shard_map/all_to_all | solution.py:59
  12.4 2.5 %collective-permute-start.3 = (s32[1,256]{1,0:T(1,128)}, s32[1,256]{1,0:T(1,128)S(1)}, u32[]{:S(2)}, u32[]{:S(2)}) collective-permute-start(s32[1,256]{1,0:T(1,128)} %own_cells.5), channel_id=1, source_target_pairs={{0,28},{1,29},{2,30},{3,31},{4,0},{5,1},{6,2},{7,3},{8,4},{9,5},{1... | collective-permute-start | bytes 3080 | tf_op jit(solution)/shard_map/ppermute | solution.py:50
  14.9 0.0 collective-permute-start.2
  14.9 1.4 %copy.30 = bf16[3,3,3,64,64]{4,0,1,3,2:T(4,128)(2,1)S(1)} copy(bf16[3,3,3,64,64]{4,3,2,1,0:T(8,128)(2,1)} %bitcast.45) | data formatting | bytes 442368 | tf_op jit(solution)/shard_map/reshape | solution.py:454
  16.3 0.0 copy-done.6
  16.3 1.3 %copy.21 = bf16[3,3,3,64,64]{3,2,1,4,0:T(4,128)(2,1)} copy(bf16[3,3,3,64,64]{4,3,2,1,0:T(8,128)(2,1)S(1)} %bitcast.46) | data formatting | bytes 442368 | tf_op jit(solution)/shard_map/reshape | solution.py:454
  17.7 0.0 copy-done.7
  17.7 0.2 copy.31
  17.8 0.0 copy-start
  17.8 0.0 copy-start.1
  17.9 0.0 copy-start.3
  17.9 0.4 reshape.46
  18.3 0.2 copy.25.wb_ref
  18.4 1.5 %reshape.45 = bf16[576,192]{0,1:T(8,128)(2,1)S(1)} reshape(bf16[3,3,64,3,64]{2,1,0,4,3:T(4,128)(2,1)} %bitcast.43) | data formatting | bytes 442368 | tf_op jit(solution)/shard_map/reshape | solution.py:455
  19.9 0.2 copy.22.wf_ref
  20.1 0.0 collective-permute-done.3.east_cells
  20.1 0.0 collective-permute-done.2.west_cells
  20.1 1.6 %all-to-all-done = bf16[32,24,128]{2,1,0:T(8,128)(2,1)S(1)} async-done(((bf16[32,24,128]{2,1,0:T(8,128)(2,1)}), bf16[32,24,128]{2,1,0:T(8,128)(2,1)S(1)}, u32[]{:S(2)}, u32[]{:S(2)}) %all-to-all-start) | async-done | bytes 196640 | tf_op jit(solution)/shard_map/all_to_all | solution.py:59
  21.8 0.0 collective-permute-done.1
  21.8 0.0 collective-permute-done
  21.8 0.0 copy-done
  21.8 0.0 copy-done.1
  21.8 0.0 copy-done.3
  21.8 1.0 %shard_map.103 = (bf16[192,256]{1,0:T(8,128)(2,1)S(1)}, bf16[192,256]{1,0:T(8,128)(2,1)S(1)}, bf16[3,64,256]{2,1,0:T(8,128)(2,1)S(1)}, bf16[3,256,256]{2,1,0:T(8,128)(2,1)S(1)}) custom-call(bf16[768,128]{1,0:T(8,128)(2,1)S(1)} %bitcast.31, bf16[64,16,256]{2,1,0:T(8,128)(2,1)S(1)} %bitcast.35, bf16[64,16,256]{2,1,0:T(8,128)(2,1)S(1)} %bitcast.39, ...), custom_call_target="tpu_custom_call" | custom-call | flops 75497472 | bytes 3222528 | tf_op jit(solution)/shard_map/pallas_call | solution.py:26
  22.8 0.1 collective-permute-start.4
  22.8 3.8 %collective-permute-start.5 = (bf16[192,256]{1,0:T(8,128)(2,1)S(1)}, bf16[192,256]{1,0:T(8,128)(2,1)S(1)}, u32[]{:S(2)}, u32[]{:S(2)}) collective-permute-start(bf16[192,256]{1,0:T(8,128)(2,1)S(1)} %get-tuple-element.32), channel_id=1, source_target_pairs={{0,3},{1,0},{2,1},{3,2},{4,7},{5,4},{6,5},{7,6},{8,11},{9,8},{10,9... | collective-permute-start | bytes 294920 | tf_op jit(solution)/shard_map/ppermute | solution.py:50
  26.6 5.1 %shard_map.104 = (bf16[16,192,256]{2,1,0:T(8,128)(2,1)S(1)}, bf16[16,64,256]{2,1,0:T(8,128)(2,1)S(1)}, f32[576,192]{1,0:T(8,128)S(1)}, f32[4,64,256]{2,1,0:T(8,1...) custom-call(bf16[3,64,256]{2,1,0:T(8,128)(2,1)S(1)} %get-tuple-element.27.values_ref, ...), custom_call_target="tpu_custom_call" | custom-call | flops 2717908992 | bytes 7801856 | tf_op jit(solution)/shard_map/pallas_call | solution.py:26
  31.7 0.0 collective-permute-done.4.north_ref
  31.7 0.0 collective-permute-done.5.south_ref
  31.7 0.6 shard_map.105
  32.3 0.1 collective-permute-start.6
  32.4 0.9 %shard_map.106 = (bf16[32,16,128]{2,1,0:T(8,128)(2,1)S(1)}, bf16[5,16,128]{2,1,0:T(8,128)(2,1)S(1)}) custom-call(f32[4,192,256]{2,1,0:T(8,128)S(1)} %get-tuple-element.36.slot_ref, bf16[3,768,256]{2,1,0:T(8,128)(2,1)S(1)} %get-tuple-element.37.plane_ref, bf16[3,256,256]{2,1,0:T(8,128)(2,1)S(1)} %get-tuple-element.28.hot_ref, ...), custom_call_target="tpu_custom_call" | custom-call | flops 113246208 | bytes 3849216 | tf_op jit(solution)/shard_map/pallas_call | solution.py:26
  33.3 0.0 copy-start.5
  33.3 0.4 collective-permute-done.6.got_ref
  33.7 0.7 %shard_map.107.in_ref = bf16[32,32,128]{2,1,0:T(8,128)(2,1)} custom-call(f32[27,16,128]{2,1,0:T(8,128)S(1)} %get-tuple-element.34.keep_ref, bf16[27,16,128]{2,1,0:T(8,128)(2,1)S(1)} %collective-permute-done.6.got_ref, bf16[32,16,128]{2,1,0:T(8,128)(2,1)S(1)} %get-tuple-element.39.slots_ref, bf16[5,16,128]{2,1,0:T(8,128)(2,1)S(1)} %get-tuple-element.40.proj_ref), custom_call_target="tpu_custom_call" | custom-call | flops 1000 | bytes 745472 | tf_op jit(solution)/shard_map/pallas_call | solution.py:26
  34.4 2.6 %all-to-all-start.1 = ((bf16[32,32,128]{2,1,0:T(8,128)(2,1)}), bf16[32,32,128]{2,1,0:T(8,128)(2,1)S(1)}, u32[]{:S(2)}, u32[]{:S(2)}) async-start(bf16[32,32,128]{2,1,0:T(8,128)(2,1)} %shard_map.108), calls=%async_computation.1 | async-start | bytes 524288 | tf_op jit(solution)/shard_map/all_to_all | solution.py:59
  37.0 10.2 %all-to-all-done.1.recv_ref = bf16[32,32,128]{2,1,0:T(8,128)(2,1)S(1)} async-done(((bf16[32,32,128]{2,1,0:T(8,128)(2,1)}), bf16[32,32,128]{2,1,0:T(8,128)(2,1)S(1)}, u32[]{:S(2)}, u32[]{:S(2)}) %all-to-all-start.1) | async-done | bytes 262176 | tf_op jit(solution)/shard_map/all_to_all | solution.py:59
  47.2 0.7 %shard_map.109 = bf16[32,16,128]{2,1,0:T(8,128)(2,1)} custom-call(bf16[32,32,128]{2,1,0:T(8,128)(2,1)S(1)} %all-to-all-done.1.recv_ref, s32[1,1]{1,0:T(1,128)} %bitcast.14.index_ref), custom_call_target="tpu_custom_call" | custom-call | flops 1000 | bytes 393220 | tf_op jit(solution)/shard_map/pallas_call | solution.py:26
  48.0 2.7 %all-to-all-start.2 = ((bf16[32,16,128]{2,1,0:T(8,128)(2,1)}), bf16[32,16,128]{2,1,0:T(8,128)(2,1)S(1)}, u32[]{:S(2)}, u32[]{:S(2)}) async-start(bf16[32,16,128]{2,1,0:T(8,128)(2,1)} %shard_map.109), calls=%async_computation.2 | async-start | bytes 262144 | tf_op jit(solution)/shard_map/all_to_all | solution.py:59
  50.7 0.0 copy-done.5
  50.7 1.4 %shard_map.110 = (f32[128,128]{1,0:T(8,128)}, bf16[64,16,256]{2,1,0:T(8,128)(2,1)}) custom-call(bf16[32,32,128]{2,1,0:T(8,128)(2,1)S(1)} %all-to-all-done.1.recv_ref, s32[1,32]{1,0:T(1,128)S(1)} %copy-done.5, bf16[64,128]{1,0:T(8,128)(2,1)S(1)} %bitcast.42, bf16[16,64,256]{2,1,0:T(8,128)(2,1)S(1)} %get-tuple-element.41.inner_ref, ...), custom_call_target="tpu_custom_call" | custom-call | flops 4194304 | bytes 1458304 | tf_op jit(solution)/shard_map/pallas_call | solution.py:26
  52.0 7.0 %all-to-all-done.2.mine_ref = bf16[32,16,128]{2,1,0:T(8,128)(2,1)S(1)} async-done(((bf16[32,16,128]{2,1,0:T(8,128)(2,1)}), bf16[32,16,128]{2,1,0:T(8,128)(2,1)S(1)}, u32[]{:S(2)}, u32[]{:S(2)}) %all-to-all-start.2) | async-done | bytes 131104 | tf_op jit(solution)/shard_map/all_to_all | solution.py:59
  59.1 0.0 collective-permute-start.7
  59.1 1.3 %collective-permute-done.7.other_ref = bf16[32,16,128]{2,1,0:T(8,128)(2,1)S(1)} collective-permute-done((bf16[32,16,128]{2,1,0:T(8,128)(2,1)S(1)}, bf16[32,16,128]{2,1,0:T(8,128)(2,1)S(1)}, u32[]{:S(2)}, u32[]{:S(2)}) %collective-permute-start.7) | collective-permute-done | bytes 131104 | tf_op jit(solution)/shard_map/ppermute | solution.py:54
  60.4 1.1 %shard_map.111 = (f32[27,64,64]{2,1,0:T(8,128)}, f32[64,128]{1,0:T(8,128)}) custom-call(s32[1]{0:T(128)} %bitcast.parity_ref, bf16[32,16,128]{2,1,0:T(8,128)(2,1)S(1)} %all-to-all-done.2.mine_ref, bf16[32,16,128]{2,1,0:T(8,128)(2,1)S(1)} %collective-permute-done.7.other_ref), custom_call_target="tpu_custom_call" | custom-call | flops 1000 | bytes 737284 | tf_op jit(solution)/shard_map/pallas_call | solution.py:26
  (1 shorter events, 0.0 us)
Async XLA Ops:
  0.6 21.1 %collective-permute-start.1 = (bf16[64,1,16,256]{3,2,0,1:T(8,128)(2,1)}, bf16[64,1,16,256]{3,2,0,1:T(8,128)(2,1)S(1)}, u32[]{:S(2)}, u32[]{:S(2)}) collective-permute-start(bf16[64,1,16,256]{3,2,0,1:T(8,128)(2,1)} %bitcast.33), channel_id=1, source_target_pairs={{0,28},{1,29},{2,30},{3,31},{4,0},{5,1},{6,2},{7,3},{8,4},{9,5},{1... | collective-permute-start | bytes 1572872 | tf_op jit(solution)/shard_map/ppermute | solution.py:50
  4.0 17.8 %collective-permute-start = (bf16[64,1,16,256]{3,2,0,1:T(8,128)(2,1)}, bf16[64,1,16,256]{3,2,0,1:T(8,128)(2,1)S(1)}, u32[]{:S(2)}, u32[]{:S(2)}) collective-permute-start(bf16[64,1,16,256]{3,2,0,1:T(8,128)(2,1)} %bitcast.34), channel_id=1, source_target_pairs={{0,4},{1,5},{2,6},{3,7},{4,8},{5,9},{6,10},{7,11},{8,12},{9,13},{1... | collective-permute-start | bytes 1572872 | tf_op jit(solution)/shard_map/ppermute | solution.py:50
  4.0 0.8 %copy-start.2 = (bf16[128,128]{1,0:T(8,128)(2,1)S(1)}, bf16[128,128]{1,0:T(8,128)(2,1)}, u32[]{:S(2)}) copy-start(bf16[128,128]{1,0:T(8,128)(2,1)} %rows_ref.1) | copy-start | bytes 98308
  4.8 0.7 %copy-start.4 = (s32[1,32]{1,0:T(1,128)S(1)}, s32[1,32]{1,0:T(1,128)}, u32[]{:S(2)}) copy-start(s32[1,32]{1,0:T(1,128)} %counts_ref.3) | copy-start | bytes 388
  5.4 10.9 %copy-start.6 = (bf16[27,64,64]{2,1,0:T(8,128)(2,1)S(1)}, bf16[27,64,64]{2,1,0:T(8,128)(2,1)}, u32[]{:S(2)}) copy-start(bf16[27,64,64]{2,1,0:T(8,128)(2,1)} %param.12) | copy-start | bytes 663556
  5.4 12.2 %copy-start.7 = (bf16[64,1,16,256]{3,2,1,0:T(8,128)(2,1)S(1)}, bf16[64,1,16,256]{3,2,1,0:T(8,128)(2,1)}, u32[]{:S(2)}) copy-start(bf16[64,1,16,256]{3,2,1,0:T(8,128)(2,1)} %param.13) | copy-start | bytes 1572868
  6.4 15.4 %all-to-all-start = ((bf16[32,24,128]{2,1,0:T(8,128)(2,1)}), bf16[32,24,128]{2,1,0:T(8,128)(2,1)S(1)}, u32[]{:S(2)}, u32[]{:S(2)}) async-start(bf16[32,24,128]{2,1,0:T(8,128)(2,1)} %bitcast.1), calls=%async_computation | async-start | bytes 393216 | tf_op jit(solution)/shard_map/all_to_all | solution.py:59
  12.4 7.7 %collective-permute-start.3 = (s32[1,256]{1,0:T(1,128)}, s32[1,256]{1,0:T(1,128)S(1)}, u32[]{:S(2)}, u32[]{:S(2)}) collective-permute-start(s32[1,256]{1,0:T(1,128)} %own_cells.5), channel_id=1, source_target_pairs={{0,28},{1,29},{2,30},{3,31},{4,0},{5,1},{6,2},{7,3},{8,4},{9,5},{1... | collective-permute-start | bytes 3080 | tf_op jit(solution)/shard_map/ppermute | solution.py:50
  14.9 5.2 %collective-permute-start.2 = (s32[1,256]{1,0:T(1,128)}, s32[1,256]{1,0:T(1,128)S(1)}, u32[]{:S(2)}, u32[]{:S(2)}) collective-permute-start(s32[1,256]{1,0:T(1,128)} %own_cells.5), channel_id=1, source_target_pairs={{0,4},{1,5},{2,6},{3,7},{4,8},{5,9},{6,10},{7,11},{8,12},{9,13},{1... | collective-permute-start | bytes 3080 | tf_op jit(solution)/shard_map/ppermute | solution.py:50
  17.8 3.9 %copy-start = (bf16[64,1,16,256]{3,2,1,0:T(8,128)(2,1)S(1)}, bf16[64,1,16,256]{3,2,1,0:T(8,128)(2,1)}, u32[]{:S(2)}) copy-start(bf16[64,1,16,256]{3,2,1,0:T(8,128)(2,1)} %param.10) | copy-start | bytes 1572868
  17.8 3.9 %copy-start.1 = (bf16[128,64]{0,1:T(8,128)(2,1)S(1)}, bf16[128,64]{0,1:T(8,128)(2,1)}, u32[]{:S(2)}) copy-start(bf16[128,64]{0,1:T(8,128)(2,1)} %param.11) | copy-start | bytes 49156
  17.9 3.9 %copy-start.3 = (s32[1,256]{1,0:T(1,128)S(1)}, s32[1,256]{1,0:T(1,128)}, u32[]{:S(2)}) copy-start(s32[1,256]{1,0:T(1,128)} %own_cells.5) | copy-start | bytes 3076
  22.8 9.0 %collective-permute-start.4 = (bf16[192,256]{1,0:T(8,128)(2,1)S(1)}, bf16[192,256]{1,0:T(8,128)(2,1)S(1)}, u32[]{:S(2)}, u32[]{:S(2)}) collective-permute-start(bf16[192,256]{1,0:T(8,128)(2,1)S(1)} %get-tuple-element.31), channel_id=1, source_target_pairs={{0,1},{1,2},{2,3},{3,0},{4,5},{5,6},{6,7},{7,4},{8,9},{9,10},{10,1... | collective-permute-start | bytes 294920 | tf_op jit(solution)/shard_map/ppermute | solution.py:50
  22.8 8.9 %collective-permute-start.5 = (bf16[192,256]{1,0:T(8,128)(2,1)S(1)}, bf16[192,256]{1,0:T(8,128)(2,1)S(1)}, u32[]{:S(2)}, u32[]{:S(2)}) collective-permute-start(bf16[192,256]{1,0:T(8,128)(2,1)S(1)} %get-tuple-element.32), channel_id=1, source_target_pairs={{0,3},{1,0},{2,1},{3,2},{4,7},{5,4},{6,5},{7,6},{8,11},{9,8},{10,9... | collective-permute-start | bytes 294920 | tf_op jit(solution)/shard_map/ppermute | solution.py:50
  32.3 1.4 %collective-permute-start.6 = (bf16[27,16,128]{2,1,0:T(8,128)(2,1)S(1)}, bf16[27,16,128]{2,1,0:T(8,128)(2,1)S(1)}, u32[]{:S(2)}, u32[]{:S(2)}) collective-permute-start(bf16[27,16,128]{2,1,0:T(8,128)(2,1)S(1)} %get-tuple-element.35), channel_id=1, source_target_pairs={{0,4},{4,0},{8,12},{12,8},{16,20},{20,16},{24,28},{28,24},{1,5},{5... | collective-permute-start | bytes 331784 | tf_op jit(solution)/shard_map/ppermute | solution.py:54
  33.3 17.4 %copy-start.5 = (s32[1,32]{1,0:T(1,128)S(1)}, s32[1,32]{1,0:T(1,128)}, u32[]{:S(2)}) copy-start(s32[1,32]{1,0:T(1,128)} %counts_ref.3) | copy-start | bytes 388
  34.4 12.8 %all-to-all-start.1 = ((bf16[32,32,128]{2,1,0:T(8,128)(2,1)}), bf16[32,32,128]{2,1,0:T(8,128)(2,1)S(1)}, u32[]{:S(2)}, u32[]{:S(2)}) async-start(bf16[32,32,128]{2,1,0:T(8,128)(2,1)} %shard_map.108), calls=%async_computation.1 | async-start | bytes 524288 | tf_op jit(solution)/shard_map/all_to_all | solution.py:59
  48.0 11.1 %all-to-all-start.2 = ((bf16[32,16,128]{2,1,0:T(8,128)(2,1)}), bf16[32,16,128]{2,1,0:T(8,128)(2,1)S(1)}, u32[]{:S(2)}, u32[]{:S(2)}) async-start(bf16[32,16,128]{2,1,0:T(8,128)(2,1)} %shard_map.109), calls=%async_computation.2 | async-start | bytes 262144 | tf_op jit(solution)/shard_map/all_to_all | solution.py:59
  59.1 1.3 %collective-permute-start.7 = (bf16[32,16,128]{2,1,0:T(8,128)(2,1)S(1)}, bf16[32,16,128]{2,1,0:T(8,128)(2,1)S(1)}, u32[]{:S(2)}, u32[]{:S(2)}) collective-permute-start(bf16[32,16,128]{2,1,0:T(8,128)(2,1)S(1)} %all-to-all-done.2.mine_ref), channel_id=1, source_target_pairs={{0,4},{4,0},{8,12},{12,8},{16,20},{20,16},{24,28},{28,24},{1,5},{5... | collective-permute-start | bytes 393224 | tf_op jit(solution)/shard_map/ppermute | solution.py:54

commit v15 on v13

--- a/solution.py
+++ b/solution.py
@@ -108,17 +108,20 @@
 
 
 def first_kernel(
-    ngx, ngy, cap, rows_far, counts_far, send_ref, rows_ref, counts_ref, sems
+    ngx, ngy, cap, rows_far, counts_far, base_far, send_ref, again_far, rows_ref, counts_ref, sems
 ):
+    again = pltpu.make_async_copy(base_far, again_far, sems.at[2])
     copies = [
         pltpu.make_async_copy(rows_far, rows_ref, sems.at[0]),
         pltpu.make_async_copy(counts_far, counts_ref, sems.at[1]),
     ]
     for copy in copies:
         copy.start()
+    again.start()
     for copy in copies:
         copy.wait()
     pick(ngx, ngy, cap, counts_ref, rows_ref, send_ref)
+    again.wait()
 
 
 def same_kernel(in_ref, out_ref):
@@ -454,22 +457,23 @@
     one = 2 * rows * rows * nz
 
     base = base_field.reshape(chans, cy, nz)
-    west, east = move(base_field, 1, 0), move(base_field, -1, 0)
-    planes = (base, west.reshape(base.shape), east.reshape(base.shape))
+    west = move(base, 1, 0)
     lists = (cell_lists, move(cell_lists, 1, 0), move(cell_lists, -1, 0))
-    (payload,) = call(
+    payload, again = call(
         functools.partial(first_kernel, ngx, ngy, cap),
-        [shape((ndev * 3 * cap, feats), BF16)],
-        (particles, send_counts),
+        [shape((ndev * 3 * cap, feats), BF16), base],
+        (particles, send_counts, base),
         2 * slots * nrows * feats,
         (
             pltpu.VMEM(particles.shape, BF16),
             pltpu.VMEM(send_counts.shape, I32),
-            pltpu.SemaphoreType.DMA((2,)),
+            pltpu.SemaphoreType.DMA((3,)),
         ),
-        far=range(2),
+        far=range(3),
+        far_out=(1,),
         limit=ALL,
     )
+    planes = (base, west, move(again, -1, 0))
     recv = exchange(payload, ndev)
 
     cot = cotangent[:, 0].transpose(1, 0, 2)

time: 61.3 us -> 77 us (1.26)
  Pallas kernels: 13.1 us -> 29.1 us
    pallas_call x10, Pallas kernels: 13.1 us -> 29.1 us  [call(): pl.pallas_call(kernel, out_shape=[jax.ShapeDtypeStruct(o.shape, o.dtype)...]
  transfers between devices with their start and end apart: 11 -> 11, of which waited for: 5 -> 5; matrix products, arithmetic and copies ran while one was open for 8% -> 7% of each run, Pallas kernels for 15% -> 33%
where the time goes in v15:
time: 77 us; the launch traced here: 76.6 us
  Pallas kernels  29.1 us (38%)
  starting transfers between devices  20.9 us (27%)
  waiting for transfers between devices  20.6 us (27%)
  local copies, waits for them, and re-layouts  5.13 us (7%)
  between operations  0.89 us (1%)
    pallas_call x10, Pallas kernels, call(): pl.pallas_call(kernel, out_shape=[jax.ShapeDtypeStruct(o.shape, o.dtype)...  29.1 us
    all_to_all x3, waiting for transfers between devices, exchange(): lax.all_to_all(payload.reshape(ndev, rows // ndev, width), AXES, split_ax...  18.9 us
    all_to_all x3, starting transfers between devices, exchange(): lax.all_to_all(payload.reshape(ndev, rows // ndev, width), AXES, split_ax...  11 us
    ppermute x6, starting transfers between devices, send(): return lax.ppermute(block, AXES, pairs)  9.8 us
    reshape x2, local copies, waits for them, and re-layouts, local(): taps = conv_weight.reshape(3, 3, 3, chans, chans)  2.74 us
    ppermute x2, waiting for transfers between devices, swap(): lax.ppermute(block, 'gx', [(i, i ^ 1) for i in range(lax.axis_size('gx'))])  1.74 us
    reshape x2, local copies, waits for them, and re-layouts, local(): wf = taps.transpose(1, 2, 3, 0, 4).reshape(9 * chans, rows)  1.65 us
  transfers between devices with their start and end apart: 11, of which 5 were waited for; matrix products, arithmetic and copies ran while one was open for 7% of the time, Pallas kernels for 33%

profile of v15, /device:TPU:0, one launch (start us, length us, event | category | flops | bytes accessed | tf_op | source)
XLA Modules:
  0.0 76.6 jit_solution(11660113615612991297)
XLA Ops:
  0.6 0.0 copy-start.4
  0.6 0.0 copy-start.5
  0.7 0.5 collective-permute-start
  1.2 17.7 %shard_map.102 = (bf16[768,128]{1,0:T(8,128)(2,1)}, bf16[64,16,256]{2,1,0:T(8,128)(2,1)}) custom-call(bf16[128,128]{1,0:T(8,128)(2,1)} %rows_far.1, s32[1,32]{1,0:T(1,128)} %counts_ref.1, bf16[64,16,256]{2,1,0:T(8,128)(2,1)} %bitcast.29), custom_call_target="tpu_custom_call" | custom-call | flops 8388608 | bytes 1278080 | tf_op jit(solution)/shard_map/pallas_call | solution.py:27
  18.9 3.0 %collective-permute-start.1 = (bf16[64,16,256]{2,1,0:T(8,128)(2,1)}, bf16[64,16,256]{2,1,0:T(8,128)(2,1)S(1)}, u32[]{:S(2)}, u32[]{:S(2)}) collective-permute-start(bf16[64,16,256]{2,1,0:T(8,128)(2,1)} %get-tuple-element.30), channel_id=1, source_target_pairs={{0,28},{1,29},{2,30},{3,31},{4,0},{5,1},{6,2},{7,3},{8,4},{9,5},{1... | collective-permute-start | bytes 1572872 | tf_op jit(solution)/shard_map/ppermute | solution.py:51
  21.8 5.7 %all-to-all-start = ((bf16[32,24,128]{2,1,0:T(8,128)(2,1)}), bf16[32,24,128]{2,1,0:T(8,128)(2,1)S(1)}, u32[]{:S(2)}, u32[]{:S(2)}) async-start(bf16[32,24,128]{2,1,0:T(8,128)(2,1)} %bitcast.40), calls=%async_computation | async-start | bytes 393216 | tf_op jit(solution)/shard_map/all_to_all | solution.py:60
  27.5 2.5 %collective-permute-start.3 = (s32[1,256]{1,0:T(1,128)}, s32[1,256]{1,0:T(1,128)S(1)}, u32[]{:S(2)}, u32[]{:S(2)}) collective-permute-start(s32[1,256]{1,0:T(1,128)} %own_cells.5), channel_id=1, source_target_pairs={{0,28},{1,29},{2,30},{3,31},{4,0},{5,1},{6,2},{7,3},{8,4},{9,5},{1... | collective-permute-start | bytes 3080 | tf_op jit(solution)/shard_map/ppermute | solution.py:51
  30.0 0.0 collective-permute-start.2
  30.0 1.4 %copy.26 = bf16[3,3,3,64,64]{4,0,1,3,2:T(4,128)(2,1)S(1)} copy(bf16[3,3,3,64,64]{4,3,2,1,0:T(8,128)(2,1)} %bitcast.38) | data formatting | bytes 442368 | tf_op jit(solution)/shard_map/reshape | solution.py:480
  31.4 0.0 copy-done.4
  31.4 1.3 %copy.17 = bf16[3,3,3,64,64]{3,2,1,4,0:T(4,128)(2,1)} copy(bf16[3,3,3,64,64]{4,3,2,1,0:T(8,128)(2,1)S(1)} %bitcast.39) | data formatting | bytes 442368 | tf_op jit(solution)/shard_map/reshape | solution.py:480
  32.7 0.0 copy-done.5
  32.7 0.2 copy.27
  32.9 0.0 copy-start
  32.9 0.0 copy-start.1
  32.9 0.0 copy-start.2
  32.9 0.4 reshape.38
  33.3 0.2 copy.21.wb_ref
  33.5 1.5 %reshape.37 = bf16[576,192]{0,1:T(8,128)(2,1)S(1)} reshape(bf16[3,3,64,3,64]{2,1,0,4,3:T(4,128)(2,1)} %bitcast.36) | data formatting | bytes 442368 | tf_op jit(solution)/shard_map/reshape | solution.py:481
  35.0 0.2 copy.18.wf_ref
  35.2 0.0 collective-permute-done.3.east_cells
  35.2 0.0 collective-permute-done.2.west_cells
  35.2 1.6 %all-to-all-done = bf16[32,24,128]{2,1,0:T(8,128)(2,1)S(1)} async-done(((bf16[32,24,128]{2,1,0:T(8,128)(2,1)}), bf16[32,24,128]{2,1,0:T(8,128)(2,1)S(1)}, u32[]{:S(2)}, u32[]{:S(2)}) %all-to-all-start) | async-done | bytes 196640 | tf_op jit(solution)/shard_map/all_to_all | solution.py:60
  36.8 0.0 collective-permute-done.west_ref
  36.8 0.0 collective-permute-done.1.east_ref
  36.8 0.0 copy-done
  36.8 0.0 copy-done.1
  36.9 0.0 copy-done.2
  36.9 1.0 %shard_map.103 = (bf16[192,256]{1,0:T(8,128)(2,1)S(1)}, bf16[192,256]{1,0:T(8,128)(2,1)S(1)}, bf16[3,64,256]{2,1,0:T(8,128)(2,1)S(1)}, bf16[3,256,256]{2,1,0:T(8,128)(2,1)S(1)}) custom-call(bf16[768,128]{1,0:T(8,128)(2,1)S(1)} %bitcast.32, bf16[64,16,256]{2,1,0:T(8,128)(2,1)S(1)} %bitcast.30, bf16[64,16,256]{2,1,0:T(8,128)(2,1)S(1)} %collective-permute-done.west_ref, ...), custom_call_target="tpu_custom_call" | custom-call | flops 75497472 | bytes 3222528 | tf_op jit(solution)/shard_map/pallas_call | solution.py:27
  37.8 0.1 collective-permute-start.4
  37.9 3.8 %collective-permute-start.5 = (bf16[192,256]{1,0:T(8,128)(2,1)S(1)}, bf16[192,256]{1,0:T(8,128)(2,1)S(1)}, u32[]{:S(2)}, u32[]{:S(2)}) collective-permute-start(bf16[192,256]{1,0:T(8,128)(2,1)S(1)} %get-tuple-element.36), channel_id=1, source_target_pairs={{0,3},{1,0},{2,1},{3,2},{4,7},{5,4},{6,5},{7,6},{8,11},{9,8},{10,9... | collective-permute-start | bytes 294920 | tf_op jit(solution)/shard_map/ppermute | solution.py:51
  41.7 5.1 %shard_map.104 = (bf16[16,192,256]{2,1,0:T(8,128)(2,1)S(1)}, bf16[16,64,256]{2,1,0:T(8,128)(2,1)S(1)}, f32[576,192]{1,0:T(8,128)S(1)}, f32[4,64,256]{2,1,0:T(8,1...) custom-call(bf16[3,64,256]{2,1,0:T(8,128)(2,1)S(1)} %get-tuple-element.31.values_ref, ...), custom_call_target="tpu_custom_call" | custom-call | flops 2717908992 | bytes 7801856 | tf_op jit(solution)/shard_map/pallas_call | solution.py:27
  46.8 0.0 collective-permute-done.4.north_ref
  46.8 0.0 collective-permute-done.5.south_ref
  46.8 0.6 shard_map.105
  47.4 0.1 collective-permute-start.6
  47.5 0.9 %shard_map.106 = (bf16[32,16,128]{2,1,0:T(8,128)(2,1)S(1)}, bf16[5,16,128]{2,1,0:T(8,128)(2,1)S(1)}) custom-call(f32[4,192,256]{2,1,0:T(8,128)S(1)} %get-tuple-element.40.slot_ref, bf16[3,768,256]{2,1,0:T(8,128)(2,1)S(1)} %get-tuple-element.41.plane_ref, bf16[3,256,256]{2,1,0:T(8,128)(2,1)S(1)} %get-tuple-element.32.hot_ref, ...), custom_call_target="tpu_custom_call" | custom-call | flops 113246208 | bytes 3849216 | tf_op jit(solution)/shard_map/pallas_call | solution.py:27
  48.4 0.0 copy-start.3
  48.4 0.4 collective-permute-done.6.got_ref
  48.8 0.7 shard_map.107.in_ref
  49.5 2.6 %all-to-all-start.1 = ((bf16[32,32,128]{2,1,0:T(8,128)(2,1)}), bf16[32,32,128]{2,1,0:T(8,128)(2,1)S(1)}, u32[]{:S(2)}, u32[]{:S(2)}) async-start(bf16[32,32,128]{2,1,0:T(8,128)(2,1)} %shard_map.108), calls=%async_computation.1 | async-start | bytes 524288 | tf_op jit(solution)/shard_map/all_to_all | solution.py:60
  52.1 10.2 %all-to-all-done.1.recv_ref = bf16[32,32,128]{2,1,0:T(8,128)(2,1)S(1)} async-done(((bf16[32,32,128]{2,1,0:T(8,128)(2,1)}), bf16[32,32,128]{2,1,0:T(8,128)(2,1)S(1)}, u32[]{:S(2)}, u32[]{:S(2)}) %all-to-all-start.1) | async-done | bytes 262176 | tf_op jit(solution)/shard_map/all_to_all | solution.py:60
  62.3 0.7 shard_map.109
  63.1 2.7 %all-to-all-start.2 = ((bf16[32,16,128]{2,1,0:T(8,128)(2,1)}), bf16[32,16,128]{2,1,0:T(8,128)(2,1)S(1)}, u32[]{:S(2)}, u32[]{:S(2)}) async-start(bf16[32,16,128]{2,1,0:T(8,128)(2,1)} %shard_map.109), calls=%async_computation.2 | async-start | bytes 262144 | tf_op jit(solution)/shard_map/all_to_all | solution.py:60
  65.7 0.0 copy-done.3
  65.8 1.4 %shard_map.110 = (f32[128,128]{1,0:T(8,128)}, bf16[64,16,256]{2,1,0:T(8,128)(2,1)}) custom-call(bf16[32,32,128]{2,1,0:T(8,128)(2,1)S(1)} %all-to-all-done.1.recv_ref, s32[1,32]{1,0:T(1,128)S(1)} %copy-done.3, bf16[64,128]{1,0:T(8,128)(2,1)S(1)} %bitcast.35, bf16[16,64,256]{2,1,0:T(8,128)(2,1)S(1)} %get-tuple-element.45.inner_ref, ...), custom_call_target="tpu_custom_call" | custom-call | flops 4194304 | bytes 1458304 | tf_op jit(solution)/shard_map/pallas_call | solution.py:27
  67.1 7.0 %all-to-all-done.2.mine_ref = bf16[32,16,128]{2,1,0:T(8,128)(2,1)S(1)} async-done(((bf16[32,16,128]{2,1,0:T(8,128)(2,1)}), bf16[32,16,128]{2,1,0:T(8,128)(2,1)S(1)}, u32[]{:S(2)}, u32[]{:S(2)}) %all-to-all-start.2) | async-done | bytes 131104 | tf_op jit(solution)/shard_map/all_to_all | solution.py:60
  74.2 0.0 collective-permute-start.7
  74.2 1.3 %collective-permute-done.7.other_ref = bf16[32,16,128]{2,1,0:T(8,128)(2,1)S(1)} collective-permute-done((bf16[32,16,128]{2,1,0:T(8,128)(2,1)S(1)}, bf16[32,16,128]{2,1,0:T(8,128)(2,1)S(1)}, u32[]{:S(2)}, u32[]{:S(2)}) %collective-permute-start.7) | collective-permute-done | bytes 131104 | tf_op jit(solution)/shard_map/ppermute | solution.py:55
  75.5 1.1 %shard_map.111 = (f32[27,64,64]{2,1,0:T(8,128)}, f32[64,128]{1,0:T(8,128)}) custom-call(s32[1]{0:T(128)} %bitcast.parity_ref, bf16[32,16,128]{2,1,0:T(8,128)(2,1)S(1)} %all-to-all-done.2.mine_ref, bf16[32,16,128]{2,1,0:T(8,128)(2,1)S(1)} %collective-permute-done.7.other_ref), custom_call_target="tpu_custom_call" | custom-call | flops 1000 | bytes 737284 | tf_op jit(solution)/shard_map/pallas_call | solution.py:27
  (1 shorter events, 0.0 us)
Async XLA Ops:
  0.6 30.8 %copy-start.4 = (bf16[27,64,64]{2,1,0:T(8,128)(2,1)S(1)}, bf16[27,64,64]{2,1,0:T(8,128)(2,1)}, u32[]{:S(2)}) copy-start(bf16[27,64,64]{2,1,0:T(8,128)(2,1)} %param.12) | copy-start | bytes 663556
  0.6 32.1 %copy-start.5 = (bf16[64,1,16,256]{3,2,1,0:T(8,128)(2,1)S(1)}, bf16[64,1,16,256]{3,2,1,0:T(8,128)(2,1)}, u32[]{:S(2)}) copy-start(bf16[64,1,16,256]{3,2,1,0:T(8,128)(2,1)} %param.13) | copy-start | bytes 1572868
  0.7 36.2 %collective-permute-start = (bf16[64,16,256]{2,1,0:T(8,128)(2,1)}, bf16[64,16,256]{2,1,0:T(8,128)(2,1)S(1)}, u32[]{:S(2)}, u32[]{:S(2)}) collective-permute-start(bf16[64,16,256]{2,1,0:T(8,128)(2,1)} %bitcast.28), channel_id=1, source_target_pairs={{0,4},{1,5},{2,6},{3,7},{4,8},{5,9},{6,10},{7,11},{8,12},{9,13},{1... | collective-permute-start | bytes 1572872 | tf_op jit(solution)/shard_map/ppermute | solution.py:51
  18.9 18.0 %collective-permute-start.1 = (bf16[64,16,256]{2,1,0:T(8,128)(2,1)}, bf16[64,16,256]{2,1,0:T(8,128)(2,1)S(1)}, u32[]{:S(2)}, u32[]{:S(2)}) collective-permute-start(bf16[64,16,256]{2,1,0:T(8,128)(2,1)} %get-tuple-element.30), channel_id=1, source_target_pairs={{0,28},{1,29},{2,30},{3,31},{4,0},{5,1},{6,2},{7,3},{8,4},{9,5},{1... | collective-permute-start | bytes 1572872 | tf_op jit(solution)/shard_map/ppermute | solution.py:51
  21.8 15.0 %all-to-all-start = ((bf16[32,24,128]{2,1,0:T(8,128)(2,1)}), bf16[32,24,128]{2,1,0:T(8,128)(2,1)S(1)}, u32[]{:S(2)}, u32[]{:S(2)}) async-start(bf16[32,24,128]{2,1,0:T(8,128)(2,1)} %bitcast.40), calls=%async_computation | async-start | bytes 393216 | tf_op jit(solution)/shard_map/all_to_all | solution.py:60
  27.5 7.7 %collective-permute-start.3 = (s32[1,256]{1,0:T(1,128)}, s32[1,256]{1,0:T(1,128)S(1)}, u32[]{:S(2)}, u32[]{:S(2)}) collective-permute-start(s32[1,256]{1,0:T(1,128)} %own_cells.5), channel_id=1, source_target_pairs={{0,28},{1,29},{2,30},{3,31},{4,0},{5,1},{6,2},{7,3},{8,4},{9,5},{1... | collective-permute-start | bytes 3080 | tf_op jit(solution)/shard_map/ppermute | solution.py:51
  30.0 5.2 %collective-permute-start.2 = (s32[1,256]{1,0:T(1,128)}, s32[1,256]{1,0:T(1,128)S(1)}, u32[]{:S(2)}, u32[]{:S(2)}) collective-permute-start(s32[1,256]{1,0:T(1,128)} %own_cells.5), channel_id=1, source_target_pairs={{0,4},{1,5},{2,6},{3,7},{4,8},{5,9},{6,10},{7,11},{8,12},{9,13},{1... | collective-permute-start | bytes 3080 | tf_op jit(solution)/shard_map/ppermute | solution.py:51
  32.9 3.9 %copy-start = (bf16[64,1,16,256]{3,2,1,0:T(8,128)(2,1)S(1)}, bf16[64,1,16,256]{3,2,1,0:T(8,128)(2,1)}, u32[]{:S(2)}) copy-start(bf16[64,1,16,256]{3,2,1,0:T(8,128)(2,1)} %param.10) | copy-start | bytes 1572868
  32.9 3.9 %copy-start.1 = (bf16[128,64]{0,1:T(8,128)(2,1)S(1)}, bf16[128,64]{0,1:T(8,128)(2,1)}, u32[]{:S(2)}) copy-start(bf16[128,64]{0,1:T(8,128)(2,1)} %param.11) | copy-start | bytes 49156
  32.9 3.9 %copy-start.2 = (s32[1,256]{1,0:T(1,128)S(1)}, s32[1,256]{1,0:T(1,128)}, u32[]{:S(2)}) copy-start(s32[1,256]{1,0:T(1,128)} %own_cells.5) | copy-start | bytes 3076
  37.8 9.0 %collective-permute-start.4 = (bf16[192,256]{1,0:T(8,128)(2,1)S(1)}, bf16[192,256]{1,0:T(8,128)(2,1)S(1)}, u32[]{:S(2)}, u32[]{:S(2)}) collective-permute-start(bf16[192,256]{1,0:T(8,128)(2,1)S(1)} %get-tuple-element.35), channel_id=1, source_target_pairs={{0,1},{1,2},{2,3},{3,0},{4,5},{5,6},{6,7},{7,4},{8,9},{9,10},{10,1... | collective-permute-start | bytes 294920 | tf_op jit(solution)/shard_map/ppermute | solution.py:51
  37.9 8.9 %collective-permute-start.5 = (bf16[192,256]{1,0:T(8,128)(2,1)S(1)}, bf16[192,256]{1,0:T(8,128)(2,1)S(1)}, u32[]{:S(2)}, u32[]{:S(2)}) collective-permute-start(bf16[192,256]{1,0:T(8,128)(2,1)S(1)} %get-tuple-element.36), channel_id=1, source_target_pairs={{0,3},{1,0},{2,1},{3,2},{4,7},{5,4},{6,5},{7,6},{8,11},{9,8},{10,9... | collective-permute-start | bytes 294920 | tf_op jit(solution)/shard_map/ppermute | solution.py:51
  47.4 1.4 %collective-permute-start.6 = (bf16[27,16,128]{2,1,0:T(8,128)(2,1)S(1)}, bf16[27,16,128]{2,1,0:T(8,128)(2,1)S(1)}, u32[]{:S(2)}, u32[]{:S(2)}) collective-permute-start(bf16[27,16,128]{2,1,0:T(8,128)(2,1)S(1)} %get-tuple-element.39), channel_id=1, source_target_pairs={{0,4},{4,0},{8,12},{12,8},{16,20},{20,16},{24,28},{28,24},{1,5},{5... | collective-permute-start | bytes 331784 | tf_op jit(solution)/shard_map/ppermute | solution.py:55
  48.4 17.4 %copy-start.3 = (s32[1,32]{1,0:T(1,128)S(1)}, s32[1,32]{1,0:T(1,128)}, u32[]{:S(2)}) copy-start(s32[1,32]{1,0:T(1,128)} %counts_ref.1) | copy-start | bytes 388
  49.5 12.8 %all-to-all-start.1 = ((bf16[32,32,128]{2,1,0:T(8,128)(2,1)}), bf16[32,32,128]{2,1,0:T(8,128)(2,1)S(1)}, u32[]{:S(2)}, u32[]{:S(2)}) async-start(bf16[32,32,128]{2,1,0:T(8,128)(2,1)} %shard_map.108), calls=%async_computation.1 | async-start | bytes 524288 | tf_op jit(solution)/shard_map/all_to_all | solution.py:60
  63.1 11.1 %all-to-all-start.2 = ((bf16[32,16,128]{2,1,0:T(8,128)(2,1)}), bf16[32,16,128]{2,1,0:T(8,128)(2,1)S(1)}, u32[]{:S(2)}, u32[]{:S(2)}) async-start(bf16[32,16,128]{2,1,0:T(8,128)(2,1)} %shard_map.109), calls=%async_computation.2 | async-start | bytes 262144 | tf_op jit(solution)/shard_map/all_to_all | solution.py:60
  74.2 1.3 %collective-permute-start.7 = (bf16[32,16,128]{2,1,0:T(8,128)(2,1)S(1)}, bf16[32,16,128]{2,1,0:T(8,128)(2,1)S(1)}, u32[]{:S(2)}, u32[]{:S(2)}) collective-permute-start(bf16[32,16,128]{2,1,0:T(8,128)(2,1)S(1)} %all-to-all-done.2.mine_ref), channel_id=1, source_target_pairs={{0,4},{4,0},{8,12},{12,8},{16,20},{20,16},{24,28},{28,24},{1,5},{5... | collective-permute-start | bytes 393224 | tf_op jit(solution)/shard_map/ppermute | solution.py:55

commit v16 on v13

--- a/solution.py
+++ b/solution.py
@@ -116,16 +116,28 @@
     ]
     for copy in copies:
         copy.start()
-    for copy in copies:
-        copy.wait()
-    pick(ngx, ngy, cap, counts_ref, rows_ref, send_ref)
+    copies[1].wait()
+    pick(ngx, ngy, cap, counts_ref, rows_ref, send_ref, copies[0])
+
+
+def turns_kernel(weight_ref, cot_ref, wf_ref, wb_ref, cot_out):
+    cot_out[...] = jnp.swapaxes(cot_ref[...], 0, 1)
+    chans = cot_ref.shape[0]
+    three = range(3)
+    for dy in three:
+        for n in three:
+            rows = pl.ds((dy * 3 + n) * chans, chans)
+            taps = [weight_ref[dx * 9 + dy * 3 + n] for dx in three]
+            wf_ref[rows] = jnp.concatenate(taps, axis=1)
+            taps = [weight_ref[n * 9 + dy * 3 + dz].astype(F32).T for dz in three]
+            wb_ref[rows] = jnp.concatenate(taps, axis=1).astype(BF16)
 
 
 def same_kernel(in_ref, out_ref):
     pass
 
 
-def pick(ngx, ngy, cap, counts_ref, rows_ref, out_ref):
+def pick(ngx, ngy, cap, counts_ref, rows_ref, out_ref, rows_copy):
     ndev = ngx * ngy
     nrows, feats = rows_ref.shape
     slots = ndev * cap
@@ -137,6 +149,7 @@
     place = lax.broadcasted_iota(I32, (ndev, cap, nrows), 1).reshape(slots, nrows).astype(F32)
     row = lax.broadcasted_iota(I32, (slots, nrows), 1).astype(F32)
     onehot = jnp.where((row == place + start) & (place < held), 1.0, 0.0).astype(BF16)
+    rows_copy.wait()
     raw = mm(onehot, rows_ref[...]).reshape(ngx, ngy, cap, feats)
     parts = [rolled(raw, dx, 0).reshape(ndev, cap, feats) for dx in (-1, 0, 1)]
     out_ref[...] = jnp.stack(parts, axis=1).reshape(out_ref.shape).astype(BF16)
@@ -472,10 +485,12 @@
     )
     recv = exchange(payload, ndev)
 
-    cot = cotangent[:, 0].transpose(1, 0, 2)
-    taps = conv_weight.reshape(3, 3, 3, chans, chans)
-    wf = taps.transpose(1, 2, 3, 0, 4).reshape(9 * chans, rows)
-    wb = taps.transpose(1, 0, 4, 2, 3).reshape(9 * chans, rows)
+    wf, wb, cot = call(
+        turns_kernel,
+        [shape((9 * chans, rows), BF16)] * 2 + [shape((cy, chans, nz), BF16)],
+        (conv_weight, cotangent.reshape(chans, cy, nz)),
+        1000,
+    )
 
     first, last, values, hots = call(
         functools.partial(outer_kernel, ndev, cap),

time: 61.3 us -> 61.3 us (level)
  local copies, waits for them, and re-layouts: 5.13 us -> 2.08 us
  waiting for transfers between devices: 20.6 us -> 23.3 us
    reshape x6 -> x0, local copies, waits for them, and re-layouts: 4.94 us -> none  [the longest x2 2.74 us: local(): taps = conv_weight.reshape(3, 3, 3, chans, chans)]
    ppermute x6, waiting for transfers between devices: 0.02 us -> 2.43 us  [send(): return lax.ppermute(block, AXES, pairs)]
    unnamed x13 -> x12, local copies, waits for them, and re-layouts: 0.19 us -> 2.08 us
    pallas_call x10 -> x11, Pallas kernels: 13.1 us -> 13.5 us  [call(): pl.pallas_call(kernel, out_shape=[jax.ShapeDtypeStruct(o.shape, o.dtype)...]
  transfers between devices with their start and end apart: 11 -> 11, of which waited for: 5 -> 7; matrix products, arithmetic and copies ran while one was open for 8% -> 0% of each run, Pallas kernels for 15% -> 15%
where the time goes in v16:
time: 61.3 us; the launch traced here: 60.9 us
  waiting for transfers between devices  23.3 us (38%)
  starting transfers between devices  21.1 us (34%)
  Pallas kernels  13.5 us (22%)
  local copies, waits for them, and re-layouts  2.08 us (3%)
  between operations  0.84 us (1%)
    all_to_all x3, waiting for transfers between devices, exchange(): lax.all_to_all(payload.reshape(ndev, rows // ndev, width), AXES, split_ax...  19.2 us
    pallas_call x11, Pallas kernels, call(): pl.pallas_call(kernel, out_shape=[jax.ShapeDtypeStruct(o.shape, o.dtype)...  13.5 us
    all_to_all x3, starting transfers between devices, exchange(): lax.all_to_all(payload.reshape(ndev, rows // ndev, width), AXES, split_ax...  11.3 us
    ppermute x6, starting transfers between devices, send(): return lax.ppermute(block, AXES, pairs)  9.73 us
    ppermute x6, waiting for transfers between devices, send(): return lax.ppermute(block, AXES, pairs)  2.43 us
    unnamed x12, local copies, waits for them, and re-layouts  2.08 us
    ppermute x2, waiting for transfers between devices, swap(): lax.ppermute(block, 'gx', [(i, i ^ 1) for i in range(lax.axis_size('gx'))])  1.74 us
  transfers between devices with their start and end apart: 11, of which 7 were waited for; matrix products, arithmetic and copies ran while one was open for 0% of the time, Pallas kernels for 15%

profile of v16, /device:TPU:0, one launch (start us, length us, event | category | flops | bytes accessed | tf_op | source)
XLA Modules:
  0.0 60.9 jit_solution(11484278474586056117)
XLA Ops:
  0.6 0.0 copy-start.1
  0.6 0.0 copy-start.4
  0.7 0.0 copy-start.3
  0.7 3.4 %collective-permute-start.1 = (bf16[64,1,16,256]{3,2,0,1:T(8,128)(2,1)}, bf16[64,1,16,256]{3,2,0,1:T(8,128)(2,1)S(1)}, u32[]{:S(2)}, u32[]{:S(2)}) collective-permute-start(bf16[64,1,16,256]{3,2,0,1:T(8,128)(2,1)} %bitcast.17), channel_id=1, source_target_pairs={{0,28},{1,29},{2,30},{3,31},{4,0},{5,1},{6,2},{7,3},{8,4},{9,5},{1... | collective-permute-start | bytes 1572872 | tf_op jit(solution)/shard_map/ppermute | solution.py:51
  4.0 0.0 collective-permute-start
  4.1 1.7 %shard_map.102 = bf16[768,128]{1,0:T(8,128)(2,1)} custom-call(bf16[128,128]{1,0:T(8,128)(2,1)} %rows_far.1, s32[1,32]{1,0:T(1,128)} %counts_ref.1), custom_call_target="tpu_custom_call" | custom-call | flops 8388608 | bytes 229504 | tf_op jit(solution)/shard_map/pallas_call | solution.py:27
  5.7 6.0 %all-to-all-start = ((bf16[32,24,128]{2,1,0:T(8,128)(2,1)}), bf16[32,24,128]{2,1,0:T(8,128)(2,1)S(1)}, u32[]{:S(2)}, u32[]{:S(2)}) async-start(bf16[32,24,128]{2,1,0:T(8,128)(2,1)} %bitcast.27), calls=%async_computation | async-start | bytes 393216 | tf_op jit(solution)/shard_map/all_to_all | solution.py:60
  11.8 2.5 %collective-permute-start.3 = (s32[1,256]{1,0:T(1,128)}, s32[1,256]{1,0:T(1,128)S(1)}, u32[]{:S(2)}, u32[]{:S(2)}) collective-permute-start(s32[1,256]{1,0:T(1,128)} %own_cells.5), channel_id=1, source_target_pairs={{0,28},{1,29},{2,30},{3,31},{4,0},{5,1},{6,2},{7,3},{8,4},{9,5},{1... | collective-permute-start | bytes 3080 | tf_op jit(solution)/shard_map/ppermute | solution.py:51
  14.3 0.0 collective-permute-start.2
  14.3 0.0 copy-start
  14.3 1.0 %copy-done = bf16[64,1,16,256]{3,2,1,0:T(8,128)(2,1)S(1)} copy-done((bf16[64,1,16,256]{3,2,1,0:T(8,128)(2,1)S(1)}, bf16[64,1,16,256]{3,2,1,0:T(8,128)(2,1)}, u32[]{:S(2)}) %copy-start) | copy-done | bytes 524312
  15.3 0.0 copy-start.2
  15.3 1.0 %copy-done.2 = bf16[27,64,64]{2,1,0:T(8,128)(2,1)S(1)} copy-done((bf16[27,64,64]{2,1,0:T(8,128)(2,1)S(1)}, bf16[27,64,64]{2,1,0:T(8,128)(2,1)}, u32[]{:S(2)}) %copy-start.2) | copy-done | bytes 221208
  16.3 0.4 shard_map.103
  16.7 0.6 %collective-permute-done.3.east_cells = s32[1,256]{1,0:T(1,128)S(1)} collective-permute-done((s32[1,256]{1,0:T(1,128)}, s32[1,256]{1,0:T(1,128)S(1)}, u32[]{:S(2)}, u32[]{:S(2)}) %collective-permute-start.3) | collective-permute-done | bytes 1056 | tf_op jit(solution)/shard_map/ppermute | solution.py:51
  17.4 1.8 %collective-permute-done.2.west_cells = s32[1,256]{1,0:T(1,128)S(1)} collective-permute-done((s32[1,256]{1,0:T(1,128)}, s32[1,256]{1,0:T(1,128)S(1)}, u32[]{:S(2)}, u32[]{:S(2)}) %collective-permute-start.2) | collective-permute-done | bytes 1056 | tf_op jit(solution)/shard_map/ppermute | solution.py:51
  19.2 2.0 %all-to-all-done = bf16[32,24,128]{2,1,0:T(8,128)(2,1)S(1)} async-done(((bf16[32,24,128]{2,1,0:T(8,128)(2,1)}), bf16[32,24,128]{2,1,0:T(8,128)(2,1)S(1)}, u32[]{:S(2)}, u32[]{:S(2)}) %all-to-all-start) | async-done | bytes 196640 | tf_op jit(solution)/shard_map/all_to_all | solution.py:60
  21.1 0.0 collective-permute-done.1
  21.1 0.0 collective-permute-done
  21.1 0.0 copy-done.1
  21.1 0.0 copy-done.4
  21.1 0.0 copy-done.3
  21.1 1.0 %shard_map.104 = (bf16[192,256]{1,0:T(8,128)(2,1)S(1)}, bf16[192,256]{1,0:T(8,128)(2,1)S(1)}, bf16[3,64,256]{2,1,0:T(8,128)(2,1)S(1)}, bf16[3,256,256]{2,1,0:T(8,128)(2,1)S(1)}) custom-call(bf16[768,128]{1,0:T(8,128)(2,1)S(1)} %bitcast.14, bf16[64,16,256]{2,1,0:T(8,128)(2,1)S(1)} %bitcast.19, bf16[64,16,256]{2,1,0:T(8,128)(2,1)S(1)} %bitcast.23, ...), custom_call_target="tpu_custom_call" | custom-call | flops 75497472 | bytes 3222528 | tf_op jit(solution)/shard_map/pallas_call | solution.py:27
  22.1 0.1 collective-permute-start.4
  22.2 3.8 %collective-permute-start.5 = (bf16[192,256]{1,0:T(8,128)(2,1)S(1)}, bf16[192,256]{1,0:T(8,128)(2,1)S(1)}, u32[]{:S(2)}, u32[]{:S(2)}) collective-permute-start(bf16[192,256]{1,0:T(8,128)(2,1)S(1)} %get-tuple-element.38), channel_id=1, source_target_pairs={{0,3},{1,0},{2,1},{3,2},{4,7},{5,4},{6,5},{7,6},{8,11},{9,8},{10,9... | collective-permute-start | bytes 294920 | tf_op jit(solution)/shard_map/ppermute | solution.py:51
  26.0 5.1 %shard_map.105 = (bf16[16,192,256]{2,1,0:T(8,128)(2,1)S(1)}, bf16[16,64,256]{2,1,0:T(8,128)(2,1)S(1)}, f32[576,192]{1,0:T(8,128)S(1)}, f32[4,64,256]{2,1,0:T(8,1...) custom-call(bf16[3,64,256]{2,1,0:T(8,128)(2,1)S(1)} %get-tuple-element.32.values_ref, ...), custom_call_target="tpu_custom_call" | custom-call | flops 2717908992 | bytes 7801856 | tf_op jit(solution)/shard_map/pallas_call | solution.py:27
  31.1 0.0 collective-permute-done.4.north_ref
  31.1 0.0 collective-permute-done.5.south_ref
  31.1 0.6 shard_map.106
  31.7 0.1 collective-permute-start.6
  31.7 0.9 %shard_map.107 = (bf16[32,16,128]{2,1,0:T(8,128)(2,1)S(1)}, bf16[5,16,128]{2,1,0:T(8,128)(2,1)S(1)}) custom-call(f32[4,192,256]{2,1,0:T(8,128)S(1)} %get-tuple-element.42.slot_ref, bf16[3,768,256]{2,1,0:T(8,128)(2,1)S(1)} %get-tuple-element.43.plane_ref, bf16[3,256,256]{2,1,0:T(8,128)(2,1)S(1)} %get-tuple-element.33.hot_ref, ...), custom_call_target="tpu_custom_call" | custom-call | flops 113246208 | bytes 3849216 | tf_op jit(solution)/shard_map/pallas_call | solution.py:27
  32.6 0.0 copy-start.5
  32.6 0.4 collective-permute-done.6.got_ref
  33.0 0.7 %shard_map.108.in_ref = bf16[32,32,128]{2,1,0:T(8,128)(2,1)} custom-call(f32[27,16,128]{2,1,0:T(8,128)S(1)} %get-tuple-element.40.keep_ref, bf16[27,16,128]{2,1,0:T(8,128)(2,1)S(1)} %collective-permute-done.6.got_ref, bf16[32,16,128]{2,1,0:T(8,128)(2,1)S(1)} %get-tuple-element.45.slots_ref, bf16[5,16,128]{2,1,0:T(8,128)(2,1)S(1)} %get-tuple-element.46.proj_ref), custom_call_target="tpu_custom_call" | custom-call | flops 1000 | bytes 745472 | tf_op jit(solution)/shard_map/pallas_call | solution.py:27
  33.8 2.6 %all-to-all-start.1 = ((bf16[32,32,128]{2,1,0:T(8,128)(2,1)}), bf16[32,32,128]{2,1,0:T(8,128)(2,1)S(1)}, u32[]{:S(2)}, u32[]{:S(2)}) async-start(bf16[32,32,128]{2,1,0:T(8,128)(2,1)} %shard_map.109), calls=%async_computation.1 | async-start | bytes 524288 | tf_op jit(solution)/shard_map/all_to_all | solution.py:60
  36.4 10.2 %all-to-all-done.1.recv_ref = bf16[32,32,128]{2,1,0:T(8,128)(2,1)S(1)} async-done(((bf16[32,32,128]{2,1,0:T(8,128)(2,1)}), bf16[32,32,128]{2,1,0:T(8,128)(2,1)S(1)}, u32[]{:S(2)}, u32[]{:S(2)}) %all-to-all-start.1) | async-done | bytes 262176 | tf_op jit(solution)/shard_map/all_to_all | solution.py:60
  46.6 0.7 %shard_map.110 = bf16[32,16,128]{2,1,0:T(8,128)(2,1)} custom-call(bf16[32,32,128]{2,1,0:T(8,128)(2,1)S(1)} %all-to-all-done.1.recv_ref, s32[1,1]{1,0:T(1,128)} %bitcast.9.index_ref), custom_call_target="tpu_custom_call" | custom-call | flops 1000 | bytes 393220 | tf_op jit(solution)/shard_map/pallas_call | solution.py:27
  47.3 2.7 %all-to-all-start.2 = ((bf16[32,16,128]{2,1,0:T(8,128)(2,1)}), bf16[32,16,128]{2,1,0:T(8,128)(2,1)S(1)}, u32[]{:S(2)}, u32[]{:S(2)}) async-start(bf16[32,16,128]{2,1,0:T(8,128)(2,1)} %shard_map.110), calls=%async_computation.2 | async-start | bytes 262144 | tf_op jit(solution)/shard_map/all_to_all | solution.py:60
  50.0 0.0 copy-done.5
  50.0 1.4 %shard_map.111 = (f32[128,128]{1,0:T(8,128)}, bf16[64,16,256]{2,1,0:T(8,128)(2,1)}) custom-call(bf16[32,32,128]{2,1,0:T(8,128)(2,1)S(1)} %all-to-all-done.1.recv_ref, s32[1,32]{1,0:T(1,128)S(1)} %copy-done.5, bf16[64,128]{1,0:T(8,128)(2,1)S(1)} %bitcast.26, bf16[16,64,256]{2,1,0:T(8,128)(2,1)S(1)} %get-tuple-element.47.inner_ref, ...), custom_call_target="tpu_custom_call" | custom-call | flops 4194304 | bytes 1458304 | tf_op jit(solution)/shard_map/pallas_call | solution.py:27
  51.4 7.0 %all-to-all-done.2.mine_ref = bf16[32,16,128]{2,1,0:T(8,128)(2,1)S(1)} async-done(((bf16[32,16,128]{2,1,0:T(8,128)(2,1)}), bf16[32,16,128]{2,1,0:T(8,128)(2,1)S(1)}, u32[]{:S(2)}, u32[]{:S(2)}) %all-to-all-start.2) | async-done | bytes 131104 | tf_op jit(solution)/shard_map/all_to_all | solution.py:60
  58.4 0.0 collective-permute-start.7
  58.4 1.3 %collective-permute-done.7.other_ref = bf16[32,16,128]{2,1,0:T(8,128)(2,1)S(1)} collective-permute-done((bf16[32,16,128]{2,1,0:T(8,128)(2,1)S(1)}, bf16[32,16,128]{2,1,0:T(8,128)(2,1)S(1)}, u32[]{:S(2)}, u32[]{:S(2)}) %collective-permute-start.7) | collective-permute-done | bytes 131104 | tf_op jit(solution)/shard_map/ppermute | solution.py:55
  59.8 1.1 %shard_map.112 = (f32[27,64,64]{2,1,0:T(8,128)}, f32[64,128]{1,0:T(8,128)}) custom-call(s32[1]{0:T(128)} %bitcast.parity_ref, bf16[32,16,128]{2,1,0:T(8,128)(2,1)S(1)} %all-to-all-done.2.mine_ref, bf16[32,16,128]{2,1,0:T(8,128)(2,1)S(1)} %collective-permute-done.7.other_ref), custom_call_target="tpu_custom_call" | custom-call | flops 1000 | bytes 737284 | tf_op jit(solution)/shard_map/pallas_call | solution.py:27
  (1 shorter events, 0.0 us)
Async XLA Ops:
  0.6 20.5 %copy-start.1 = (bf16[64,1,16,256]{3,2,1,0:T(8,128)(2,1)S(1)}, bf16[64,1,16,256]{3,2,1,0:T(8,128)(2,1)}, u32[]{:S(2)}) copy-start(bf16[64,1,16,256]{3,2,1,0:T(8,128)(2,1)} %param.10) | copy-start | bytes 1572868
  0.6 20.5 %copy-start.4 = (s32[1,256]{1,0:T(1,128)S(1)}, s32[1,256]{1,0:T(1,128)}, u32[]{:S(2)}) copy-start(s32[1,256]{1,0:T(1,128)} %own_cells.5) | copy-start | bytes 3076
  0.7 20.5 %copy-start.3 = (bf16[128,64]{0,1:T(8,128)(2,1)S(1)}, bf16[128,64]{0,1:T(8,128)(2,1)}, u32[]{:S(2)}) copy-start(bf16[128,64]{0,1:T(8,128)(2,1)} %param.11) | copy-start | bytes 49156
  0.7 20.5 %collective-permute-start.1 = (bf16[64,1,16,256]{3,2,0,1:T(8,128)(2,1)}, bf16[64,1,16,256]{3,2,0,1:T(8,128)(2,1)S(1)}, u32[]{:S(2)}, u32[]{:S(2)}) collective-permute-start(bf16[64,1,16,256]{3,2,0,1:T(8,128)(2,1)} %bitcast.17), channel_id=1, source_target_pairs={{0,28},{1,29},{2,30},{3,31},{4,0},{5,1},{6,2},{7,3},{8,4},{9,5},{1... | collective-permute-start | bytes 1572872 | tf_op jit(solution)/shard_map/ppermute | solution.py:51
  4.0 17.1 %collective-permute-start = (bf16[64,1,16,256]{3,2,0,1:T(8,128)(2,1)}, bf16[64,1,16,256]{3,2,0,1:T(8,128)(2,1)S(1)}, u32[]{:S(2)}, u32[]{:S(2)}) collective-permute-start(bf16[64,1,16,256]{3,2,0,1:T(8,128)(2,1)} %bitcast.18), channel_id=1, source_target_pairs={{0,4},{1,5},{2,6},{3,7},{4,8},{5,9},{6,10},{7,11},{8,12},{9,13},{1... | collective-permute-start | bytes 1572872 | tf_op jit(solution)/shard_map/ppermute | solution.py:51
  5.7 15.4 %all-to-all-start = ((bf16[32,24,128]{2,1,0:T(8,128)(2,1)}), bf16[32,24,128]{2,1,0:T(8,128)(2,1)S(1)}, u32[]{:S(2)}, u32[]{:S(2)}) async-start(bf16[32,24,128]{2,1,0:T(8,128)(2,1)} %bitcast.27), calls=%async_computation | async-start | bytes 393216 | tf_op jit(solution)/shard_map/all_to_all | solution.py:60
  11.8 5.6 %collective-permute-start.3 = (s32[1,256]{1,0:T(1,128)}, s32[1,256]{1,0:T(1,128)S(1)}, u32[]{:S(2)}, u32[]{:S(2)}) collective-permute-start(s32[1,256]{1,0:T(1,128)} %own_cells.5), channel_id=1, source_target_pairs={{0,28},{1,29},{2,30},{3,31},{4,0},{5,1},{6,2},{7,3},{8,4},{9,5},{1... | collective-permute-start | bytes 3080 | tf_op jit(solution)/shard_map/ppermute | solution.py:51
  14.3 4.9 %collective-permute-start.2 = (s32[1,256]{1,0:T(1,128)}, s32[1,256]{1,0:T(1,128)S(1)}, u32[]{:S(2)}, u32[]{:S(2)}) collective-permute-start(s32[1,256]{1,0:T(1,128)} %own_cells.5), channel_id=1, source_target_pairs={{0,4},{1,5},{2,6},{3,7},{4,8},{5,9},{6,10},{7,11},{8,12},{9,13},{1... | collective-permute-start | bytes 3080 | tf_op jit(solution)/shard_map/ppermute | solution.py:51
  14.3 1.0 %copy-start = (bf16[64,1,16,256]{3,2,1,0:T(8,128)(2,1)S(1)}, bf16[64,1,16,256]{3,2,1,0:T(8,128)(2,1)}, u32[]{:S(2)}) copy-start(bf16[64,1,16,256]{3,2,1,0:T(8,128)(2,1)} %param.13) | copy-start | bytes 1572868
  15.3 1.0 %copy-start.2 = (bf16[27,64,64]{2,1,0:T(8,128)(2,1)S(1)}, bf16[27,64,64]{2,1,0:T(8,128)(2,1)}, u32[]{:S(2)}) copy-start(bf16[27,64,64]{2,1,0:T(8,128)(2,1)} %weight_ref.1) | copy-start | bytes 663556
  22.1 8.9 %collective-permute-start.4 = (bf16[192,256]{1,0:T(8,128)(2,1)S(1)}, bf16[192,256]{1,0:T(8,128)(2,1)S(1)}, u32[]{:S(2)}, u32[]{:S(2)}) collective-permute-start(bf16[192,256]{1,0:T(8,128)(2,1)S(1)} %get-tuple-element.37), channel_id=1, source_target_pairs={{0,1},{1,2},{2,3},{3,0},{4,5},{5,6},{6,7},{7,4},{8,9},{9,10},{10,1... | collective-permute-start | bytes 294920 | tf_op jit(solution)/shard_map/ppermute | solution.py:51
  22.2 8.9 %collective-permute-start.5 = (bf16[192,256]{1,0:T(8,128)(2,1)S(1)}, bf16[192,256]{1,0:T(8,128)(2,1)S(1)}, u32[]{:S(2)}, u32[]{:S(2)}) collective-permute-start(bf16[192,256]{1,0:T(8,128)(2,1)S(1)} %get-tuple-element.38), channel_id=1, source_target_pairs={{0,3},{1,0},{2,1},{3,2},{4,7},{5,4},{6,5},{7,6},{8,11},{9,8},{10,9... | collective-permute-start | bytes 294920 | tf_op jit(solution)/shard_map/ppermute | solution.py:51
  31.7 1.4 %collective-permute-start.6 = (bf16[27,16,128]{2,1,0:T(8,128)(2,1)S(1)}, bf16[27,16,128]{2,1,0:T(8,128)(2,1)S(1)}, u32[]{:S(2)}, u32[]{:S(2)}) collective-permute-start(bf16[27,16,128]{2,1,0:T(8,128)(2,1)S(1)} %get-tuple-element.41), channel_id=1, source_target_pairs={{0,4},{4,0},{8,12},{12,8},{16,20},{20,16},{24,28},{28,24},{1,5},{5... | collective-permute-start | bytes 331784 | tf_op jit(solution)/shard_map/ppermute | solution.py:55
  32.6 17.4 %copy-start.5 = (s32[1,32]{1,0:T(1,128)S(1)}, s32[1,32]{1,0:T(1,128)}, u32[]{:S(2)}) copy-start(s32[1,32]{1,0:T(1,128)} %counts_ref.1) | copy-start | bytes 388
  33.8 12.8 %all-to-all-start.1 = ((bf16[32,32,128]{2,1,0:T(8,128)(2,1)}), bf16[32,32,128]{2,1,0:T(8,128)(2,1)S(1)}, u32[]{:S(2)}, u32[]{:S(2)}) async-start(bf16[32,32,128]{2,1,0:T(8,128)(2,1)} %shard_map.109), calls=%async_computation.1 | async-start | bytes 524288 | tf_op jit(solution)/shard_map/all_to_all | solution.py:60
  47.3 11.1 %all-to-all-start.2 = ((bf16[32,16,128]{2,1,0:T(8,128)(2,1)}), bf16[32,16,128]{2,1,0:T(8,128)(2,1)S(1)}, u32[]{:S(2)}, u32[]{:S(2)}) async-start(bf16[32,16,128]{2,1,0:T(8,128)(2,1)} %shard_map.110), calls=%async_computation.2 | async-start | bytes 262144 | tf_op jit(solution)/shard_map/all_to_all | solution.py:60
  58.4 1.3 %collective-permute-start.7 = (bf16[32,16,128]{2,1,0:T(8,128)(2,1)S(1)}, bf16[32,16,128]{2,1,0:T(8,128)(2,1)S(1)}, u32[]{:S(2)}, u32[]{:S(2)}) collective-permute-start(bf16[32,16,128]{2,1,0:T(8,128)(2,1)S(1)} %all-to-all-done.2.mine_ref), channel_id=1, source_target_pairs={{0,4},{4,0},{8,12},{12,8},{16,20},{20,16},{24,28},{28,24},{1,5},{5... | collective-permute-start | bytes 393224 | tf_op jit(solution)/shard_map/ppermute | solution.py:55

commit v17 on v16

--- a/solution.py
+++ b/solution.py
@@ -500,7 +500,9 @@
         4 * one,
         (pltpu.VMEM((4 * chans, slots), BF16), pltpu.VMEM((4, rows, nz), BF16)),
     )
-    south, north = move(first, 0, -1), move(last, 0, 1)
+    south = move(first, 0, -1)
+    (last,) = call(same_kernel, [last], (last,), 0, aliases={0: 0})
+    north = move(last, 0, 1)
     x_all, out_rows, total, pre_edge, slot_edge, plane = call(
         conv_kernel,
         [

time: 61.3 us -> 61.3 us (level)
    pallas_call x11 -> x12, Pallas kernels: 13.5 us -> 13.5 us  [call(): pl.pallas_call(kernel, out_shape=[jax.ShapeDtypeStruct(o.shape, o.dtype)...]
where the time goes in v17:
time: 61.3 us; the launch traced here: 60.9 us
  waiting for transfers between devices  23.3 us (38%)
  starting transfers between devices  21.1 us (34%)
  Pallas kernels  13.5 us (22%)
  local copies, waits for them, and re-layouts  2.08 us (3%)
  between operations  0.85 us (1%)
    all_to_all x3, waiting for transfers between devices, exchange(): lax.all_to_all(payload.reshape(ndev, rows // ndev, width), AXES, split_ax...  19.2 us
    pallas_call x12, Pallas kernels, call(): pl.pallas_call(kernel, out_shape=[jax.ShapeDtypeStruct(o.shape, o.dtype)...  13.5 us
    all_to_all x3, starting transfers between devices, exchange(): lax.all_to_all(payload.reshape(ndev, rows // ndev, width), AXES, split_ax...  11.3 us
    ppermute x6, starting transfers between devices, send(): return lax.ppermute(block, AXES, pairs)  9.73 us
    ppermute x6, waiting for transfers between devices, send(): return lax.ppermute(block, AXES, pairs)  2.43 us
    unnamed x12, local copies, waits for them, and re-layouts  2.08 us
    ppermute x2, waiting for transfers between devices, swap(): lax.ppermute(block, 'gx', [(i, i ^ 1) for i in range(lax.axis_size('gx'))])  1.74 us
  transfers between devices with their start and end apart: 11, of which 7 were waited for; matrix products, arithmetic and copies ran while one was open for 0% of the time, Pallas kernels for 15%

profile of v17, /device:TPU:0, one launch (start us, length us, event | category | flops | bytes accessed | tf_op | source)
XLA Modules:
  0.0 60.9 jit_solution(17558425080211660679)
XLA Ops:
  0.6 0.0 copy-start.1
  0.6 0.0 copy-start.4
  0.7 0.0 copy-start.3
  0.7 3.4 %collective-permute-start.1 = (bf16[64,1,16,256]{3,2,0,1:T(8,128)(2,1)}, bf16[64,1,16,256]{3,2,0,1:T(8,128)(2,1)S(1)}, u32[]{:S(2)}, u32[]{:S(2)}) collective-permute-start(bf16[64,1,16,256]{3,2,0,1:T(8,128)(2,1)} %bitcast.17), channel_id=1, source_target_pairs={{0,28},{1,29},{2,30},{3,31},{4,0},{5,1},{6,2},{7,3},{8,4},{9,5},{1... | collective-permute-start | bytes 1572872 | tf_op jit(solution)/shard_map/ppermute | solution.py:51
  4.0 0.0 collective-permute-start
  4.1 1.7 %shard_map.102 = bf16[768,128]{1,0:T(8,128)(2,1)} custom-call(bf16[128,128]{1,0:T(8,128)(2,1)} %rows_far.1, s32[1,32]{1,0:T(1,128)} %counts_ref.1), custom_call_target="tpu_custom_call" | custom-call | flops 8388608 | bytes 229504 | tf_op jit(solution)/shard_map/pallas_call | solution.py:27
  5.7 6.0 %all-to-all-start = ((bf16[32,24,128]{2,1,0:T(8,128)(2,1)}), bf16[32,24,128]{2,1,0:T(8,128)(2,1)S(1)}, u32[]{:S(2)}, u32[]{:S(2)}) async-start(bf16[32,24,128]{2,1,0:T(8,128)(2,1)} %bitcast.27), calls=%async_computation | async-start | bytes 393216 | tf_op jit(solution)/shard_map/all_to_all | solution.py:60
  11.8 2.5 %collective-permute-start.3 = (s32[1,256]{1,0:T(1,128)}, s32[1,256]{1,0:T(1,128)S(1)}, u32[]{:S(2)}, u32[]{:S(2)}) collective-permute-start(s32[1,256]{1,0:T(1,128)} %own_cells.5), channel_id=1, source_target_pairs={{0,28},{1,29},{2,30},{3,31},{4,0},{5,1},{6,2},{7,3},{8,4},{9,5},{1... | collective-permute-start | bytes 3080 | tf_op jit(solution)/shard_map/ppermute | solution.py:51
  14.3 0.0 collective-permute-start.2
  14.3 0.0 copy-start
  14.3 1.0 %copy-done = bf16[64,1,16,256]{3,2,1,0:T(8,128)(2,1)S(1)} copy-done((bf16[64,1,16,256]{3,2,1,0:T(8,128)(2,1)S(1)}, bf16[64,1,16,256]{3,2,1,0:T(8,128)(2,1)}, u32[]{:S(2)}) %copy-start) | copy-done | bytes 524312
  15.3 0.0 copy-start.2
  15.3 1.0 %copy-done.2 = bf16[27,64,64]{2,1,0:T(8,128)(2,1)S(1)} copy-done((bf16[27,64,64]{2,1,0:T(8,128)(2,1)S(1)}, bf16[27,64,64]{2,1,0:T(8,128)(2,1)}, u32[]{:S(2)}) %copy-start.2) | copy-done | bytes 221208
  16.3 0.4 shard_map.103
  16.7 0.6 %collective-permute-done.3.east_cells = s32[1,256]{1,0:T(1,128)S(1)} collective-permute-done((s32[1,256]{1,0:T(1,128)}, s32[1,256]{1,0:T(1,128)S(1)}, u32[]{:S(2)}, u32[]{:S(2)}) %collective-permute-start.3) | collective-permute-done | bytes 1056 | tf_op jit(solution)/shard_map/ppermute | solution.py:51
  17.4 1.8 %collective-permute-done.2.west_cells = s32[1,256]{1,0:T(1,128)S(1)} collective-permute-done((s32[1,256]{1,0:T(1,128)}, s32[1,256]{1,0:T(1,128)S(1)}, u32[]{:S(2)}, u32[]{:S(2)}) %collective-permute-start.2) | collective-permute-done | bytes 1056 | tf_op jit(solution)/shard_map/ppermute | solution.py:51
  19.2 2.0 %all-to-all-done = bf16[32,24,128]{2,1,0:T(8,128)(2,1)S(1)} async-done(((bf16[32,24,128]{2,1,0:T(8,128)(2,1)}), bf16[32,24,128]{2,1,0:T(8,128)(2,1)S(1)}, u32[]{:S(2)}, u32[]{:S(2)}) %all-to-all-start) | async-done | bytes 196640 | tf_op jit(solution)/shard_map/all_to_all | solution.py:60
  21.1 0.0 collective-permute-done.1
  21.1 0.0 collective-permute-done
  21.1 0.0 copy-done.1
  21.1 0.0 copy-done.4
  21.1 0.0 copy-done.3
  21.1 1.0 %shard_map.104 = (bf16[192,256]{1,0:T(8,128)(2,1)S(1)}, bf16[192,256]{1,0:T(8,128)(2,1)S(1)}, bf16[3,64,256]{2,1,0:T(8,128)(2,1)S(1)}, bf16[3,256,256]{2,1,0:T(8,128)(2,1)S(1)}) custom-call(bf16[768,128]{1,0:T(8,128)(2,1)S(1)} %bitcast.14, bf16[64,16,256]{2,1,0:T(8,128)(2,1)S(1)} %bitcast.19, bf16[64,16,256]{2,1,0:T(8,128)(2,1)S(1)} %bitcast.23, ...), custom_call_target="tpu_custom_call" | custom-call | flops 75497472 | bytes 3222528 | tf_op jit(solution)/shard_map/pallas_call | solution.py:27
  22.1 0.1 collective-permute-start.4
  22.2 3.8 %collective-permute-start.5 = (bf16[192,256]{1,0:T(8,128)(2,1)S(1)}, bf16[192,256]{1,0:T(8,128)(2,1)S(1)}, u32[]{:S(2)}, u32[]{:S(2)}) collective-permute-start(bf16[192,256]{1,0:T(8,128)(2,1)S(1)} %get-tuple-element.38), channel_id=1, source_target_pairs={{0,3},{1,0},{2,1},{3,2},{4,7},{5,4},{6,5},{7,6},{8,11},{9,8},{10,9... | collective-permute-start | bytes 294920 | tf_op jit(solution)/shard_map/ppermute | solution.py:51
  26.0 5.1 %shard_map.105 = (bf16[16,192,256]{2,1,0:T(8,128)(2,1)S(1)}, bf16[16,64,256]{2,1,0:T(8,128)(2,1)S(1)}, f32[576,192]{1,0:T(8,128)S(1)}, f32[4,64,256]{2,1,0:T(8,1...) custom-call(bf16[3,64,256]{2,1,0:T(8,128)(2,1)S(1)} %get-tuple-element.32.values_ref, ...), custom_call_target="tpu_custom_call" | custom-call | flops 2717908992 | bytes 7801856 | tf_op jit(solution)/shard_map/pallas_call | solution.py:27
  31.1 0.0 collective-permute-done.4.north_ref
  31.1 0.0 collective-permute-done.5.south_ref
  31.1 0.6 shard_map.107
  31.7 0.1 collective-permute-start.6
  31.7 0.9 %shard_map.108 = (bf16[32,16,128]{2,1,0:T(8,128)(2,1)S(1)}, bf16[5,16,128]{2,1,0:T(8,128)(2,1)S(1)}) custom-call(f32[4,192,256]{2,1,0:T(8,128)S(1)} %get-tuple-element.42.slot_ref, bf16[3,768,256]{2,1,0:T(8,128)(2,1)S(1)} %get-tuple-element.43.plane_ref, bf16[3,256,256]{2,1,0:T(8,128)(2,1)S(1)} %get-tuple-element.33.hot_ref, ...), custom_call_target="tpu_custom_call" | custom-call | flops 113246208 | bytes 3849216 | tf_op jit(solution)/shard_map/pallas_call | solution.py:27
  32.6 0.0 copy-start.5
  32.7 0.4 collective-permute-done.6.got_ref
  33.1 0.7 %shard_map.109.in_ref = bf16[32,32,128]{2,1,0:T(8,128)(2,1)} custom-call(f32[27,16,128]{2,1,0:T(8,128)S(1)} %get-tuple-element.40.keep_ref, bf16[27,16,128]{2,1,0:T(8,128)(2,1)S(1)} %collective-permute-done.6.got_ref, bf16[32,16,128]{2,1,0:T(8,128)(2,1)S(1)} %get-tuple-element.45.slots_ref, bf16[5,16,128]{2,1,0:T(8,128)(2,1)S(1)} %get-tuple-element.46.proj_ref), custom_call_target="tpu_custom_call" | custom-call | flops 1000 | bytes 745472 | tf_op jit(solution)/shard_map/pallas_call | solution.py:27
  33.8 2.6 %all-to-all-start.1 = ((bf16[32,32,128]{2,1,0:T(8,128)(2,1)}), bf16[32,32,128]{2,1,0:T(8,128)(2,1)S(1)}, u32[]{:S(2)}, u32[]{:S(2)}) async-start(bf16[32,32,128]{2,1,0:T(8,128)(2,1)} %shard_map.110), calls=%async_computation.1 | async-start | bytes 524288 | tf_op jit(solution)/shard_map/all_to_all | solution.py:60
  36.4 10.2 %all-to-all-done.1.recv_ref = bf16[32,32,128]{2,1,0:T(8,128)(2,1)S(1)} async-done(((bf16[32,32,128]{2,1,0:T(8,128)(2,1)}), bf16[32,32,128]{2,1,0:T(8,128)(2,1)S(1)}, u32[]{:S(2)}, u32[]{:S(2)}) %all-to-all-start.1) | async-done | bytes 262176 | tf_op jit(solution)/shard_map/all_to_all | solution.py:60
  46.6 0.7 %shard_map.111 = bf16[32,16,128]{2,1,0:T(8,128)(2,1)} custom-call(bf16[32,32,128]{2,1,0:T(8,128)(2,1)S(1)} %all-to-all-done.1.recv_ref, s32[1,1]{1,0:T(1,128)} %bitcast.9.index_ref), custom_call_target="tpu_custom_call" | custom-call | flops 1000 | bytes 393220 | tf_op jit(solution)/shard_map/pallas_call | solution.py:27
  47.3 2.7 %all-to-all-start.2 = ((bf16[32,16,128]{2,1,0:T(8,128)(2,1)}), bf16[32,16,128]{2,1,0:T(8,128)(2,1)S(1)}, u32[]{:S(2)}, u32[]{:S(2)}) async-start(bf16[32,16,128]{2,1,0:T(8,128)(2,1)} %shard_map.111), calls=%async_computation.2 | async-start | bytes 262144 | tf_op jit(solution)/shard_map/all_to_all | solution.py:60
  50.0 0.0 copy-done.5
  50.0 1.4 %shard_map.112 = (f32[128,128]{1,0:T(8,128)}, bf16[64,16,256]{2,1,0:T(8,128)(2,1)}) custom-call(bf16[32,32,128]{2,1,0:T(8,128)(2,1)S(1)} %all-to-all-done.1.recv_ref, s32[1,32]{1,0:T(1,128)S(1)} %copy-done.5, bf16[64,128]{1,0:T(8,128)(2,1)S(1)} %bitcast.26, bf16[16,64,256]{2,1,0:T(8,128)(2,1)S(1)} %get-tuple-element.47.inner_ref, ...), custom_call_target="tpu_custom_call" | custom-call | flops 4194304 | bytes 1458304 | tf_op jit(solution)/shard_map/pallas_call | solution.py:27
  51.4 7.0 %all-to-all-done.2.mine_ref = bf16[32,16,128]{2,1,0:T(8,128)(2,1)S(1)} async-done(((bf16[32,16,128]{2,1,0:T(8,128)(2,1)}), bf16[32,16,128]{2,1,0:T(8,128)(2,1)S(1)}, u32[]{:S(2)}, u32[]{:S(2)}) %all-to-all-start.2) | async-done | bytes 131104 | tf_op jit(solution)/shard_map/all_to_all | solution.py:60
  58.4 0.0 collective-permute-start.7
  58.4 1.3 %collective-permute-done.7.other_ref = bf16[32,16,128]{2,1,0:T(8,128)(2,1)S(1)} collective-permute-done((bf16[32,16,128]{2,1,0:T(8,128)(2,1)S(1)}, bf16[32,16,128]{2,1,0:T(8,128)(2,1)S(1)}, u32[]{:S(2)}, u32[]{:S(2)}) %collective-permute-start.7) | collective-permute-done | bytes 131104 | tf_op jit(solution)/shard_map/ppermute | solution.py:55
  59.8 1.1 %shard_map.113 = (f32[27,64,64]{2,1,0:T(8,128)}, f32[64,128]{1,0:T(8,128)}) custom-call(s32[1]{0:T(128)} %bitcast.parity_ref, bf16[32,16,128]{2,1,0:T(8,128)(2,1)S(1)} %all-to-all-done.2.mine_ref, bf16[32,16,128]{2,1,0:T(8,128)(2,1)S(1)} %collective-permute-done.7.other_ref), custom_call_target="tpu_custom_call" | custom-call | flops 1000 | bytes 737284 | tf_op jit(solution)/shard_map/pallas_call | solution.py:27
  (2 shorter events, 0.0 us)
Async XLA Ops:
  0.6 20.5 %copy-start.1 = (bf16[64,1,16,256]{3,2,1,0:T(8,128)(2,1)S(1)}, bf16[64,1,16,256]{3,2,1,0:T(8,128)(2,1)}, u32[]{:S(2)}) copy-start(bf16[64,1,16,256]{3,2,1,0:T(8,128)(2,1)} %param.10) | copy-start | bytes 1572868
  0.6 20.5 %copy-start.4 = (s32[1,256]{1,0:T(1,128)S(1)}, s32[1,256]{1,0:T(1,128)}, u32[]{:S(2)}) copy-start(s32[1,256]{1,0:T(1,128)} %own_cells.5) | copy-start | bytes 3076
  0.7 20.5 %copy-start.3 = (bf16[128,64]{0,1:T(8,128)(2,1)S(1)}, bf16[128,64]{0,1:T(8,128)(2,1)}, u32[]{:S(2)}) copy-start(bf16[128,64]{0,1:T(8,128)(2,1)} %param.11) | copy-start | bytes 49156
  0.7 20.5 %collective-permute-start.1 = (bf16[64,1,16,256]{3,2,0,1:T(8,128)(2,1)}, bf16[64,1,16,256]{3,2,0,1:T(8,128)(2,1)S(1)}, u32[]{:S(2)}, u32[]{:S(2)}) collective-permute-start(bf16[64,1,16,256]{3,2,0,1:T(8,128)(2,1)} %bitcast.17), channel_id=1, source_target_pairs={{0,28},{1,29},{2,30},{3,31},{4,0},{5,1},{6,2},{7,3},{8,4},{9,5},{1... | collective-permute-start | bytes 1572872 | tf_op jit(solution)/shard_map/ppermute | solution.py:51
  4.0 17.1 %collective-permute-start = (bf16[64,1,16,256]{3,2,0,1:T(8,128)(2,1)}, bf16[64,1,16,256]{3,2,0,1:T(8,128)(2,1)S(1)}, u32[]{:S(2)}, u32[]{:S(2)}) collective-permute-start(bf16[64,1,16,256]{3,2,0,1:T(8,128)(2,1)} %bitcast.18), channel_id=1, source_target_pairs={{0,4},{1,5},{2,6},{3,7},{4,8},{5,9},{6,10},{7,11},{8,12},{9,13},{1... | collective-permute-start | bytes 1572872 | tf_op jit(solution)/shard_map/ppermute | solution.py:51
  5.7 15.4 %all-to-all-start = ((bf16[32,24,128]{2,1,0:T(8,128)(2,1)}), bf16[32,24,128]{2,1,0:T(8,128)(2,1)S(1)}, u32[]{:S(2)}, u32[]{:S(2)}) async-start(bf16[32,24,128]{2,1,0:T(8,128)(2,1)} %bitcast.27), calls=%async_computation | async-start | bytes 393216 | tf_op jit(solution)/shard_map/all_to_all | solution.py:60
  11.8 5.6 %collective-permute-start.3 = (s32[1,256]{1,0:T(1,128)}, s32[1,256]{1,0:T(1,128)S(1)}, u32[]{:S(2)}, u32[]{:S(2)}) collective-permute-start(s32[1,256]{1,0:T(1,128)} %own_cells.5), channel_id=1, source_target_pairs={{0,28},{1,29},{2,30},{3,31},{4,0},{5,1},{6,2},{7,3},{8,4},{9,5},{1... | collective-permute-start | bytes 3080 | tf_op jit(solution)/shard_map/ppermute | solution.py:51
  14.3 4.9 %collective-permute-start.2 = (s32[1,256]{1,0:T(1,128)}, s32[1,256]{1,0:T(1,128)S(1)}, u32[]{:S(2)}, u32[]{:S(2)}) collective-permute-start(s32[1,256]{1,0:T(1,128)} %own_cells.5), channel_id=1, source_target_pairs={{0,4},{1,5},{2,6},{3,7},{4,8},{5,9},{6,10},{7,11},{8,12},{9,13},{1... | collective-permute-start | bytes 3080 | tf_op jit(solution)/shard_map/ppermute | solution.py:51
  14.3 1.0 %copy-start = (bf16[64,1,16,256]{3,2,1,0:T(8,128)(2,1)S(1)}, bf16[64,1,16,256]{3,2,1,0:T(8,128)(2,1)}, u32[]{:S(2)}) copy-start(bf16[64,1,16,256]{3,2,1,0:T(8,128)(2,1)} %param.13) | copy-start | bytes 1572868
  15.3 1.0 %copy-start.2 = (bf16[27,64,64]{2,1,0:T(8,128)(2,1)S(1)}, bf16[27,64,64]{2,1,0:T(8,128)(2,1)}, u32[]{:S(2)}) copy-start(bf16[27,64,64]{2,1,0:T(8,128)(2,1)} %weight_ref.1) | copy-start | bytes 663556
  22.1 9.0 %collective-permute-start.4 = (bf16[192,256]{1,0:T(8,128)(2,1)S(1)}, bf16[192,256]{1,0:T(8,128)(2,1)S(1)}, u32[]{:S(2)}, u32[]{:S(2)}) collective-permute-start(bf16[192,256]{1,0:T(8,128)(2,1)S(1)} %shard_map.106), channel_id=1, source_target_pairs={{0,1},{1,2},{2,3},{3,0},{4,5},{5,6},{6,7},{7,4},{8,9},{9,10},{10,1... | collective-permute-start | bytes 294920 | tf_op jit(solution)/shard_map/ppermute | solution.py:51
  22.2 8.9 %collective-permute-start.5 = (bf16[192,256]{1,0:T(8,128)(2,1)S(1)}, bf16[192,256]{1,0:T(8,128)(2,1)S(1)}, u32[]{:S(2)}, u32[]{:S(2)}) collective-permute-start(bf16[192,256]{1,0:T(8,128)(2,1)S(1)} %get-tuple-element.38), channel_id=1, source_target_pairs={{0,3},{1,0},{2,1},{3,2},{4,7},{5,4},{6,5},{7,6},{8,11},{9,8},{10,9... | collective-permute-start | bytes 294920 | tf_op jit(solution)/shard_map/ppermute | solution.py:51
  31.7 1.4 %collective-permute-start.6 = (bf16[27,16,128]{2,1,0:T(8,128)(2,1)S(1)}, bf16[27,16,128]{2,1,0:T(8,128)(2,1)S(1)}, u32[]{:S(2)}, u32[]{:S(2)}) collective-permute-start(bf16[27,16,128]{2,1,0:T(8,128)(2,1)S(1)} %get-tuple-element.41), channel_id=1, source_target_pairs={{0,4},{4,0},{8,12},{12,8},{16,20},{20,16},{24,28},{28,24},{1,5},{5... | collective-permute-start | bytes 331784 | tf_op jit(solution)/shard_map/ppermute | solution.py:55
  32.6 17.4 %copy-start.5 = (s32[1,32]{1,0:T(1,128)S(1)}, s32[1,32]{1,0:T(1,128)}, u32[]{:S(2)}) copy-start(s32[1,32]{1,0:T(1,128)} %counts_ref.1) | copy-start | bytes 388
  33.8 12.8 %all-to-all-start.1 = ((bf16[32,32,128]{2,1,0:T(8,128)(2,1)}), bf16[32,32,128]{2,1,0:T(8,128)(2,1)S(1)}, u32[]{:S(2)}, u32[]{:S(2)}) async-start(bf16[32,32,128]{2,1,0:T(8,128)(2,1)} %shard_map.110), calls=%async_computation.1 | async-start | bytes 524288 | tf_op jit(solution)/shard_map/all_to_all | solution.py:60
  47.3 11.1 %all-to-all-start.2 = ((bf16[32,16,128]{2,1,0:T(8,128)(2,1)}), bf16[32,16,128]{2,1,0:T(8,128)(2,1)S(1)}, u32[]{:S(2)}, u32[]{:S(2)}) async-start(bf16[32,16,128]{2,1,0:T(8,128)(2,1)} %shard_map.111), calls=%async_computation.2 | async-start | bytes 262144 | tf_op jit(solution)/shard_map/all_to_all | solution.py:60
  58.4 1.3 %collective-permute-start.7 = (bf16[32,16,128]{2,1,0:T(8,128)(2,1)S(1)}, bf16[32,16,128]{2,1,0:T(8,128)(2,1)S(1)}, u32[]{:S(2)}, u32[]{:S(2)}) collective-permute-start(bf16[32,16,128]{2,1,0:T(8,128)(2,1)S(1)} %all-to-all-done.2.mine_ref), channel_id=1, source_target_pairs={{0,4},{4,0},{8,12},{12,8},{16,20},{20,16},{24,28},{28,24},{1,5},{5... | collective-permute-start | bytes 393224 | tf_op jit(solution)/shard_map/ppermute | solution.py:55

commit v18 on v16

--- a/solution.py
+++ b/solution.py
@@ -209,7 +209,7 @@
 def conv_kernel(
     values_ref, hot_ref, own_ref, west_ref, east_ref, own_cells, west_cells, east_cells,
     cot_ref, wf_ref, wb_ref,
-    x_ref, out_ref, total_ref, pre_ref, slot_ref, plane, acc, grads, back, masked,
+    x_ref, out_ref, total_ref, pre_ref, slot_ref, plane, grads, acc, back, masked,
 ):
     cy, chans, nz = cot_ref.shape
     rows = 3 * chans
@@ -275,11 +275,13 @@
     slot_ref[0] = spread_back(1)
     taps(2)
     slot_ref[1] = spread_back(2) + back[1]
-    for n in range(3, cy - 1):
+    late = plane.shape[1] // chans + 2
+    for n in range(3, late + 1):
         backward(n)
-    taps(cy - 1)
-    slot_ref[2] = back[cy - 2]
-    slot_ref[3] = back[cy - 1]
+    for n in range(late + 1, cy):
+        taps(n)
+    slot_ref[2] = back[late]
+    slot_ref[3] = back[late + 1]
 
 
 def at_slots(part, y, onehot, first):
@@ -327,7 +329,7 @@
 
 
 def slots_kernel(
-    ndev, cap, part, full, slot_ref, plane_ref, hot_ref, grads_ref, wb_ref, cot_ref,
+    ndev, cap, part, full, slot_ref, plane_ref, inner_ref, hot_ref, grads_ref, wb_ref, cot_ref,
     own_cells, west_cells, east_cells, recv_ref, slots_ref, proj_ref,
 ):
     cy, chans, nz = cot_ref.shape
@@ -335,19 +337,26 @@
     inner = mm(wb_ref[pl.ds(rows, 2 * rows)], grads_ref[1])
     top = slot_ref[0] + inner[:rows] + mm(wb_ref[pl.ds(2 * rows, rows)], grads_ref[0])
     second = slot_ref[1] + inner[rows:]
+    late = plane_ref.shape[1] // chans + 2
+    third, bottom = slot_ref[2], slot_ref[3]
+    values = {}
+    for n in range(late + 1, cy - 1):
+        terms = mm(wb_ref[...], inner_ref[n + 1])
+        values[n - 1] = third + terms[:rows]
+        third, bottom = bottom + terms[rows : 2 * rows], terms[2 * rows :]
     inner = mm(wb_ref[pl.ds(0, 2 * rows)], grads_ref[2])
-    third = slot_ref[2] + inner[:rows]
-    bottom = slot_ref[3] + inner[rows:] + mm(wb_ref[pl.ds(0, rows)], grads_ref[3])
-    at = (0, 1, cy - 2, cy - 1)
+    third = third + inner[:rows]
+    bottom = bottom + inner[rows:] + mm(wb_ref[pl.ds(0, rows)], grads_ref[3])
+    values.update({0: top, 1: second, cy - 2: third, cy - 1: bottom})
     found = []
     for dx, cells_ref in enumerate((west_cells, own_cells, east_cells)):
-        parts = [value[dx * chans : (dx + 1) * chans] for value in (top, second, third, bottom)]
+        parts = [value[dx * chans : (dx + 1) * chans] for value in values.values()]
         if dx == 1:
-            parts = [value + cot_ref[n].astype(F32) for value, n in zip(parts, at)]
-        parts = [value.astype(BF16) for value in parts]
+            parts = [part + cot_ref[n].astype(F32) for part, n in zip(parts, values)]
+        parts = [part.astype(BF16) for part in parts]
         terms = jnp.concatenate([plane_ref[dx], *parts], axis=0)
         y, _ = place(cells_ref, nz)
-        found.append(at_slots(terms, y, hot_ref[dx], (*range(2, cy - 2), *at)))
+        found.append(at_slots(terms, y, hot_ref[dx], (*range(2, late), *values)))
     sides = jnp.concatenate([found[0], found[2]], axis=0).T
     middle = jnp.concatenate([found[1], jnp.zeros_like(found[1])], axis=0).T
     width = recv_ref.shape[1]
@@ -501,7 +510,8 @@
         (pltpu.VMEM((4 * chans, slots), BF16), pltpu.VMEM((4, rows, nz), BF16)),
     )
     south, north = move(first, 0, -1), move(last, 0, 1)
-    x_all, out_rows, total, pre_edge, slot_edge, plane = call(
+    late = cy // 2 + 1
+    x_all, out_rows, total, pre_edge, slot_edge, plane, inner = call(
         conv_kernel,
         [
             shape((cy, rows, nz), BF16),
@@ -509,13 +519,13 @@
             shape((9 * chans, rows), F32),
             shape((4, chans, nz), F32),
             shape((4, rows, nz), F32),
-            shape((3, (cy - 4) * chans, nz), BF16),
+            shape((3, (late - 2) * chans, nz), BF16),
+            shape((cy + 2, rows, nz), BF16),
         ],
         (values, hots, *planes, *lists, cot, wf, wb),
         3 * cy * 3 * one,
         (
             pltpu.VMEM((cy + 1, rows, nz), F32),
-            pltpu.VMEM((cy + 2, rows, nz), BF16),
             pltpu.VMEM((cy, rows, nz), F32),
             pltpu.VMEM((cy * chans, slots), BF16),
         ),
@@ -543,7 +553,7 @@
     back, proj = call(
         functools.partial(slots_kernel, ndev, cap, part, full),
         [shape((ndev, 2 * cap, feats), BF16), shape((ndev - full, part, feats), BF16)],
-        (slot_edge, plane, hots, grads, wb, cot, *lists, recv),
+        (slot_edge, plane, inner, hots, grads, wb, cot, *lists, recv),
         6 * one,
     )
     (payload,) = call(

time: 61.3 us -> 63.2 us (1.031)
  local copies, waits for them, and re-layouts: 2.08 us -> 3.47 us
  Pallas kernels: 13.5 us -> 14.3 us
    unnamed x12 -> x16, local copies, waits for them, and re-layouts: 2.08 us -> 3.47 us
    pallas_call x11, Pallas kernels: 13.5 us -> 14.3 us  [call(): pl.pallas_call(kernel, out_shape=[jax.ShapeDtypeStruct(o.shape, o.dtype)...]
  transfers between devices with their start and end apart: 11 -> 11, of which waited for: 7 -> 6; matrix products, arithmetic and copies ran while one was open for 0% -> 0% of each run, Pallas kernels for 15% -> 16%
where the time goes in v18:
time: 63.2 us; the launch traced here: 62.7 us
  waiting for transfers between devices  22.9 us (36%)
  starting transfers between devices  21.1 us (33%)
  Pallas kernels  14.3 us (23%)
  local copies, waits for them, and re-layouts  3.47 us (5%)
  between operations  0.84 us (1%)
    all_to_all x3, waiting for transfers between devices, exchange(): lax.all_to_all(payload.reshape(ndev, rows // ndev, width), AXES, split_ax...  19.2 us
    pallas_call x11, Pallas kernels, call(): pl.pallas_call(kernel, out_shape=[jax.ShapeDtypeStruct(o.shape, o.dtype)...  14.3 us
    all_to_all x3, starting transfers between devices, exchange(): lax.all_to_all(payload.reshape(ndev, rows // ndev, width), AXES, split_ax...  11.3 us
    ppermute x6, starting transfers between devices, send(): return lax.ppermute(block, AXES, pairs)  9.73 us
    unnamed x16, local copies, waits for them, and re-layouts  3.47 us
    ppermute x6, waiting for transfers between devices, send(): return lax.ppermute(block, AXES, pairs)  2.43 us
    ppermute x2, waiting for transfers between devices, swap(): lax.ppermute(block, 'gx', [(i, i ^ 1) for i in range(lax.axis_size('gx'))])  1.35 us
  transfers between devices with their start and end apart: 11, of which 6 were waited for; matrix products, arithmetic and copies ran while one was open for 0% of the time, Pallas kernels for 16%

profile of v18, /device:TPU:0, one launch (start us, length us, event | category | flops | bytes accessed | tf_op | source)
XLA Modules:
  0.0 62.7 jit_solution(10861007560586892644)
XLA Ops:
  0.6 0.0 copy-start.1
  0.6 3.4 %collective-permute-start.1 = (bf16[64,1,16,256]{3,2,0,1:T(8,128)(2,1)}, bf16[64,1,16,256]{3,2,0,1:T(8,128)(2,1)S(1)}, u32[]{:S(2)}, u32[]{:S(2)}) collective-permute-start(bf16[64,1,16,256]{3,2,0,1:T(8,128)(2,1)} %bitcast.17), channel_id=1, source_target_pairs={{0,28},{1,29},{2,30},{3,31},{4,0},{5,1},{6,2},{7,3},{8,4},{9,5},{1... | collective-permute-start | bytes 1572872 | tf_op jit(solution)/shard_map/ppermute | solution.py:51
  4.0 0.0 collective-permute-start
  4.0 1.7 %shard_map.102 = bf16[768,128]{1,0:T(8,128)(2,1)} custom-call(bf16[128,128]{1,0:T(8,128)(2,1)} %rows_far.1, s32[1,32]{1,0:T(1,128)} %counts_ref.1), custom_call_target="tpu_custom_call" | custom-call | flops 8388608 | bytes 229504 | tf_op jit(solution)/shard_map/pallas_call | solution.py:27
  5.7 6.1 %all-to-all-start = ((bf16[32,24,128]{2,1,0:T(8,128)(2,1)}), bf16[32,24,128]{2,1,0:T(8,128)(2,1)S(1)}, u32[]{:S(2)}, u32[]{:S(2)}) async-start(bf16[32,24,128]{2,1,0:T(8,128)(2,1)} %bitcast.27), calls=%async_computation | async-start | bytes 393216 | tf_op jit(solution)/shard_map/all_to_all | solution.py:60
  11.8 2.5 %collective-permute-start.3 = (s32[1,256]{1,0:T(1,128)}, s32[1,256]{1,0:T(1,128)S(1)}, u32[]{:S(2)}, u32[]{:S(2)}) collective-permute-start(s32[1,256]{1,0:T(1,128)} %own_cells.5), channel_id=1, source_target_pairs={{0,28},{1,29},{2,30},{3,31},{4,0},{5,1},{6,2},{7,3},{8,4},{9,5},{1... | collective-permute-start | bytes 3080 | tf_op jit(solution)/shard_map/ppermute | solution.py:51
  14.2 0.0 collective-permute-start.2
  14.2 0.0 copy-start
  14.2 1.0 %copy-done = bf16[64,1,16,256]{3,2,1,0:T(8,128)(2,1)S(1)} copy-done((bf16[64,1,16,256]{3,2,1,0:T(8,128)(2,1)S(1)}, bf16[64,1,16,256]{3,2,1,0:T(8,128)(2,1)}, u32[]{:S(2)}) %copy-start) | copy-done | bytes 524312
  15.3 0.0 copy-start.2
  15.3 1.0 %copy-done.2 = bf16[27,64,64]{2,1,0:T(8,128)(2,1)S(1)} copy-done((bf16[27,64,64]{2,1,0:T(8,128)(2,1)S(1)}, bf16[27,64,64]{2,1,0:T(8,128)(2,1)}, u32[]{:S(2)}) %copy-start.2) | copy-done | bytes 221208
  16.3 0.0 copy-start.6
  16.3 0.4 shard_map.103
  16.7 0.6 %collective-permute-done.3.east_cells = s32[1,256]{1,0:T(1,128)S(1)} collective-permute-done((s32[1,256]{1,0:T(1,128)}, s32[1,256]{1,0:T(1,128)S(1)}, u32[]{:S(2)}, u32[]{:S(2)}) %collective-permute-start.3) | collective-permute-done | bytes 1056 | tf_op jit(solution)/shard_map/ppermute | solution.py:51
  17.4 1.8 %collective-permute-done.2.west_cells = s32[1,256]{1,0:T(1,128)S(1)} collective-permute-done((s32[1,256]{1,0:T(1,128)}, s32[1,256]{1,0:T(1,128)S(1)}, u32[]{:S(2)}, u32[]{:S(2)}) %collective-permute-start.2) | collective-permute-done | bytes 1056 | tf_op jit(solution)/shard_map/ppermute | solution.py:51
  19.2 1.9 %all-to-all-done = bf16[32,24,128]{2,1,0:T(8,128)(2,1)S(1)} async-done(((bf16[32,24,128]{2,1,0:T(8,128)(2,1)}), bf16[32,24,128]{2,1,0:T(8,128)(2,1)S(1)}, u32[]{:S(2)}, u32[]{:S(2)}) %all-to-all-start) | async-done | bytes 196640 | tf_op jit(solution)/shard_map/all_to_all | solution.py:60
  21.1 0.0 collective-permute-done.1
  21.1 0.0 collective-permute-done
  21.1 0.0 copy-done.1
  21.1 0.0 copy-start.3
  21.1 0.7 %copy-done.3 = bf16[128,64]{0,1:T(8,128)(2,1)S(1)} copy-done((bf16[128,64]{0,1:T(8,128)(2,1)S(1)}, bf16[128,64]{0,1:T(8,128)(2,1)}, u32[]{:S(2)}) %copy-start.3) | copy-done | bytes 16408
  21.8 0.0 copy-start.5
  21.8 0.7 %copy-done.5 = s32[1,256]{1,0:T(1,128)S(1)} copy-done((s32[1,256]{1,0:T(1,128)S(1)}, s32[1,256]{1,0:T(1,128)}, u32[]{:S(2)}) %copy-start.5) | copy-done | bytes 1048
  22.5 1.0 %shard_map.104 = (bf16[192,256]{1,0:T(8,128)(2,1)S(1)}, bf16[192,256]{1,0:T(8,128)(2,1)S(1)}, bf16[3,64,256]{2,1,0:T(8,128)(2,1)S(1)}, bf16[3,256,256]{2,1,0:T(8,128)(2,1)S(1)}) custom-call(bf16[768,128]{1,0:T(8,128)(2,1)S(1)} %bitcast.14, bf16[64,16,256]{2,1,0:T(8,128)(2,1)S(1)} %bitcast.19, bf16[64,16,256]{2,1,0:T(8,128)(2,1)S(1)} %bitcast.23, ...), custom_call_target="tpu_custom_call" | custom-call | flops 75497472 | bytes 3222528 | tf_op jit(solution)/shard_map/pallas_call | solution.py:27
  23.5 0.1 collective-permute-start.4
  23.5 3.8 %collective-permute-start.5 = (bf16[192,256]{1,0:T(8,128)(2,1)S(1)}, bf16[192,256]{1,0:T(8,128)(2,1)S(1)}, u32[]{:S(2)}, u32[]{:S(2)}) collective-permute-start(bf16[192,256]{1,0:T(8,128)(2,1)S(1)} %get-tuple-element.39), channel_id=1, source_target_pairs={{0,3},{1,0},{2,1},{3,2},{4,7},{5,4},{6,5},{7,6},{8,11},{9,8},{10,9... | collective-permute-start | bytes 294920 | tf_op jit(solution)/shard_map/ppermute | solution.py:51
  27.4 0.0 copy-done.6
  27.4 4.9 %shard_map.105 = (bf16[16,192,256]{2,1,0:T(8,128)(2,1)S(1)}, bf16[16,64,256]{2,1,0:T(8,128)(2,1)S(1)}, f32[576,192]{1,0:T(8,128)S(1)}, f32[4,64,256]{2,1,0:T(8,1...) custom-call(bf16[3,64,256]{2,1,0:T(8,128)(2,1)S(1)} %get-tuple-element.33.v, ...), custom_call_target="tpu_custom_call" | custom-call | flops 2717908992 | bytes 9079808 | tf_op jit(solution)/shard_map/pallas_call | solution.py:27
  32.3 0.0 collective-permute-done.4.north_ref
  32.3 0.0 collective-permute-done.5.south_ref
  32.3 0.6 shard_map.106
  32.9 0.1 collective-permute-start.6
  32.9 1.9 %shard_map.107 = (bf16[32,16,128]{2,1,0:T(8,128)(2,1)S(1)}, bf16[5,16,128]{2,1,0:T(8,128)(2,1)S(1)}) custom-call(f32[4,192,256]{2,1,0:T(8,128)S(1)} %get-tuple-element.43.slot_ref, bf16[3,448,256]{2,1,0:T(8,128)(2,1)S(1)} %get-tuple-element.44.plane_ref, bf16[18,192,256]{2,1,0:T(8,128)(2,1)S(1)} %get-tuple-element.45.inner_ref, ...), custom_call_target="tpu_custom_call" | custom-call | flops 113246208 | bytes 5127168 | tf_op jit(solution)/shard_map/pallas_call | solution.py:27
  34.8 0.0 copy-start.4
  34.8 0.0 copy-start.7
  34.8 0.0 collective-permute-done.6.got_ref
  34.8 0.7 %shard_map.108.in_ref = bf16[32,32,128]{2,1,0:T(8,128)(2,1)} custom-call(f32[27,16,128]{2,1,0:T(8,128)S(1)} %get-tuple-element.41.keep_ref, bf16[27,16,128]{2,1,0:T(8,128)(2,1)S(1)} %collective-permute-done.6.got_ref, bf16[32,16,128]{2,1,0:T(8,128)(2,1)S(1)} %get-tuple-element.47.slots_ref, bf16[5,16,128]{2,1,0:T(8,128)(2,1)S(1)} %get-tuple-element.48.proj_ref), custom_call_target="tpu_custom_call" | custom-call | flops 1000 | bytes 745472 | tf_op jit(solution)/shard_map/pallas_call | solution.py:27
  35.6 2.6 %all-to-all-start.1 = ((bf16[32,32,128]{2,1,0:T(8,128)(2,1)}), bf16[32,32,128]{2,1,0:T(8,128)(2,1)S(1)}, u32[]{:S(2)}, u32[]{:S(2)}) async-start(bf16[32,32,128]{2,1,0:T(8,128)(2,1)} %shard_map.109), calls=%async_computation.1 | async-start | bytes 524288 | tf_op jit(solution)/shard_map/all_to_all | solution.py:60
  38.2 10.2 %all-to-all-done.1.recv_ref = bf16[32,32,128]{2,1,0:T(8,128)(2,1)S(1)} async-done(((bf16[32,32,128]{2,1,0:T(8,128)(2,1)}), bf16[32,32,128]{2,1,0:T(8,128)(2,1)S(1)}, u32[]{:S(2)}, u32[]{:S(2)}) %all-to-all-start.1) | async-done | bytes 262176 | tf_op jit(solution)/shard_map/all_to_all | solution.py:60
  48.4 0.7 %shard_map.110 = bf16[32,16,128]{2,1,0:T(8,128)(2,1)} custom-call(bf16[32,32,128]{2,1,0:T(8,128)(2,1)S(1)} %all-to-all-done.1.recv_ref, s32[1,1]{1,0:T(1,128)} %bitcast.9.index_ref), custom_call_target="tpu_custom_call" | custom-call | flops 1000 | bytes 393220 | tf_op jit(solution)/shard_map/pallas_call | solution.py:27
  49.1 2.7 %all-to-all-start.2 = ((bf16[32,16,128]{2,1,0:T(8,128)(2,1)}), bf16[32,16,128]{2,1,0:T(8,128)(2,1)S(1)}, u32[]{:S(2)}, u32[]{:S(2)}) async-start(bf16[32,16,128]{2,1,0:T(8,128)(2,1)} %shard_map.110), calls=%async_computation.2 | async-start | bytes 262144 | tf_op jit(solution)/shard_map/all_to_all | solution.py:60
  51.8 0.0 copy-done.4
  51.8 0.0 copy-done.7
  51.8 1.4 %shard_map.111 = (f32[128,128]{1,0:T(8,128)}, bf16[64,16,256]{2,1,0:T(8,128)(2,1)}) custom-call(bf16[32,32,128]{2,1,0:T(8,128)(2,1)S(1)} %all-to-all-done.1.recv_ref, s32[1,32]{1,0:T(1,128)S(1)} %copy-done.7, bf16[64,128]{1,0:T(8,128)(2,1)S(1)} %bitcast.26, bf16[16,64,256]{2,1,0:T(8,128)(2,1)S(1)} %get-tuple-element.49.inner_ref, ...), custom_call_target="tpu_custom_call" | custom-call | flops 4194304 | bytes 1458304 | tf_op jit(solution)/shard_map/pallas_call | solution.py:27
  53.2 7.0 %all-to-all-done.2.mine_ref = bf16[32,16,128]{2,1,0:T(8,128)(2,1)S(1)} async-done(((bf16[32,16,128]{2,1,0:T(8,128)(2,1)}), bf16[32,16,128]{2,1,0:T(8,128)(2,1)S(1)}, u32[]{:S(2)}, u32[]{:S(2)}) %all-to-all-start.2) | async-done | bytes 131104 | tf_op jit(solution)/shard_map/all_to_all | solution.py:60
  60.2 0.0 collective-permute-start.7
  60.2 1.3 %collective-permute-done.7.other_ref = bf16[32,16,128]{2,1,0:T(8,128)(2,1)S(1)} collective-permute-done((bf16[32,16,128]{2,1,0:T(8,128)(2,1)S(1)}, bf16[32,16,128]{2,1,0:T(8,128)(2,1)S(1)}, u32[]{:S(2)}, u32[]{:S(2)}) %collective-permute-start.7) | collective-permute-done | bytes 131104 | tf_op jit(solution)/shard_map/ppermute | solution.py:55
  61.6 1.1 %shard_map.112 = (f32[27,64,64]{2,1,0:T(8,128)}, f32[64,128]{1,0:T(8,128)}) custom-call(s32[1]{0:T(128)} %bitcast.parity_ref, bf16[32,16,128]{2,1,0:T(8,128)(2,1)S(1)} %all-to-all-done.2.mine_ref, bf16[32,16,128]{2,1,0:T(8,128)(2,1)S(1)} %collective-permute-done.7.other_ref), custom_call_target="tpu_custom_call" | custom-call | flops 1000 | bytes 737284 | tf_op jit(solution)/shard_map/pallas_call | solution.py:27
  (1 shorter events, 0.0 us)
Async XLA Ops:
  0.6 20.5 %copy-start.1 = (bf16[64,1,16,256]{3,2,1,0:T(8,128)(2,1)S(1)}, bf16[64,1,16,256]{3,2,1,0:T(8,128)(2,1)}, u32[]{:S(2)}) copy-start(bf16[64,1,16,256]{3,2,1,0:T(8,128)(2,1)} %param.10) | copy-start | bytes 1572868
  0.6 20.5 %collective-permute-start.1 = (bf16[64,1,16,256]{3,2,0,1:T(8,128)(2,1)}, bf16[64,1,16,256]{3,2,0,1:T(8,128)(2,1)S(1)}, u32[]{:S(2)}, u32[]{:S(2)}) collective-permute-start(bf16[64,1,16,256]{3,2,0,1:T(8,128)(2,1)} %bitcast.17), channel_id=1, source_target_pairs={{0,28},{1,29},{2,30},{3,31},{4,0},{5,1},{6,2},{7,3},{8,4},{9,5},{1... | collective-permute-start | bytes 1572872 | tf_op jit(solution)/shard_map/ppermute | solution.py:51
  4.0 17.1 %collective-permute-start = (bf16[64,1,16,256]{3,2,0,1:T(8,128)(2,1)}, bf16[64,1,16,256]{3,2,0,1:T(8,128)(2,1)S(1)}, u32[]{:S(2)}, u32[]{:S(2)}) collective-permute-start(bf16[64,1,16,256]{3,2,0,1:T(8,128)(2,1)} %bitcast.18), channel_id=1, source_target_pairs={{0,4},{1,5},{2,6},{3,7},{4,8},{5,9},{6,10},{7,11},{8,12},{9,13},{1... | collective-permute-start | bytes 1572872 | tf_op jit(solution)/shard_map/ppermute | solution.py:51
  5.7 15.4 %all-to-all-start = ((bf16[32,24,128]{2,1,0:T(8,128)(2,1)}), bf16[32,24,128]{2,1,0:T(8,128)(2,1)S(1)}, u32[]{:S(2)}, u32[]{:S(2)}) async-start(bf16[32,24,128]{2,1,0:T(8,128)(2,1)} %bitcast.27), calls=%async_computation | async-start | bytes 393216 | tf_op jit(solution)/shard_map/all_to_all | solution.py:60
  11.8 5.6 %collective-permute-start.3 = (s32[1,256]{1,0:T(1,128)}, s32[1,256]{1,0:T(1,128)S(1)}, u32[]{:S(2)}, u32[]{:S(2)}) collective-permute-start(s32[1,256]{1,0:T(1,128)} %own_cells.5), channel_id=1, source_target_pairs={{0,28},{1,29},{2,30},{3,31},{4,0},{5,1},{6,2},{7,3},{8,4},{9,5},{1... | collective-permute-start | bytes 3080 | tf_op jit(solution)/shard_map/ppermute | solution.py:51
  14.2 4.9 %collective-permute-start.2 = (s32[1,256]{1,0:T(1,128)}, s32[1,256]{1,0:T(1,128)S(1)}, u32[]{:S(2)}, u32[]{:S(2)}) collective-permute-start(s32[1,256]{1,0:T(1,128)} %own_cells.5), channel_id=1, source_target_pairs={{0,4},{1,5},{2,6},{3,7},{4,8},{5,9},{6,10},{7,11},{8,12},{9,13},{1... | collective-permute-start | bytes 3080 | tf_op jit(solution)/shard_map/ppermute | solution.py:51
  14.2 1.0 %copy-start = (bf16[64,1,16,256]{3,2,1,0:T(8,128)(2,1)S(1)}, bf16[64,1,16,256]{3,2,1,0:T(8,128)(2,1)}, u32[]{:S(2)}) copy-start(bf16[64,1,16,256]{3,2,1,0:T(8,128)(2,1)} %param.13) | copy-start | bytes 1572868
  15.3 1.0 %copy-start.2 = (bf16[27,64,64]{2,1,0:T(8,128)(2,1)S(1)}, bf16[27,64,64]{2,1,0:T(8,128)(2,1)}, u32[]{:S(2)}) copy-start(bf16[27,64,64]{2,1,0:T(8,128)(2,1)} %weight_ref.1) | copy-start | bytes 663556
  16.3 11.1 %copy-start.6 = (s32[1,256]{1,0:T(1,128)S(1)}, s32[1,256]{1,0:T(1,128)}, u32[]{:S(2)}) copy-start(s32[1,256]{1,0:T(1,128)} %own_cells.5) | copy-start | bytes 3076
  21.1 0.7 %copy-start.3 = (bf16[128,64]{0,1:T(8,128)(2,1)S(1)}, bf16[128,64]{0,1:T(8,128)(2,1)}, u32[]{:S(2)}) copy-start(bf16[128,64]{0,1:T(8,128)(2,1)} %param.11) | copy-start | bytes 49156
  21.8 0.7 %copy-start.5 = (s32[1,256]{1,0:T(1,128)S(1)}, s32[1,256]{1,0:T(1,128)}, u32[]{:S(2)}) copy-start(s32[1,256]{1,0:T(1,128)} %own_cells.5) | copy-start | bytes 3076
  23.5 8.8 %collective-permute-start.4 = (bf16[192,256]{1,0:T(8,128)(2,1)S(1)}, bf16[192,256]{1,0:T(8,128)(2,1)S(1)}, u32[]{:S(2)}, u32[]{:S(2)}) collective-permute-start(bf16[192,256]{1,0:T(8,128)(2,1)S(1)} %get-tuple-element.38), channel_id=1, source_target_pairs={{0,1},{1,2},{2,3},{3,0},{4,5},{5,6},{6,7},{7,4},{8,9},{9,10},{10,1... | collective-permute-start | bytes 294920 | tf_op jit(solution)/shard_map/ppermute | solution.py:51
  23.5 8.7 %collective-permute-start.5 = (bf16[192,256]{1,0:T(8,128)(2,1)S(1)}, bf16[192,256]{1,0:T(8,128)(2,1)S(1)}, u32[]{:S(2)}, u32[]{:S(2)}) collective-permute-start(bf16[192,256]{1,0:T(8,128)(2,1)S(1)} %get-tuple-element.39), channel_id=1, source_target_pairs={{0,3},{1,0},{2,1},{3,2},{4,7},{5,4},{6,5},{7,6},{8,11},{9,8},{10,9... | collective-permute-start | bytes 294920 | tf_op jit(solution)/shard_map/ppermute | solution.py:51
  32.9 2.0 %collective-permute-start.6 = (bf16[27,16,128]{2,1,0:T(8,128)(2,1)S(1)}, bf16[27,16,128]{2,1,0:T(8,128)(2,1)S(1)}, u32[]{:S(2)}, u32[]{:S(2)}) collective-permute-start(bf16[27,16,128]{2,1,0:T(8,128)(2,1)S(1)} %get-tuple-element.42), channel_id=1, source_target_pairs={{0,4},{4,0},{8,12},{12,8},{16,20},{20,16},{24,28},{28,24},{1,5},{5... | collective-permute-start | bytes 331784 | tf_op jit(solution)/shard_map/ppermute | solution.py:55
  34.8 17.0 %copy-start.4 = (bf16[128,64]{0,1:T(8,128)(2,1)S(1)}, bf16[128,64]{0,1:T(8,128)(2,1)}, u32[]{:S(2)}) copy-start(bf16[128,64]{0,1:T(8,128)(2,1)} %param.11) | copy-start | bytes 49156
  34.8 17.0 %copy-start.7 = (s32[1,32]{1,0:T(1,128)S(1)}, s32[1,32]{1,0:T(1,128)}, u32[]{:S(2)}) copy-start(s32[1,32]{1,0:T(1,128)} %counts_ref.1) | copy-start | bytes 388
  35.6 12.8 %all-to-all-start.1 = ((bf16[32,32,128]{2,1,0:T(8,128)(2,1)}), bf16[32,32,128]{2,1,0:T(8,128)(2,1)S(1)}, u32[]{:S(2)}, u32[]{:S(2)}) async-start(bf16[32,32,128]{2,1,0:T(8,128)(2,1)} %shard_map.109), calls=%async_computation.1 | async-start | bytes 524288 | tf_op jit(solution)/shard_map/all_to_all | solution.py:60
  49.1 11.1 %all-to-all-start.2 = ((bf16[32,16,128]{2,1,0:T(8,128)(2,1)}), bf16[32,16,128]{2,1,0:T(8,128)(2,1)S(1)}, u32[]{:S(2)}, u32[]{:S(2)}) async-start(bf16[32,16,128]{2,1,0:T(8,128)(2,1)} %shard_map.110), calls=%async_computation.2 | async-start | bytes 262144 | tf_op jit(solution)/shard_map/all_to_all | solution.py:60
  60.2 1.3 %collective-permute-start.7 = (bf16[32,16,128]{2,1,0:T(8,128)(2,1)S(1)}, bf16[32,16,128]{2,1,0:T(8,128)(2,1)S(1)}, u32[]{:S(2)}, u32[]{:S(2)}) collective-permute-start(bf16[32,16,128]{2,1,0:T(8,128)(2,1)S(1)} %all-to-all-done.2.mine_ref), channel_id=1, source_target_pairs={{0,4},{4,0},{8,12},{12,8},{16,20},{20,16},{24,28},{28,24},{1,5},{5... | collective-permute-start | bytes 393224 | tf_op jit(solution)/shard_map/ppermute | solution.py:55

commit v19 on v16

--- a/solution.py
+++ b/solution.py
@@ -171,26 +171,33 @@
     out_ref[pl.ds(2 * chans, chans)] = cot
 
 
+def planes_kernel(
+    own_ref, west_ref, east_ref, own_cells, west_cells, east_cells, turned_ref, hot_ref
+):
+    planes = ((west_ref, west_cells), (own_ref, own_cells), (east_ref, east_cells))
+    for dx, (ref, cells_ref) in enumerate(planes):
+        turned_ref[dx] = jnp.swapaxes(ref[...], 0, 1)
+        _, z = place(cells_ref, ref.shape[2])
+        hot_ref[dx] = picked_depth(z, ref.shape[2])
+
+
 def outer_kernel(
-    ndev, cap, recv_ref, own_ref, west_ref, east_ref, own_cells, west_cells, east_cells,
-    proj_t_ref, cot_ref, wf_ref, first_ref, last_ref, values_ref, hot_ref, masked, field,
+    ndev, cap, recv_ref, turned_ref, hot_ref, own_cells, west_cells, east_cells,
+    proj_t_ref, cot_ref, wf_ref, first_ref, last_ref, values_ref, masked, field,
 ):
-    chans, cy, nz = own_ref.shape
+    cy, chans, nz = cot_ref.shape
     rows = 3 * chans
     raws = rows_in(recv_ref, ndev, cap)
     ns = (0, 1, cy - 2, cy - 1)
-    planes = ((west_ref, west_cells), (own_ref, own_cells), (east_ref, east_cells))
-    for dx, (ref, cells_ref) in enumerate(planes):
+    for dx, cells_ref in enumerate((west_cells, own_cells, east_cells)):
         values = mm(proj_t_ref[...], raws[dx], NT).astype(BF16)
-        y, z = place(cells_ref, nz)
-        onehot = picked_depth(z, nz)
+        y, _ = place(cells_ref, nz)
         values_ref[dx] = values
-        hot_ref[dx] = onehot
-        painted = painted_rows(values, y, onehot, ns, masked)
-        base = turned(ref)
+        painted = painted_rows(values, y, hot_ref[dx], ns, masked)
         for n, row in enumerate(ns):
             part = painted[n * chans : (n + 1) * chans]
-            field[n, pl.ds(dx * chans, chans)] = (base[row] + part).astype(BF16)
+            base = turned_ref[dx, row].astype(F32)
+            field[n, pl.ds(dx * chans, chans)] = (base + part).astype(BF16)
     near = mm(wf_ref[pl.ds(0, 2 * rows)], field[3])
     add_to_rows(near, mm(wf_ref[pl.ds(0, rows)], field[2]), cot_ref[cy - 1], False, last_ref)
     near = mm(wf_ref[pl.ds(rows, 2 * rows)], field[0])
@@ -202,22 +209,16 @@
     return cells // nz, cells % nz
 
 
-def turned(ref):
-    return jnp.swapaxes(ref[...], 0, 1).astype(F32)
-
-
 def conv_kernel(
-    values_ref, hot_ref, own_ref, west_ref, east_ref, own_cells, west_cells, east_cells,
-    cot_ref, wf_ref, wb_ref,
+    values_ref, hot_ref, turned_ref, own_cells, west_cells, east_cells, cot_ref, wf_ref, wb_ref,
     x_ref, out_ref, total_ref, pre_ref, slot_ref, plane, acc, grads, back, masked,
 ):
     cy, chans, nz = cot_ref.shape
     rows = 3 * chans
-    planes = ((west_ref, west_cells), (own_ref, own_cells), (east_ref, east_cells))
-    for dx, (ref, cells_ref) in enumerate(planes):
+    for dx, cells_ref in enumerate((west_cells, own_cells, east_cells)):
         y, _ = place(cells_ref, nz)
         painted = painted_rows(values_ref[dx], y, hot_ref[dx], range(cy), masked)
-        field = turned(ref) + painted.reshape(cy, chans, nz)
+        field = turned_ref[dx].astype(F32) + painted.reshape(cy, chans, nz)
         x_ref[:, pl.ds(dx * chans, chans)] = field.astype(BF16)
     own = pl.ds(chans, chans)
     zeros = jnp.zeros((rows, nz), BF16)
@@ -492,11 +493,16 @@
         1000,
     )
 
-    first, last, values, hots = call(
+    turned, hots = call(
+        planes_kernel,
+        [shape((3, cy, chans, nz), BF16), shape((3, nz, slots), BF16)],
+        (*planes, *lists),
+        1000,
+    )
+    first, last, values = call(
         functools.partial(outer_kernel, ndev, cap),
-        [shape((rows, nz), BF16)] * 2
-        + [shape((3, chans, slots), BF16), shape((3, nz, slots), BF16)],
-        (recv, *planes, *lists, proj_t, cot, wf),
+        [shape((rows, nz), BF16)] * 2 + [shape((3, chans, slots), BF16)],
+        (recv, turned, hots, *lists, proj_t, cot, wf),
         4 * one,
         (pltpu.VMEM((4 * chans, slots), BF16), pltpu.VMEM((4, rows, nz), BF16)),
     )
@@ -511,7 +517,7 @@
             shape((4, rows, nz), F32),
             shape((3, (cy - 4) * chans, nz), BF16),
         ],
-        (values, hots, *planes, *lists, cot, wf, wb),
+        (values, hots, turned, *lists, cot, wf, wb),
         3 * cy * 3 * one,
         (
             pltpu.VMEM((cy + 1, rows, nz), F32),

time: 61.3 us -> 64.3 us (1.049)
  local copies, waits for them, and re-layouts: 2.08 us -> 6.45 us
  waiting for transfers between devices: 23.3 us -> 20.7 us
  starting transfers between devices: 21.1 us -> 22.2 us
    unnamed x12 -> x24, local copies, waits for them, and re-layouts: 2.08 us -> 6.45 us
    all_to_all x3, waiting for transfers between devices: 19.2 us -> 17.2 us  [exchange(): lax.all_to_all(payload.reshape(ndev, rows // ndev, width), AXES, split_ax...]
    ppermute x6, waiting for transfers between devices: 2.43 us -> 1.72 us  [send(): return lax.ppermute(block, AXES, pairs)]
    pallas_call x11 -> x12, Pallas kernels: 13.5 us -> 13.7 us  [call(): pl.pallas_call(kernel, out_shape=[jax.ShapeDtypeStruct(o.shape, o.dtype)...]
  transfers between devices with their start and end apart: 11 -> 11, of which waited for: 7 -> 5; matrix products, arithmetic and copies ran while one was open for 0% -> 0% of each run, Pallas kernels for 15% -> 15%
where the time goes in v19:
time: 64.3 us; the launch traced here: 63.8 us
  starting transfers between devices  22.2 us (35%)
  waiting for transfers between devices  20.7 us (32%)
  Pallas kernels  13.7 us (21%)
  local copies, waits for them, and re-layouts  6.45 us (10%)
  between operations  0.84 us (1%)
    all_to_all x3, waiting for transfers between devices, exchange(): lax.all_to_all(payload.reshape(ndev, rows // ndev, width), AXES, split_ax...  17.2 us
    pallas_call x12, Pallas kernels, call(): pl.pallas_call(kernel, out_shape=[jax.ShapeDtypeStruct(o.shape, o.dtype)...  13.7 us
    all_to_all x3, starting transfers between devices, exchange(): lax.all_to_all(payload.reshape(ndev, rows // ndev, width), AXES, split_ax...  11.9 us
    ppermute x6, starting transfers between devices, send(): return lax.ppermute(block, AXES, pairs)  10.2 us
    unnamed x24, local copies, waits for them, and re-layouts  6.45 us
    ppermute x2, waiting for transfers between devices, swap(): lax.ppermute(block, 'gx', [(i, i ^ 1) for i in range(lax.axis_size('gx'))])  1.73 us
    ppermute x6, waiting for transfers between devices, send(): return lax.ppermute(block, AXES, pairs)  1.72 us
  transfers between devices with their start and end apart: 11, of which 5 were waited for; matrix products, arithmetic and copies ran while one was open for 0% of the time, Pallas kernels for 15%

profile of v19, /device:TPU:0, one launch (start us, length us, event | category | flops | bytes accessed | tf_op | source)
XLA Modules:
  0.0 63.8 jit_solution(5424225383742975385)
XLA Ops:
  0.6 0.0 copy-start
  0.6 0.0 copy-start.10
  0.7 0.0 copy-start.9
  0.7 3.4 %collective-permute-start.1 = (bf16[64,1,16,256]{3,2,0,1:T(8,128)(2,1)}, bf16[64,1,16,256]{3,2,0,1:T(8,128)(2,1)S(1)}, u32[]{:S(2)}, u32[]{:S(2)}) collective-permute-start(bf16[64,1,16,256]{3,2,0,1:T(8,128)(2,1)} %bitcast.16), channel_id=1, source_target_pairs={{0,28},{1,29},{2,30},{3,31},{4,0},{5,1},{6,2},{7,3},{8,4},{9,5},{1... | collective-permute-start | bytes 1572872 | tf_op jit(solution)/shard_map/ppermute | solution.py:51
  4.0 0.0 collective-permute-start
  4.1 1.7 %shard_map.102 = bf16[768,128]{1,0:T(8,128)(2,1)} custom-call(bf16[128,128]{1,0:T(8,128)(2,1)} %rows_far.1, s32[1,32]{1,0:T(1,128)} %counts_ref.1), custom_call_target="tpu_custom_call" | custom-call | flops 8388608 | bytes 229504 | tf_op jit(solution)/shard_map/pallas_call | solution.py:27
  5.7 6.0 %all-to-all-start = ((bf16[32,24,128]{2,1,0:T(8,128)(2,1)}), bf16[32,24,128]{2,1,0:T(8,128)(2,1)S(1)}, u32[]{:S(2)}, u32[]{:S(2)}) async-start(bf16[32,24,128]{2,1,0:T(8,128)(2,1)} %bitcast.24), calls=%async_computation | async-start | bytes 393216 | tf_op jit(solution)/shard_map/all_to_all | solution.py:60
  11.8 2.5 %collective-permute-start.3 = (s32[1,256]{1,0:T(1,128)}, s32[1,256]{1,0:T(1,128)S(1)}, u32[]{:S(2)}, u32[]{:S(2)}) collective-permute-start(s32[1,256]{1,0:T(1,128)} %own_cells.7), channel_id=1, source_target_pairs={{0,28},{1,29},{2,30},{3,31},{4,0},{5,1},{6,2},{7,3},{8,4},{9,5},{1... | collective-permute-start | bytes 3080 | tf_op jit(solution)/shard_map/ppermute | solution.py:51
  14.3 0.0 collective-permute-start.2
  14.3 0.0 copy-start.5
  14.3 1.0 %copy-done.5 = bf16[64,1,16,256]{3,2,1,0:T(8,128)(2,1)S(1)} copy-done((bf16[64,1,16,256]{3,2,1,0:T(8,128)(2,1)S(1)}, bf16[64,1,16,256]{3,2,1,0:T(8,128)(2,1)}, u32[]{:S(2)}) %copy-start.5) | copy-done | bytes 524312
  15.3 0.0 copy-start.6
  15.3 1.0 %copy-done.6 = bf16[27,64,64]{2,1,0:T(8,128)(2,1)S(1)} copy-done((bf16[27,64,64]{2,1,0:T(8,128)(2,1)S(1)}, bf16[27,64,64]{2,1,0:T(8,128)(2,1)}, u32[]{:S(2)}) %copy-start.6) | copy-done | bytes 221208
  16.3 0.4 shard_map.104
  16.7 0.0 copy-start.7
  16.7 0.7 %copy-done.7 = bf16[576,192]{1,0:T(8,128)(2,1)} copy-done((bf16[576,192]{1,0:T(8,128)(2,1)}, bf16[576,192]{1,0:T(8,128)(2,1)S(1)}, u32[]{:S(2)}) %copy-start.7) | copy-done | bytes 221208
  17.4 0.0 collective-permute-done.3.east_cells
  17.4 1.7 %collective-permute-done.2.west_cells = s32[1,256]{1,0:T(1,128)S(1)} collective-permute-done((s32[1,256]{1,0:T(1,128)}, s32[1,256]{1,0:T(1,128)S(1)}, u32[]{:S(2)}, u32[]{:S(2)}) %collective-permute-start.2) | collective-permute-done | bytes 1056 | tf_op jit(solution)/shard_map/ppermute | solution.py:51
  19.2 0.0 collective-permute-done.1
  19.2 0.0 copy-start.1
  19.2 0.8 %copy-done.1 = bf16[64,1,16,256]{3,2,0,1:T(8,128)(2,1)} copy-done((bf16[64,1,16,256]{3,2,0,1:T(8,128)(2,1)}, bf16[64,1,16,256]{3,2,0,1:T(8,128)(2,1)S(1)}, u32[]{:S(2)}) %copy-start.1) | copy-done | bytes 524312
  20.0 0.0 collective-permute-done
  20.0 0.0 copy-start.3
  20.0 0.8 %copy-done.3 = bf16[64,1,16,256]{3,2,0,1:T(8,128)(2,1)} copy-done((bf16[64,1,16,256]{3,2,0,1:T(8,128)(2,1)}, bf16[64,1,16,256]{3,2,0,1:T(8,128)(2,1)S(1)}, u32[]{:S(2)}) %copy-start.3) | copy-done | bytes 524312
  20.8 0.0 copy-done
  20.8 0.0 copy-done.10
  20.8 0.0 copy-start.2
  20.8 1.0 %copy-done.2 = bf16[64,1,16,256]{3,2,0,1:T(8,128)(2,1)S(1)} copy-done((bf16[64,1,16,256]{3,2,0,1:T(8,128)(2,1)S(1)}, bf16[64,1,16,256]{3,2,0,1:T(8,128)(2,1)}, u32[]{:S(2)}) %copy-start.2) | copy-done | bytes 524312
  21.8 0.0 copy-start.4
  21.8 1.0 %copy-done.4 = bf16[64,1,16,256]{3,2,0,1:T(8,128)(2,1)S(1)} copy-done((bf16[64,1,16,256]{3,2,0,1:T(8,128)(2,1)S(1)}, bf16[64,1,16,256]{3,2,0,1:T(8,128)(2,1)}, u32[]{:S(2)}) %copy-start.4) | copy-done | bytes 524312
  22.8 0.5 shard_map.103
  23.3 0.0 all-to-all-done
  23.3 0.0 copy-start.8
  23.3 0.0 copy-done.9
  23.3 0.9 %shard_map.105 = (bf16[192,256]{1,0:T(8,128)(2,1)S(1)}, bf16[192,256]{1,0:T(8,128)(2,1)S(1)}, bf16[3,64,256]{2,1,0:T(8,128)(2,1)S(1)}) custom-call(bf16[768,128]{1,0:T(8,128)(2,1)S(1)} %bitcast.14, bf16[3,16,64,256]{3,2,1,0:T(8,128)(2,1)S(1)} %get-tuple-element.31.turned_ref, bf16[3,256,256]{2,1,0:T(8,128)(2,1)S(1)} %get-tuple-element.32.hot_ref, ...), custom_call_target="tpu_custom_call" | custom-call | flops 75497472 | bytes 3222528 | tf_op jit(solution)/shard_map/pallas_call | solution.py:27
  24.3 2.0 %collective-permute-start.4 = (bf16[192,256]{1,0:T(8,128)(2,1)S(1)}, bf16[192,256]{1,0:T(8,128)(2,1)S(1)}, u32[]{:S(2)}, u32[]{:S(2)}) collective-permute-start(bf16[192,256]{1,0:T(8,128)(2,1)S(1)} %get-tuple-element.39), channel_id=1, source_target_pairs={{0,1},{1,2},{2,3},{3,0},{4,5},{5,6},{6,7},{7,4},{8,9},{9,10},{10,1... | collective-permute-start | bytes 294920 | tf_op jit(solution)/shard_map/ppermute | solution.py:51
  26.3 2.3 %collective-permute-start.5 = (bf16[192,256]{1,0:T(8,128)(2,1)S(1)}, bf16[192,256]{1,0:T(8,128)(2,1)S(1)}, u32[]{:S(2)}, u32[]{:S(2)}) collective-permute-start(bf16[192,256]{1,0:T(8,128)(2,1)S(1)} %get-tuple-element.40), channel_id=1, source_target_pairs={{0,3},{1,0},{2,1},{3,2},{4,7},{5,4},{6,5},{7,6},{8,11},{9,8},{10,9... | collective-permute-start | bytes 294920 | tf_op jit(solution)/shard_map/ppermute | solution.py:51
  28.6 0.0 copy-done.8
  28.6 4.8 %shard_map.106 = (bf16[16,192,256]{2,1,0:T(8,128)(2,1)S(1)}, bf16[16,64,256]{2,1,0:T(8,128)(2,1)S(1)}, f32[576,192]{1,0:T(8,128)S(1)}, f32[4,64,256]{2,1,0:T(8,1...) custom-call(bf16[3,64,256]{2,1,0:T(8,128)(2,1)S(1)} %get-tuple-element.35.values_ref, ...), custom_call_target="tpu_custom_call" | custom-call | flops 2717908992 | bytes 7801856 | tf_op jit(solution)/shard_map/pallas_call | solution.py:27
  33.4 0.0 collective-permute-done.4.north_ref
  33.4 0.0 collective-permute-done.5.south_ref
  33.4 0.6 shard_map.107
  34.0 0.1 collective-permute-start.6
  34.0 0.9 %shard_map.108 = (bf16[32,16,128]{2,1,0:T(8,128)(2,1)S(1)}, bf16[5,16,128]{2,1,0:T(8,128)(2,1)S(1)}) custom-call(f32[4,192,256]{2,1,0:T(8,128)S(1)} %get-tuple-element.44.slot_ref, bf16[3,768,256]{2,1,0:T(8,128)(2,1)S(1)} %get-tuple-element.45.plane_ref, bf16[3,256,256]{2,1,0:T(8,128)(2,1)S(1)} %get-tuple-element.32.hot_ref, ...), custom_call_target="tpu_custom_call" | custom-call | flops 113246208 | bytes 3849216 | tf_op jit(solution)/shard_map/pallas_call | solution.py:27
  35.0 0.0 copy-start.11
  35.0 0.4 collective-permute-done.6.got_ref
  35.4 0.7 %shard_map.109.in_ref = bf16[32,32,128]{2,1,0:T(8,128)(2,1)} custom-call(f32[27,16,128]{2,1,0:T(8,128)S(1)} %get-tuple-element.42.keep_ref, bf16[27,16,128]{2,1,0:T(8,128)(2,1)S(1)} %collective-permute-done.6.got_ref, bf16[32,16,128]{2,1,0:T(8,128)(2,1)S(1)} %get-tuple-element.47.slots_ref, bf16[5,16,128]{2,1,0:T(8,128)(2,1)S(1)} %get-tuple-element.48.proj_ref), custom_call_target="tpu_custom_call" | custom-call | flops 1000 | bytes 745472 | tf_op jit(solution)/shard_map/pallas_call | solution.py:27
  36.1 3.2 %all-to-all-start.1 = ((bf16[32,32,128]{2,1,0:T(8,128)(2,1)}), bf16[32,32,128]{2,1,0:T(8,128)(2,1)S(1)}, u32[]{:S(2)}, u32[]{:S(2)}) async-start(bf16[32,32,128]{2,1,0:T(8,128)(2,1)} %shard_map.110), calls=%async_computation.1 | async-start | bytes 524288 | tf_op jit(solution)/shard_map/all_to_all | solution.py:60
  39.3 10.2 %all-to-all-done.1.recv_ref = bf16[32,32,128]{2,1,0:T(8,128)(2,1)S(1)} async-done(((bf16[32,32,128]{2,1,0:T(8,128)(2,1)}), bf16[32,32,128]{2,1,0:T(8,128)(2,1)S(1)}, u32[]{:S(2)}, u32[]{:S(2)}) %all-to-all-start.1) | async-done | bytes 262176 | tf_op jit(solution)/shard_map/all_to_all | solution.py:60
  49.5 0.7 %shard_map.111 = bf16[32,16,128]{2,1,0:T(8,128)(2,1)} custom-call(bf16[32,32,128]{2,1,0:T(8,128)(2,1)S(1)} %all-to-all-done.1.recv_ref, s32[1,1]{1,0:T(1,128)} %bitcast.9.index_ref), custom_call_target="tpu_custom_call" | custom-call | flops 1000 | bytes 393220 | tf_op jit(solution)/shard_map/pallas_call | solution.py:27
  50.2 2.7 %all-to-all-start.2 = ((bf16[32,16,128]{2,1,0:T(8,128)(2,1)}), bf16[32,16,128]{2,1,0:T(8,128)(2,1)S(1)}, u32[]{:S(2)}, u32[]{:S(2)}) async-start(bf16[32,16,128]{2,1,0:T(8,128)(2,1)} %shard_map.111), calls=%async_computation.2 | async-start | bytes 262144 | tf_op jit(solution)/shard_map/all_to_all | solution.py:60
  52.9 0.0 copy-done.11
  53.0 1.4 %shard_map.112 = (f32[128,128]{1,0:T(8,128)}, bf16[64,16,256]{2,1,0:T(8,128)(2,1)}) custom-call(bf16[32,32,128]{2,1,0:T(8,128)(2,1)S(1)} %all-to-all-done.1.recv_ref, s32[1,32]{1,0:T(1,128)S(1)} %copy-done.11, bf16[64,128]{1,0:T(8,128)(2,1)S(1)} %bitcast.23, bf16[16,64,256]{2,1,0:T(8,128)(2,1)S(1)} %get-tuple-element.49.inner_ref, ...), custom_call_target="tpu_custom_call" | custom-call | flops 4194304 | bytes 1458304 | tf_op jit(solution)/shard_map/pallas_call | solution.py:27
  54.3 7.0 %all-to-all-done.2.mine_ref = bf16[32,16,128]{2,1,0:T(8,128)(2,1)S(1)} async-done(((bf16[32,16,128]{2,1,0:T(8,128)(2,1)}), bf16[32,16,128]{2,1,0:T(8,128)(2,1)S(1)}, u32[]{:S(2)}, u32[]{:S(2)}) %all-to-all-start.2) | async-done | bytes 131104 | tf_op jit(solution)/shard_map/all_to_all | solution.py:60
  61.3 0.0 collective-permute-start.7
  61.3 1.3 %collective-permute-done.7.other_ref = bf16[32,16,128]{2,1,0:T(8,128)(2,1)S(1)} collective-permute-done((bf16[32,16,128]{2,1,0:T(8,128)(2,1)S(1)}, bf16[32,16,128]{2,1,0:T(8,128)(2,1)S(1)}, u32[]{:S(2)}, u32[]{:S(2)}) %collective-permute-start.7) | collective-permute-done | bytes 131104 | tf_op jit(solution)/shard_map/ppermute | solution.py:55
  62.7 1.1 %shard_map.113 = (f32[27,64,64]{2,1,0:T(8,128)}, f32[64,128]{1,0:T(8,128)}) custom-call(s32[1]{0:T(128)} %bitcast.parity_ref, bf16[32,16,128]{2,1,0:T(8,128)(2,1)S(1)} %all-to-all-done.2.mine_ref, bf16[32,16,128]{2,1,0:T(8,128)(2,1)S(1)} %collective-permute-done.7.other_ref), custom_call_target="tpu_custom_call" | custom-call | flops 1000 | bytes 737284 | tf_op jit(solution)/shard_map/pallas_call | solution.py:27
  (1 shorter events, 0.0 us)
Async XLA Ops:
  0.6 20.1 %copy-start = (bf16[64,1,16,256]{3,2,1,0:T(8,128)(2,1)S(1)}, bf16[64,1,16,256]{3,2,1,0:T(8,128)(2,1)}, u32[]{:S(2)}) copy-start(bf16[64,1,16,256]{3,2,1,0:T(8,128)(2,1)} %param.10) | copy-start | bytes 1572868
  0.6 20.1 %copy-start.10 = (s32[1,256]{1,0:T(1,128)S(1)}, s32[1,256]{1,0:T(1,128)}, u32[]{:S(2)}) copy-start(s32[1,256]{1,0:T(1,128)} %own_cells.7) | copy-start | bytes 3076
  0.7 22.7 %copy-start.9 = (bf16[128,64]{0,1:T(8,128)(2,1)S(1)}, bf16[128,64]{0,1:T(8,128)(2,1)}, u32[]{:S(2)}) copy-start(bf16[128,64]{0,1:T(8,128)(2,1)} %param.11) | copy-start | bytes 49156
  0.7 18.5 %collective-permute-start.1 = (bf16[64,1,16,256]{3,2,0,1:T(8,128)(2,1)}, bf16[64,1,16,256]{3,2,0,1:T(8,128)(2,1)S(1)}, u32[]{:S(2)}, u32[]{:S(2)}) collective-permute-start(bf16[64,1,16,256]{3,2,0,1:T(8,128)(2,1)} %bitcast.16), channel_id=1, source_target_pairs={{0,28},{1,29},{2,30},{3,31},{4,0},{5,1},{6,2},{7,3},{8,4},{9,5},{1... | collective-permute-start | bytes 1572872 | tf_op jit(solution)/shard_map/ppermute | solution.py:51
  4.0 15.9 %collective-permute-start = (bf16[64,1,16,256]{3,2,0,1:T(8,128)(2,1)}, bf16[64,1,16,256]{3,2,0,1:T(8,128)(2,1)S(1)}, u32[]{:S(2)}, u32[]{:S(2)}) collective-permute-start(bf16[64,1,16,256]{3,2,0,1:T(8,128)(2,1)} %bitcast.17), channel_id=1, source_target_pairs={{0,4},{1,5},{2,6},{3,7},{4,8},{5,9},{6,10},{7,11},{8,12},{9,13},{1... | collective-permute-start | bytes 1572872 | tf_op jit(solution)/shard_map/ppermute | solution.py:51
  5.7 17.6 %all-to-all-start = ((bf16[32,24,128]{2,1,0:T(8,128)(2,1)}), bf16[32,24,128]{2,1,0:T(8,128)(2,1)S(1)}, u32[]{:S(2)}, u32[]{:S(2)}) async-start(bf16[32,24,128]{2,1,0:T(8,128)(2,1)} %bitcast.24), calls=%async_computation | async-start | bytes 393216 | tf_op jit(solution)/shard_map/all_to_all | solution.py:60
  11.8 5.7 %collective-permute-start.3 = (s32[1,256]{1,0:T(1,128)}, s32[1,256]{1,0:T(1,128)S(1)}, u32[]{:S(2)}, u32[]{:S(2)}) collective-permute-start(s32[1,256]{1,0:T(1,128)} %own_cells.7), channel_id=1, source_target_pairs={{0,28},{1,29},{2,30},{3,31},{4,0},{5,1},{6,2},{7,3},{8,4},{9,5},{1... | collective-permute-start | bytes 3080 | tf_op jit(solution)/shard_map/ppermute | solution.py:51
  14.3 4.9 %collective-permute-start.2 = (s32[1,256]{1,0:T(1,128)}, s32[1,256]{1,0:T(1,128)S(1)}, u32[]{:S(2)}, u32[]{:S(2)}) collective-permute-start(s32[1,256]{1,0:T(1,128)} %own_cells.7), channel_id=1, source_target_pairs={{0,4},{1,5},{2,6},{3,7},{4,8},{5,9},{6,10},{7,11},{8,12},{9,13},{1... | collective-permute-start | bytes 3080 | tf_op jit(solution)/shard_map/ppermute | solution.py:51
  14.3 1.0 %copy-start.5 = (bf16[64,1,16,256]{3,2,1,0:T(8,128)(2,1)S(1)}, bf16[64,1,16,256]{3,2,1,0:T(8,128)(2,1)}, u32[]{:S(2)}) copy-start(bf16[64,1,16,256]{3,2,1,0:T(8,128)(2,1)} %param.13) | copy-start | bytes 1572868
  15.3 1.0 %copy-start.6 = (bf16[27,64,64]{2,1,0:T(8,128)(2,1)S(1)}, bf16[27,64,64]{2,1,0:T(8,128)(2,1)}, u32[]{:S(2)}) copy-start(bf16[27,64,64]{2,1,0:T(8,128)(2,1)} %weight_ref.1) | copy-start | bytes 663556
  16.7 0.7 %copy-start.7 = (bf16[576,192]{1,0:T(8,128)(2,1)}, bf16[576,192]{1,0:T(8,128)(2,1)S(1)}, u32[]{:S(2)}) copy-start(bf16[576,192]{1,0:T(8,128)(2,1)S(1)} %get-tuple-element.36.wb_ref) | copy-start | bytes 663556
  19.2 0.8 %copy-start.1 = (bf16[64,1,16,256]{3,2,0,1:T(8,128)(2,1)}, bf16[64,1,16,256]{3,2,0,1:T(8,128)(2,1)S(1)}, u32[]{:S(2)}) copy-start(bf16[64,1,16,256]{3,2,0,1:T(8,128)(2,1)S(1)} %collective-permute-done.1) | copy-start | bytes 1572868
  20.0 0.8 %copy-start.3 = (bf16[64,1,16,256]{3,2,0,1:T(8,128)(2,1)}, bf16[64,1,16,256]{3,2,0,1:T(8,128)(2,1)S(1)}, u32[]{:S(2)}) copy-start(bf16[64,1,16,256]{3,2,0,1:T(8,128)(2,1)S(1)} %collective-permute-done) | copy-start | bytes 1572868
  20.8 1.0 %copy-start.2 = (bf16[64,1,16,256]{3,2,0,1:T(8,128)(2,1)S(1)}, bf16[64,1,16,256]{3,2,0,1:T(8,128)(2,1)}, u32[]{:S(2)}) copy-start(bf16[64,1,16,256]{3,2,0,1:T(8,128)(2,1)} %copy-done.1) | copy-start | bytes 1572868
  21.8 1.0 %copy-start.4 = (bf16[64,1,16,256]{3,2,0,1:T(8,128)(2,1)S(1)}, bf16[64,1,16,256]{3,2,0,1:T(8,128)(2,1)}, u32[]{:S(2)}) copy-start(bf16[64,1,16,256]{3,2,0,1:T(8,128)(2,1)} %copy-done.3) | copy-start | bytes 1572868
  23.3 5.3 %copy-start.8 = (bf16[576,192]{1,0:T(8,128)(2,1)S(1)}, bf16[576,192]{1,0:T(8,128)(2,1)}, u32[]{:S(2)}) copy-start(bf16[576,192]{1,0:T(8,128)(2,1)} %copy-done.7) | copy-start | bytes 663556
  24.3 9.1 %collective-permute-start.4 = (bf16[192,256]{1,0:T(8,128)(2,1)S(1)}, bf16[192,256]{1,0:T(8,128)(2,1)S(1)}, u32[]{:S(2)}, u32[]{:S(2)}) collective-permute-start(bf16[192,256]{1,0:T(8,128)(2,1)S(1)} %get-tuple-element.39), channel_id=1, source_target_pairs={{0,1},{1,2},{2,3},{3,0},{4,5},{5,6},{6,7},{7,4},{8,9},{9,10},{10,1... | collective-permute-start | bytes 294920 | tf_op jit(solution)/shard_map/ppermute | solution.py:51
  26.3 7.1 %collective-permute-start.5 = (bf16[192,256]{1,0:T(8,128)(2,1)S(1)}, bf16[192,256]{1,0:T(8,128)(2,1)S(1)}, u32[]{:S(2)}, u32[]{:S(2)}) collective-permute-start(bf16[192,256]{1,0:T(8,128)(2,1)S(1)} %get-tuple-element.40), channel_id=1, source_target_pairs={{0,3},{1,0},{2,1},{3,2},{4,7},{5,4},{6,5},{7,6},{8,11},{9,8},{10,9... | collective-permute-start | bytes 294920 | tf_op jit(solution)/shard_map/ppermute | solution.py:51
  34.0 1.4 %collective-permute-start.6 = (bf16[27,16,128]{2,1,0:T(8,128)(2,1)S(1)}, bf16[27,16,128]{2,1,0:T(8,128)(2,1)S(1)}, u32[]{:S(2)}, u32[]{:S(2)}) collective-permute-start(bf16[27,16,128]{2,1,0:T(8,128)(2,1)S(1)} %get-tuple-element.43), channel_id=1, source_target_pairs={{0,4},{4,0},{8,12},{12,8},{16,20},{20,16},{24,28},{28,24},{1,5},{5... | collective-permute-start | bytes 331784 | tf_op jit(solution)/shard_map/ppermute | solution.py:55
  35.0 18.0 %copy-start.11 = (s32[1,32]{1,0:T(1,128)S(1)}, s32[1,32]{1,0:T(1,128)}, u32[]{:S(2)}) copy-start(s32[1,32]{1,0:T(1,128)} %counts_ref.1) | copy-start | bytes 388
  36.1 13.4 %all-to-all-start.1 = ((bf16[32,32,128]{2,1,0:T(8,128)(2,1)}), bf16[32,32,128]{2,1,0:T(8,128)(2,1)S(1)}, u32[]{:S(2)}, u32[]{:S(2)}) async-start(bf16[32,32,128]{2,1,0:T(8,128)(2,1)} %shard_map.110), calls=%async_computation.1 | async-start | bytes 524288 | tf_op jit(solution)/shard_map/all_to_all | solution.py:60
  50.2 11.1 %all-to-all-start.2 = ((bf16[32,16,128]{2,1,0:T(8,128)(2,1)}), bf16[32,16,128]{2,1,0:T(8,128)(2,1)S(1)}, u32[]{:S(2)}, u32[]{:S(2)}) async-start(bf16[32,16,128]{2,1,0:T(8,128)(2,1)} %shard_map.111), calls=%async_computation.2 | async-start | bytes 262144 | tf_op jit(solution)/shard_map/all_to_all | solution.py:60
  61.3 1.3 %collective-permute-start.7 = (bf16[32,16,128]{2,1,0:T(8,128)(2,1)S(1)}, bf16[32,16,128]{2,1,0:T(8,128)(2,1)S(1)}, u32[]{:S(2)}, u32[]{:S(2)}) collective-permute-start(bf16[32,16,128]{2,1,0:T(8,128)(2,1)S(1)} %all-to-all-done.2.mine_ref), channel_id=1, source_target_pairs={{0,4},{4,0},{8,12},{12,8},{16,20},{20,16},{24,28},{28,24},{1,5},{5... | collective-permute-start | bytes 393224 | tf_op jit(solution)/shard_map/ppermute | solution.py:55

commit v20 on v19

--- a/solution.py
+++ b/solution.py
@@ -11,7 +11,7 @@
 AXES = ("gx", "gy")
 F32, BF16, I32 = jnp.float32, jnp.bfloat16, jnp.int32
 LIMIT = 40 * 1024 * 1024
-ALL = 60 * 1024 * 1024
+ALL = 50 * 1024 * 1024
 NT = (((1,), (1,)), ((), ()))
 NN = (((1,), (0,)), ((), ()))
 

time: 64.3 us -> 64.4 us (level)
  local copies, waits for them, and re-layouts: 6.45 us -> 7.86 us
  waiting for transfers between devices: 20.7 us -> 19.9 us
    unnamed x24 -> x28, local copies, waits for them, and re-layouts: 6.45 us -> 7.86 us
    ppermute x6, waiting for transfers between devices: 1.72 us -> 0.93 us  [send(): return lax.ppermute(block, AXES, pairs)]
  transfers between devices with their start and end apart: 11 -> 11, of which waited for: 5 -> 5; matrix products, arithmetic and copies ran while one was open for 0% -> 0% of each run, Pallas kernels for 15% -> 14%
where the time goes in v20:
time: 64.4 us; the launch traced here: 63.8 us
  starting transfers between devices  22.2 us (34%)
  waiting for transfers between devices  19.9 us (31%)
  Pallas kernels  13.1 us (20%)
  local copies, waits for them, and re-layouts  7.86 us (12%)
  between operations  0.83 us (1%)
    all_to_all x3, waiting for transfers between devices, exchange(): lax.all_to_all(payload.reshape(ndev, rows // ndev, width), AXES, split_ax...  17.2 us
    pallas_call x12, Pallas kernels, call(): pl.pallas_call(kernel, out_shape=[jax.ShapeDtypeStruct(o.shape, o.dtype)...  13.1 us
    all_to_all x3, starting transfers between devices, exchange(): lax.all_to_all(payload.reshape(ndev, rows // ndev, width), AXES, split_ax...  12.1 us
    ppermute x6, starting transfers between devices, send(): return lax.ppermute(block, AXES, pairs)  9.97 us
    unnamed x28, local copies, waits for them, and re-layouts  7.86 us
    ppermute x2, waiting for transfers between devices, swap(): lax.ppermute(block, 'gx', [(i, i ^ 1) for i in range(lax.axis_size('gx'))])  1.72 us
  transfers between devices with their start and end apart: 11, of which 5 were waited for; matrix products, arithmetic and copies ran while one was open for 0% of the time, Pallas kernels for 14%

profile of v20, /device:TPU:0, one launch (start us, length us, event | category | flops | bytes accessed | tf_op | source)
XLA Modules:
  0.0 63.8 jit_solution(607363386585121043)
XLA Ops:
  0.6 0.0 copy-start
  0.6 0.0 copy-start.9
  0.7 3.4 %collective-permute-start.1 = (bf16[64,1,16,256]{3,2,0,1:T(8,128)(2,1)}, bf16[64,1,16,256]{3,2,0,1:T(8,128)(2,1)S(1)}, u32[]{:S(2)}, u32[]{:S(2)}) collective-permute-start(bf16[64,1,16,256]{3,2,0,1:T(8,128)(2,1)} %bitcast.16), channel_id=1, source_target_pairs={{0,28},{1,29},{2,30},{3,31},{4,0},{5,1},{6,2},{7,3},{8,4},{9,5},{1... | collective-permute-start | bytes 1572872 | tf_op jit(solution)/shard_map/ppermute | solution.py:51
  4.0 0.0 collective-permute-start
  4.0 0.0 copy-start.10
  4.0 0.8 %copy-done.10 = bf16[128,128]{1,0:T(8,128)(2,1)S(1)} copy-done((bf16[128,128]{1,0:T(8,128)(2,1)S(1)}, bf16[128,128]{1,0:T(8,128)(2,1)}, u32[]{:S(2)}) %copy-start.10) | copy-done | bytes 32792
  4.8 0.0 copy-start.12
  4.8 0.7 %copy-done.12 = s32[1,32]{1,0:T(1,128)S(1)} copy-done((s32[1,32]{1,0:T(1,128)S(1)}, s32[1,32]{1,0:T(1,128)}, u32[]{:S(2)}) %copy-start.12) | copy-done | bytes 152
  5.5 0.0 copy-start.11
  5.5 1.0 %shard_map.102 = bf16[768,128]{1,0:T(8,128)(2,1)} custom-call(bf16[128,128]{1,0:T(8,128)(2,1)S(1)} %copy-done.10, s32[1,32]{1,0:T(1,128)S(1)} %copy-done.12), custom_call_target="tpu_custom_call" | custom-call | flops 8388608 | bytes 229504 | tf_op jit(solution)/shard_map/pallas_call | solution.py:27
  6.5 6.1 %all-to-all-start = ((bf16[32,24,128]{2,1,0:T(8,128)(2,1)}), bf16[32,24,128]{2,1,0:T(8,128)(2,1)S(1)}, u32[]{:S(2)}, u32[]{:S(2)}) async-start(bf16[32,24,128]{2,1,0:T(8,128)(2,1)} %bitcast.1), calls=%async_computation | async-start | bytes 393216 | tf_op jit(solution)/shard_map/all_to_all | solution.py:60
  12.5 2.5 %collective-permute-start.3 = (s32[1,256]{1,0:T(1,128)}, s32[1,256]{1,0:T(1,128)S(1)}, u32[]{:S(2)}, u32[]{:S(2)}) collective-permute-start(s32[1,256]{1,0:T(1,128)} %own_cells.7), channel_id=1, source_target_pairs={{0,28},{1,29},{2,30},{3,31},{4,0},{5,1},{6,2},{7,3},{8,4},{9,5},{1... | collective-permute-start | bytes 3080 | tf_op jit(solution)/shard_map/ppermute | solution.py:51
  15.0 0.0 collective-permute-start.2
  15.0 0.0 copy-start.5
  15.0 1.0 %copy-done.5 = bf16[64,1,16,256]{3,2,1,0:T(8,128)(2,1)S(1)} copy-done((bf16[64,1,16,256]{3,2,1,0:T(8,128)(2,1)S(1)}, bf16[64,1,16,256]{3,2,1,0:T(8,128)(2,1)}, u32[]{:S(2)}) %copy-start.5) | copy-done | bytes 524312
  16.1 0.0 copy-start.6
  16.1 1.0 %copy-done.6 = bf16[27,64,64]{2,1,0:T(8,128)(2,1)S(1)} copy-done((bf16[27,64,64]{2,1,0:T(8,128)(2,1)S(1)}, bf16[27,64,64]{2,1,0:T(8,128)(2,1)}, u32[]{:S(2)}) %copy-start.6) | copy-done | bytes 221208
  17.1 0.4 shard_map.104
  17.5 0.0 copy-start.7
  17.5 0.7 %copy-done.7 = bf16[576,192]{1,0:T(8,128)(2,1)} copy-done((bf16[576,192]{1,0:T(8,128)(2,1)}, bf16[576,192]{1,0:T(8,128)(2,1)S(1)}, u32[]{:S(2)}) %copy-start.7) | copy-done | bytes 221208
  18.2 0.0 collective-permute-done.3.east_cells
  18.2 0.9 %collective-permute-done.2.west_cells = s32[1,256]{1,0:T(1,128)S(1)} collective-permute-done((s32[1,256]{1,0:T(1,128)}, s32[1,256]{1,0:T(1,128)S(1)}, u32[]{:S(2)}, u32[]{:S(2)}) %collective-permute-start.2) | collective-permute-done | bytes 1056 | tf_op jit(solution)/shard_map/ppermute | solution.py:51
  19.1 0.0 collective-permute-done.1
  19.1 0.0 copy-start.1
  19.1 0.8 %copy-done.1 = bf16[64,1,16,256]{3,2,0,1:T(8,128)(2,1)} copy-done((bf16[64,1,16,256]{3,2,0,1:T(8,128)(2,1)}, bf16[64,1,16,256]{3,2,0,1:T(8,128)(2,1)S(1)}, u32[]{:S(2)}) %copy-start.1) | copy-done | bytes 524312
  19.9 0.0 collective-permute-done
  19.9 0.0 copy-start.3
  19.9 0.8 %copy-done.3 = bf16[64,1,16,256]{3,2,0,1:T(8,128)(2,1)} copy-done((bf16[64,1,16,256]{3,2,0,1:T(8,128)(2,1)}, bf16[64,1,16,256]{3,2,0,1:T(8,128)(2,1)S(1)}, u32[]{:S(2)}) %copy-start.3) | copy-done | bytes 524312
  20.7 0.0 copy-done
  20.7 0.0 copy-done.11
  20.7 0.0 copy-start.2
  20.7 1.0 %copy-done.2 = bf16[64,1,16,256]{3,2,0,1:T(8,128)(2,1)S(1)} copy-done((bf16[64,1,16,256]{3,2,0,1:T(8,128)(2,1)S(1)}, bf16[64,1,16,256]{3,2,0,1:T(8,128)(2,1)}, u32[]{:S(2)}) %copy-start.2) | copy-done | bytes 524312
  21.8 0.0 copy-start.4
  21.8 1.0 %copy-done.4 = bf16[64,1,16,256]{3,2,0,1:T(8,128)(2,1)S(1)} copy-done((bf16[64,1,16,256]{3,2,0,1:T(8,128)(2,1)S(1)}, bf16[64,1,16,256]{3,2,0,1:T(8,128)(2,1)}, u32[]{:S(2)}) %copy-start.4) | copy-done | bytes 524312
  22.8 0.5 shard_map.103
  23.3 0.0 all-to-all-done
  23.3 0.0 copy-start.8
  23.3 0.0 copy-done.9
  23.3 0.9 %shard_map.105 = (bf16[192,256]{1,0:T(8,128)(2,1)S(1)}, bf16[192,256]{1,0:T(8,128)(2,1)S(1)}, bf16[3,64,256]{2,1,0:T(8,128)(2,1)S(1)}) custom-call(bf16[768,128]{1,0:T(8,128)(2,1)S(1)} %bitcast.14, bf16[3,16,64,256]{3,2,1,0:T(8,128)(2,1)S(1)} %get-tuple-element.31.turned_ref, bf16[3,256,256]{2,1,0:T(8,128)(2,1)S(1)} %get-tuple-element.32.hot_ref, ...), custom_call_target="tpu_custom_call" | custom-call | flops 75497472 | bytes 3222528 | tf_op jit(solution)/shard_map/pallas_call | solution.py:27
  24.2 1.7 %collective-permute-start.4 = (bf16[192,256]{1,0:T(8,128)(2,1)S(1)}, bf16[192,256]{1,0:T(8,128)(2,1)S(1)}, u32[]{:S(2)}, u32[]{:S(2)}) collective-permute-start(bf16[192,256]{1,0:T(8,128)(2,1)S(1)} %get-tuple-element.39), channel_id=1, source_target_pairs={{0,1},{1,2},{2,3},{3,0},{4,5},{5,6},{6,7},{7,4},{8,9},{9,10},{10,1... | collective-permute-start | bytes 294920 | tf_op jit(solution)/shard_map/ppermute | solution.py:51
  25.9 2.4 %collective-permute-start.5 = (bf16[192,256]{1,0:T(8,128)(2,1)S(1)}, bf16[192,256]{1,0:T(8,128)(2,1)S(1)}, u32[]{:S(2)}, u32[]{:S(2)}) collective-permute-start(bf16[192,256]{1,0:T(8,128)(2,1)S(1)} %get-tuple-element.40), channel_id=1, source_target_pairs={{0,3},{1,0},{2,1},{3,2},{4,7},{5,4},{6,5},{7,6},{8,11},{9,8},{10,9... | collective-permute-start | bytes 294920 | tf_op jit(solution)/shard_map/ppermute | solution.py:51
  28.4 0.0 copy-done.8
  28.4 4.8 %shard_map.106 = (bf16[16,192,256]{2,1,0:T(8,128)(2,1)S(1)}, bf16[16,64,256]{2,1,0:T(8,128)(2,1)S(1)}, f32[576,192]{1,0:T(8,128)S(1)}, f32[4,64,256]{2,1,0:T(8,1...) custom-call(bf16[3,64,256]{2,1,0:T(8,128)(2,1)S(1)} %get-tuple-element.35.values_ref, ...), custom_call_target="tpu_custom_call" | custom-call | flops 2717908992 | bytes 7801856 | tf_op jit(solution)/shard_map/pallas_call | solution.py:27
  33.2 0.0 collective-permute-done.4.north_ref
  33.2 0.0 collective-permute-done.5.south_ref
  33.2 0.6 shard_map.107
  33.8 0.1 collective-permute-start.6
  33.9 0.9 %shard_map.108 = (bf16[32,16,128]{2,1,0:T(8,128)(2,1)S(1)}, bf16[5,16,128]{2,1,0:T(8,128)(2,1)S(1)}) custom-call(f32[4,192,256]{2,1,0:T(8,128)S(1)} %get-tuple-element.44.slot_ref, bf16[3,768,256]{2,1,0:T(8,128)(2,1)S(1)} %get-tuple-element.45.plane_ref, bf16[3,256,256]{2,1,0:T(8,128)(2,1)S(1)} %get-tuple-element.32.hot_ref, ...), custom_call_target="tpu_custom_call" | custom-call | flops 113246208 | bytes 3849216 | tf_op jit(solution)/shard_map/pallas_call | solution.py:27
  34.8 0.0 copy-start.13
  34.8 0.4 collective-permute-done.6.got_ref
  35.2 0.7 %shard_map.109.in_ref = bf16[32,32,128]{2,1,0:T(8,128)(2,1)} custom-call(f32[27,16,128]{2,1,0:T(8,128)S(1)} %get-tuple-element.42.keep_ref, bf16[27,16,128]{2,1,0:T(8,128)(2,1)S(1)} %collective-permute-done.6.got_ref, bf16[32,16,128]{2,1,0:T(8,128)(2,1)S(1)} %get-tuple-element.47.slots_ref, bf16[5,16,128]{2,1,0:T(8,128)(2,1)S(1)} %get-tuple-element.48.proj_ref), custom_call_target="tpu_custom_call" | custom-call | flops 1000 | bytes 745472 | tf_op jit(solution)/shard_map/pallas_call | solution.py:27
  35.9 3.4 %all-to-all-start.1 = ((bf16[32,32,128]{2,1,0:T(8,128)(2,1)}), bf16[32,32,128]{2,1,0:T(8,128)(2,1)S(1)}, u32[]{:S(2)}, u32[]{:S(2)}) async-start(bf16[32,32,128]{2,1,0:T(8,128)(2,1)} %shard_map.110), calls=%async_computation.1 | async-start | bytes 524288 | tf_op jit(solution)/shard_map/all_to_all | solution.py:60
  39.3 10.2 %all-to-all-done.1.recv_ref = bf16[32,32,128]{2,1,0:T(8,128)(2,1)S(1)} async-done(((bf16[32,32,128]{2,1,0:T(8,128)(2,1)}), bf16[32,32,128]{2,1,0:T(8,128)(2,1)S(1)}, u32[]{:S(2)}, u32[]{:S(2)}) %all-to-all-start.1) | async-done | bytes 262176 | tf_op jit(solution)/shard_map/all_to_all | solution.py:60
  49.5 0.7 %shard_map.111 = bf16[32,16,128]{2,1,0:T(8,128)(2,1)} custom-call(bf16[32,32,128]{2,1,0:T(8,128)(2,1)S(1)} %all-to-all-done.1.recv_ref, s32[1,1]{1,0:T(1,128)} %bitcast.9.index_ref), custom_call_target="tpu_custom_call" | custom-call | flops 1000 | bytes 393220 | tf_op jit(solution)/shard_map/pallas_call | solution.py:27
  50.2 2.7 %all-to-all-start.2 = ((bf16[32,16,128]{2,1,0:T(8,128)(2,1)}), bf16[32,16,128]{2,1,0:T(8,128)(2,1)S(1)}, u32[]{:S(2)}, u32[]{:S(2)}) async-start(bf16[32,16,128]{2,1,0:T(8,128)(2,1)} %shard_map.111), calls=%async_computation.2 | async-start | bytes 262144 | tf_op jit(solution)/shard_map/all_to_all | solution.py:60
  52.9 0.0 copy-done.13
  53.0 1.4 %shard_map.112 = (f32[128,128]{1,0:T(8,128)}, bf16[64,16,256]{2,1,0:T(8,128)(2,1)}) custom-call(bf16[32,32,128]{2,1,0:T(8,128)(2,1)S(1)} %all-to-all-done.1.recv_ref, s32[1,32]{1,0:T(1,128)S(1)} %copy-done.13, bf16[64,128]{1,0:T(8,128)(2,1)S(1)} %bitcast.23, bf16[16,64,256]{2,1,0:T(8,128)(2,1)S(1)} %get-tuple-element.49.inner_ref, ...), custom_call_target="tpu_custom_call" | custom-call | flops 4194304 | bytes 1458304 | tf_op jit(solution)/shard_map/pallas_call | solution.py:27
  54.3 7.0 %all-to-all-done.2.mine_ref = bf16[32,16,128]{2,1,0:T(8,128)(2,1)S(1)} async-done(((bf16[32,16,128]{2,1,0:T(8,128)(2,1)}), bf16[32,16,128]{2,1,0:T(8,128)(2,1)S(1)}, u32[]{:S(2)}, u32[]{:S(2)}) %all-to-all-start.2) | async-done | bytes 131104 | tf_op jit(solution)/shard_map/all_to_all | solution.py:60
  61.4 0.0 collective-permute-start.7
  61.4 1.3 %collective-permute-done.7.other_ref = bf16[32,16,128]{2,1,0:T(8,128)(2,1)S(1)} collective-permute-done((bf16[32,16,128]{2,1,0:T(8,128)(2,1)S(1)}, bf16[32,16,128]{2,1,0:T(8,128)(2,1)S(1)}, u32[]{:S(2)}, u32[]{:S(2)}) %collective-permute-start.7) | collective-permute-done | bytes 131104 | tf_op jit(solution)/shard_map/ppermute | solution.py:55
  62.7 1.1 %shard_map.113 = (f32[27,64,64]{2,1,0:T(8,128)}, f32[64,128]{1,0:T(8,128)}) custom-call(s32[1]{0:T(128)} %bitcast.parity_ref, bf16[32,16,128]{2,1,0:T(8,128)(2,1)S(1)} %all-to-all-done.2.mine_ref, bf16[32,16,128]{2,1,0:T(8,128)(2,1)S(1)} %collective-permute-done.7.other_ref), custom_call_target="tpu_custom_call" | custom-call | flops 1000 | bytes 737284 | tf_op jit(solution)/shard_map/pallas_call | solution.py:27
  (1 shorter events, 0.0 us)
Async XLA Ops:
  0.6 20.1 %copy-start = (bf16[64,1,16,256]{3,2,1,0:T(8,128)(2,1)S(1)}, bf16[64,1,16,256]{3,2,1,0:T(8,128)(2,1)}, u32[]{:S(2)}) copy-start(bf16[64,1,16,256]{3,2,1,0:T(8,128)(2,1)} %param.10) | copy-start | bytes 1572868
  0.6 22.7 %copy-start.9 = (bf16[128,64]{0,1:T(8,128)(2,1)S(1)}, bf16[128,64]{0,1:T(8,128)(2,1)}, u32[]{:S(2)}) copy-start(bf16[128,64]{0,1:T(8,128)(2,1)} %param.11) | copy-start | bytes 49156
  0.7 18.5 %collective-permute-start.1 = (bf16[64,1,16,256]{3,2,0,1:T(8,128)(2,1)}, bf16[64,1,16,256]{3,2,0,1:T(8,128)(2,1)S(1)}, u32[]{:S(2)}, u32[]{:S(2)}) collective-permute-start(bf16[64,1,16,256]{3,2,0,1:T(8,128)(2,1)} %bitcast.16), channel_id=1, source_target_pairs={{0,28},{1,29},{2,30},{3,31},{4,0},{5,1},{6,2},{7,3},{8,4},{9,5},{1... | collective-permute-start | bytes 1572872 | tf_op jit(solution)/shard_map/ppermute | solution.py:51
  4.0 15.9 %collective-permute-start = (bf16[64,1,16,256]{3,2,0,1:T(8,128)(2,1)}, bf16[64,1,16,256]{3,2,0,1:T(8,128)(2,1)S(1)}, u32[]{:S(2)}, u32[]{:S(2)}) collective-permute-start(bf16[64,1,16,256]{3,2,0,1:T(8,128)(2,1)} %bitcast.17), channel_id=1, source_target_pairs={{0,4},{1,5},{2,6},{3,7},{4,8},{5,9},{6,10},{7,11},{8,12},{9,13},{1... | collective-permute-start | bytes 1572872 | tf_op jit(solution)/shard_map/ppermute | solution.py:51
  4.0 0.8 %copy-start.10 = (bf16[128,128]{1,0:T(8,128)(2,1)S(1)}, bf16[128,128]{1,0:T(8,128)(2,1)}, u32[]{:S(2)}) copy-start(bf16[128,128]{1,0:T(8,128)(2,1)} %rows_far.1) | copy-start | bytes 98308
  4.8 0.7 %copy-start.12 = (s32[1,32]{1,0:T(1,128)S(1)}, s32[1,32]{1,0:T(1,128)}, u32[]{:S(2)}) copy-start(s32[1,32]{1,0:T(1,128)} %counts_ref.1) | copy-start | bytes 388
  5.5 15.3 %copy-start.11 = (s32[1,256]{1,0:T(1,128)S(1)}, s32[1,256]{1,0:T(1,128)}, u32[]{:S(2)}) copy-start(s32[1,256]{1,0:T(1,128)} %own_cells.7) | copy-start | bytes 3076
  6.5 16.8 %all-to-all-start = ((bf16[32,24,128]{2,1,0:T(8,128)(2,1)}), bf16[32,24,128]{2,1,0:T(8,128)(2,1)S(1)}, u32[]{:S(2)}, u32[]{:S(2)}) async-start(bf16[32,24,128]{2,1,0:T(8,128)(2,1)} %bitcast.1), calls=%async_computation | async-start | bytes 393216 | tf_op jit(solution)/shard_map/all_to_all | solution.py:60
  12.5 5.7 %collective-permute-start.3 = (s32[1,256]{1,0:T(1,128)}, s32[1,256]{1,0:T(1,128)S(1)}, u32[]{:S(2)}, u32[]{:S(2)}) collective-permute-start(s32[1,256]{1,0:T(1,128)} %own_cells.7), channel_id=1, source_target_pairs={{0,28},{1,29},{2,30},{3,31},{4,0},{5,1},{6,2},{7,3},{8,4},{9,5},{1... | collective-permute-start | bytes 3080 | tf_op jit(solution)/shard_map/ppermute | solution.py:51
  15.0 4.1 %collective-permute-start.2 = (s32[1,256]{1,0:T(1,128)}, s32[1,256]{1,0:T(1,128)S(1)}, u32[]{:S(2)}, u32[]{:S(2)}) collective-permute-start(s32[1,256]{1,0:T(1,128)} %own_cells.7), channel_id=1, source_target_pairs={{0,4},{1,5},{2,6},{3,7},{4,8},{5,9},{6,10},{7,11},{8,12},{9,13},{1... | collective-permute-start | bytes 3080 | tf_op jit(solution)/shard_map/ppermute | solution.py:51
  15.0 1.0 %copy-start.5 = (bf16[64,1,16,256]{3,2,1,0:T(8,128)(2,1)S(1)}, bf16[64,1,16,256]{3,2,1,0:T(8,128)(2,1)}, u32[]{:S(2)}) copy-start(bf16[64,1,16,256]{3,2,1,0:T(8,128)(2,1)} %param.13) | copy-start | bytes 1572868
  16.1 1.0 %copy-start.6 = (bf16[27,64,64]{2,1,0:T(8,128)(2,1)S(1)}, bf16[27,64,64]{2,1,0:T(8,128)(2,1)}, u32[]{:S(2)}) copy-start(bf16[27,64,64]{2,1,0:T(8,128)(2,1)} %weight_ref.1) | copy-start | bytes 663556
  17.5 0.7 %copy-start.7 = (bf16[576,192]{1,0:T(8,128)(2,1)}, bf16[576,192]{1,0:T(8,128)(2,1)S(1)}, u32[]{:S(2)}) copy-start(bf16[576,192]{1,0:T(8,128)(2,1)S(1)} %get-tuple-element.36.wb_ref) | copy-start | bytes 663556
  19.1 0.8 %copy-start.1 = (bf16[64,1,16,256]{3,2,0,1:T(8,128)(2,1)}, bf16[64,1,16,256]{3,2,0,1:T(8,128)(2,1)S(1)}, u32[]{:S(2)}) copy-start(bf16[64,1,16,256]{3,2,0,1:T(8,128)(2,1)S(1)} %collective-permute-done.1) | copy-start | bytes 1572868
  19.9 0.8 %copy-start.3 = (bf16[64,1,16,256]{3,2,0,1:T(8,128)(2,1)}, bf16[64,1,16,256]{3,2,0,1:T(8,128)(2,1)S(1)}, u32[]{:S(2)}) copy-start(bf16[64,1,16,256]{3,2,0,1:T(8,128)(2,1)S(1)} %collective-permute-done) | copy-start | bytes 1572868
  20.7 1.0 %copy-start.2 = (bf16[64,1,16,256]{3,2,0,1:T(8,128)(2,1)S(1)}, bf16[64,1,16,256]{3,2,0,1:T(8,128)(2,1)}, u32[]{:S(2)}) copy-start(bf16[64,1,16,256]{3,2,0,1:T(8,128)(2,1)} %copy-done.1) | copy-start | bytes 1572868
  21.8 1.0 %copy-start.4 = (bf16[64,1,16,256]{3,2,0,1:T(8,128)(2,1)S(1)}, bf16[64,1,16,256]{3,2,0,1:T(8,128)(2,1)}, u32[]{:S(2)}) copy-start(bf16[64,1,16,256]{3,2,0,1:T(8,128)(2,1)} %copy-done.3) | copy-start | bytes 1572868
  23.3 5.1 %copy-start.8 = (bf16[576,192]{1,0:T(8,128)(2,1)S(1)}, bf16[576,192]{1,0:T(8,128)(2,1)}, u32[]{:S(2)}) copy-start(bf16[576,192]{1,0:T(8,128)(2,1)} %copy-done.7) | copy-start | bytes 663556
  24.2 8.9 %collective-permute-start.4 = (bf16[192,256]{1,0:T(8,128)(2,1)S(1)}, bf16[192,256]{1,0:T(8,128)(2,1)S(1)}, u32[]{:S(2)}, u32[]{:S(2)}) collective-permute-start(bf16[192,256]{1,0:T(8,128)(2,1)S(1)} %get-tuple-element.39), channel_id=1, source_target_pairs={{0,1},{1,2},{2,3},{3,0},{4,5},{5,6},{6,7},{7,4},{8,9},{9,10},{10,1... | collective-permute-start | bytes 294920 | tf_op jit(solution)/shard_map/ppermute | solution.py:51
  25.9 7.3 %collective-permute-start.5 = (bf16[192,256]{1,0:T(8,128)(2,1)S(1)}, bf16[192,256]{1,0:T(8,128)(2,1)S(1)}, u32[]{:S(2)}, u32[]{:S(2)}) collective-permute-start(bf16[192,256]{1,0:T(8,128)(2,1)S(1)} %get-tuple-element.40), channel_id=1, source_target_pairs={{0,3},{1,0},{2,1},{3,2},{4,7},{5,4},{6,5},{7,6},{8,11},{9,8},{10,9... | collective-permute-start | bytes 294920 | tf_op jit(solution)/shard_map/ppermute | solution.py:51
  33.8 1.4 %collective-permute-start.6 = (bf16[27,16,128]{2,1,0:T(8,128)(2,1)S(1)}, bf16[27,16,128]{2,1,0:T(8,128)(2,1)S(1)}, u32[]{:S(2)}, u32[]{:S(2)}) collective-permute-start(bf16[27,16,128]{2,1,0:T(8,128)(2,1)S(1)} %get-tuple-element.43), channel_id=1, source_target_pairs={{0,4},{4,0},{8,12},{12,8},{16,20},{20,16},{24,28},{28,24},{1,5},{5... | collective-permute-start | bytes 331784 | tf_op jit(solution)/shard_map/ppermute | solution.py:55
  34.8 18.2 %copy-start.13 = (s32[1,32]{1,0:T(1,128)S(1)}, s32[1,32]{1,0:T(1,128)}, u32[]{:S(2)}) copy-start(s32[1,32]{1,0:T(1,128)} %counts_ref.1) | copy-start | bytes 388
  35.9 13.6 %all-to-all-start.1 = ((bf16[32,32,128]{2,1,0:T(8,128)(2,1)}), bf16[32,32,128]{2,1,0:T(8,128)(2,1)S(1)}, u32[]{:S(2)}, u32[]{:S(2)}) async-start(bf16[32,32,128]{2,1,0:T(8,128)(2,1)} %shard_map.110), calls=%async_computation.1 | async-start | bytes 524288 | tf_op jit(solution)/shard_map/all_to_all | solution.py:60
  50.2 11.1 %all-to-all-start.2 = ((bf16[32,16,128]{2,1,0:T(8,128)(2,1)}), bf16[32,16,128]{2,1,0:T(8,128)(2,1)S(1)}, u32[]{:S(2)}, u32[]{:S(2)}) async-start(bf16[32,16,128]{2,1,0:T(8,128)(2,1)} %shard_map.111), calls=%async_computation.2 | async-start | bytes 262144 | tf_op jit(solution)/shard_map/all_to_all | solution.py:60
  61.4 1.3 %collective-permute-start.7 = (bf16[32,16,128]{2,1,0:T(8,128)(2,1)S(1)}, bf16[32,16,128]{2,1,0:T(8,128)(2,1)S(1)}, u32[]{:S(2)}, u32[]{:S(2)}) collective-permute-start(bf16[32,16,128]{2,1,0:T(8,128)(2,1)S(1)} %all-to-all-done.2.mine_ref), channel_id=1, source_target_pairs={{0,4},{4,0},{8,12},{12,8},{16,20},{20,16},{24,28},{28,24},{1,5},{5... | collective-permute-start | bytes 393224 | tf_op jit(solution)/shard_map/ppermute | solution.py:55

commit v21 on v16

--- a/solution.py
+++ b/solution.py
@@ -361,21 +361,13 @@
     proj_ref[...] = proj.astype(BF16)
 
 
-def pair_kernel(keep_ref, got_ref, slots_ref, proj_ref, send_far, sums_send, sems):
+def pair_kernel(keep_ref, got_ref, slots_ref, proj_ref, send_ref):
     full, part, _ = keep_ref.shape
     ndev, back, _ = slots_ref.shape
-    pieces = (
-        (slots_ref, send_far.at[:, pl.ds(part, back)]),
-        (proj_ref, send_far.at[pl.ds(full, ndev - full), pl.ds(0, part)]),
-        (sums_send, send_far.at[pl.ds(0, full), pl.ds(0, part)]),
-    )
-    copies = [pltpu.make_async_copy(src, dst, sems.at[n]) for n, (src, dst) in enumerate(pieces)]
-    copies[0].start()
-    copies[1].start()
-    sums_send[...] = (keep_ref[...] + got_ref[...].astype(F32)).astype(BF16)
-    copies[2].start()
-    for copy in copies:
-        copy.wait()
+    send_ref[:, pl.ds(part, back)] = slots_ref[...]
+    send_ref[pl.ds(full, ndev - full), pl.ds(0, part)] = proj_ref[...]
+    sums = keep_ref[...] + got_ref[...].astype(F32)
+    send_ref[pl.ds(0, full), pl.ds(0, part)] = sums.astype(BF16)
 
 
 def sums_kernel(ngx, ngy, full, cap, recv_ref, index_ref, sums_ref):
@@ -551,8 +543,6 @@
         [shape((ndev, part + 2 * cap, feats), BF16)],
         (keep, got, back, proj),
         1000,
-        (pltpu.VMEM((full, part, feats), BF16), pltpu.SemaphoreType.DMA((3,))),
-        far_out=(0,),
     )
     (payload,) = call(same_kernel, [payload], (payload,), 0, far=(0,), far_out=(0,), aliases={0: 0})
     recv = exchange(payload.reshape(-1, feats), ndev).reshape(payload.shape)

time: 61.3 us -> 61.3 us (level)
  no operation moved by 1% of the time
where the time goes in v21:
time: 61.3 us; the launch traced here: 60.9 us
  waiting for transfers between devices  23.3 us (38%)
  starting transfers between devices  21.1 us (34%)
  Pallas kernels  13.5 us (22%)
  local copies, waits for them, and re-layouts  2.08 us (3%)
  between operations  0.82 us (1%)
    all_to_all x3, waiting for transfers between devices, exchange(): lax.all_to_all(payload.reshape(ndev, rows // ndev, width), AXES, split_ax...  19.2 us
    pallas_call x11, Pallas kernels, call(): pl.pallas_call(kernel, out_shape=[jax.ShapeDtypeStruct(o.shape, o.dtype)...  13.5 us
    all_to_all x3, starting transfers between devices, exchange(): lax.all_to_all(payload.reshape(ndev, rows // ndev, width), AXES, split_ax...  11.3 us
    ppermute x6, starting transfers between devices, send(): return lax.ppermute(block, AXES, pairs)  9.73 us
    ppermute x6, waiting for transfers between devices, send(): return lax.ppermute(block, AXES, pairs)  2.43 us
    unnamed x12, local copies, waits for them, and re-layouts  2.08 us
    ppermute x2, waiting for transfers between devices, swap(): lax.ppermute(block, 'gx', [(i, i ^ 1) for i in range(lax.axis_size('gx'))])  1.74 us
  transfers between devices with their start and end apart: 11, of which 7 were waited for; matrix products, arithmetic and copies ran while one was open for 0% of the time, Pallas kernels for 15%

profile of v21, /device:TPU:0, one launch (start us, length us, event | category | flops | bytes accessed | tf_op | source)
XLA Modules:
  0.0 60.9 jit_solution(17770979595829832112)
XLA Ops:
  0.6 0.0 copy-start.1
  0.6 0.0 copy-start.4
  0.7 0.0 copy-start.3
  0.7 3.4 %collective-permute-start.1 = (bf16[64,1,16,256]{3,2,0,1:T(8,128)(2,1)}, bf16[64,1,16,256]{3,2,0,1:T(8,128)(2,1)S(1)}, u32[]{:S(2)}, u32[]{:S(2)}) collective-permute-start(bf16[64,1,16,256]{3,2,0,1:T(8,128)(2,1)} %bitcast.17), channel_id=1, source_target_pairs={{0,28},{1,29},{2,30},{3,31},{4,0},{5,1},{6,2},{7,3},{8,4},{9,5},{1... | collective-permute-start | bytes 1572872 | tf_op jit(solution)/shard_map/ppermute | solution.py:51
  4.0 0.0 collective-permute-start
  4.1 1.7 %shard_map.102 = bf16[768,128]{1,0:T(8,128)(2,1)} custom-call(bf16[128,128]{1,0:T(8,128)(2,1)} %rows_far.1, s32[1,32]{1,0:T(1,128)} %counts_ref.1), custom_call_target="tpu_custom_call" | custom-call | flops 8388608 | bytes 229504 | tf_op jit(solution)/shard_map/pallas_call | solution.py:27
  5.7 6.0 %all-to-all-start = ((bf16[32,24,128]{2,1,0:T(8,128)(2,1)}), bf16[32,24,128]{2,1,0:T(8,128)(2,1)S(1)}, u32[]{:S(2)}, u32[]{:S(2)}) async-start(bf16[32,24,128]{2,1,0:T(8,128)(2,1)} %bitcast.27), calls=%async_computation | async-start | bytes 393216 | tf_op jit(solution)/shard_map/all_to_all | solution.py:60
  11.8 2.5 %collective-permute-start.3 = (s32[1,256]{1,0:T(1,128)}, s32[1,256]{1,0:T(1,128)S(1)}, u32[]{:S(2)}, u32[]{:S(2)}) collective-permute-start(s32[1,256]{1,0:T(1,128)} %own_cells.5), channel_id=1, source_target_pairs={{0,28},{1,29},{2,30},{3,31},{4,0},{5,1},{6,2},{7,3},{8,4},{9,5},{1... | collective-permute-start | bytes 3080 | tf_op jit(solution)/shard_map/ppermute | solution.py:51
  14.3 0.0 collective-permute-start.2
  14.3 0.0 copy-start
  14.3 1.0 %copy-done = bf16[64,1,16,256]{3,2,1,0:T(8,128)(2,1)S(1)} copy-done((bf16[64,1,16,256]{3,2,1,0:T(8,128)(2,1)S(1)}, bf16[64,1,16,256]{3,2,1,0:T(8,128)(2,1)}, u32[]{:S(2)}) %copy-start) | copy-done | bytes 524312
  15.3 0.0 copy-start.2
  15.3 1.0 %copy-done.2 = bf16[27,64,64]{2,1,0:T(8,128)(2,1)S(1)} copy-done((bf16[27,64,64]{2,1,0:T(8,128)(2,1)S(1)}, bf16[27,64,64]{2,1,0:T(8,128)(2,1)}, u32[]{:S(2)}) %copy-start.2) | copy-done | bytes 221208
  16.3 0.4 shard_map.103
  16.7 0.6 %collective-permute-done.3.east_cells = s32[1,256]{1,0:T(1,128)S(1)} collective-permute-done((s32[1,256]{1,0:T(1,128)}, s32[1,256]{1,0:T(1,128)S(1)}, u32[]{:S(2)}, u32[]{:S(2)}) %collective-permute-start.3) | collective-permute-done | bytes 1056 | tf_op jit(solution)/shard_map/ppermute | solution.py:51
  17.4 1.8 %collective-permute-done.2.west_cells = s32[1,256]{1,0:T(1,128)S(1)} collective-permute-done((s32[1,256]{1,0:T(1,128)}, s32[1,256]{1,0:T(1,128)S(1)}, u32[]{:S(2)}, u32[]{:S(2)}) %collective-permute-start.2) | collective-permute-done | bytes 1056 | tf_op jit(solution)/shard_map/ppermute | solution.py:51
  19.2 2.0 %all-to-all-done = bf16[32,24,128]{2,1,0:T(8,128)(2,1)S(1)} async-done(((bf16[32,24,128]{2,1,0:T(8,128)(2,1)}), bf16[32,24,128]{2,1,0:T(8,128)(2,1)S(1)}, u32[]{:S(2)}, u32[]{:S(2)}) %all-to-all-start) | async-done | bytes 196640 | tf_op jit(solution)/shard_map/all_to_all | solution.py:60
  21.1 0.0 collective-permute-done.1
  21.1 0.0 collective-permute-done
  21.1 0.0 copy-done.1
  21.1 0.0 copy-done.4
  21.1 0.0 copy-done.3
  21.1 1.0 %shard_map.104 = (bf16[192,256]{1,0:T(8,128)(2,1)S(1)}, bf16[192,256]{1,0:T(8,128)(2,1)S(1)}, bf16[3,64,256]{2,1,0:T(8,128)(2,1)S(1)}, bf16[3,256,256]{2,1,0:T(8,128)(2,1)S(1)}) custom-call(bf16[768,128]{1,0:T(8,128)(2,1)S(1)} %bitcast.14, bf16[64,16,256]{2,1,0:T(8,128)(2,1)S(1)} %bitcast.19, bf16[64,16,256]{2,1,0:T(8,128)(2,1)S(1)} %bitcast.23, ...), custom_call_target="tpu_custom_call" | custom-call | flops 75497472 | bytes 3222528 | tf_op jit(solution)/shard_map/pallas_call | solution.py:27
  22.1 0.1 collective-permute-start.4
  22.2 3.8 %collective-permute-start.5 = (bf16[192,256]{1,0:T(8,128)(2,1)S(1)}, bf16[192,256]{1,0:T(8,128)(2,1)S(1)}, u32[]{:S(2)}, u32[]{:S(2)}) collective-permute-start(bf16[192,256]{1,0:T(8,128)(2,1)S(1)} %get-tuple-element.38), channel_id=1, source_target_pairs={{0,3},{1,0},{2,1},{3,2},{4,7},{5,4},{6,5},{7,6},{8,11},{9,8},{10,9... | collective-permute-start | bytes 294920 | tf_op jit(solution)/shard_map/ppermute | solution.py:51
  26.0 5.1 %shard_map.105 = (bf16[16,192,256]{2,1,0:T(8,128)(2,1)S(1)}, bf16[16,64,256]{2,1,0:T(8,128)(2,1)S(1)}, f32[576,192]{1,0:T(8,128)S(1)}, f32[4,64,256]{2,1,0:T(8,1...) custom-call(bf16[3,64,256]{2,1,0:T(8,128)(2,1)S(1)} %get-tuple-element.32.values_ref, ...), custom_call_target="tpu_custom_call" | custom-call | flops 2717908992 | bytes 7801856 | tf_op jit(solution)/shard_map/pallas_call | solution.py:27
  31.1 0.0 collective-permute-done.4.north_ref
  31.1 0.0 collective-permute-done.5.south_ref
  31.1 0.6 shard_map.106
  31.7 0.1 collective-permute-start.6
  31.7 0.9 %shard_map.107 = (bf16[32,16,128]{2,1,0:T(8,128)(2,1)S(1)}, bf16[5,16,128]{2,1,0:T(8,128)(2,1)S(1)}) custom-call(f32[4,192,256]{2,1,0:T(8,128)S(1)} %get-tuple-element.42.slot_ref, bf16[3,768,256]{2,1,0:T(8,128)(2,1)S(1)} %get-tuple-element.43.plane_ref, bf16[3,256,256]{2,1,0:T(8,128)(2,1)S(1)} %get-tuple-element.33.hot_ref, ...), custom_call_target="tpu_custom_call" | custom-call | flops 113246208 | bytes 3849216 | tf_op jit(solution)/shard_map/pallas_call | solution.py:27
  32.6 0.0 copy-start.5
  32.6 0.4 collective-permute-done.6.got_ref
  33.0 0.7 %shard_map.108.in_ref = bf16[32,32,128]{2,1,0:T(8,128)(2,1)} custom-call(f32[27,16,128]{2,1,0:T(8,128)S(1)} %get-tuple-element.40.keep_ref, bf16[27,16,128]{2,1,0:T(8,128)(2,1)S(1)} %collective-permute-done.6.got_ref, bf16[32,16,128]{2,1,0:T(8,128)(2,1)S(1)} %get-tuple-element.45.slots_ref, bf16[5,16,128]{2,1,0:T(8,128)(2,1)S(1)} %get-tuple-element.46.proj_ref), custom_call_target="tpu_custom_call" | custom-call | flops 1000 | bytes 745472 | tf_op jit(solution)/shard_map/pallas_call | solution.py:27
  33.8 2.6 %all-to-all-start.1 = ((bf16[32,32,128]{2,1,0:T(8,128)(2,1)}), bf16[32,32,128]{2,1,0:T(8,128)(2,1)S(1)}, u32[]{:S(2)}, u32[]{:S(2)}) async-start(bf16[32,32,128]{2,1,0:T(8,128)(2,1)} %shard_map.109), calls=%async_computation.1 | async-start | bytes 524288 | tf_op jit(solution)/shard_map/all_to_all | solution.py:60
  36.4 10.2 %all-to-all-done.1.recv_ref = bf16[32,32,128]{2,1,0:T(8,128)(2,1)S(1)} async-done(((bf16[32,32,128]{2,1,0:T(8,128)(2,1)}), bf16[32,32,128]{2,1,0:T(8,128)(2,1)S(1)}, u32[]{:S(2)}, u32[]{:S(2)}) %all-to-all-start.1) | async-done | bytes 262176 | tf_op jit(solution)/shard_map/all_to_all | solution.py:60
  46.6 0.7 %shard_map.110 = bf16[32,16,128]{2,1,0:T(8,128)(2,1)} custom-call(bf16[32,32,128]{2,1,0:T(8,128)(2,1)S(1)} %all-to-all-done.1.recv_ref, s32[1,1]{1,0:T(1,128)} %bitcast.9.index_ref), custom_call_target="tpu_custom_call" | custom-call | flops 1000 | bytes 393220 | tf_op jit(solution)/shard_map/pallas_call | solution.py:27
  47.3 2.7 %all-to-all-start.2 = ((bf16[32,16,128]{2,1,0:T(8,128)(2,1)}), bf16[32,16,128]{2,1,0:T(8,128)(2,1)S(1)}, u32[]{:S(2)}, u32[]{:S(2)}) async-start(bf16[32,16,128]{2,1,0:T(8,128)(2,1)} %shard_map.110), calls=%async_computation.2 | async-start | bytes 262144 | tf_op jit(solution)/shard_map/all_to_all | solution.py:60
  50.0 0.0 copy-done.5
  50.0 1.4 %shard_map.111 = (f32[128,128]{1,0:T(8,128)}, bf16[64,16,256]{2,1,0:T(8,128)(2,1)}) custom-call(bf16[32,32,128]{2,1,0:T(8,128)(2,1)S(1)} %all-to-all-done.1.recv_ref, s32[1,32]{1,0:T(1,128)S(1)} %copy-done.5, bf16[64,128]{1,0:T(8,128)(2,1)S(1)} %bitcast.26, bf16[16,64,256]{2,1,0:T(8,128)(2,1)S(1)} %get-tuple-element.47.inner_ref, ...), custom_call_target="tpu_custom_call" | custom-call | flops 4194304 | bytes 1458304 | tf_op jit(solution)/shard_map/pallas_call | solution.py:27
  51.4 7.0 %all-to-all-done.2.mine_ref = bf16[32,16,128]{2,1,0:T(8,128)(2,1)S(1)} async-done(((bf16[32,16,128]{2,1,0:T(8,128)(2,1)}), bf16[32,16,128]{2,1,0:T(8,128)(2,1)S(1)}, u32[]{:S(2)}, u32[]{:S(2)}) %all-to-all-start.2) | async-done | bytes 131104 | tf_op jit(solution)/shard_map/all_to_all | solution.py:60
  58.4 0.0 collective-permute-start.7
  58.4 1.3 %collective-permute-done.7.other_ref = bf16[32,16,128]{2,1,0:T(8,128)(2,1)S(1)} collective-permute-done((bf16[32,16,128]{2,1,0:T(8,128)(2,1)S(1)}, bf16[32,16,128]{2,1,0:T(8,128)(2,1)S(1)}, u32[]{:S(2)}, u32[]{:S(2)}) %collective-permute-start.7) | collective-permute-done | bytes 131104 | tf_op jit(solution)/shard_map/ppermute | solution.py:55
  59.8 1.1 %shard_map.112 = (f32[27,64,64]{2,1,0:T(8,128)}, f32[64,128]{1,0:T(8,128)}) custom-call(s32[1]{0:T(128)} %bitcast.parity_ref, bf16[32,16,128]{2,1,0:T(8,128)(2,1)S(1)} %all-to-all-done.2.mine_ref, bf16[32,16,128]{2,1,0:T(8,128)(2,1)S(1)} %collective-permute-done.7.other_ref), custom_call_target="tpu_custom_call" | custom-call | flops 1000 | bytes 737284 | tf_op jit(solution)/shard_map/pallas_call | solution.py:27
  (1 shorter events, 0.0 us)
Async XLA Ops:
  0.6 20.5 %copy-start.1 = (bf16[64,1,16,256]{3,2,1,0:T(8,128)(2,1)S(1)}, bf16[64,1,16,256]{3,2,1,0:T(8,128)(2,1)}, u32[]{:S(2)}) copy-start(bf16[64,1,16,256]{3,2,1,0:T(8,128)(2,1)} %param.10) | copy-start | bytes 1572868
  0.6 20.5 %copy-start.4 = (s32[1,256]{1,0:T(1,128)S(1)}, s32[1,256]{1,0:T(1,128)}, u32[]{:S(2)}) copy-start(s32[1,256]{1,0:T(1,128)} %own_cells.5) | copy-start | bytes 3076
  0.7 20.5 %copy-start.3 = (bf16[128,64]{0,1:T(8,128)(2,1)S(1)}, bf16[128,64]{0,1:T(8,128)(2,1)}, u32[]{:S(2)}) copy-start(bf16[128,64]{0,1:T(8,128)(2,1)} %param.11) | copy-start | bytes 49156
  0.7 20.5 %collective-permute-start.1 = (bf16[64,1,16,256]{3,2,0,1:T(8,128)(2,1)}, bf16[64,1,16,256]{3,2,0,1:T(8,128)(2,1)S(1)}, u32[]{:S(2)}, u32[]{:S(2)}) collective-permute-start(bf16[64,1,16,256]{3,2,0,1:T(8,128)(2,1)} %bitcast.17), channel_id=1, source_target_pairs={{0,28},{1,29},{2,30},{3,31},{4,0},{5,1},{6,2},{7,3},{8,4},{9,5},{1... | collective-permute-start | bytes 1572872 | tf_op jit(solution)/shard_map/ppermute | solution.py:51
  4.0 17.1 %collective-permute-start = (bf16[64,1,16,256]{3,2,0,1:T(8,128)(2,1)}, bf16[64,1,16,256]{3,2,0,1:T(8,128)(2,1)S(1)}, u32[]{:S(2)}, u32[]{:S(2)}) collective-permute-start(bf16[64,1,16,256]{3,2,0,1:T(8,128)(2,1)} %bitcast.18), channel_id=1, source_target_pairs={{0,4},{1,5},{2,6},{3,7},{4,8},{5,9},{6,10},{7,11},{8,12},{9,13},{1... | collective-permute-start | bytes 1572872 | tf_op jit(solution)/shard_map/ppermute | solution.py:51
  5.7 15.4 %all-to-all-start = ((bf16[32,24,128]{2,1,0:T(8,128)(2,1)}), bf16[32,24,128]{2,1,0:T(8,128)(2,1)S(1)}, u32[]{:S(2)}, u32[]{:S(2)}) async-start(bf16[32,24,128]{2,1,0:T(8,128)(2,1)} %bitcast.27), calls=%async_computation | async-start | bytes 393216 | tf_op jit(solution)/shard_map/all_to_all | solution.py:60
  11.8 5.6 %collective-permute-start.3 = (s32[1,256]{1,0:T(1,128)}, s32[1,256]{1,0:T(1,128)S(1)}, u32[]{:S(2)}, u32[]{:S(2)}) collective-permute-start(s32[1,256]{1,0:T(1,128)} %own_cells.5), channel_id=1, source_target_pairs={{0,28},{1,29},{2,30},{3,31},{4,0},{5,1},{6,2},{7,3},{8,4},{9,5},{1... | collective-permute-start | bytes 3080 | tf_op jit(solution)/shard_map/ppermute | solution.py:51
  14.3 4.9 %collective-permute-start.2 = (s32[1,256]{1,0:T(1,128)}, s32[1,256]{1,0:T(1,128)S(1)}, u32[]{:S(2)}, u32[]{:S(2)}) collective-permute-start(s32[1,256]{1,0:T(1,128)} %own_cells.5), channel_id=1, source_target_pairs={{0,4},{1,5},{2,6},{3,7},{4,8},{5,9},{6,10},{7,11},{8,12},{9,13},{1... | collective-permute-start | bytes 3080 | tf_op jit(solution)/shard_map/ppermute | solution.py:51
  14.3 1.0 %copy-start = (bf16[64,1,16,256]{3,2,1,0:T(8,128)(2,1)S(1)}, bf16[64,1,16,256]{3,2,1,0:T(8,128)(2,1)}, u32[]{:S(2)}) copy-start(bf16[64,1,16,256]{3,2,1,0:T(8,128)(2,1)} %param.13) | copy-start | bytes 1572868
  15.3 1.0 %copy-start.2 = (bf16[27,64,64]{2,1,0:T(8,128)(2,1)S(1)}, bf16[27,64,64]{2,1,0:T(8,128)(2,1)}, u32[]{:S(2)}) copy-start(bf16[27,64,64]{2,1,0:T(8,128)(2,1)} %weight_ref.1) | copy-start | bytes 663556
  22.1 8.9 %collective-permute-start.4 = (bf16[192,256]{1,0:T(8,128)(2,1)S(1)}, bf16[192,256]{1,0:T(8,128)(2,1)S(1)}, u32[]{:S(2)}, u32[]{:S(2)}) collective-permute-start(bf16[192,256]{1,0:T(8,128)(2,1)S(1)} %get-tuple-element.37), channel_id=1, source_target_pairs={{0,1},{1,2},{2,3},{3,0},{4,5},{5,6},{6,7},{7,4},{8,9},{9,10},{10,1... | collective-permute-start | bytes 294920 | tf_op jit(solution)/shard_map/ppermute | solution.py:51
  22.2 8.9 %collective-permute-start.5 = (bf16[192,256]{1,0:T(8,128)(2,1)S(1)}, bf16[192,256]{1,0:T(8,128)(2,1)S(1)}, u32[]{:S(2)}, u32[]{:S(2)}) collective-permute-start(bf16[192,256]{1,0:T(8,128)(2,1)S(1)} %get-tuple-element.38), channel_id=1, source_target_pairs={{0,3},{1,0},{2,1},{3,2},{4,7},{5,4},{6,5},{7,6},{8,11},{9,8},{10,9... | collective-permute-start | bytes 294920 | tf_op jit(solution)/shard_map/ppermute | solution.py:51
  31.7 1.4 %collective-permute-start.6 = (bf16[27,16,128]{2,1,0:T(8,128)(2,1)S(1)}, bf16[27,16,128]{2,1,0:T(8,128)(2,1)S(1)}, u32[]{:S(2)}, u32[]{:S(2)}) collective-permute-start(bf16[27,16,128]{2,1,0:T(8,128)(2,1)S(1)} %get-tuple-element.41), channel_id=1, source_target_pairs={{0,4},{4,0},{8,12},{12,8},{16,20},{20,16},{24,28},{28,24},{1,5},{5... | collective-permute-start | bytes 331784 | tf_op jit(solution)/shard_map/ppermute | solution.py:55
  32.6 17.4 %copy-start.5 = (s32[1,32]{1,0:T(1,128)S(1)}, s32[1,32]{1,0:T(1,128)}, u32[]{:S(2)}) copy-start(s32[1,32]{1,0:T(1,128)} %counts_ref.1) | copy-start | bytes 388
  33.8 12.8 %all-to-all-start.1 = ((bf16[32,32,128]{2,1,0:T(8,128)(2,1)}), bf16[32,32,128]{2,1,0:T(8,128)(2,1)S(1)}, u32[]{:S(2)}, u32[]{:S(2)}) async-start(bf16[32,32,128]{2,1,0:T(8,128)(2,1)} %shard_map.109), calls=%async_computation.1 | async-start | bytes 524288 | tf_op jit(solution)/shard_map/all_to_all | solution.py:60
  47.3 11.1 %all-to-all-start.2 = ((bf16[32,16,128]{2,1,0:T(8,128)(2,1)}), bf16[32,16,128]{2,1,0:T(8,128)(2,1)S(1)}, u32[]{:S(2)}, u32[]{:S(2)}) async-start(bf16[32,16,128]{2,1,0:T(8,128)(2,1)} %shard_map.110), calls=%async_computation.2 | async-start | bytes 262144 | tf_op jit(solution)/shard_map/all_to_all | solution.py:60
  58.4 1.3 %collective-permute-start.7 = (bf16[32,16,128]{2,1,0:T(8,128)(2,1)S(1)}, bf16[32,16,128]{2,1,0:T(8,128)(2,1)S(1)}, u32[]{:S(2)}, u32[]{:S(2)}) collective-permute-start(bf16[32,16,128]{2,1,0:T(8,128)(2,1)S(1)} %all-to-all-done.2.mine_ref), channel_id=1, source_target_pairs={{0,4},{4,0},{8,12},{12,8},{16,20},{20,16},{24,28},{28,24},{1,5},{5... | collective-permute-start | bytes 393224 | tf_op jit(solution)/shard_map/ppermute | solution.py:55

commit v22 on v16

--- a/solution.py
+++ b/solution.py
@@ -292,7 +292,7 @@
 
 
 def edge_kernel(
-    part, parity_ref, pre_ref, total_ref, north_ref, south_ref, x_ref, cot_ref,
+    part, parity_ref, pre_ref, total_ref, south_ref, north_ref, x_ref, cot_ref,
     out_ref, grads_ref, keep_ref, give_ref, total, sums,
 ):
     cy, chans, nz = cot_ref.shape
@@ -500,7 +500,7 @@
         4 * one,
         (pltpu.VMEM((4 * chans, slots), BF16), pltpu.VMEM((4, rows, nz), BF16)),
     )
-    south, north = move(first, 0, -1), move(last, 0, 1)
+    north, south = move(last, 0, 1), move(first, 0, -1)
     x_all, out_rows, total, pre_edge, slot_edge, plane = call(
         conv_kernel,
         [
@@ -534,7 +534,7 @@
             shape((full, part, feats), F32),
             shape((full, part, feats), BF16),
         ],
-        (parity, pre_edge, total, north, south, x_all, cot),
+        (parity, pre_edge, total, south, north, x_all, cot),
         6 * one,
         (pltpu.VMEM((9 * chans, rows), F32), pltpu.VMEM((full, 2, part, feats), F32)),
         scalar=(0,),

time: 61.3 us -> 62.2 us (1.015)
  waiting for transfers between devices: 23.3 us -> 24.7 us
    ppermute x6, starting transfers between devices: 9.73 us -> 8.14 us  [send(): return lax.ppermute(block, AXES, pairs)]
    ppermute x6, waiting for transfers between devices: 2.43 us -> 3.75 us  [send(): return lax.ppermute(block, AXES, pairs)]
    all_to_all x3, starting transfers between devices: 11.3 us -> 12.5 us  [exchange(): lax.all_to_all(payload.reshape(ndev, rows // ndev, width), AXES, split_ax...]
  transfers between devices with their start and end apart: 11 -> 11, of which waited for: 7 -> 8; matrix products, arithmetic and copies ran while one was open for 0% -> 0% of each run, Pallas kernels for 15% -> 15%
where the time goes in v22:
time: 62.2 us; the launch traced here: 61.7 us
  waiting for transfers between devices  24.7 us (40%)
  starting transfers between devices  20.7 us (33%)
  Pallas kernels  13.5 us (22%)
  local copies, waits for them, and re-layouts  2.08 us (3%)
  between operations  0.82 us (1%)
    all_to_all x3, waiting for transfers between devices, exchange(): lax.all_to_all(payload.reshape(ndev, rows // ndev, width), AXES, split_ax...  19.2 us
    pallas_call x11, Pallas kernels, call(): pl.pallas_call(kernel, out_shape=[jax.ShapeDtypeStruct(o.shape, o.dtype)...  13.5 us
    all_to_all x3, starting transfers between devices, exchange(): lax.all_to_all(payload.reshape(ndev, rows // ndev, width), AXES, split_ax...  12.5 us
    ppermute x6, starting transfers between devices, send(): return lax.ppermute(block, AXES, pairs)  8.14 us
    ppermute x6, waiting for transfers between devices, send(): return lax.ppermute(block, AXES, pairs)  3.75 us
    unnamed x12, local copies, waits for them, and re-layouts  2.08 us
    ppermute x2, waiting for transfers between devices, swap(): lax.ppermute(block, 'gx', [(i, i ^ 1) for i in range(lax.axis_size('gx'))])  1.74 us
  transfers between devices with their start and end apart: 11, of which 8 were waited for; matrix products, arithmetic and copies ran while one was open for 0% of the time, Pallas kernels for 15%

profile of v22, /device:TPU:0, one launch (start us, length us, event | category | flops | bytes accessed | tf_op | source)
XLA Modules:
  0.0 61.7 jit_solution(1431340178385995351)
XLA Ops:
  0.6 0.0 copy-start.1
  0.6 0.0 copy-start.4
  0.7 0.0 copy-start.3
  0.7 3.4 %collective-permute-start.1 = (bf16[64,1,16,256]{3,2,0,1:T(8,128)(2,1)}, bf16[64,1,16,256]{3,2,0,1:T(8,128)(2,1)S(1)}, u32[]{:S(2)}, u32[]{:S(2)}) collective-permute-start(bf16[64,1,16,256]{3,2,0,1:T(8,128)(2,1)} %bitcast.17), channel_id=1, source_target_pairs={{0,28},{1,29},{2,30},{3,31},{4,0},{5,1},{6,2},{7,3},{8,4},{9,5},{1... | collective-permute-start | bytes 1572872 | tf_op jit(solution)/shard_map/ppermute | solution.py:51
  4.0 0.0 collective-permute-start
  4.1 1.7 %shard_map.102 = bf16[768,128]{1,0:T(8,128)(2,1)} custom-call(bf16[128,128]{1,0:T(8,128)(2,1)} %rows_far.1, s32[1,32]{1,0:T(1,128)} %counts_ref.1), custom_call_target="tpu_custom_call" | custom-call | flops 8388608 | bytes 229504 | tf_op jit(solution)/shard_map/pallas_call | solution.py:27
  5.7 6.0 %all-to-all-start = ((bf16[32,24,128]{2,1,0:T(8,128)(2,1)}), bf16[32,24,128]{2,1,0:T(8,128)(2,1)S(1)}, u32[]{:S(2)}, u32[]{:S(2)}) async-start(bf16[32,24,128]{2,1,0:T(8,128)(2,1)} %bitcast.27), calls=%async_computation | async-start | bytes 393216 | tf_op jit(solution)/shard_map/all_to_all | solution.py:60
  11.8 2.5 %collective-permute-start.3 = (s32[1,256]{1,0:T(1,128)}, s32[1,256]{1,0:T(1,128)S(1)}, u32[]{:S(2)}, u32[]{:S(2)}) collective-permute-start(s32[1,256]{1,0:T(1,128)} %own_cells.5), channel_id=1, source_target_pairs={{0,28},{1,29},{2,30},{3,31},{4,0},{5,1},{6,2},{7,3},{8,4},{9,5},{1... | collective-permute-start | bytes 3080 | tf_op jit(solution)/shard_map/ppermute | solution.py:51
  14.3 0.0 collective-permute-start.2
  14.3 0.0 copy-start
  14.3 1.0 %copy-done = bf16[64,1,16,256]{3,2,1,0:T(8,128)(2,1)S(1)} copy-done((bf16[64,1,16,256]{3,2,1,0:T(8,128)(2,1)S(1)}, bf16[64,1,16,256]{3,2,1,0:T(8,128)(2,1)}, u32[]{:S(2)}) %copy-start) | copy-done | bytes 524312
  15.3 0.0 copy-start.2
  15.3 1.0 %copy-done.2 = bf16[27,64,64]{2,1,0:T(8,128)(2,1)S(1)} copy-done((bf16[27,64,64]{2,1,0:T(8,128)(2,1)S(1)}, bf16[27,64,64]{2,1,0:T(8,128)(2,1)}, u32[]{:S(2)}) %copy-start.2) | copy-done | bytes 221208
  16.3 0.4 shard_map.103
  16.7 0.6 %collective-permute-done.3.east_cells = s32[1,256]{1,0:T(1,128)S(1)} collective-permute-done((s32[1,256]{1,0:T(1,128)}, s32[1,256]{1,0:T(1,128)S(1)}, u32[]{:S(2)}, u32[]{:S(2)}) %collective-permute-start.3) | collective-permute-done | bytes 1056 | tf_op jit(solution)/shard_map/ppermute | solution.py:51
  17.4 1.8 %collective-permute-done.2.west_cells = s32[1,256]{1,0:T(1,128)S(1)} collective-permute-done((s32[1,256]{1,0:T(1,128)}, s32[1,256]{1,0:T(1,128)S(1)}, u32[]{:S(2)}, u32[]{:S(2)}) %collective-permute-start.2) | collective-permute-done | bytes 1056 | tf_op jit(solution)/shard_map/ppermute | solution.py:51
  19.2 2.0 %all-to-all-done = bf16[32,24,128]{2,1,0:T(8,128)(2,1)S(1)} async-done(((bf16[32,24,128]{2,1,0:T(8,128)(2,1)}), bf16[32,24,128]{2,1,0:T(8,128)(2,1)S(1)}, u32[]{:S(2)}, u32[]{:S(2)}) %all-to-all-start) | async-done | bytes 196640 | tf_op jit(solution)/shard_map/all_to_all | solution.py:60
  21.1 0.0 collective-permute-done.1
  21.1 0.0 collective-permute-done
  21.1 0.0 copy-done.1
  21.1 0.0 copy-done.4
  21.1 0.0 copy-done.3
  21.1 1.0 %shard_map.104 = (bf16[192,256]{1,0:T(8,128)(2,1)S(1)}, bf16[192,256]{1,0:T(8,128)(2,1)S(1)}, bf16[3,64,256]{2,1,0:T(8,128)(2,1)S(1)}, bf16[3,256,256]{2,1,0:T(8,128)(2,1)S(1)}) custom-call(bf16[768,128]{1,0:T(8,128)(2,1)S(1)} %bitcast.14, bf16[64,16,256]{2,1,0:T(8,128)(2,1)S(1)} %bitcast.19, bf16[64,16,256]{2,1,0:T(8,128)(2,1)S(1)} %bitcast.23, ...), custom_call_target="tpu_custom_call" | custom-call | flops 75497472 | bytes 3222528 | tf_op jit(solution)/shard_map/pallas_call | solution.py:27
  22.1 2.3 %collective-permute-start.4 = (bf16[192,256]{1,0:T(8,128)(2,1)S(1)}, bf16[192,256]{1,0:T(8,128)(2,1)S(1)}, u32[]{:S(2)}, u32[]{:S(2)}) collective-permute-start(bf16[192,256]{1,0:T(8,128)(2,1)S(1)} %get-tuple-element.37), channel_id=1, source_target_pairs={{0,3},{1,0},{2,1},{3,2},{4,7},{5,4},{6,5},{7,6},{8,11},{9,8},{10,9... | collective-permute-start | bytes 294920 | tf_op jit(solution)/shard_map/ppermute | solution.py:51
  24.4 0.0 collective-permute-start.5
  24.4 5.1 %shard_map.105 = (bf16[16,192,256]{2,1,0:T(8,128)(2,1)S(1)}, bf16[16,64,256]{2,1,0:T(8,128)(2,1)S(1)}, f32[576,192]{1,0:T(8,128)S(1)}, f32[4,64,256]{2,1,0:T(8,1...) custom-call(bf16[3,64,256]{2,1,0:T(8,128)(2,1)S(1)} %get-tuple-element.32.values_ref, ...), custom_call_target="tpu_custom_call" | custom-call | flops 2717908992 | bytes 7801856 | tf_op jit(solution)/shard_map/pallas_call | solution.py:27
  29.5 0.0 collective-permute-done.4.south_ref
  29.5 1.3 %collective-permute-done.5.north_ref = bf16[192,256]{1,0:T(8,128)(2,1)S(1)} collective-permute-done((bf16[192,256]{1,0:T(8,128)(2,1)S(1)}, bf16[192,256]{1,0:T(8,128)(2,1)S(1)}, u32[]{:S(2)}, u32[]{:S(2)}) %collective-permute-start.5) | collective-permute-done | bytes 98336 | tf_op jit(solution)/shard_map/ppermute | solution.py:51
  30.8 0.6 shard_map.106
  31.4 0.1 collective-permute-start.6
  31.4 0.9 %shard_map.107 = (bf16[32,16,128]{2,1,0:T(8,128)(2,1)S(1)}, bf16[5,16,128]{2,1,0:T(8,128)(2,1)S(1)}) custom-call(f32[4,192,256]{2,1,0:T(8,128)S(1)} %get-tuple-element.42.slot_ref, bf16[3,768,256]{2,1,0:T(8,128)(2,1)S(1)} %get-tuple-element.43.plane_ref, bf16[3,256,256]{2,1,0:T(8,128)(2,1)S(1)} %get-tuple-element.33.hot_ref, ...), custom_call_target="tpu_custom_call" | custom-call | flops 113246208 | bytes 3849216 | tf_op jit(solution)/shard_map/pallas_call | solution.py:27
  32.3 0.0 copy-start.5
  32.4 0.4 collective-permute-done.6.got_ref
  32.7 0.7 %shard_map.108.in_ref = bf16[32,32,128]{2,1,0:T(8,128)(2,1)} custom-call(f32[27,16,128]{2,1,0:T(8,128)S(1)} %get-tuple-element.40.keep_ref, bf16[27,16,128]{2,1,0:T(8,128)(2,1)S(1)} %collective-permute-done.6.got_ref, bf16[32,16,128]{2,1,0:T(8,128)(2,1)S(1)} %get-tuple-element.45.slots_ref, bf16[5,16,128]{2,1,0:T(8,128)(2,1)S(1)} %get-tuple-element.46.proj_ref), custom_call_target="tpu_custom_call" | custom-call | flops 1000 | bytes 745472 | tf_op jit(solution)/shard_map/pallas_call | solution.py:27
  33.5 3.7 %all-to-all-start.1 = ((bf16[32,32,128]{2,1,0:T(8,128)(2,1)}), bf16[32,32,128]{2,1,0:T(8,128)(2,1)S(1)}, u32[]{:S(2)}, u32[]{:S(2)}) async-start(bf16[32,32,128]{2,1,0:T(8,128)(2,1)} %shard_map.109), calls=%async_computation.1 | async-start | bytes 524288 | tf_op jit(solution)/shard_map/all_to_all | solution.py:60
  37.2 10.2 %all-to-all-done.1.recv_ref = bf16[32,32,128]{2,1,0:T(8,128)(2,1)S(1)} async-done(((bf16[32,32,128]{2,1,0:T(8,128)(2,1)}), bf16[32,32,128]{2,1,0:T(8,128)(2,1)S(1)}, u32[]{:S(2)}, u32[]{:S(2)}) %all-to-all-start.1) | async-done | bytes 262176 | tf_op jit(solution)/shard_map/all_to_all | solution.py:60
  47.4 0.7 %shard_map.110 = bf16[32,16,128]{2,1,0:T(8,128)(2,1)} custom-call(bf16[32,32,128]{2,1,0:T(8,128)(2,1)S(1)} %all-to-all-done.1.recv_ref, s32[1,1]{1,0:T(1,128)} %bitcast.9.index_ref), custom_call_target="tpu_custom_call" | custom-call | flops 1000 | bytes 393220 | tf_op jit(solution)/shard_map/pallas_call | solution.py:27
  48.2 2.7 %all-to-all-start.2 = ((bf16[32,16,128]{2,1,0:T(8,128)(2,1)}), bf16[32,16,128]{2,1,0:T(8,128)(2,1)S(1)}, u32[]{:S(2)}, u32[]{:S(2)}) async-start(bf16[32,16,128]{2,1,0:T(8,128)(2,1)} %shard_map.110), calls=%async_computation.2 | async-start | bytes 262144 | tf_op jit(solution)/shard_map/all_to_all | solution.py:60
  50.9 0.0 copy-done.5
  50.9 1.4 %shard_map.111 = (f32[128,128]{1,0:T(8,128)}, bf16[64,16,256]{2,1,0:T(8,128)(2,1)}) custom-call(bf16[32,32,128]{2,1,0:T(8,128)(2,1)S(1)} %all-to-all-done.1.recv_ref, s32[1,32]{1,0:T(1,128)S(1)} %copy-done.5, bf16[64,128]{1,0:T(8,128)(2,1)S(1)} %bitcast.26, bf16[16,64,256]{2,1,0:T(8,128)(2,1)S(1)} %get-tuple-element.47.inner_ref, ...), custom_call_target="tpu_custom_call" | custom-call | flops 4194304 | bytes 1458304 | tf_op jit(solution)/shard_map/pallas_call | solution.py:27
  52.3 7.0 %all-to-all-done.2.mine_ref = bf16[32,16,128]{2,1,0:T(8,128)(2,1)S(1)} async-done(((bf16[32,16,128]{2,1,0:T(8,128)(2,1)}), bf16[32,16,128]{2,1,0:T(8,128)(2,1)S(1)}, u32[]{:S(2)}, u32[]{:S(2)}) %all-to-all-start.2) | async-done | bytes 131104 | tf_op jit(solution)/shard_map/all_to_all | solution.py:60
  59.3 0.0 collective-permute-start.7
  59.3 1.3 %collective-permute-done.7.other_ref = bf16[32,16,128]{2,1,0:T(8,128)(2,1)S(1)} collective-permute-done((bf16[32,16,128]{2,1,0:T(8,128)(2,1)S(1)}, bf16[32,16,128]{2,1,0:T(8,128)(2,1)S(1)}, u32[]{:S(2)}, u32[]{:S(2)}) %collective-permute-start.7) | collective-permute-done | bytes 131104 | tf_op jit(solution)/shard_map/ppermute | solution.py:55
  60.6 1.1 %shard_map.112 = (f32[27,64,64]{2,1,0:T(8,128)}, f32[64,128]{1,0:T(8,128)}) custom-call(s32[1]{0:T(128)} %bitcast.parity_ref, bf16[32,16,128]{2,1,0:T(8,128)(2,1)S(1)} %all-to-all-done.2.mine_ref, bf16[32,16,128]{2,1,0:T(8,128)(2,1)S(1)} %collective-permute-done.7.other_ref), custom_call_target="tpu_custom_call" | custom-call | flops 1000 | bytes 737284 | tf_op jit(solution)/shard_map/pallas_call | solution.py:27
  (1 shorter events, 0.0 us)
Async XLA Ops:
  0.6 20.5 %copy-start.1 = (bf16[64,1,16,256]{3,2,1,0:T(8,128)(2,1)S(1)}, bf16[64,1,16,256]{3,2,1,0:T(8,128)(2,1)}, u32[]{:S(2)}) copy-start(bf16[64,1,16,256]{3,2,1,0:T(8,128)(2,1)} %param.10) | copy-start | bytes 1572868
  0.6 20.5 %copy-start.4 = (s32[1,256]{1,0:T(1,128)S(1)}, s32[1,256]{1,0:T(1,128)}, u32[]{:S(2)}) copy-start(s32[1,256]{1,0:T(1,128)} %own_cells.5) | copy-start | bytes 3076
  0.7 20.5 %copy-start.3 = (bf16[128,64]{0,1:T(8,128)(2,1)S(1)}, bf16[128,64]{0,1:T(8,128)(2,1)}, u32[]{:S(2)}) copy-start(bf16[128,64]{0,1:T(8,128)(2,1)} %param.11) | copy-start | bytes 49156
  0.7 20.5 %collective-permute-start.1 = (bf16[64,1,16,256]{3,2,0,1:T(8,128)(2,1)}, bf16[64,1,16,256]{3,2,0,1:T(8,128)(2,1)S(1)}, u32[]{:S(2)}, u32[]{:S(2)}) collective-permute-start(bf16[64,1,16,256]{3,2,0,1:T(8,128)(2,1)} %bitcast.17), channel_id=1, source_target_pairs={{0,28},{1,29},{2,30},{3,31},{4,0},{5,1},{6,2},{7,3},{8,4},{9,5},{1... | collective-permute-start | bytes 1572872 | tf_op jit(solution)/shard_map/ppermute | solution.py:51
  4.0 17.1 %collective-permute-start = (bf16[64,1,16,256]{3,2,0,1:T(8,128)(2,1)}, bf16[64,1,16,256]{3,2,0,1:T(8,128)(2,1)S(1)}, u32[]{:S(2)}, u32[]{:S(2)}) collective-permute-start(bf16[64,1,16,256]{3,2,0,1:T(8,128)(2,1)} %bitcast.18), channel_id=1, source_target_pairs={{0,4},{1,5},{2,6},{3,7},{4,8},{5,9},{6,10},{7,11},{8,12},{9,13},{1... | collective-permute-start | bytes 1572872 | tf_op jit(solution)/shard_map/ppermute | solution.py:51
  5.7 15.4 %all-to-all-start = ((bf16[32,24,128]{2,1,0:T(8,128)(2,1)}), bf16[32,24,128]{2,1,0:T(8,128)(2,1)S(1)}, u32[]{:S(2)}, u32[]{:S(2)}) async-start(bf16[32,24,128]{2,1,0:T(8,128)(2,1)} %bitcast.27), calls=%async_computation | async-start | bytes 393216 | tf_op jit(solution)/shard_map/all_to_all | solution.py:60
  11.8 5.6 %collective-permute-start.3 = (s32[1,256]{1,0:T(1,128)}, s32[1,256]{1,0:T(1,128)S(1)}, u32[]{:S(2)}, u32[]{:S(2)}) collective-permute-start(s32[1,256]{1,0:T(1,128)} %own_cells.5), channel_id=1, source_target_pairs={{0,28},{1,29},{2,30},{3,31},{4,0},{5,1},{6,2},{7,3},{8,4},{9,5},{1... | collective-permute-start | bytes 3080 | tf_op jit(solution)/shard_map/ppermute | solution.py:51
  14.3 4.9 %collective-permute-start.2 = (s32[1,256]{1,0:T(1,128)}, s32[1,256]{1,0:T(1,128)S(1)}, u32[]{:S(2)}, u32[]{:S(2)}) collective-permute-start(s32[1,256]{1,0:T(1,128)} %own_cells.5), channel_id=1, source_target_pairs={{0,4},{1,5},{2,6},{3,7},{4,8},{5,9},{6,10},{7,11},{8,12},{9,13},{1... | collective-permute-start | bytes 3080 | tf_op jit(solution)/shard_map/ppermute | solution.py:51
  14.3 1.0 %copy-start = (bf16[64,1,16,256]{3,2,1,0:T(8,128)(2,1)S(1)}, bf16[64,1,16,256]{3,2,1,0:T(8,128)(2,1)}, u32[]{:S(2)}) copy-start(bf16[64,1,16,256]{3,2,1,0:T(8,128)(2,1)} %param.13) | copy-start | bytes 1572868
  15.3 1.0 %copy-start.2 = (bf16[27,64,64]{2,1,0:T(8,128)(2,1)S(1)}, bf16[27,64,64]{2,1,0:T(8,128)(2,1)}, u32[]{:S(2)}) copy-start(bf16[27,64,64]{2,1,0:T(8,128)(2,1)} %weight_ref.1) | copy-start | bytes 663556
  22.1 7.3 %collective-permute-start.4 = (bf16[192,256]{1,0:T(8,128)(2,1)S(1)}, bf16[192,256]{1,0:T(8,128)(2,1)S(1)}, u32[]{:S(2)}, u32[]{:S(2)}) collective-permute-start(bf16[192,256]{1,0:T(8,128)(2,1)S(1)} %get-tuple-element.37), channel_id=1, source_target_pairs={{0,3},{1,0},{2,1},{3,2},{4,7},{5,4},{6,5},{7,6},{8,11},{9,8},{10,9... | collective-permute-start | bytes 294920 | tf_op jit(solution)/shard_map/ppermute | solution.py:51
  24.4 6.4 %collective-permute-start.5 = (bf16[192,256]{1,0:T(8,128)(2,1)S(1)}, bf16[192,256]{1,0:T(8,128)(2,1)S(1)}, u32[]{:S(2)}, u32[]{:S(2)}) collective-permute-start(bf16[192,256]{1,0:T(8,128)(2,1)S(1)} %get-tuple-element.38), channel_id=1, source_target_pairs={{0,1},{1,2},{2,3},{3,0},{4,5},{5,6},{6,7},{7,4},{8,9},{9,10},{10,1... | collective-permute-start | bytes 294920 | tf_op jit(solution)/shard_map/ppermute | solution.py:51
  31.4 1.4 %collective-permute-start.6 = (bf16[27,16,128]{2,1,0:T(8,128)(2,1)S(1)}, bf16[27,16,128]{2,1,0:T(8,128)(2,1)S(1)}, u32[]{:S(2)}, u32[]{:S(2)}) collective-permute-start(bf16[27,16,128]{2,1,0:T(8,128)(2,1)S(1)} %get-tuple-element.41), channel_id=1, source_target_pairs={{0,4},{4,0},{8,12},{12,8},{16,20},{20,16},{24,28},{28,24},{1,5},{5... | collective-permute-start | bytes 331784 | tf_op jit(solution)/shard_map/ppermute | solution.py:55
  32.3 18.5 %copy-start.5 = (s32[1,32]{1,0:T(1,128)S(1)}, s32[1,32]{1,0:T(1,128)}, u32[]{:S(2)}) copy-start(s32[1,32]{1,0:T(1,128)} %counts_ref.1) | copy-start | bytes 388
  33.5 13.9 %all-to-all-start.1 = ((bf16[32,32,128]{2,1,0:T(8,128)(2,1)}), bf16[32,32,128]{2,1,0:T(8,128)(2,1)S(1)}, u32[]{:S(2)}, u32[]{:S(2)}) async-start(bf16[32,32,128]{2,1,0:T(8,128)(2,1)} %shard_map.109), calls=%async_computation.1 | async-start | bytes 524288 | tf_op jit(solution)/shard_map/all_to_all | solution.py:60
  48.2 11.1 %all-to-all-start.2 = ((bf16[32,16,128]{2,1,0:T(8,128)(2,1)}), bf16[32,16,128]{2,1,0:T(8,128)(2,1)S(1)}, u32[]{:S(2)}, u32[]{:S(2)}) async-start(bf16[32,16,128]{2,1,0:T(8,128)(2,1)} %shard_map.110), calls=%async_computation.2 | async-start | bytes 262144 | tf_op jit(solution)/shard_map/all_to_all | solution.py:60
  59.3 1.3 %collective-permute-start.7 = (bf16[32,16,128]{2,1,0:T(8,128)(2,1)S(1)}, bf16[32,16,128]{2,1,0:T(8,128)(2,1)S(1)}, u32[]{:S(2)}, u32[]{:S(2)}) collective-permute-start(bf16[32,16,128]{2,1,0:T(8,128)(2,1)S(1)} %all-to-all-done.2.mine_ref), channel_id=1, source_target_pairs={{0,4},{4,0},{8,12},{12,8},{16,20},{20,16},{24,28},{28,24},{1,5},{5... | collective-permute-start | bytes 393224 | tf_op jit(solution)/shard_map/ppermute | solution.py:55
